TPU v7x, 32 devices: a whole 2x2x4 slice. The times are simulated.
32 devices in a mesh: mol: 2 (over y), row: 4 (over x, core), col: 4 (over z).
Axes of the slice: x: 2, y: 2, z: 4, core: 2. Of those that a mesh axis runs over, the one named last changes fastest.
Arguments:
- amplitudes: float32 [2048, 1536], P(('mol', 'row', 'col')), parts along dimension 0, may hold values from -6 to 6
- integrals: float32 [3072, 1536], P(('mol', 'row'), 'col'), parts along dimension 0, may hold values from -0.21875 to 0.21875
- amp_mask: int32 [64, 16], P('mol'), parts along dimension 0, may hold values 0 or 1
- int_mask: int32 [32, 16], P('mol'), parts along dimension 0, may hold values 0 or 1
- owner_map: int32 [32], P('mol'), parts along dimension 0, may hold values from 0 to 15, each once
Outputs:
- ladder: float32 [2048, 1536], P(('mol', 'row', 'col')), parts along dimension 0
There are 2 independent parts, one for each index of `mol`. A program takes and returns all parts, laid end to end along the dimension named above; each array names one. Nothing has to cross between parts.
Inputs may be any that keep to these rules, and one draw needn't show every extreme that they name: `owner_map`: each pair tile number stands in exactly one slot.
All inputs are finite; a program needn't handle non-finite values.
Results may differ from a plain program's by a relative error of at most 0.00007.
Values sent between devices are 32-bit elements; how exact they have to be, the bound alone decides.
No kernel may reach another device: no remote copies, remote signals or barrier semaphores. Data moves between devices by JAX's collectives and lax.ppermute only.
A program may use at most 128 MiB of HBM per device.

v0:
```python
import jax
import jax.numpy as jnp
from jax import lax
from jax.sharding import PartitionSpec as P

TB = 96
OTB = 32


def on_device(amplitudes, integrals, amp_mask, int_mask, owner_map):
    rows_dev, pairs = amplitudes.shape
    tiles = pairs // TB
    occ_tiles = rows_dev // OTB
    block = lax.axis_index(("row", "col"))
    amp_local = lax.dynamic_slice_in_dim(amp_mask, block * occ_tiles, occ_tiles, 0).astype(
        jnp.float32
    )
    masked = (amplitudes.reshape(occ_tiles, OTB, tiles, TB) * amp_local[:, None, :, None]).reshape(
        rows_dev, pairs
    )
    slab_rows, slab_cols = integrals.shape
    row_tiles = slab_rows // TB
    col_tiles = slab_cols // TB
    numbers = jnp.arange(tiles, dtype=jnp.int32)
    mask_rows = lax.dynamic_slice_in_dim(
        int_mask, lax.axis_index("row") * row_tiles, row_tiles, 0
    ).astype(jnp.float32)
    slot_tiles = lax.dynamic_slice_in_dim(
        owner_map, lax.axis_index("col") * col_tiles, col_tiles, 0
    )
    select = (slot_tiles[:, None] == numbers[None, :]).astype(jnp.float32)
    mask_local = jnp.dot(
        mask_rows, select.T, precision=lax.Precision.HIGHEST, preferred_element_type=jnp.float32
    )
    integral_local = (
        integrals.reshape(row_tiles, TB, col_tiles, TB) * mask_local[:, None, :, None]
    ).reshape(slab_rows, slab_cols)
    hits = owner_map[:, None] == numbers[None, :]
    inverse = jnp.sum(jnp.where(hits, numbers[:, None], jnp.int32(0)), axis=0)
    slab = lax.all_to_all(masked, "row", split_axis=1, concat_axis=0, tiled=True)
    partial_value = jnp.dot(
        slab,
        lax.all_gather(integral_local, "col", axis=1, tiled=True),
        precision=lax.Precision.HIGHEST,
        preferred_element_type=jnp.float32,
    )
    summed = lax.psum_scatter(partial_value, "row", scatter_dimension=1, tiled=True)
    stored = lax.all_to_all(summed, "row", split_axis=0, concat_axis=1, tiled=True)
    return jnp.take(stored.reshape(rows_dev, tiles, TB), inverse, axis=1).reshape(rows_dev, pairs)


def solution(mesh):
    placed = (
        P(("mol", "row", "col"), None),
        P(("mol", "row"), "col"),
        P("mol", None),
        P("mol", None),
        P("mol"),
    )
    return jax.shard_map(
        on_device,
        mesh=mesh,
        in_specs=placed,
        out_specs=P(("mol", "row", "col"), None),
        check_vma=False,
    )
```

profile of v0, /device:TPU:0, one launch (start us, length us, event | category | flops | bytes accessed | tf_op | source)
XLA Modules:
  0.0 116.0 jit_solution(5732767805239521581)
XLA Ops:
  6.5 0.0 copy-start
  6.5 0.8 dynamic_slice.11
  7.3 0.9 fusion
  8.2 0.2 mul.38
  8.4 0.0 copy-start.2
  8.4 0.4 mul.39
  8.8 0.0 copy-done.1
  8.8 0.9 mul.40
  9.7 0.0 all-gather.2.cloned.1.call-update
  9.7 0.0 reduce-scatter.2.cloned.1.call-start
  9.8 0.1 constant_dynamic-slice_fusion
  9.9 0.1 copy.30
  9.9 0.1 mul.34
  10.1 0.2 mul.35
  10.3 0.0 copy-done.2
  10.4 11.5 %all_to_all.35 = f32[64,4,384]{2,0,1:T(8,128)S(1)} all-to-all(f32[64,4,384]{2,0,1:T(8,128)S(1)} %bitcast.21), channel_id=1, replica_groups=mesh['mol'=2,'row'=4,'col'=4] {'row'}, dimensions={1} | all-to-all | bytes 786432 | tf_op jit(solution)/shard_map/all_to_all | solution.py:40
  21.8 41.2 %all-gather.2.cloned.1.call-done = f32[384,1536]{1,0:T(8,128)} async-done(((f32[384,384]{1,0:T(8,128)}), f32[384,1536]{1,0:T(8,128)}) %all-gather.2.cloned.1.call-update) | async-done | bytes 2359312 | tf_op jit(solution)/shard_map/all_gather | solution.py:43
  63.0 5.5 %fusion.6 = f32[256,1536]{1,0:T(8,128)} fusion(f32[256,384]{1,0:T(8,128)S(1)} %bitcast.20, f32[384,1536]{1,0:T(8,128)} %all-gather.2.cloned.1.call-done), kind=kOutput, calls=%fused_computation.17 | convolution fusion | flops 1811939328 | bytes 4325376 | tf_op jit(solution)/shard_map/dot_general | solution.py:41
  68.5 0.0 reduce-scatter.2.cloned.1.call-update
  68.6 0.1 select_reduce_fusion
  68.7 0.1 broadcast_in_dim.35
  68.7 0.1 broadcast_in_dim.36
  68.8 26.9 %reduce-scatter.2.cloned.1.call-done = f32[256,384]{1,0:T(8,128)} async-done(((f32[256,1536]{1,0:T(8,128)}), f32[256,384]{1,0:T(8,128)}) %reduce-scatter.2.cloned.1.call-update) | async-done | bytes 393232 | tf_op jit(solution)/shard_map/reduce_scatter | solution.py:47
  95.7 3.5 %all-to-all-start.1 = ((f32[4,64,384]{2,1,0:T(8,128)}), f32[4,64,384]{2,1,0:T(8,128)S(1)}, u32[]{:S(2)}, u32[]{:S(2)}) async-start(f32[4,64,384]{2,1,0:T(8,128)} %bitcast.23), calls=%async_computation.2 | async-start | bytes 786432 | tf_op jit(solution)/shard_map/all_to_all | solution.py:48
  99.2 7.4 %all-to-all-done.1 = f32[4,64,384]{2,1,0:T(8,128)S(1)} async-done(((f32[4,64,384]{2,1,0:T(8,128)}), f32[4,64,384]{2,1,0:T(8,128)S(1)}, u32[]{:S(2)}, u32[]{:S(2)}) %all-to-all-start.1) | async-done | bytes 393248 | tf_op jit(solution)/shard_map/all_to_all | solution.py:48
  106.6 0.3 copy.27
  106.9 0.2 reshape.41
  107.1 0.2 copy.28
  107.3 0.6 gather_fusion
  107.9 0.3 copy.29
  108.2 0.2 gather.7
  108.4 0.8 broadcast_select_fusion
  (11 shorter events, 0.1 us)
Async XLA Ops:
  6.5 3.2 %copy-start = (s32[32,16]{0,1:T(8,128)S(1)}, s32[32,16]{0,1:T(8,128)}, u32[]{:S(2)}) copy-start(s32[32,16]{0,1:T(8,128)} %param.7) | copy-start | bytes 6148
  6.5 2.3 %copy-start.1 = (f32[384,384]{1,0:T(8,128)S(1)}, f32[384,384]{1,0:T(8,128)}, u32[]{:S(2)}) copy-start(f32[384,384]{1,0:T(8,128)} %param.6) | copy-start | bytes 1769476
  6.5 56.5 %all-gather.2.cloned.1.call-start = ((), (), s32[]{:S(2)}) async-start(), calls=%async_computation.3 | async-start | bytes 2949120 | tf_op jit(solution)/shard_map/all_gather | solution.py:43
  8.4 1.9 %copy-start.2 = (f32[64,1536]{1,0:T(8,128)S(1)}, f32[64,1536]{1,0:T(8,128)}, u32[]{:S(2)}) copy-start(f32[64,1536]{1,0:T(8,128)} %param.5) | copy-start | bytes 1179652
  9.7 86.0 %reduce-scatter.2.cloned.1.call-start = ((), (), s32[]{:S(2)}) async-start(), calls=%async_computation.4 | async-start | bytes 1966080 | tf_op jit(solution)/shard_map/reduce_scatter | solution.py:47
  63.0 5.5 %copy-start.3 = (s32[16]{0:T(128)S(1)}, s32[16]{0:T(128)}, u32[]{:S(2)}) copy-start(s32[16]{0:T(128)} %param.9) | copy-start | bytes 196
  95.7 10.9 %all-to-all-start.1 = ((f32[4,64,384]{2,1,0:T(8,128)}), f32[4,64,384]{2,1,0:T(8,128)S(1)}, u32[]{:S(2)}, u32[]{:S(2)}) async-start(f32[4,64,384]{2,1,0:T(8,128)} %bitcast.23), calls=%async_computation.2 | async-start | bytes 786432 | tf_op jit(solution)/shard_map/all_to_all | solution.py:48
Sparse Core Ops, SparseCore 0:
  9.8 53.1 all-gather.1
  68.7 27.0 reduce-scatter.1
where the time goes:
time: 116 us
  waiting for transfers between devices  75.5 us (65%)
  between operations  13.5 us (12%)
  blocking collectives  11.5 us (10%)
  matrix products  6.39 us (6%)
  local copies, waits for them, and re-layouts  3.84 us (3%)
  starting transfers between devices  3.5 us (3%)
  other arithmetic  1.83 us (2%)
    all_gather x1, waiting for transfers between devices, on_device(): lax.all_gather(integral_local, 'col', axis=1, tiled=True)  41.2 us
    reduce_scatter x1, waiting for transfers between devices, on_device(): lax.psum_scatter(partial_value, 'row', scatter_dimension=1, tiled=True)  26.9 us
    all_to_all x1, blocking collectives, on_device(): lax.all_to_all(masked, 'row', split_axis=1, concat_axis=0, tiled=True)  11.5 us
    all_to_all x1, waiting for transfers between devices, on_device(): lax.all_to_all(summed, 'row', split_axis=0, concat_axis=1, tiled=True)  7.38 us
    dot_general x1, matrix products, on_device(): jnp.dot(slab, lax.all_gather(integral_local, 'col', axis=1, tiled=True),...  5.52 us
    all_to_all x1, starting transfers between devices, on_device(): lax.all_to_all(summed, 'row', split_axis=0, concat_axis=1, tiled=True)  3.46 us
  transfers between devices with their start and end apart: 3, of which 3 were waited for; matrix products, arithmetic and copies ran while one was open for 1% of the time, Pallas kernels for 0%

commit v1 on v0

v1 whole, which is shorter than its diff:
```python
import functools

import jax
import jax.numpy as jnp
from jax import lax
from jax.experimental import pallas as pl
from jax.experimental.pallas import tpu as pltpu
from jax.sharding import PartitionSpec as P

TB = 96
OTB = 32
GROUP = 384
PER = GROUP // TB

VMEM = pl.BlockSpec(memory_space=pltpu.VMEM)
SMEM = pl.BlockSpec(memory_space=pltpu.SMEM)


def split(x):
    high = x.astype(jnp.bfloat16)
    low = (x - high.astype(jnp.float32)).astype(jnp.bfloat16)
    return high, low


def lane_mask(values, lane_tile):
    out = jnp.zeros(lane_tile.shape, jnp.float32)
    for i, v in enumerate(values):
        out = jnp.where(lane_tile == i, v.astype(jnp.float32), out)
    return out


def prepare_kernel(n_row, n_col, *refs):
    place, amp_mask = refs[0], refs[1]
    pieces = refs[2 : 2 + n_row]
    high_ref, low_ref = refs[2 + n_row :]
    r, c = place[0], place[1]
    rows, depth = pieces[0].shape
    k_tiles = depth // TB
    occ = rows // OTB
    lane_tile = lax.broadcasted_iota(jnp.int32, (OTB, depth), 1) // TB
    for d in range(n_row):
        block = (r ^ d) * n_col + c
        for o in range(occ):
            mask = lane_mask(
                [amp_mask[block * occ + o, r * k_tiles + k] for k in range(k_tiles)], lane_tile
            )
            high, low = split(pieces[d][o * OTB : (o + 1) * OTB, :] * mask)
            at = pl.ds(d * rows + o * OTB, OTB)
            high_ref[at, :] = high
            low_ref[at, :] = low


def multiply_kernel(n_row, step, side, place, int_mask, owner, high, low, *refs):
    n_in = 2 if side == 0 else 1
    blocks, outs = refs[:n_in], refs[n_in:]
    r, c, n_col = place[0], place[1], place[2]
    depth, width = blocks[0].shape
    k_tiles, c_tiles = depth // TB, width // TB
    if side == 0:
        from_left = c >= step
        source = jnp.where(from_left, c - step, c + step)
    else:
        source = c + step * side
    valid = (source >= 0) & (source < n_col)

    @pl.when(valid)
    def _():
        lane_tile = lax.broadcasted_iota(jnp.int32, (TB, width), 1) // TB
        tiles = [owner[source * c_tiles + i] for i in range(c_tiles)]
        highs, lows = [], []
        for k in range(k_tiles):
            mask = lane_mask([int_mask[r * k_tiles + k, t] for t in tiles], lane_tile)
            at = pl.ds(k * TB, TB)
            if side == 0:
                piece = jnp.where(from_left, blocks[0][at, :], blocks[1][at, :])
            else:
                piece = blocks[0][at, :]
            h, l = split(piece * mask)
            highs.append(h)
            lows.append(l)
        b_high = jnp.concatenate(highs, axis=0)
        b_low = jnp.concatenate(lows, axis=0)
        rows = outs[0].shape[0]
        for d in range(n_row):
            at = pl.ds(d * rows, rows)
            dot = functools.partial(jnp.dot, preferred_element_type=jnp.float32)
            outs[d][...] = dot(high[at, :], b_high) + (
                dot(high[at, :], b_low) + dot(low[at, :], b_high)
            )


def finish_kernel(n_row, slots, place, owner, *refs):
    out = refs[-1]
    c, n_col = place[1], place[2]
    rows, width = refs[0].shape
    lane_tile = lax.broadcasted_iota(jnp.int32, (rows, GROUP), 1) // TB
    for s, (step, side) in enumerate(slots):
        shares = refs[s * n_row : (s + 1) * n_row]
        if side == 0:
            source = jnp.where(c >= step, c - step, c + step)
        else:
            source = c + step * side

        @pl.when((source >= 0) & (source < n_col))
        def _(shares=shares, source=source):
            for g in range(width // GROUP):
                at = pl.ds(g * GROUP, GROUP)
                total = shares[0][:, at]
                for share in shares[1:]:
                    total = total + share[:, at]
                for i in range(PER):
                    tile = owner[source * (width // TB) + g * PER + i]
                    home, spot = tile // PER, tile % PER
                    turned = pltpu.roll(total, ((spot - i + PER) % PER) * TB, 1)
                    to = pl.ds(pl.multiple_of(home * GROUP, GROUP), GROUP)
                    out[:, to] = jnp.where(lane_tile == spot, turned, out[:, to])


def cost(flops, moved):
    return pl.CostEstimate(flops=int(flops), bytes_accessed=int(moved), transcendentals=0)


def on_device(n_row, n_col, amplitudes, integrals, amp_mask, int_mask, owner_map):
    rows, pairs = amplitudes.shape
    depth, width = integrals.shape
    r, c = lax.axis_index("row"), lax.axis_index("col")
    place = jnp.stack([r, c, jnp.int32(n_col)]).astype(jnp.int32)

    def shift(x, by):
        pairs_ = [(i, i + by) for i in range(n_col) if 0 <= i + by < n_col]
        return lax.ppermute(x, "col", pairs_)

    def swap(x, d):
        return lax.ppermute(x, "row", [(i, i ^ d) for i in range(n_row)])

    right, left = shift(integrals, 1), shift(integrals, -1)

    def columns(d):
        return lax.dynamic_slice_in_dim(amplitudes, (r ^ d) * depth, depth, 1)

    pieces = [columns(0)] + [swap(columns(d), d) for d in range(1, n_row)]
    total = n_row * rows
    high, low = pl.pallas_call(
        functools.partial(prepare_kernel, n_row, n_col),
        out_shape=[jax.ShapeDtypeStruct((total, depth), jnp.bfloat16)] * 2,
        in_specs=[SMEM, SMEM] + [VMEM] * n_row,
        out_specs=[VMEM] * 2,
        compiler_params=pltpu.CompilerParams(vmem_limit_bytes=32 * 2**20),
        cost_estimate=cost(total * depth * 4, total * depth * 8),
        name="prepare",
    )(place, amp_mask, *pieces)

    def multiply(step, side, *blocks):
        return pl.pallas_call(
            functools.partial(multiply_kernel, n_row, step, side),
            out_shape=[jax.ShapeDtypeStruct((rows, width), jnp.float32)] * n_row,
            in_specs=[SMEM] * 3 + [VMEM] * (2 + len(blocks)),
            out_specs=[VMEM] * n_row,
            compiler_params=pltpu.CompilerParams(vmem_limit_bytes=32 * 2**20),
            cost_estimate=cost(6 * total * depth * width, total * (depth + width) * 4),
            name="multiply",
        )(place, int_mask, owner_map, high, low, *blocks)

    slots, shares = [], []

    def exchange(step, side, *blocks):
        parts = multiply(step, side, *blocks)
        slots.append((step, side))
        shares.extend([parts[0]] + [swap(parts[d], d) for d in range(1, n_row)])

    exchange(0, 1, integrals)
    for step in range(1, n_col):
        if 2 * step <= n_col - 1:
            exchange(step, -1, right)
            exchange(step, 1, left)
        else:
            exchange(step, 0, right, left)
        if step < n_col - 1:
            right, left = shift(right, 1), shift(left, -1)

    return pl.pallas_call(
        functools.partial(finish_kernel, n_row, tuple(slots)),
        out_shape=jax.ShapeDtypeStruct((rows, pairs), jnp.float32),
        in_specs=[SMEM] * 2 + [VMEM] * len(shares),
        out_specs=VMEM,
        compiler_params=pltpu.CompilerParams(vmem_limit_bytes=48 * 2**20),
        cost_estimate=cost(rows * pairs * n_row, rows * pairs * (n_row + 1) * 4),
        name="finish",
    )(place, owner_map, *shares)


def solution(mesh):
    placed = (
        P(("mol", "row", "col"), None),
        P(("mol", "row"), "col"),
        P("mol", None),
        P("mol", None),
        P("mol"),
    )
    return jax.shard_map(
        functools.partial(on_device, mesh.shape["row"], mesh.shape["col"]),
        mesh=mesh,
        in_specs=placed,
        out_specs=P(("mol", "row", "col"), None),
        check_vma=False,
    )
```

time: 116 us -> 83.3 us (0.72)
  waiting for transfers between devices: 75.5 us -> 38.2 us
  starting transfers between devices: 3.5 us -> 30.4 us
  between operations: 13.5 us -> 0.2 us
  blocking collectives: 11.5 us -> 0 us
  Pallas kernels: 0 us -> 9.9 us
  matrix products: 6.39 us -> 0 us
  other arithmetic: 1.83 us -> 0.08 us
    all_gather x1 -> x0, waiting for transfers between devices: 41.2 us -> none  [on_device(): lax.all_gather(integral_local, 'col', axis=1, tiled=True)]
    ppermute x0 -> x24, waiting for transfers between devices: none -> 38.2 us  [the longest x6 21.5 us: shift(): return lax.ppermute(x, 'col', pairs_)]
    ppermute x0 -> x24, starting transfers between devices: none -> 30.4 us  [the longest x6 18.4 us: shift(): return lax.ppermute(x, 'col', pairs_)]
    reduce_scatter x1 -> x0, waiting for transfers between devices: 26.9 us -> none  [on_device(): lax.psum_scatter(partial_value, 'row', scatter_dimension=1, tiled=True)]
    all_to_all x1 -> x0, blocking collectives: 11.5 us -> none  [on_device(): lax.all_to_all(masked, 'row', split_axis=1, concat_axis=0, tiled=True)]
    pallas_call x0 -> x7, Pallas kernels: none -> 9.9 us  [the longest x5 6.72 us: multiply(): pl.pallas_call(functools.partial(multiply_kernel, n_row, step, side), out...]
    all_to_all x1 -> x0, waiting for transfers between devices: 7.38 us -> none  [on_device(): lax.all_to_all(summed, 'row', split_axis=0, concat_axis=1, tiled=True)]
    dot_general x2 -> x0, matrix products: 6.39 us -> none  [the longest x1 5.52 us: on_device(): jnp.dot(slab, lax.all_gather(integral_local, 'col', axis=1, tiled=True),...]
  transfers between devices with their start and end apart: 3 -> 24, of which waited for: 3 -> 12; matrix products, arithmetic and copies ran while one was open for 1% -> 3% of each run, Pallas kernels for 0% -> 9%
where the time goes in v1:
time: 83.3 us; the launch traced here: 82.9 us
  waiting for transfers between devices  38.2 us (46%)
  starting transfers between devices  30.4 us (36%)
  Pallas kernels  9.9 us (12%)
  local copies, waits for them, and re-layouts  4.16 us (5%)
    ppermute x6, waiting for transfers between devices, shift(): return lax.ppermute(x, 'col', pairs_)  21.5 us
    ppermute x6, starting transfers between devices, shift(): return lax.ppermute(x, 'col', pairs_)  18.4 us
    ppermute x18, waiting for transfers between devices, swap(): return lax.ppermute(x, 'row', [(i, i ^ d) for i in range(n_row)])  16.6 us
    ppermute x18, starting transfers between devices, swap(): return lax.ppermute(x, 'row', [(i, i ^ d) for i in range(n_row)])  12 us
    pallas_call x5, Pallas kernels, multiply(): pl.pallas_call(functools.partial(multiply_kernel, n_row, step, side), out...  6.72 us
    unnamed x9, local copies, waits for them, and re-layouts  2.3 us
    pallas_call x1, Pallas kernels, on_device(): pl.pallas_call(functools.partial(finish_kernel, n_row, tuple(slots)), out...  2.07 us
    dynamic_slice x1, local copies, waits for them, and re-layouts, columns(): return lax.dynamic_slice_in_dim(amplitudes, (r ^ d) * depth, depth, 1)  1.86 us
  transfers between devices with their start and end apart: 24, of which 12 were waited for; matrix products, arithmetic and copies ran while one was open for 3% of the time, Pallas kernels for 9%

profile of v1, /device:TPU:0, one launch (start us, length us, event | category | flops | bytes accessed | tf_op | source)
XLA Modules:
  0.0 82.9 jit_solution(141902558301304030)
XLA Ops:
  0.0 5.0 %collective-permute-start.6 = (f32[384,384]{1,0:T(8,128)}, f32[384,384]{1,0:T(8,128)S(1)}, u32[]{:S(2)}, u32[]{:S(2)}) collective-permute-start(f32[384,384]{1,0:T(8,128)} %refs_0_.1), channel_id=1, source_target_pairs={{0,1},{1,2},{2,3},{4,5},{5,6},{6,7},{8,9},{9,10},{10,11},{12,13},{... | collective-permute-start | bytes 1769480 | tf_op jit(solution)/shard_map/ppermute | solution.py:131
  5.0 1.3 %collective-permute-start.10 = (f32[384,384]{1,0:T(8,128)}, f32[384,384]{1,0:T(8,128)S(1)}, u32[]{:S(2)}, u32[]{:S(2)}) collective-permute-start(f32[384,384]{1,0:T(8,128)} %refs_0_.1), channel_id=1, source_target_pairs={{1,0},{2,1},{3,2},{5,4},{6,5},{7,6},{9,8},{10,9},{11,10},{13,12},{... | collective-permute-start | bytes 1769480 | tf_op jit(solution)/shard_map/ppermute | solution.py:131
  6.3 11.5 %collective-permute-done.6.refs_0_ = f32[384,384]{1,0:T(8,128)S(1)} collective-permute-done((f32[384,384]{1,0:T(8,128)}, f32[384,384]{1,0:T(8,128)S(1)}, u32[]{:S(2)}, u32[]{:S(2)}) %collective-permute-start.6) | collective-permute-done | bytes 589856 | tf_op jit(solution)/shard_map/ppermute | solution.py:131
  17.8 5.1 %collective-permute-start.14 = (f32[384,384]{1,0:T(8,128)S(1)}, f32[384,384]{1,0:T(8,128)}, u32[]{:S(2)}, u32[]{:S(2)}) collective-permute-start(f32[384,384]{1,0:T(8,128)S(1)} %collective-permute-done.6.refs_0_), channel_id=1, source_target_pairs={{0,1},{1,2},{2,3},{4,5},{5,6},{6,7},{8,9},{9,10},{10,11},{12,13},{... | collective-permute-start | bytes 1769480 | tf_op jit(solution)/shard_map/ppermute | solution.py:131
  22.9 1.3 %collective-permute-start.15 = (f32[384,384]{1,0:T(8,128)S(1)}, f32[384,384]{1,0:T(8,128)S(1)}, u32[]{:S(2)}, u32[]{:S(2)}) collective-permute-start(f32[384,384]{1,0:T(8,128)S(1)} %collective-permute-done.10.refs_0_), channel_id=1, source_target_pairs={{1,0},{2,1},{3,2},{5,4},{6,5},{7,6},{9,8},{10,9},{11,10},{13,12},{... | collective-permute-start | bytes 1769480 | tf_op jit(solution)/shard_map/ppermute | solution.py:131
  24.2 9.6 %collective-permute-done.14.refs_0_ = f32[384,384]{1,0:T(8,128)} collective-permute-done((f32[384,384]{1,0:T(8,128)S(1)}, f32[384,384]{1,0:T(8,128)}, u32[]{:S(2)}, u32[]{:S(2)}) %collective-permute-start.14) | collective-permute-done | bytes 589856 | tf_op jit(solution)/shard_map/ppermute | solution.py:131
  33.8 4.5 %collective-permute-start.19 = (f32[384,384]{1,0:T(8,128)}, f32[384,384]{1,0:T(8,128)S(1)}, u32[]{:S(2)}, u32[]{:S(2)}) collective-permute-start(f32[384,384]{1,0:T(8,128)} %collective-permute-done.14.refs_0_), channel_id=1, source_target_pairs={{0,1},{1,2},{2,3},{4,5},{5,6},{6,7},{8,9},{9,10},{10,11},{12,13},{... | collective-permute-start | bytes 1769480 | tf_op jit(solution)/shard_map/ppermute | solution.py:131
  38.7 1.3 %collective-permute-start.20 = (f32[384,384]{1,0:T(8,128)S(1)}, f32[384,384]{1,0:T(8,128)S(1)}, u32[]{:S(2)}, u32[]{:S(2)}) collective-permute-start(f32[384,384]{1,0:T(8,128)S(1)} %collective-permute-done.15.refs_1_), channel_id=1, source_target_pairs={{1,0},{2,1},{3,2},{5,4},{6,5},{7,6},{9,8},{10,9},{11,10},{13,12},{... | collective-permute-start | bytes 1769480 | tf_op jit(solution)/shard_map/ppermute | solution.py:131
  40.0 1.9 %constant_dynamic-slice_fusion = (f32[64,384]{1,0:T(8,128)}, f32[64,384]{1,0:T(8,128)}, f32[64,384]{1,0:T(8,128)}, f32[64,384]{1,0:T(8,128)}) fusion(f32[64,1536]{1,0:T(8,128)} %param.5, s32[]{:T(128)S(6)} %select_n.15, s32[]{:T(128)S(6)} %select_n.13, s32[]{:T(128)S(6)} %select_n.12, s32[]{:T(128)S(6)} %select_n.14), kind=kLoop, calls=%fused_computation | loop fusion | bytes 786448 | tf_op jit(solution)/shard_map/dynamic_slice | solution.py:139
  41.9 1.5 %collective-permute-start.1 = (f32[64,384]{1,0:T(8,128)}, f32[64,384]{1,0:T(8,128)}, u32[]{:S(2)}, u32[]{:S(2)}) collective-permute-start(f32[64,384]{1,0:T(8,128)} %get-tuple-element.52), channel_id=1, source_target_pairs={{0,8},{4,12},{8,0},{12,4},{1,9},{5,13},{9,1},{13,5},{2,10},{6,14},... | collective-permute-start | bytes 294920 | tf_op jit(solution)/shard_map/ppermute | solution.py:134
  43.8 0.8 copy.6.refs_1_
  44.6 3.2 %collective-permute-done.1.refs_4_ = f32[64,384]{1,0:T(8,128)} collective-permute-done((f32[64,384]{1,0:T(8,128)}, f32[64,384]{1,0:T(8,128)}, u32[]{:S(2)}, u32[]{:S(2)}) %collective-permute-start.1) | collective-permute-done | bytes 98336 | tf_op jit(solution)/shard_map/ppermute | solution.py:134
  47.8 1.3 %collective-permute-done.2.refs_5_ = f32[64,384]{1,0:T(8,128)} collective-permute-done((f32[64,384]{1,0:T(8,128)}, f32[64,384]{1,0:T(8,128)}, u32[]{:S(2)}, u32[]{:S(2)}) %collective-permute-start.2) | collective-permute-done | bytes 98336 | tf_op jit(solution)/shard_map/ppermute | solution.py:134
  49.1 0.9 %copy-done.1 = f32[64,384]{1,0:T(8,128)S(1)} copy-done((f32[64,384]{1,0:T(8,128)S(1)}, f32[64,384]{1,0:T(8,128)}, u32[]{:S(2)}) %copy-start.1) | copy-done | bytes 98328
  50.0 1.1 %prepare.1 = (bf16[256,384]{1,0:T(8,128)(2,1)S(1)}, bf16[256,384]{1,0:T(8,128)(2,1)S(1)}) custom-call(s32[3]{0:T(128)S(1)} %pad_add_fusion.refs_0_.place, s32[32,16]{1,0:T(8,128)S(1)} %copy.6.refs_1_, f32[64,384]{1,0:T(8,128)S(1)} %copy-done.1, f32[64,384]{1,0:T(8,128)} %collective-permute-done.refs_3_, f32[64,384]{1,0:T(8,128)} %collective-permute-done.1.refs_4_, ...), custom_call_target="tpu_custom_call" | custom-call | flops 393216 | bytes 786432 | tf_op jit(solution)/shard_map/prepare/pallas_call | solution.py:143
  51.8 1.4 %multiply.5 = (f32[64,384]{1,0:T(8,128)S(1)}, f32[64,384]{1,0:T(8,128)S(1)}, f32[64,384]{1,0:T(8,128)S(1)}, f32[64,384]{1,0:T(8,128)S(1)}) custom-call(s32[3]{0:T(128)S(1)} %pad_add_fusion.refs_0_.place, s32[16,16]{1,0:T(8,128)S(1)} %copy-done.2, s32[16]{0:T(128)S(1)} %copy-done.3, bf16[256,384]{1,0:T(8,128)(2,1)S(1)} %get-tuple-element.27.high, ...), custom_call_target="tpu_custom_call" | custom-call | flops 226492416 | bytes 786432 | tf_op jit(solution)/shard_map/multiply/pallas_call | solution.py:154
  53.7 1.5 %collective-permute-start.4 = (f32[64,384]{1,0:T(8,128)S(1)}, f32[64,384]{1,0:T(8,128)S(1)}, u32[]{:S(2)}, u32[]{:S(2)}) collective-permute-start(f32[64,384]{1,0:T(8,128)S(1)} %get-tuple-element.31), channel_id=1, source_target_pairs={{0,8},{4,12},{8,0},{12,4},{1,9},{5,13},{9,1},{13,5},{2,10},{6,14},... | collective-permute-start | bytes 294920 | tf_op jit(solution)/shard_map/ppermute | solution.py:134
  55.9 0.7 collective-permute-start.7
  56.6 2.2 %collective-permute-done.4.refs_2_ = f32[64,384]{1,0:T(8,128)S(1)} collective-permute-done((f32[64,384]{1,0:T(8,128)S(1)}, f32[64,384]{1,0:T(8,128)S(1)}, u32[]{:S(2)}, u32[]{:S(2)}) %collective-permute-start.4) | collective-permute-done | bytes 98336 | tf_op jit(solution)/shard_map/ppermute | solution.py:134
  58.8 2.0 %collective-permute-start.8 = (f32[64,384]{1,0:T(8,128)S(1)}, f32[64,384]{1,0:T(8,128)S(1)}, u32[]{:S(2)}, u32[]{:S(2)}) collective-permute-start(f32[64,384]{1,0:T(8,128)S(1)} %get-tuple-element.35), channel_id=1, source_target_pairs={{0,8},{4,12},{8,0},{12,4},{1,9},{5,13},{9,1},{13,5},{2,10},{6,14},... | collective-permute-start | bytes 294920 | tf_op jit(solution)/shard_map/ppermute | solution.py:134
  60.8 1.4 %multiply.7 = (f32[64,384]{1,0:T(8,128)S(1)}, f32[64,384]{1,0:T(8,128)S(1)}, f32[64,384]{1,0:T(8,128)S(1)}, f32[64,384]{1,0:T(8,128)S(1)}) custom-call(s32[3]{0:T(128)S(1)} %pad_add_fusion.refs_0_.place, s32[16,16]{1,0:T(8,128)S(1)} %copy-done.2, s32[16]{0:T(128)S(1)} %copy-done.3, bf16[256,384]{1,0:T(8,128)(2,1)S(1)} %get-tuple-element.27.high, ...), custom_call_target="tpu_custom_call" | custom-call | flops 226492416 | bytes 786432 | tf_op jit(solution)/shard_map/multiply/pallas_call | solution.py:154
  62.2 1.8 %multiply.8 = (f32[64,384]{1,0:T(8,128)S(1)}, f32[64,384]{1,0:T(8,128)S(1)}, f32[64,384]{1,0:T(8,128)S(1)}, f32[64,384]{1,0:T(8,128)S(1)}) custom-call(s32[3]{0:T(128)S(1)} %pad_add_fusion.refs_0_.place, s32[16,16]{1,0:T(8,128)S(1)} %copy-done.2, s32[16]{0:T(128)S(1)} %copy-done.3, bf16[256,384]{1,0:T(8,128)(2,1)S(1)} %get-tuple-element.27.high, ...), custom_call_target="tpu_custom_call" | custom-call | flops 226492416 | bytes 786432 | tf_op jit(solution)/shard_map/multiply/pallas_call | solution.py:154
  64.3 2.0 %collective-permute-start.12 = (f32[64,384]{1,0:T(8,128)S(1)}, f32[64,384]{1,0:T(8,128)S(1)}, u32[]{:S(2)}, u32[]{:S(2)}) collective-permute-start(f32[64,384]{1,0:T(8,128)S(1)} %get-tuple-element.39), channel_id=1, source_target_pairs={{0,8},{4,12},{8,0},{12,4},{1,9},{5,13},{9,1},{13,5},{2,10},{6,14},... | collective-permute-start | bytes 294920 | tf_op jit(solution)/shard_map/ppermute | solution.py:134
  66.5 1.4 %multiply.9 = (f32[64,384]{1,0:T(8,128)S(1)}, f32[64,384]{1,0:T(8,128)S(1)}, f32[64,384]{1,0:T(8,128)S(1)}, f32[64,384]{1,0:T(8,128)S(1)}) custom-call(s32[3]{0:T(128)S(1)} %pad_add_fusion.refs_0_.place, s32[16,16]{1,0:T(8,128)S(1)} %copy-done.2, s32[16]{0:T(128)S(1)} %copy-done.3, bf16[256,384]{1,0:T(8,128)(2,1)S(1)} %get-tuple-element.27.high, ...), custom_call_target="tpu_custom_call" | custom-call | flops 226492416 | bytes 786432 | tf_op jit(solution)/shard_map/multiply/pallas_call | solution.py:154
  68.5 1.4 %collective-permute-start.17 = (f32[64,384]{1,0:T(8,128)S(1)}, f32[64,384]{1,0:T(8,128)S(1)}, u32[]{:S(2)}, u32[]{:S(2)}) collective-permute-start(f32[64,384]{1,0:T(8,128)S(1)} %get-tuple-element.43), channel_id=1, source_target_pairs={{0,8},{4,12},{8,0},{12,4},{1,9},{5,13},{9,1},{13,5},{2,10},{6,14},... | collective-permute-start | bytes 294920 | tf_op jit(solution)/shard_map/ppermute | solution.py:134
  69.9 0.7 collective-permute-start.21
  70.7 2.0 %collective-permute-done.13.refs_11_ = f32[64,384]{1,0:T(8,128)S(1)} collective-permute-done((f32[64,384]{1,0:T(8,128)S(1)}, f32[64,384]{1,0:T(8,128)S(1)}, u32[]{:S(2)}, u32[]{:S(2)}) %collective-permute-start.13) | collective-permute-done | bytes 98336 | tf_op jit(solution)/shard_map/ppermute | solution.py:134
  73.5 0.7 collective-permute-done.17.refs_14_
  74.2 2.6 %collective-permute-done.18.refs_15_ = f32[64,384]{1,0:T(8,128)S(1)} collective-permute-done((f32[64,384]{1,0:T(8,128)S(1)}, f32[64,384]{1,0:T(8,128)S(1)}, u32[]{:S(2)}, u32[]{:S(2)}) %collective-permute-start.18) | collective-permute-done | bytes 98336 | tf_op jit(solution)/shard_map/ppermute | solution.py:134
  76.8 1.6 %collective-permute-done.22.refs_18_ = f32[64,384]{1,0:T(8,128)S(1)} collective-permute-done((f32[64,384]{1,0:T(8,128)S(1)}, f32[64,384]{1,0:T(8,128)S(1)}, u32[]{:S(2)}, u32[]{:S(2)}) %collective-permute-start.22) | collective-permute-done | bytes 98336 | tf_op jit(solution)/shard_map/ppermute | solution.py:134
  78.5 2.4 %collective-permute-done.23.refs_19_ = f32[64,384]{1,0:T(8,128)S(1)} collective-permute-done((f32[64,384]{1,0:T(8,128)S(1)}, f32[64,384]{1,0:T(8,128)S(1)}, u32[]{:S(2)}, u32[]{:S(2)}) %collective-permute-start.23) | collective-permute-done | bytes 98336 | tf_op jit(solution)/shard_map/ppermute | solution.py:134
  80.8 2.1 %finish.1 = f32[64,1536]{1,0:T(8,128)} custom-call(s32[3]{0:T(128)S(1)} %pad_add_fusion.refs_0_.place, s32[16]{0:T(128)S(1)} %copy-done.3, f32[64,384]{1,0:T(8,128)S(1)} %get-tuple-element.29.refs_0_, f32[64,384]{1,0:T(8,128)S(1)} %collective-permute-done.3.refs_1_, f32[64,384]{1,0:T(8,128)S(1)} %collective-permute-done.4.refs_2_, ...), custom_call_target="tpu_custom_call" | custom-call | flops 393216 | bytes 1966080 | tf_op jit(solution)/shard_map/finish/pallas_call | solution.py:181
  (34 shorter events, 4.5 us)
Async XLA Ops:
  0.0 17.8 %collective-permute-start.6 = (f32[384,384]{1,0:T(8,128)}, f32[384,384]{1,0:T(8,128)S(1)}, u32[]{:S(2)}, u32[]{:S(2)}) collective-permute-start(f32[384,384]{1,0:T(8,128)} %refs_0_.1), channel_id=1, source_target_pairs={{0,1},{1,2},{2,3},{4,5},{5,6},{6,7},{8,9},{9,10},{10,11},{12,13},{... | collective-permute-start | bytes 1769480 | tf_op jit(solution)/shard_map/ppermute | solution.py:131
  5.0 17.9 %collective-permute-start.10 = (f32[384,384]{1,0:T(8,128)}, f32[384,384]{1,0:T(8,128)S(1)}, u32[]{:S(2)}, u32[]{:S(2)}) collective-permute-start(f32[384,384]{1,0:T(8,128)} %refs_0_.1), channel_id=1, source_target_pairs={{1,0},{2,1},{3,2},{5,4},{6,5},{7,6},{9,8},{10,9},{11,10},{13,12},{... | collective-permute-start | bytes 1769480 | tf_op jit(solution)/shard_map/ppermute | solution.py:131
  17.8 16.0 %collective-permute-start.14 = (f32[384,384]{1,0:T(8,128)S(1)}, f32[384,384]{1,0:T(8,128)}, u32[]{:S(2)}, u32[]{:S(2)}) collective-permute-start(f32[384,384]{1,0:T(8,128)S(1)} %collective-permute-done.6.refs_0_), channel_id=1, source_target_pairs={{0,1},{1,2},{2,3},{4,5},{5,6},{6,7},{8,9},{9,10},{10,11},{12,13},{... | collective-permute-start | bytes 1769480 | tf_op jit(solution)/shard_map/ppermute | solution.py:131
  22.9 15.8 %collective-permute-start.15 = (f32[384,384]{1,0:T(8,128)S(1)}, f32[384,384]{1,0:T(8,128)S(1)}, u32[]{:S(2)}, u32[]{:S(2)}) collective-permute-start(f32[384,384]{1,0:T(8,128)S(1)} %collective-permute-done.10.refs_0_), channel_id=1, source_target_pairs={{1,0},{2,1},{3,2},{5,4},{6,5},{7,6},{9,8},{10,9},{11,10},{13,12},{... | collective-permute-start | bytes 1769480 | tf_op jit(solution)/shard_map/ppermute | solution.py:131
  33.8 32.5 %collective-permute-start.19 = (f32[384,384]{1,0:T(8,128)}, f32[384,384]{1,0:T(8,128)S(1)}, u32[]{:S(2)}, u32[]{:S(2)}) collective-permute-start(f32[384,384]{1,0:T(8,128)} %collective-permute-done.14.refs_0_), channel_id=1, source_target_pairs={{0,1},{1,2},{2,3},{4,5},{5,6},{6,7},{8,9},{9,10},{10,11},{12,13},{... | collective-permute-start | bytes 1769480 | tf_op jit(solution)/shard_map/ppermute | solution.py:131
  38.7 27.6 %collective-permute-start.20 = (f32[384,384]{1,0:T(8,128)S(1)}, f32[384,384]{1,0:T(8,128)S(1)}, u32[]{:S(2)}, u32[]{:S(2)}) collective-permute-start(f32[384,384]{1,0:T(8,128)S(1)} %collective-permute-done.15.refs_1_), channel_id=1, source_target_pairs={{1,0},{2,1},{3,2},{5,4},{6,5},{7,6},{9,8},{10,9},{11,10},{13,12},{... | collective-permute-start | bytes 1769480 | tf_op jit(solution)/shard_map/ppermute | solution.py:131
  40.0 11.1 %copy-start = (f32[384,384]{1,0:T(8,128)S(1)}, f32[384,384]{1,0:T(8,128)}, u32[]{:S(2)}) copy-start(f32[384,384]{1,0:T(8,128)} %refs_0_.1) | copy-start | bytes 1769476
  41.9 2.7 %collective-permute-start = (f32[64,384]{1,0:T(8,128)}, f32[64,384]{1,0:T(8,128)}, u32[]{:S(2)}, u32[]{:S(2)}) collective-permute-start(f32[64,384]{1,0:T(8,128)} %get-tuple-element.50), channel_id=1, source_target_pairs={{0,4},{4,0},{8,12},{12,8},{1,5},{5,1},{9,13},{13,9},{2,6},{6,2},{1... | collective-permute-start | bytes 294920 | tf_op jit(solution)/shard_map/ppermute | solution.py:134
  41.9 5.9 %collective-permute-start.1 = (f32[64,384]{1,0:T(8,128)}, f32[64,384]{1,0:T(8,128)}, u32[]{:S(2)}, u32[]{:S(2)}) collective-permute-start(f32[64,384]{1,0:T(8,128)} %get-tuple-element.52), channel_id=1, source_target_pairs={{0,8},{4,12},{8,0},{12,4},{1,9},{5,13},{9,1},{13,5},{2,10},{6,14},... | collective-permute-start | bytes 294920 | tf_op jit(solution)/shard_map/ppermute | solution.py:134
  43.4 5.7 %collective-permute-start.2 = (f32[64,384]{1,0:T(8,128)}, f32[64,384]{1,0:T(8,128)}, u32[]{:S(2)}, u32[]{:S(2)}) collective-permute-start(f32[64,384]{1,0:T(8,128)} %get-tuple-element.49), channel_id=1, source_target_pairs={{0,12},{4,8},{8,4},{12,0},{1,13},{5,9},{9,5},{13,1},{2,14},{6,10},... | collective-permute-start | bytes 294920 | tf_op jit(solution)/shard_map/ppermute | solution.py:134
  49.1 0.9 %copy-start.1 = (f32[64,384]{1,0:T(8,128)S(1)}, f32[64,384]{1,0:T(8,128)}, u32[]{:S(2)}) copy-start(f32[64,384]{1,0:T(8,128)} %get-tuple-element.51.refs_2_) | copy-start | bytes 294916
  50.0 1.1 %copy-start.2 = (s32[16,16]{1,0:T(8,128)S(1)}, s32[16,16]{1,0:T(8,128)}, u32[]{:S(2)}) copy-start(s32[16,16]{1,0:T(8,128)} %int_mask.9) | copy-start | bytes 3076
  51.1 0.7 copy-start.3
  53.2 2.7 %collective-permute-start.3 = (f32[64,384]{1,0:T(8,128)S(1)}, f32[64,384]{1,0:T(8,128)S(1)}, u32[]{:S(2)}, u32[]{:S(2)}) collective-permute-start(f32[64,384]{1,0:T(8,128)S(1)} %get-tuple-element.30), channel_id=1, source_target_pairs={{0,4},{4,0},{8,12},{12,8},{1,5},{5,1},{9,13},{13,9},{2,6},{6,2},{1... | collective-permute-start | bytes 294920 | tf_op jit(solution)/shard_map/ppermute | solution.py:134
  53.7 5.1 %collective-permute-start.4 = (f32[64,384]{1,0:T(8,128)S(1)}, f32[64,384]{1,0:T(8,128)S(1)}, u32[]{:S(2)}, u32[]{:S(2)}) collective-permute-start(f32[64,384]{1,0:T(8,128)S(1)} %get-tuple-element.31), channel_id=1, source_target_pairs={{0,8},{4,12},{8,0},{12,4},{1,9},{5,13},{9,1},{13,5},{2,10},{6,14},... | collective-permute-start | bytes 294920 | tf_op jit(solution)/shard_map/ppermute | solution.py:134
  55.2 8.9 %collective-permute-start.5 = (f32[64,384]{1,0:T(8,128)S(1)}, f32[64,384]{1,0:T(8,128)S(1)}, u32[]{:S(2)}, u32[]{:S(2)}) collective-permute-start(f32[64,384]{1,0:T(8,128)S(1)} %get-tuple-element.32), channel_id=1, source_target_pairs={{0,12},{4,8},{8,4},{12,0},{1,13},{5,9},{9,5},{13,1},{2,14},{6,10},... | collective-permute-start | bytes 294920 | tf_op jit(solution)/shard_map/ppermute | solution.py:134
  55.9 8.3 %collective-permute-start.7 = (f32[64,384]{1,0:T(8,128)S(1)}, f32[64,384]{1,0:T(8,128)S(1)}, u32[]{:S(2)}, u32[]{:S(2)}) collective-permute-start(f32[64,384]{1,0:T(8,128)S(1)} %get-tuple-element.34), channel_id=1, source_target_pairs={{0,4},{4,0},{8,12},{12,8},{1,5},{5,1},{9,13},{13,9},{2,6},{6,2},{1... | collective-permute-start | bytes 294920 | tf_op jit(solution)/shard_map/ppermute | solution.py:134
  58.8 5.5 %collective-permute-start.8 = (f32[64,384]{1,0:T(8,128)S(1)}, f32[64,384]{1,0:T(8,128)S(1)}, u32[]{:S(2)}, u32[]{:S(2)}) collective-permute-start(f32[64,384]{1,0:T(8,128)S(1)} %get-tuple-element.35), channel_id=1, source_target_pairs={{0,8},{4,12},{8,0},{12,4},{1,9},{5,13},{9,1},{13,5},{2,10},{6,14},... | collective-permute-start | bytes 294920 | tf_op jit(solution)/shard_map/ppermute | solution.py:134
  64.1 4.4 %collective-permute-start.9 = (f32[64,384]{1,0:T(8,128)S(1)}, f32[64,384]{1,0:T(8,128)S(1)}, u32[]{:S(2)}, u32[]{:S(2)}) collective-permute-start(f32[64,384]{1,0:T(8,128)S(1)} %get-tuple-element.36), channel_id=1, source_target_pairs={{0,12},{4,8},{8,4},{12,0},{1,13},{5,9},{9,5},{13,1},{2,14},{6,10},... | collective-permute-start | bytes 294920 | tf_op jit(solution)/shard_map/ppermute | solution.py:134
  64.2 5.8 %collective-permute-start.11 = (f32[64,384]{1,0:T(8,128)S(1)}, f32[64,384]{1,0:T(8,128)S(1)}, u32[]{:S(2)}, u32[]{:S(2)}) collective-permute-start(f32[64,384]{1,0:T(8,128)S(1)} %get-tuple-element.38), channel_id=1, source_target_pairs={{0,4},{4,0},{8,12},{12,8},{1,5},{5,1},{9,13},{13,9},{2,6},{6,2},{1... | collective-permute-start | bytes 294920 | tf_op jit(solution)/shard_map/ppermute | solution.py:134
  64.3 5.7 %collective-permute-start.12 = (f32[64,384]{1,0:T(8,128)S(1)}, f32[64,384]{1,0:T(8,128)S(1)}, u32[]{:S(2)}, u32[]{:S(2)}) collective-permute-start(f32[64,384]{1,0:T(8,128)S(1)} %get-tuple-element.39), channel_id=1, source_target_pairs={{0,8},{4,12},{8,0},{12,4},{1,9},{5,13},{9,1},{13,5},{2,10},{6,14},... | collective-permute-start | bytes 294920 | tf_op jit(solution)/shard_map/ppermute | solution.py:134
  66.3 6.3 %collective-permute-start.13 = (f32[64,384]{1,0:T(8,128)S(1)}, f32[64,384]{1,0:T(8,128)S(1)}, u32[]{:S(2)}, u32[]{:S(2)}) collective-permute-start(f32[64,384]{1,0:T(8,128)S(1)} %get-tuple-element.40), channel_id=1, source_target_pairs={{0,12},{4,8},{8,4},{12,0},{1,13},{5,9},{9,5},{13,1},{2,14},{6,10},... | collective-permute-start | bytes 294920 | tf_op jit(solution)/shard_map/ppermute | solution.py:134
  66.3 6.6 %collective-permute-start.16 = (f32[64,384]{1,0:T(8,128)S(1)}, f32[64,384]{1,0:T(8,128)S(1)}, u32[]{:S(2)}, u32[]{:S(2)}) collective-permute-start(f32[64,384]{1,0:T(8,128)S(1)} %get-tuple-element.42), channel_id=1, source_target_pairs={{0,4},{4,0},{8,12},{12,8},{1,5},{5,1},{9,13},{13,9},{2,6},{6,2},{1... | collective-permute-start | bytes 294920 | tf_op jit(solution)/shard_map/ppermute | solution.py:134
  68.5 5.7 %collective-permute-start.17 = (f32[64,384]{1,0:T(8,128)S(1)}, f32[64,384]{1,0:T(8,128)S(1)}, u32[]{:S(2)}, u32[]{:S(2)}) collective-permute-start(f32[64,384]{1,0:T(8,128)S(1)} %get-tuple-element.43), channel_id=1, source_target_pairs={{0,8},{4,12},{8,0},{12,4},{1,9},{5,13},{9,1},{13,5},{2,10},{6,14},... | collective-permute-start | bytes 294920 | tf_op jit(solution)/shard_map/ppermute | solution.py:134
  69.9 6.9 %collective-permute-start.18 = (f32[64,384]{1,0:T(8,128)S(1)}, f32[64,384]{1,0:T(8,128)S(1)}, u32[]{:S(2)}, u32[]{:S(2)}) collective-permute-start(f32[64,384]{1,0:T(8,128)S(1)} %get-tuple-element.44), channel_id=1, source_target_pairs={{0,12},{4,8},{8,4},{12,0},{1,13},{5,9},{9,5},{13,1},{2,14},{6,10},... | collective-permute-start | bytes 294920 | tf_op jit(solution)/shard_map/ppermute | solution.py:134
  69.9 6.9 %collective-permute-start.21 = (f32[64,384]{1,0:T(8,128)S(1)}, f32[64,384]{1,0:T(8,128)S(1)}, u32[]{:S(2)}, u32[]{:S(2)}) collective-permute-start(f32[64,384]{1,0:T(8,128)S(1)} %get-tuple-element.46), channel_id=1, source_target_pairs={{0,4},{4,0},{8,12},{12,8},{1,5},{5,1},{9,13},{13,9},{2,6},{6,2},{1... | collective-permute-start | bytes 294920 | tf_op jit(solution)/shard_map/ppermute | solution.py:134
  72.6 5.8 %collective-permute-start.22 = (f32[64,384]{1,0:T(8,128)S(1)}, f32[64,384]{1,0:T(8,128)S(1)}, u32[]{:S(2)}, u32[]{:S(2)}) collective-permute-start(f32[64,384]{1,0:T(8,128)S(1)} %get-tuple-element.47), channel_id=1, source_target_pairs={{0,8},{4,12},{8,0},{12,4},{1,9},{5,13},{9,1},{13,5},{2,10},{6,14},... | collective-permute-start | bytes 294920 | tf_op jit(solution)/shard_map/ppermute | solution.py:134
  72.8 8.0 %collective-permute-start.23 = (f32[64,384]{1,0:T(8,128)S(1)}, f32[64,384]{1,0:T(8,128)S(1)}, u32[]{:S(2)}, u32[]{:S(2)}) collective-permute-start(f32[64,384]{1,0:T(8,128)S(1)} %get-tuple-element.48), channel_id=1, source_target_pairs={{0,12},{4,8},{8,4},{12,0},{1,13},{5,9},{9,5},{13,1},{2,14},{6,10},... | collective-permute-start | bytes 294920 | tf_op jit(solution)/shard_map/ppermute | solution.py:134

commit v2 on v1

v2 whole, which is shorter than its diff:
```python
import functools

import jax
import jax.numpy as jnp
from jax import lax
from jax.experimental import pallas as pl
from jax.experimental.pallas import tpu as pltpu
from jax.sharding import PartitionSpec as P

TB = 96
OTB = 32
GROUP = 384
PER = GROUP // TB

VMEM = pl.BlockSpec(memory_space=pltpu.VMEM)
SMEM = pl.BlockSpec(memory_space=pltpu.SMEM)
EVEN, ODD, OWN = 0, 1, 2


def split(x):
    high = x.astype(jnp.bfloat16)
    low = (x - high.astype(jnp.float32)).astype(jnp.bfloat16)
    return high, low


def lane_mask(values, lane_tile):
    out = jnp.zeros(lane_tile.shape, jnp.float32)
    for i, v in enumerate(values):
        out = jnp.where(lane_tile == i, v.astype(jnp.float32), out)
    return out


def source_of(kind, step, c):
    if kind == OWN:
        return c
    up = (c % 2) == kind
    return jnp.where(up, c + step, c - step)


def inside(index, n):
    return (index >= 0) & (index < n)


def prepare_kernel(order, n_col, *refs):
    n_row = len(order)
    place, amp_mask = refs[0], refs[1]
    pieces = refs[2 : 2 + n_row]
    high_ref, low_ref, slab_ref = refs[2 + n_row :]
    r, c = place[0], place[1]
    rows, depth = pieces[0].shape
    k_tiles = depth // TB
    occ = rows // OTB
    lane_tile = lax.broadcasted_iota(jnp.int32, (OTB, depth), 1) // TB
    for p, d in enumerate(order):
        block = (r ^ d) * n_col + c
        for o in range(occ):
            mask = lane_mask(
                [amp_mask[block * occ + o, r * k_tiles + k] for k in range(k_tiles)], lane_tile
            )
            masked = pieces[p][o * OTB : (o + 1) * OTB, :] * mask
            high, low = split(masked)
            at = pl.ds(p * rows + o * OTB, OTB)
            slab_ref[at, :] = masked
            high_ref[at, :] = high
            low_ref[at, :] = low
    used = n_row * rows
    if slab_ref.shape[0] > used:
        slab_ref[used:, :] = jnp.zeros((slab_ref.shape[0] - used, depth), jnp.float32)


def masked_halves(place, int_mask, owner, source, piece_of, depth, width):
    r = place[0]
    k_tiles, c_tiles = depth // TB, width // TB
    lane_tile = lax.broadcasted_iota(jnp.int32, (TB, width), 1) // TB
    tiles = [owner[source * c_tiles + i] for i in range(c_tiles)]
    highs, lows = [], []
    for k in range(k_tiles):
        mask = lane_mask([int_mask[r * k_tiles + k, t] for t in tiles], lane_tile)
        h, l = split(piece_of(pl.ds(k * TB, TB)) * mask)
        highs.append(h)
        lows.append(l)
    return jnp.concatenate(highs, axis=0), jnp.concatenate(lows, axis=0)


def product(a_high, a_low, b_high, b_low):
    dot = functools.partial(jnp.dot, preferred_element_type=jnp.float32)
    return dot(a_high, b_high) + (dot(a_high, b_low) + dot(a_low, b_high))


def multiply_kernel(kind, step, place, int_mask, owner, high, low, *refs):
    blocks, (keep, give) = refs[:-2], refs[-2:]
    c, n_col = place[1], place[2]
    depth, width = blocks[0].shape
    if kind is None:
        even_source = source_of(EVEN, step, c)
        take_even = inside(even_source, n_col)
        source = jnp.where(take_even, even_source, source_of(ODD, step, c))

        def piece_of(at):
            return jnp.where(take_even, blocks[0][at, :], blocks[1][at, :])
    else:
        source = source_of(kind, step, c)

        def piece_of(at):
            return blocks[0][at, :]

    @pl.when(inside(source, n_col))
    def _():
        b_high, b_low = masked_halves(place, int_mask, owner, source, piece_of, depth, width)
        half = keep.shape[0]
        for out, start in ((give, half), (keep, 0)):
            at = pl.ds(start, half)
            out[...] = product(high[at, :], low[at, :], b_high, b_low)


def corner_kernel(step, place, int_mask, owner, slab, block, keep, give):
    c, n_col = place[1], place[2]
    depth, width = block.shape
    source = source_of(ODD, step, c)

    @pl.when(inside(source, n_col))
    def _():
        b_high, b_low = masked_halves(
            place, int_mask, owner, source, lambda at: block[at, :], depth, width
        )
        half = keep.shape[0]
        for out, start in ((give, half), (keep, 0)):
            a_high, a_low = split(slab[pl.ds(start, half), :])
            out[...] = product(a_high, a_low, b_high, b_low)


def fold_kernel(keep, got, *outs):
    rows = outs[0].shape[0]
    for i, out in enumerate(outs):
        at = pl.ds(i * rows, rows)
        out[...] = keep[at, :] + got[at, :]


def add_kernel(*refs):
    total = refs[0][...]
    for share in refs[1:-1]:
        total = total + share[...]
    refs[-1][...] = total


def finish_kernel(n_share, slots, place, owner, *refs):
    out = refs[-1]
    n_in = sum(n for _, _, n in slots)
    refs = refs[:-1]
    if len(refs) > n_in:
        out[...] = refs[0][...]
        refs = refs[1:]
    c, n_col = place[1], place[2]
    rows, width = refs[0].shape
    lane_tile = lax.broadcasted_iota(jnp.int32, (rows, GROUP), 1) // TB
    first = 0
    for kind, step, count in slots:
        shares = refs[first : first + count]
        first += count
        if kind == "corner":
            source = jnp.where(c == 0, n_col - 1, 0)
            there = (c == 0) | (c == n_col - 1)
        elif kind is None:
            even_source = source_of(EVEN, step, c)
            take_even = inside(even_source, n_col)
            source = jnp.where(take_even, even_source, source_of(ODD, step, c))
            there = inside(source, n_col)
        else:
            source = source_of(kind, step, c)
            there = inside(source, n_col)

        @pl.when(there)
        def _(shares=shares, source=source):
            for g in range(width // GROUP):
                at = pl.ds(g * GROUP, GROUP)
                total = shares[0][:, at]
                for share in shares[1:]:
                    total = total + share[:, at]
                for i in range(PER):
                    tile = owner[source * (width // TB) + g * PER + i]
                    home, spot = tile // PER, tile % PER
                    turned = pltpu.roll(total, ((spot - i + PER) % PER) * TB, 1)
                    to = pl.ds(pl.multiple_of(home * GROUP, GROUP), GROUP)
                    out[:, to] = jnp.where(lane_tile == spot, turned, out[:, to])


def call(kernel, name, outs, n_smem, *args, flops=0, after=()):
    moved = sum(x.size * x.dtype.itemsize for x in list(args) + list(outs))
    n_args, n_after = len(args), len(after)

    def body(*refs):
        kernel(*refs[:n_args], *refs[n_args + n_after :])

    return pl.pallas_call(
        body,
        out_shape=outs,
        in_specs=[SMEM] * n_smem
        + [VMEM] * (len(args) - n_smem)
        + [pl.BlockSpec(memory_space=pl.ANY)] * n_after,
        out_specs=[VMEM] * len(outs),
        compiler_params=pltpu.CompilerParams(vmem_limit_bytes=40 * 2**20),
        cost_estimate=pl.CostEstimate(
            flops=int(flops), bytes_accessed=int(moved), transcendentals=0
        ),
        name=name,
    )(*args, *after)


def f32(*shape):
    return jax.ShapeDtypeStruct(shape, jnp.float32)


def on_device(n_row, n_col, amplitudes, integrals, amp_mask, int_mask, owner_map):
    rows, pairs = amplitudes.shape
    depth, width = integrals.shape
    total = n_row * rows
    r, c = lax.axis_index("row"), lax.axis_index("col")
    place = jnp.stack([r, c, jnp.int32(n_col)]).astype(jnp.int32)
    order = list(range(0, n_row, 2)) + list(range(1, n_row, 2))

    def swap_line(x, kind):
        ends = [(i, i) for i in range(n_col) if not 0 <= (i + kind ^ 1) - kind < n_col]
        inner = [(i, (i + kind ^ 1) - kind) for i in range(n_col)]
        return lax.ppermute(x, "col", ends + [p for p in inner if 0 <= p[1] < n_col])

    def swap(x, d):
        return lax.ppermute(x, "row", [(i, i ^ d) for i in range(n_row)])

    even, odd = swap_line(integrals, EVEN), swap_line(integrals, ODD)

    def columns(d):
        return lax.dynamic_slice_in_dim(amplitudes, (r ^ d) * depth, depth, 1)

    pieces = [swap(columns(d), d) if d else columns(0) for d in order]
    corner = n_col >= 4 and total <= depth and depth <= width
    slab_rows = depth if corner else total
    high, low, slab = call(
        functools.partial(prepare_kernel, order, n_col),
        "prepare",
        [jax.ShapeDtypeStruct((total, depth), jnp.bfloat16)] * 2 + [f32(slab_rows, depth)],
        2,
        place,
        amp_mask,
        *pieces,
        flops=total * depth * 4,
    )
    if corner and depth < width:
        slab = jnp.pad(slab, ((0, 0), (0, width - depth)))

    def exchange(keep, give):
        got = swap(give, 1)
        pieces = call(fold_kernel, "fold", [f32(rows, width)] * (n_row // 2), 0, keep, got)
        return [pieces[0]] + [swap(pieces[i], 2 * i) for i in range(1, n_row // 2)]

    def multiply(kind, step, *blocks, after=()):
        keep, give = call(
            functools.partial(multiply_kernel, kind, step),
            "multiply",
            [f32(total // 2, width)] * 2,
            3,
            place,
            int_mask,
            owner_map,
            high,
            low,
            *blocks,
            flops=6 * total * depth * width,
            after=after,
        )
        shares = exchange(keep, give)
        return (kind, step, len(shares)), shares

    def finish(slots, so_far=None):
        shares = [x for _, xs in slots for x in xs]
        return call(
            functools.partial(finish_kernel, n_row // 2, tuple(s for s, _ in slots)),
            "finish",
            [f32(rows, pairs)],
            2,
            place,
            owner_map,
            *([] if so_far is None else [so_far]),
            *shares,
            flops=rows * pairs * n_row,
        )[0]

    slots = [multiply(OWN, 0, integrals)]
    last = n_col - 2 if corner else n_col - 1
    for step in range(1, last + 1):
        if step > 1:
            going = odd
            if corner and step == 2:
                going = jnp.where((c == 0) | (c == n_col - 1), slab, odd)
            even, odd = swap_line(going, EVEN), swap_line(even, ODD)
            if corner and step == 2:
                end_slab = even
        if 2 * step <= n_col - 1:
            slots.append(multiply(EVEN, step, even))
            slots.append(multiply(ODD, step, odd))
        else:
            after = ()
            if step == last:
                out = finish(slots)
                slots, after = [], (out,)
            if corner and step == last:
                keep, give = call(
                    functools.partial(corner_kernel, step),
                    "corner",
                    [f32(total // 2, width)] * 2,
                    3,
                    place,
                    int_mask,
                    owner_map,
                    end_slab,
                    odd,
                    flops=6 * total * depth * width,
                    after=(out,),
                )
                shares = exchange(keep, give)
                summed = call(add_kernel, "add", [f32(rows, width)], 0, *shares)[0]
                slots.append((("corner", step, 1), [swap_line(summed, EVEN)]))
            slots.append(multiply(None, step, even, odd, after=after))
    return finish(slots, out)


def solution(mesh):
    placed = (
        P(("mol", "row", "col"), None),
        P(("mol", "row"), "col"),
        P("mol", None),
        P("mol", None),
        P("mol"),
    )
    return jax.shard_map(
        functools.partial(on_device, mesh.shape["row"], mesh.shape["col"]),
        mesh=mesh,
        in_specs=placed,
        out_specs=P(("mol", "row", "col"), None),
        check_vma=False,
    )
```

time: 83.3 us -> 53.1 us (0.64)
  waiting for transfers between devices: 38.2 us -> 16.4 us
  starting transfers between devices: 30.4 us -> 25.5 us
  local copies, waits for them, and re-layouts: 4.16 us -> 1.79 us
  Pallas kernels: 9.9 us -> 8.81 us
    ppermute x6 -> x5, waiting for transfers between devices: 21.5 us -> 2.6 us  [swap_line(): lax.ppermute(x, 'col', ends + [p for p in inner if 0 <= p[1] < n_col])]
    ppermute x18 -> x13, waiting for transfers between devices: 16.6 us -> 13.8 us  [swap(): return lax.ppermute(x, 'row', [(i, i ^ d) for i in range(n_row)])]
    ppermute x6 -> x5, starting transfers between devices: 18.4 us -> 15.9 us  [swap_line(): lax.ppermute(x, 'col', ends + [p for p in inner if 0 <= p[1] < n_col])]
    ppermute x18 -> x13, starting transfers between devices: 12 us -> 9.59 us  [swap(): return lax.ppermute(x, 'row', [(i, i ^ d) for i in range(n_row)])]
    unnamed x9, local copies, waits for them, and re-layouts: 2.3 us -> 0.72 us
    pallas_call x7 -> x14, Pallas kernels: 9.9 us -> 8.81 us  [call(): pl.pallas_call(body, out_shape=outs, in_specs=[SMEM] * n_smem + [VMEM] *...]
  transfers between devices with their start and end apart: 24 -> 18, of which waited for: 12 -> 7; matrix products, arithmetic and copies ran while one was open for 3% -> 2% of each run, Pallas kernels for 9% -> 12%
where the time goes in v2:
time: 53.1 us; the launch traced here: 52.8 us
  starting transfers between devices  25.5 us (48%)
  waiting for transfers between devices  16.4 us (31%)
  Pallas kernels  8.81 us (17%)
  local copies, waits for them, and re-layouts  1.79 us (3%)
    ppermute x5, starting transfers between devices, swap_line(): lax.ppermute(x, 'col', ends + [p for p in inner if 0 <= p[1] < n_col])  15.9 us
    ppermute x13, waiting for transfers between devices, swap(): return lax.ppermute(x, 'row', [(i, i ^ d) for i in range(n_row)])  13.8 us
    ppermute x13, starting transfers between devices, swap(): return lax.ppermute(x, 'row', [(i, i ^ d) for i in range(n_row)])  9.59 us
    pallas_call x14, Pallas kernels, call(): pl.pallas_call(body, out_shape=outs, in_specs=[SMEM] * n_smem + [VMEM] *...  8.81 us
    ppermute x5, waiting for transfers between devices, swap_line(): lax.ppermute(x, 'col', ends + [p for p in inner if 0 <= p[1] < n_col])  2.6 us
    dynamic_slice x1, local copies, waits for them, and re-layouts, columns(): return lax.dynamic_slice_in_dim(amplitudes, (r ^ d) * depth, depth, 1)  1.06 us
  transfers between devices with their start and end apart: 18, of which 7 were waited for; matrix products, arithmetic and copies ran while one was open for 2% of the time, Pallas kernels for 12%

profile of v2, /device:TPU:0, one launch (start us, length us, event | category | flops | bytes accessed | tf_op | source)
XLA Modules:
  0.0 52.8 jit_solution(12998779438045404210)
XLA Ops:
  0.0 1.7 %collective-permute-start.8 = (f32[384,384]{1,0:T(8,128)}, f32[384,384]{1,0:T(8,128)S(1)}, u32[]{:S(2)}, u32[]{:S(2)}) collective-permute-start(f32[384,384]{1,0:T(8,128)} %refs_5_.1), channel_id=1, source_target_pairs={{0,0},{3,3},{1,2},{2,1},{4,4},{7,7},{5,6},{6,5},{8,8},{11,11},{9,1... | collective-permute-start | bytes 1769480 | tf_op jit(solution)/shard_map/ppermute | solution.py:224
  1.7 4.9 %collective-permute-start.5 = (f32[384,384]{1,0:T(8,128)}, f32[384,384]{1,0:T(8,128)S(1)}, u32[]{:S(2)}, u32[]{:S(2)}) collective-permute-start(f32[384,384]{1,0:T(8,128)} %refs_5_.1), channel_id=1, source_target_pairs={{0,1},{1,0},{2,3},{3,2},{4,5},{5,4},{6,7},{7,6},{8,9},{9,8},{10,11... | collective-permute-start | bytes 1769480 | tf_op jit(solution)/shard_map/ppermute | solution.py:224
  6.6 1.1 %constant_dynamic-slice_fusion = (f32[64,384]{1,0:T(8,128)S(1)}, f32[64,384]{1,0:T(8,128)S(1)}, f32[64,384]{1,0:T(8,128)S(1)}, f32[64,384]{1,0:T(8,128)S(1)}) fusion(f32[64,1536]{1,0:T(8,128)} %param.5, s32[]{:T(128)S(6)} %select_n.23, s32[]{:T(128)S(6)} %select_n.21, s32[]{:T(128)S(6)} %select_n.20, s32[]{:T(128)S(6)} %select_n.22), kind=kLoop, calls=%fused_computation.1 | loop fusion | bytes 786448 | tf_op jit(solution)/shard_map/dynamic_slice | solution.py:232
  7.7 0.4 collective-permute-start.2
  8.1 1.2 %collective-permute-start = (f32[64,384]{1,0:T(8,128)S(1)}, f32[64,384]{1,0:T(8,128)S(1)}, u32[]{:S(2)}, u32[]{:S(2)}) collective-permute-start(f32[64,384]{1,0:T(8,128)S(1)} %get-tuple-element.52), channel_id=1, source_target_pairs={{0,8},{4,12},{8,0},{12,4},{1,9},{5,13},{9,1},{13,5},{2,10},{6,14},... | collective-permute-start | bytes 294920 | tf_op jit(solution)/shard_map/ppermute | solution.py:227
  9.3 0.3 collective-permute-start.1
  9.7 3.0 %collective-permute-done.2.refs_5_ = f32[64,384]{1,0:T(8,128)S(1)} collective-permute-done((f32[64,384]{1,0:T(8,128)S(1)}, f32[64,384]{1,0:T(8,128)S(1)}, u32[]{:S(2)}, u32[]{:S(2)}) %collective-permute-start.2) | collective-permute-done | bytes 98336 | tf_op jit(solution)/shard_map/ppermute | solution.py:227
  12.8 2.2 %collective-permute-done.refs_3_ = f32[64,384]{1,0:T(8,128)S(1)} collective-permute-done((f32[64,384]{1,0:T(8,128)S(1)}, f32[64,384]{1,0:T(8,128)S(1)}, u32[]{:S(2)}, u32[]{:S(2)}) %collective-permute-start) | collective-permute-done | bytes 98336 | tf_op jit(solution)/shard_map/ppermute | solution.py:227
  14.9 0.9 %prepare.1 = (bf16[256,384]{1,0:T(8,128)(2,1)S(1)}, bf16[256,384]{1,0:T(8,128)(2,1)S(1)}, f32[384,384]{1,0:T(8,128)S(1)}) custom-call(s32[3]{0:T(128)S(1)} %pad_add_fusion.refs_0_, s32[32,16]{1,0:T(8,128)S(1)} %copy.6.refs_1_, f32[64,384]{1,0:T(8,128)S(1)} %get-tuple-element.53.refs_2_, f32[64,384]{1,0:T(8,128)S(1)} %collective-permute-done.refs_3_, ...), custom_call_target="tpu_custom_call" | custom-call | flops 393216 | bytes 1378316 | tf_op jit(solution)/shard_map/prepare/pallas_call | solution.py:194
  16.0 4.4 %collective-permute-start.11 = (f32[384,384]{1,0:T(8,128)S(1)}, f32[384,384]{1,0:T(8,128)S(1)}, u32[]{:S(2)}, u32[]{:S(2)}) collective-permute-start(f32[384,384]{1,0:T(8,128)S(1)} %broadcast_select_fusion), channel_id=1, source_target_pairs={{0,1},{1,0},{2,3},{3,2},{4,5},{5,4},{6,7},{7,6},{8,9},{9,8},{10,11... | collective-permute-start | bytes 1769480 | tf_op jit(solution)/shard_map/ppermute | solution.py:224
  20.3 0.7 %collective-permute-start.12 = (f32[384,384]{1,0:T(8,128)S(1)}, f32[384,384]{1,0:T(8,128)S(1)}, u32[]{:S(2)}, u32[]{:S(2)}) collective-permute-start(f32[384,384]{1,0:T(8,128)S(1)} %collective-permute-done.5.refs_5_), channel_id=1, source_target_pairs={{0,0},{3,3},{1,2},{2,1},{4,4},{7,7},{5,6},{6,5},{8,8},{11,11},{9,1... | collective-permute-start | bytes 1769480 | tf_op jit(solution)/shard_map/ppermute | solution.py:224
  21.1 0.6 %copy-done.2 = s32[16]{0:T(128)S(1)} copy-done((s32[16]{0:T(128)S(1)}, s32[16]{0:T(128)}, u32[]{:S(2)}) %copy-start.2) | copy-done | bytes 88
  21.7 1.2 %multiply.4 = (f32[128,384]{1,0:T(8,128)S(1)}, f32[128,384]{1,0:T(8,128)S(1)}) custom-call(s32[3]{0:T(128)S(1)} %pad_add_fusion.refs_0_, s32[16,16]{1,0:T(8,128)S(1)} %copy-done.1, s32[16]{0:T(128)S(1)} %copy-done.2, bf16[256,384]{1,0:T(8,128)(2,1)S(1)} %get-tuple-element.28.refs_3_, bf16[256,384]{1,0:T(8,128)(2,1)S(1)} %get-tuple-element.29.refs_4_, ...), custom_call_target="tpu_custom_call" | custom-call | flops 226492416 | bytes 1377356 | tf_op jit(solution)/shard_map/multiply/pallas_call | solution.py:194
  23.0 0.7 %multiply.6 = (f32[128,384]{1,0:T(8,128)S(1)}, f32[128,384]{1,0:T(8,128)S(1)}) custom-call(s32[3]{0:T(128)S(1)} %pad_add_fusion.refs_0_, s32[16,16]{1,0:T(8,128)S(1)} %copy-done.1, s32[16]{0:T(128)S(1)} %copy-done.2, bf16[256,384]{1,0:T(8,128)(2,1)S(1)} %get-tuple-element.28.refs_3_, bf16[256,384]{1,0:T(8,128)(2,1)S(1)} %get-tuple-element.29.refs_4_, ...), custom_call_target="tpu_custom_call" | custom-call | flops 226492416 | bytes 1377356 | tf_op jit(solution)/shard_map/multiply/pallas_call | solution.py:194
  23.7 0.6 %collective-permute-start.9 = (f32[128,384]{1,0:T(8,128)S(1)}, f32[128,384]{1,0:T(8,128)S(1)}, u32[]{:S(2)}, u32[]{:S(2)}) collective-permute-start(f32[128,384]{1,0:T(8,128)S(1)} %get-tuple-element.39), channel_id=1, source_target_pairs={{0,4},{4,0},{8,12},{12,8},{1,5},{5,1},{9,13},{13,9},{2,6},{6,2},{1... | collective-permute-start | bytes 589832 | tf_op jit(solution)/shard_map/ppermute | solution.py:227
  24.3 1.3 %multiply.5 = (f32[128,384]{1,0:T(8,128)S(1)}, f32[128,384]{1,0:T(8,128)S(1)}) custom-call(s32[3]{0:T(128)S(1)} %pad_add_fusion.refs_0_, s32[16,16]{1,0:T(8,128)S(1)} %copy-done.1, s32[16]{0:T(128)S(1)} %copy-done.2, bf16[256,384]{1,0:T(8,128)(2,1)S(1)} %get-tuple-element.28.refs_3_, bf16[256,384]{1,0:T(8,128)(2,1)S(1)} %get-tuple-element.29.refs_4_, ...), custom_call_target="tpu_custom_call" | custom-call | flops 226492416 | bytes 1377356 | tf_op jit(solution)/shard_map/multiply/pallas_call | solution.py:194
  25.7 1.6 %collective-permute-start.4 = (f32[64,384]{1,0:T(8,128)S(1)}, f32[64,384]{1,0:T(8,128)S(1)}, u32[]{:S(2)}, u32[]{:S(2)}) collective-permute-start(f32[64,384]{1,0:T(8,128)S(1)} %get-tuple-element.33), channel_id=1, source_target_pairs={{0,8},{4,12},{8,0},{12,4},{1,9},{5,13},{9,1},{13,5},{2,10},{6,14},... | collective-permute-start | bytes 294920 | tf_op jit(solution)/shard_map/ppermute | solution.py:227
  27.2 0.6 %collective-permute-start.10 = (f32[64,384]{1,0:T(8,128)S(1)}, f32[64,384]{1,0:T(8,128)S(1)}, u32[]{:S(2)}, u32[]{:S(2)}) collective-permute-start(f32[64,384]{1,0:T(8,128)S(1)} %get-tuple-element.41), channel_id=1, source_target_pairs={{0,8},{4,12},{8,0},{12,4},{1,9},{5,13},{9,1},{13,5},{2,10},{6,14},... | collective-permute-start | bytes 294920 | tf_op jit(solution)/shard_map/ppermute | solution.py:227
  27.9 1.6 %collective-permute-start.7 = (f32[64,384]{1,0:T(8,128)S(1)}, f32[64,384]{1,0:T(8,128)S(1)}, u32[]{:S(2)}, u32[]{:S(2)}) collective-permute-start(f32[64,384]{1,0:T(8,128)S(1)} %get-tuple-element.37), channel_id=1, source_target_pairs={{0,8},{4,12},{8,0},{12,4},{1,9},{5,13},{9,1},{13,5},{2,10},{6,14},... | collective-permute-start | bytes 294920 | tf_op jit(solution)/shard_map/ppermute | solution.py:227
  29.4 1.9 %collective-permute-done.4.refs_3_ = f32[64,384]{1,0:T(8,128)S(1)} collective-permute-done((f32[64,384]{1,0:T(8,128)S(1)}, f32[64,384]{1,0:T(8,128)S(1)}, u32[]{:S(2)}, u32[]{:S(2)}) %collective-permute-start.4) | collective-permute-done | bytes 98336 | tf_op jit(solution)/shard_map/ppermute | solution.py:227
  31.3 2.1 %collective-permute-done.10.refs_7_ = f32[64,384]{1,0:T(8,128)S(1)} collective-permute-done((f32[64,384]{1,0:T(8,128)S(1)}, f32[64,384]{1,0:T(8,128)S(1)}, u32[]{:S(2)}, u32[]{:S(2)}) %collective-permute-start.10) | collective-permute-done | bytes 98336 | tf_op jit(solution)/shard_map/ppermute | solution.py:227
  33.4 1.7 %collective-permute-done.7.refs_5_ = f32[64,384]{1,0:T(8,128)S(1)} collective-permute-done((f32[64,384]{1,0:T(8,128)S(1)}, f32[64,384]{1,0:T(8,128)S(1)}, u32[]{:S(2)}, u32[]{:S(2)}) %collective-permute-start.7) | collective-permute-done | bytes 98336 | tf_op jit(solution)/shard_map/ppermute | solution.py:227
  35.1 0.9 %finish.2.refs_5_.refs_7_.refs_2_ = f32[64,1536]{1,0:T(8,128)S(1)} custom-call(s32[3]{0:T(128)S(1)} %pad_add_fusion.refs_0_, s32[16]{0:T(128)S(1)} %copy-done.2, f32[64,384]{1,0:T(8,128)S(1)} %get-tuple-element.32.refs_2_, f32[64,384]{1,0:T(8,128)S(1)} %collective-permute-done.4.refs_3_, f32[64,384]{1,0:T(8,128)S(1)} %get-tuple-element.36.refs_4_, ...), custom_call_target="tpu_custom_call" | custom-call | flops 393216 | bytes 983116 | tf_op jit(solution)/shard_map/finish/pallas_call | solution.py:194
  36.1 0.7 %corner.1 = (f32[128,384]{1,0:T(8,128)S(1)}, f32[128,384]{1,0:T(8,128)S(1)}) custom-call(s32[3]{0:T(128)S(1)} %pad_add_fusion.refs_0_, s32[16,16]{1,0:T(8,128)S(1)} %copy-done.1, s32[16]{0:T(128)S(1)} %copy-done.2, f32[384,384]{1,0:T(8,128)S(1)} %collective-permute-done.11.refs_3_.refs_5_, f32[384,384]{1,0:T(8,128)S(1)} %collective-permute-done.12.refs_4_.refs_6_, ...), custom_call_target="tpu_custom_call" | custom-call | flops 226492416 | bytes 1573964 | tf_op jit(solution)/shard_map/corner/pallas_call | solution.py:194
  36.9 1.2 %multiply.7 = (f32[128,384]{1,0:T(8,128)S(1)}, f32[128,384]{1,0:T(8,128)S(1)}) custom-call(s32[3]{0:T(128)S(1)} %pad_add_fusion.refs_0_, s32[16,16]{1,0:T(8,128)S(1)} %copy-done.1, s32[16]{0:T(128)S(1)} %copy-done.2, bf16[256,384]{1,0:T(8,128)(2,1)S(1)} %get-tuple-element.28.refs_3_, bf16[256,384]{1,0:T(8,128)(2,1)S(1)} %get-tuple-element.29.refs_4_, ...), custom_call_target="tpu_custom_call" | custom-call | flops 226492416 | bytes 1967180 | tf_op jit(solution)/shard_map/multiply/pallas_call | solution.py:194
  38.1 0.6 %collective-permute-start.16 = (f32[128,384]{1,0:T(8,128)S(1)}, f32[128,384]{1,0:T(8,128)S(1)}, u32[]{:S(2)}, u32[]{:S(2)}) collective-permute-start(f32[128,384]{1,0:T(8,128)S(1)} %get-tuple-element.48), channel_id=1, source_target_pairs={{0,4},{4,0},{8,12},{12,8},{1,5},{5,1},{9,13},{13,9},{2,6},{6,2},{1... | collective-permute-start | bytes 589832 | tf_op jit(solution)/shard_map/ppermute | solution.py:227
  38.7 1.6 %collective-permute-start.14 = (f32[64,384]{1,0:T(8,128)S(1)}, f32[64,384]{1,0:T(8,128)S(1)}, u32[]{:S(2)}, u32[]{:S(2)}) collective-permute-start(f32[64,384]{1,0:T(8,128)S(1)} %get-tuple-element.46), channel_id=1, source_target_pairs={{0,8},{4,12},{8,0},{12,4},{1,9},{5,13},{9,1},{13,5},{2,10},{6,14},... | collective-permute-start | bytes 294920 | tf_op jit(solution)/shard_map/ppermute | solution.py:227
  40.3 1.1 %collective-permute-start.17 = (f32[64,384]{1,0:T(8,128)S(1)}, f32[64,384]{1,0:T(8,128)S(1)}, u32[]{:S(2)}, u32[]{:S(2)}) collective-permute-start(f32[64,384]{1,0:T(8,128)S(1)} %get-tuple-element.50), channel_id=1, source_target_pairs={{0,8},{4,12},{8,0},{12,4},{1,9},{5,13},{9,1},{13,5},{2,10},{6,14},... | collective-permute-start | bytes 294920 | tf_op jit(solution)/shard_map/ppermute | solution.py:227
  41.3 2.9 %collective-permute-done.14.refs_1_ = f32[64,384]{1,0:T(8,128)S(1)} collective-permute-done((f32[64,384]{1,0:T(8,128)S(1)}, f32[64,384]{1,0:T(8,128)S(1)}, u32[]{:S(2)}, u32[]{:S(2)}) %collective-permute-start.14) | collective-permute-done | bytes 98336 | tf_op jit(solution)/shard_map/ppermute | solution.py:227
  44.3 4.3 %collective-permute-start.15 = (f32[64,384]{1,0:T(8,128)S(1)}, f32[64,384]{1,0:T(8,128)S(1)}, u32[]{:S(2)}, u32[]{:S(2)}) collective-permute-start(f32[64,384]{1,0:T(8,128)S(1)} %add.21), channel_id=1, source_target_pairs={{0,1},{1,0},{2,3},{3,2},{4,5},{5,4},{6,7},{7,6},{8,9},{9,8},{10,11... | collective-permute-start | bytes 294920 | tf_op jit(solution)/shard_map/ppermute | solution.py:224
  48.6 2.6 %collective-permute-done.15.refs_3_ = f32[64,384]{1,0:T(8,128)S(1)} collective-permute-done((f32[64,384]{1,0:T(8,128)S(1)}, f32[64,384]{1,0:T(8,128)S(1)}, u32[]{:S(2)}, u32[]{:S(2)}) %collective-permute-start.15) | collective-permute-done | bytes 98336 | tf_op jit(solution)/shard_map/ppermute | solution.py:224
  51.1 1.7 %finish.3 = f32[64,1536]{1,0:T(8,128)} custom-call(s32[3]{0:T(128)S(1)} %pad_add_fusion.refs_0_, s32[16]{0:T(128)S(1)} %copy-done.2, f32[64,1536]{1,0:T(8,128)S(1)} %finish.2.refs_5_.refs_7_.refs_2_, f32[64,384]{1,0:T(8,128)S(1)} %collective-permute-done.15.refs_3_, f32[64,384]{1,0:T(8,128)S(1)} %get-tuple-element.49.refs_4_, ...), custom_call_target="tpu_custom_call" | custom-call | flops 393216 | bytes 1081420 | tf_op jit(solution)/shard_map/finish/pallas_call | solution.py:194
  (30 shorter events, 0.6 us)
Async XLA Ops:
  0.0 15.8 %collective-permute-start.8 = (f32[384,384]{1,0:T(8,128)}, f32[384,384]{1,0:T(8,128)S(1)}, u32[]{:S(2)}, u32[]{:S(2)}) collective-permute-start(f32[384,384]{1,0:T(8,128)} %refs_5_.1), channel_id=1, source_target_pairs={{0,0},{3,3},{1,2},{2,1},{4,4},{7,7},{5,6},{6,5},{8,8},{11,11},{9,1... | collective-permute-start | bytes 1769480 | tf_op jit(solution)/shard_map/ppermute | solution.py:224
  1.7 18.6 %collective-permute-start.5 = (f32[384,384]{1,0:T(8,128)}, f32[384,384]{1,0:T(8,128)S(1)}, u32[]{:S(2)}, u32[]{:S(2)}) collective-permute-start(f32[384,384]{1,0:T(8,128)} %refs_5_.1), channel_id=1, source_target_pairs={{0,1},{1,0},{2,3},{3,2},{4,5},{5,4},{6,7},{7,6},{8,9},{9,8},{10,11... | collective-permute-start | bytes 1769480 | tf_op jit(solution)/shard_map/ppermute | solution.py:224
  7.6 1.9 %copy-start.3 = (s32[32,16]{0,1:T(8,128)S(1)}, s32[32,16]{0,1:T(8,128)}, u32[]{:S(2)}) copy-start(s32[32,16]{0,1:T(8,128)} %param.7) | copy-start | bytes 6148
  7.7 5.1 %collective-permute-start.2 = (f32[64,384]{1,0:T(8,128)S(1)}, f32[64,384]{1,0:T(8,128)S(1)}, u32[]{:S(2)}, u32[]{:S(2)}) collective-permute-start(f32[64,384]{1,0:T(8,128)S(1)} %get-tuple-element.51), channel_id=1, source_target_pairs={{0,12},{4,8},{8,4},{12,0},{1,13},{5,9},{9,5},{13,1},{2,14},{6,10},... | collective-permute-start | bytes 294920 | tf_op jit(solution)/shard_map/ppermute | solution.py:227
  8.1 6.8 %collective-permute-start = (f32[64,384]{1,0:T(8,128)S(1)}, f32[64,384]{1,0:T(8,128)S(1)}, u32[]{:S(2)}, u32[]{:S(2)}) collective-permute-start(f32[64,384]{1,0:T(8,128)S(1)} %get-tuple-element.52), channel_id=1, source_target_pairs={{0,8},{4,12},{8,0},{12,4},{1,9},{5,13},{9,1},{13,5},{2,10},{6,14},... | collective-permute-start | bytes 294920 | tf_op jit(solution)/shard_map/ppermute | solution.py:227
  9.3 5.6 %collective-permute-start.1 = (f32[64,384]{1,0:T(8,128)S(1)}, f32[64,384]{1,0:T(8,128)S(1)}, u32[]{:S(2)}, u32[]{:S(2)}) collective-permute-start(f32[64,384]{1,0:T(8,128)S(1)} %get-tuple-element.54), channel_id=1, source_target_pairs={{0,4},{4,0},{8,12},{12,8},{1,5},{5,1},{9,13},{13,9},{2,6},{6,2},{1... | collective-permute-start | bytes 294920 | tf_op jit(solution)/shard_map/ppermute | solution.py:227
  15.9 5.2 %copy-start = (f32[384,384]{1,0:T(8,128)S(1)}, f32[384,384]{1,0:T(8,128)}, u32[]{:S(2)}) copy-start(f32[384,384]{1,0:T(8,128)} %refs_5_.1) | copy-start | bytes 1769476
  15.9 5.2 %copy-start.1 = (s32[16,16]{1,0:T(8,128)S(1)}, s32[16,16]{1,0:T(8,128)}, u32[]{:S(2)}) copy-start(s32[16,16]{1,0:T(8,128)} %refs_1_.13) | copy-start | bytes 3076
  16.0 20.1 %collective-permute-start.11 = (f32[384,384]{1,0:T(8,128)S(1)}, f32[384,384]{1,0:T(8,128)S(1)}, u32[]{:S(2)}, u32[]{:S(2)}) collective-permute-start(f32[384,384]{1,0:T(8,128)S(1)} %broadcast_select_fusion), channel_id=1, source_target_pairs={{0,1},{1,0},{2,3},{3,2},{4,5},{5,4},{6,7},{7,6},{8,9},{9,8},{10,11... | collective-permute-start | bytes 1769480 | tf_op jit(solution)/shard_map/ppermute | solution.py:224
  20.3 15.8 %collective-permute-start.12 = (f32[384,384]{1,0:T(8,128)S(1)}, f32[384,384]{1,0:T(8,128)S(1)}, u32[]{:S(2)}, u32[]{:S(2)}) collective-permute-start(f32[384,384]{1,0:T(8,128)S(1)} %collective-permute-done.5.refs_5_), channel_id=1, source_target_pairs={{0,0},{3,3},{1,2},{2,1},{4,4},{7,7},{5,6},{6,5},{8,8},{11,11},{9,1... | collective-permute-start | bytes 1769480 | tf_op jit(solution)/shard_map/ppermute | solution.py:224
  21.0 0.7 %copy-start.2 = (s32[16]{0:T(128)S(1)}, s32[16]{0:T(128)}, u32[]{:S(2)}) copy-start(s32[16]{0:T(128)} %refs_1_.14) | copy-start | bytes 196
  22.9 2.7 %collective-permute-start.3 = (f32[128,384]{1,0:T(8,128)S(1)}, f32[128,384]{1,0:T(8,128)S(1)}, u32[]{:S(2)}, u32[]{:S(2)}) collective-permute-start(f32[128,384]{1,0:T(8,128)S(1)} %get-tuple-element.31), channel_id=1, source_target_pairs={{0,4},{4,0},{8,12},{12,8},{1,5},{5,1},{9,13},{13,9},{2,6},{6,2},{1... | collective-permute-start | bytes 589832 | tf_op jit(solution)/shard_map/ppermute | solution.py:227
  23.7 3.5 %collective-permute-start.9 = (f32[128,384]{1,0:T(8,128)S(1)}, f32[128,384]{1,0:T(8,128)S(1)}, u32[]{:S(2)}, u32[]{:S(2)}) collective-permute-start(f32[128,384]{1,0:T(8,128)S(1)} %get-tuple-element.39), channel_id=1, source_target_pairs={{0,4},{4,0},{8,12},{12,8},{1,5},{5,1},{9,13},{13,9},{2,6},{6,2},{1... | collective-permute-start | bytes 589832 | tf_op jit(solution)/shard_map/ppermute | solution.py:227
  25.5 2.3 %collective-permute-start.6 = (f32[128,384]{1,0:T(8,128)S(1)}, f32[128,384]{1,0:T(8,128)S(1)}, u32[]{:S(2)}, u32[]{:S(2)}) collective-permute-start(f32[128,384]{1,0:T(8,128)S(1)} %get-tuple-element.35), channel_id=1, source_target_pairs={{0,4},{4,0},{8,12},{12,8},{1,5},{5,1},{9,13},{13,9},{2,6},{6,2},{1... | collective-permute-start | bytes 589832 | tf_op jit(solution)/shard_map/ppermute | solution.py:227
  25.7 5.7 %collective-permute-start.4 = (f32[64,384]{1,0:T(8,128)S(1)}, f32[64,384]{1,0:T(8,128)S(1)}, u32[]{:S(2)}, u32[]{:S(2)}) collective-permute-start(f32[64,384]{1,0:T(8,128)S(1)} %get-tuple-element.33), channel_id=1, source_target_pairs={{0,8},{4,12},{8,0},{12,4},{1,9},{5,13},{9,1},{13,5},{2,10},{6,14},... | collective-permute-start | bytes 294920 | tf_op jit(solution)/shard_map/ppermute | solution.py:227
  27.2 6.2 %collective-permute-start.10 = (f32[64,384]{1,0:T(8,128)S(1)}, f32[64,384]{1,0:T(8,128)S(1)}, u32[]{:S(2)}, u32[]{:S(2)}) collective-permute-start(f32[64,384]{1,0:T(8,128)S(1)} %get-tuple-element.41), channel_id=1, source_target_pairs={{0,8},{4,12},{8,0},{12,4},{1,9},{5,13},{9,1},{13,5},{2,10},{6,14},... | collective-permute-start | bytes 294920 | tf_op jit(solution)/shard_map/ppermute | solution.py:227
  27.9 7.2 %collective-permute-start.7 = (f32[64,384]{1,0:T(8,128)S(1)}, f32[64,384]{1,0:T(8,128)S(1)}, u32[]{:S(2)}, u32[]{:S(2)}) collective-permute-start(f32[64,384]{1,0:T(8,128)S(1)} %get-tuple-element.37), channel_id=1, source_target_pairs={{0,8},{4,12},{8,0},{12,4},{1,9},{5,13},{9,1},{13,5},{2,10},{6,14},... | collective-permute-start | bytes 294920 | tf_op jit(solution)/shard_map/ppermute | solution.py:227
  36.8 1.9 %collective-permute-start.13 = (f32[128,384]{1,0:T(8,128)S(1)}, f32[128,384]{1,0:T(8,128)S(1)}, u32[]{:S(2)}, u32[]{:S(2)}) collective-permute-start(f32[128,384]{1,0:T(8,128)S(1)} %get-tuple-element.44), channel_id=1, source_target_pairs={{0,4},{4,0},{8,12},{12,8},{1,5},{5,1},{9,13},{13,9},{2,6},{6,2},{1... | collective-permute-start | bytes 589832 | tf_op jit(solution)/shard_map/ppermute | solution.py:227
  38.1 2.1 %collective-permute-start.16 = (f32[128,384]{1,0:T(8,128)S(1)}, f32[128,384]{1,0:T(8,128)S(1)}, u32[]{:S(2)}, u32[]{:S(2)}) collective-permute-start(f32[128,384]{1,0:T(8,128)S(1)} %get-tuple-element.48), channel_id=1, source_target_pairs={{0,4},{4,0},{8,12},{12,8},{1,5},{5,1},{9,13},{13,9},{2,6},{6,2},{1... | collective-permute-start | bytes 589832 | tf_op jit(solution)/shard_map/ppermute | solution.py:227
  38.7 5.6 %collective-permute-start.14 = (f32[64,384]{1,0:T(8,128)S(1)}, f32[64,384]{1,0:T(8,128)S(1)}, u32[]{:S(2)}, u32[]{:S(2)}) collective-permute-start(f32[64,384]{1,0:T(8,128)S(1)} %get-tuple-element.46), channel_id=1, source_target_pairs={{0,8},{4,12},{8,0},{12,4},{1,9},{5,13},{9,1},{13,5},{2,10},{6,14},... | collective-permute-start | bytes 294920 | tf_op jit(solution)/shard_map/ppermute | solution.py:227
  40.3 8.3 %collective-permute-start.17 = (f32[64,384]{1,0:T(8,128)S(1)}, f32[64,384]{1,0:T(8,128)S(1)}, u32[]{:S(2)}, u32[]{:S(2)}) collective-permute-start(f32[64,384]{1,0:T(8,128)S(1)} %get-tuple-element.50), channel_id=1, source_target_pairs={{0,8},{4,12},{8,0},{12,4},{1,9},{5,13},{9,1},{13,5},{2,10},{6,14},... | collective-permute-start | bytes 294920 | tf_op jit(solution)/shard_map/ppermute | solution.py:227
  44.3 6.9 %collective-permute-start.15 = (f32[64,384]{1,0:T(8,128)S(1)}, f32[64,384]{1,0:T(8,128)S(1)}, u32[]{:S(2)}, u32[]{:S(2)}) collective-permute-start(f32[64,384]{1,0:T(8,128)S(1)} %add.21), channel_id=1, source_target_pairs={{0,1},{1,0},{2,3},{3,2},{4,5},{5,4},{6,7},{7,6},{8,9},{9,8},{10,11... | collective-permute-start | bytes 294920 | tf_op jit(solution)/shard_map/ppermute | solution.py:224

commit v3 on v0

v3 whole, which is shorter than its diff:
```python
import functools

import jax
import jax.numpy as jnp
from jax import lax
from jax.experimental import pallas as pl
from jax.experimental.pallas import tpu as pltpu
from jax.sharding import PartitionSpec as P

TB = 96
OTB = 32
GROUP = 384
PER = GROUP // TB

VMEM = pl.BlockSpec(memory_space=pltpu.VMEM)
SMEM = pl.BlockSpec(memory_space=pltpu.SMEM)
EVEN, ODD, OWN, CORNER = 0, 1, 2, 3
WEIGHT = 10**10


def split(x):
    high = x.astype(jnp.bfloat16)
    low = (x - high.astype(jnp.float32)).astype(jnp.bfloat16)
    return high, low


def lane_mask(values, lane_tile):
    out = jnp.zeros(lane_tile.shape, jnp.float32)
    for i, v in enumerate(values):
        out = jnp.where(lane_tile == i, v.astype(jnp.float32), out)
    return out


def source_of(kind, step, c):
    if kind == OWN:
        return c
    if kind == CORNER:
        return jnp.where(c == 0, step, jnp.where(c == step, 0, -1))
    up = (c % 2) == kind
    return jnp.where(up, c + step, c - step)


def inside(index, n):
    return (index >= 0) & (index < n)


def tables_kernel(kinds, order, place, amp_mask, int_mask, owner, amp_rows, at_end, *refs):
    r, c, n_col = place[0], place[1], place[2]
    at_end[...] = jnp.broadcast_to(((c == 0) | (c == n_col - 1)).astype(jnp.float32), at_end.shape)
    count, depth = amp_rows.shape
    occ = count // len(order)
    lane_tile = lax.broadcasted_iota(jnp.int32, (1, depth), 1) // TB
    for p, d in enumerate(order):
        for o in range(occ):
            row = ((r ^ d) * n_col + c) * occ + o
            bits = [amp_mask[row, r * (depth // TB) + k] for k in range(depth // TB)]
            amp_rows[p * occ + o : p * occ + o + 1, :] = lane_mask(bits, lane_tile)
    for i, (kind, step) in enumerate(kinds):
        masks, homes = refs[2 * i : 2 * i + 2]
        source = source_of(kind, step, c)
        there = inside(source, n_col)
        source = jnp.clip(source, 0, n_col - 1)
        k_tiles, width = masks.shape
        c_tiles = width // TB
        tiles = [owner[source * c_tiles + t] for t in range(c_tiles)]
        lane_tile = lax.broadcasted_iota(jnp.int32, (1, width), 1) // TB
        for k in range(k_tiles):
            bits = [jnp.where(there, int_mask[r * k_tiles + k, t], 0) for t in tiles]
            masks[k : k + 1, :] = lane_mask(bits, lane_tile)
        rows = homes.shape[0] // (width // GROUP)
        at_home = lax.broadcasted_iota(jnp.int32, (rows, GROUP), 0)
        spot = lax.broadcasted_iota(jnp.int32, (rows, GROUP), 1) // TB
        for g in range(width // GROUP):
            marks = jnp.zeros((rows, GROUP), jnp.float32)
            for t in range(PER):
                tile = tiles[g * PER + t]
                turn = (tile - t + PER) % PER
                hit = (at_home == (tile // PER) * PER + turn) & (spot == tile % PER) & there
                marks = jnp.where(hit, 1.0, marks)
            homes[pl.ds(g * rows, rows), :] = marks


def masked_halves(pairs):
    k_tiles = pairs[0][1].shape[0]
    highs, lows = [], []
    for k in range(k_tiles):
        at = pl.ds(k * TB, TB)
        piece = sum(block[at, :] * masks[k : k + 1, :] for block, masks in pairs)
        h, l = split(piece)
        highs.append(h)
        lows.append(l)
    return jnp.concatenate(highs, axis=0), jnp.concatenate(lows, axis=0)


def product(a_high, a_low, b_high, b_low):
    dot = functools.partial(jnp.dot, preferred_element_type=jnp.float32)
    return dot(a_high, b_high) + (dot(a_high, b_low) + dot(a_low, b_high))


def multiply_kernel(groups, high, low, *refs):
    pairs, (keep, give) = refs[:-2], refs[-2:]
    pairs = list(zip(pairs[::2], pairs[1::2]))
    half, width = keep.shape[0], keep.shape[1] // len(groups)
    for g, count in enumerate(groups):
        b_high, b_low = masked_halves(pairs[:count])
        pairs = pairs[count:]
        for out, start in ((give, half), (keep, 0)):
            at = pl.ds(start, half)
            out[:, g * width : (g + 1) * width] = product(high[at, :], low[at, :], b_high, b_low)


def own_kernel(n_row, amp_rows, *refs):
    pieces, (block, masks, high, low, slab, keep, give) = refs[:n_row], refs[n_row:]
    rows = pieces[0].shape[0]
    occ = rows // OTB
    for p, piece in enumerate(pieces):
        for o in range(occ):
            masked = piece[o * OTB : (o + 1) * OTB, :] * amp_rows[p * occ + o : p * occ + o + 1, :]
            at = pl.ds(p * rows + o * OTB, OTB)
            slab[at, :] = masked
            high[at, :], low[at, :] = split(masked)
    used = n_row * rows
    if slab.shape[0] > used:
        slab[used:, :] = jnp.zeros((slab.shape[0] - used, slab.shape[1]), jnp.float32)
    multiply_kernel((1,), high, low, block, masks, keep, give)


def pick_kernel(at_end, slab, block, out):
    out[...] = jnp.where(at_end[0:1, :] > 0.5, slab[...], block[...])


def halves_kernel(*refs):
    pairs, (high, low) = refs[:-2], refs[-2:]
    high[...], low[...] = masked_halves(list(zip(pairs[::2], pairs[1::2])))


def last_kernel(high, low, b_high, b_low, keep, give):
    half = keep.shape[0]
    for out, start in ((give, half), (keep, 0)):
        at = pl.ds(start, half)
        out[...] = product(high[at, :], low[at, :], b_high[...], b_low[...])


def corner_kernel(slab, b_high, b_low, keep, give):
    half = keep.shape[0]
    for out, start in ((give, half), (keep, 0)):
        a_high, a_low = split(slab[pl.ds(start, half), :])
        out[...] = product(a_high, a_low, b_high[...], b_low[...])


def fold_kernel(keep, got, *outs):
    rows = outs[0].shape[0]
    for i, out in enumerate(outs):
        at = pl.ds(i * rows, rows)
        out[...] = keep[at, :] + got[at, :]


def add_kernel(*refs):
    total = refs[0][...]
    for share in refs[1:-1]:
        total = total + share[...]
    refs[-1][...] = total


def finish_kernel(counts, *refs):
    out = refs[-1]
    n_in = sum(counts) + len(counts)
    rows = out.shape[0]
    n_home = out.shape[1] // GROUP
    slots, first = [], 0
    for count in counts:
        slots.append((refs[first], refs[first + 1 : first + 1 + count]))
        first += 1 + count
    totals = []
    for homes, shares in slots:
        total = shares[0][...]
        for share in shares[1:]:
            total = total + share[...]
        for g in range(total.shape[1] // GROUP):
            part = total[:, g * GROUP : (g + 1) * GROUP]
            turned = [part] + [pltpu.roll(part, t * TB, 1) for t in range(1, PER)]
            totals.append((homes, g * n_home * PER, turned))
    for home in range(n_home):
        to = pl.ds(home * GROUP, GROUP)
        if len(refs) - 1 > n_in:
            value = refs[n_in][:, to]
        else:
            value = jnp.zeros((rows, GROUP), jnp.float32)
        for homes, base, turned in totals:
            for t in range(PER):
                row = base + home * PER + t
                value = jnp.where(homes[row : row + 1, :] > 0.5, turned[t], value)
        out[:, to] = value


def call(kernel, name, outs, n_smem, *args, flops=0, after=()):
    moved = sum(x.size * x.dtype.itemsize for x in list(args) + list(outs))
    n_args, n_after = len(args), len(after)

    def body(*refs):
        kernel(*refs[:n_args], *refs[n_args + n_after :])

    return pl.pallas_call(
        body,
        out_shape=outs,
        in_specs=[SMEM] * n_smem
        + [VMEM] * (len(args) - n_smem)
        + [pl.BlockSpec(memory_space=pl.ANY)] * n_after,
        out_specs=[VMEM] * len(outs),
        compiler_params=pltpu.CompilerParams(vmem_limit_bytes=40 * 2**20),
        cost_estimate=pl.CostEstimate(
            flops=int(flops), bytes_accessed=int(moved), transcendentals=0
        ),
        name=name,
    )(*args, *after)


def f32(*shape):
    return jax.ShapeDtypeStruct(shape, jnp.float32)


def on_device(n_row, n_col, amplitudes, integrals, amp_mask, int_mask, owner_map):
    rows, pairs = amplitudes.shape
    depth, width = integrals.shape
    total = n_row * rows
    r, c = lax.axis_index("row"), lax.axis_index("col")
    place = jnp.stack([r, c, jnp.int32(n_col)]).astype(jnp.int32)
    order = list(range(0, n_row, 2)) + list(range(1, n_row, 2))

    def swap_line(x, kind):
        ends = [(i, i) for i in range(n_col) if not 0 <= (i + kind ^ 1) - kind < n_col]
        inner = [(i, (i + kind ^ 1) - kind) for i in range(n_col)]
        return lax.ppermute(x, "col", ends + [p for p in inner if 0 <= p[1] < n_col])

    def swap(x, d):
        return lax.ppermute(x, "row", [(i, i ^ d) for i in range(n_row)])

    even, odd = swap_line(integrals, EVEN), swap_line(integrals, ODD)

    def columns(d):
        return lax.dynamic_slice_in_dim(amplitudes, (r ^ d) * depth, depth, 1)

    pieces = [swap(columns(d), d) if d else columns(0) for d in order]
    corner = n_col >= 4 and total <= depth and depth == width
    last = n_col - 2 if corner else n_col - 1
    kinds = [(OWN, 0)] + [(kind, step) for step in range(1, last + 1) for kind in (EVEN, ODD)]
    ends = (CORNER, n_col - 1)
    k_tiles, tiles = depth // TB, pairs // TB
    per_slot = [f32(k_tiles, width), f32(width // GROUP * tiles, GROUP)]
    amp_rows, at_end, *made = call(
        functools.partial(tables_kernel, kinds + [ends], order),
        "tables",
        [f32(total // OTB, depth), f32(8, width)] + per_slot * (len(kinds) + 1),
        4,
        place,
        amp_mask,
        int_mask,
        owner_map,
    )
    masks = dict(zip(kinds + [ends], made[::2]))
    homes = dict(zip(kinds + [ends], made[1::2]))

    def exchange(keep, give):
        got = swap(give, 1)
        shape = f32(rows, keep.shape[1])
        pieces = call(fold_kernel, "fold", [shape] * (n_row // 2), 0, keep, got)
        return [pieces[0]] + [swap(pieces[i], 2 * i) for i in range(1, n_row // 2)]

    def multiply(name, *groups, after=()):
        keep, give = call(
            functools.partial(multiply_kernel, tuple(len(group) for group in groups)),
            name,
            [f32(total // 2, len(groups) * width)] * 2,
            0,
            high,
            low,
            *[x for group in groups for slot, block in group for x in (block, masks[slot])],
            flops=6 * total * depth * width * len(groups),
            after=after,
        )
        return [[slot for slot, _ in group] for group in groups], exchange(keep, give)

    def finish(slots, *so_far):
        args, counts = [], []
        for groups, shares in slots:
            args.append(jnp.concatenate([sum(homes[name] for name in names) for names in groups]))
            args.extend(shares)
            counts.append(len(shares))
        return call(
            functools.partial(finish_kernel, counts),
            "finish",
            [f32(rows, pairs)],
            0,
            *args,
            *so_far,
            flops=rows * pairs * n_row,
        )[0]

    high, low, slab, keep, give = call(
        functools.partial(own_kernel, n_row),
        "own",
        [jax.ShapeDtypeStruct((total, depth), jnp.bfloat16)] * 2
        + [f32(depth if corner else total, depth)]
        + [f32(total // 2, width)] * 2,
        0,
        amp_rows,
        *pieces,
        integrals,
        masks[OWN, 0],
        flops=6 * total * depth * width,
    )
    slots = [([[(OWN, 0)]], exchange(keep, give))]
    for step in range(1, last + 1):
        if step > 1:
            going = odd
            if corner and step == 2:
                going = call(
                    pick_kernel,
                    "pick",
                    [f32(depth, width)],
                    0,
                    at_end,
                    slab,
                    odd,
                    after=(slots[0][1][0],),
                )[0]
            even, odd = swap_line(going, EVEN), swap_line(even, ODD)
            if corner and step == 2:
                end_slab = even
        if 2 * step <= n_col - 1:
            slots.append(multiply("pair", [((EVEN, step), even)], [((ODD, step), odd)]))
            continue
        if step < last:
            slots.append(multiply("both", [((EVEN, step), even), ((ODD, step), odd)]))
            continue
        out = finish(slots)
        b_halves = call(
            halves_kernel,
            "halves",
            [jax.ShapeDtypeStruct((depth, width), jnp.bfloat16)] * 2,
            0,
            even,
            masks[EVEN, step],
            odd,
            masks[ODD, step],
            flops=WEIGHT,
        )
        after = tuple(share for _, shares in slots for share in shares)
        sums = [f32(total // 2, width)] * 2
        flops = 6 * total * depth * width
        slots = []
        if corner:
            parts = call(corner_kernel, "corner", sums, 0, end_slab, *b_halves, flops=flops, after=after)
            summed = call(add_kernel, "add", [f32(rows, width)], 0, *exchange(*parts))[0]
            slots.append(([[ends]], [swap_line(summed, EVEN)]))
        parts = call(last_kernel, "last", sums, 0, high, low, *b_halves, flops=flops, after=after)
        slots.append(([[(EVEN, step), (ODD, step)]], exchange(*parts)))
    return finish(slots, out)


def solution(mesh):
    placed = (
        P(("mol", "row", "col"), None),
        P(("mol", "row"), "col"),
        P("mol", None),
        P("mol", None),
        P("mol"),
    )
    return jax.shard_map(
        functools.partial(on_device, mesh.shape["row"], mesh.shape["col"]),
        mesh=mesh,
        in_specs=placed,
        out_specs=P(("mol", "row", "col"), None),
        check_vma=False,
    )
```

time: 116 us -> 49.4 us (0.43)
  waiting for transfers between devices: 75.5 us -> 15.8 us
  starting transfers between devices: 3.5 us -> 24.9 us
  between operations: 13.5 us -> 0.16 us
  blocking collectives: 11.5 us -> 0 us
  Pallas kernels: 0 us -> 6.43 us
  matrix products: 6.39 us -> 0 us
  local copies, waits for them, and re-layouts: 3.84 us -> 1.73 us
  other arithmetic: 1.83 us -> 0.08 us
    all_gather x1 -> x0, waiting for transfers between devices: 41.2 us -> none  [on_device(): lax.all_gather(integral_local, 'col', axis=1, tiled=True)]
    reduce_scatter x1 -> x0, waiting for transfers between devices: 26.9 us -> none  [on_device(): lax.psum_scatter(partial_value, 'row', scatter_dimension=1, tiled=True)]
    ppermute x0 -> x16, starting transfers between devices: none -> 24.9 us  [the longest x5 16 us: swap_line(): lax.ppermute(x, 'col', ends + [p for p in inner if 0 <= p[1] < n_col])]
    ppermute x0 -> x16, waiting for transfers between devices: none -> 15.8 us  [the longest x5 9.55 us: swap_line(): lax.ppermute(x, 'col', ends + [p for p in inner if 0 <= p[1] < n_col])]
    all_to_all x1 -> x0, blocking collectives: 11.5 us -> none  [on_device(): lax.all_to_all(masked, 'row', split_axis=1, concat_axis=0, tiled=True)]
    all_to_all x1 -> x0, waiting for transfers between devices: 7.38 us -> none  [on_device(): lax.all_to_all(summed, 'row', split_axis=0, concat_axis=1, tiled=True)]
    pallas_call x0 -> x14, Pallas kernels: none -> 6.43 us  [call(): pl.pallas_call(body, out_shape=outs, in_specs=[SMEM] * n_smem + [VMEM] *...]
    dot_general x2 -> x0, matrix products: 6.39 us -> none  [the longest x1 5.52 us: on_device(): jnp.dot(slab, lax.all_gather(integral_local, 'col', axis=1, tiled=True),...]
  transfers between devices with their start and end apart: 3 -> 16, of which waited for: 3 -> 7; matrix products, arithmetic and copies ran while one was open for 1% -> 2% of each run, Pallas kernels for 0% -> 10%
where the time goes in v3:
time: 49.4 us; the launch traced here: 49.1 us
  starting transfers between devices  24.9 us (50%)
  waiting for transfers between devices  15.8 us (32%)
  Pallas kernels  6.43 us (13%)
  local copies, waits for them, and re-layouts  1.73 us (4%)
    ppermute x5, starting transfers between devices, swap_line(): lax.ppermute(x, 'col', ends + [p for p in inner if 0 <= p[1] < n_col])  16 us
    ppermute x5, waiting for transfers between devices, swap_line(): lax.ppermute(x, 'col', ends + [p for p in inner if 0 <= p[1] < n_col])  9.55 us
    ppermute x11, starting transfers between devices, swap(): return lax.ppermute(x, 'row', [(i, i ^ d) for i in range(n_row)])  8.97 us
    pallas_call x14, Pallas kernels, call(): pl.pallas_call(body, out_shape=outs, in_specs=[SMEM] * n_smem + [VMEM] *...  6.43 us
    ppermute x11, waiting for transfers between devices, swap(): return lax.ppermute(x, 'row', [(i, i ^ d) for i in range(n_row)])  6.27 us
    dynamic_slice x1, local copies, waits for them, and re-layouts, columns(): return lax.dynamic_slice_in_dim(amplitudes, (r ^ d) * depth, depth, 1)  1.06 us
  transfers between devices with their start and end apart: 16, of which 7 were waited for; matrix products, arithmetic and copies ran while one was open for 2% of the time, Pallas kernels for 10%

profile of v3, /device:TPU:0, one launch (start us, length us, event | category | flops | bytes accessed | tf_op | source)
XLA Modules:
  0.0 49.1 jit_solution(12052266823681896078)
XLA Ops:
  0.0 1.8 %collective-permute-start.3 = (f32[384,384]{1,0:T(8,128)}, f32[384,384]{1,0:T(8,128)S(1)}, u32[]{:S(2)}, u32[]{:S(2)}) collective-permute-start(f32[384,384]{1,0:T(8,128)} %refs_5_.1), channel_id=1, source_target_pairs={{0,0},{3,3},{1,2},{2,1},{4,4},{7,7},{5,6},{6,5},{8,8},{11,11},{9,1... | collective-permute-start | bytes 1769480 | tf_op jit(solution)/shard_map/ppermute | solution.py:233
  1.8 4.9 %collective-permute-start.6 = (f32[384,384]{1,0:T(8,128)}, f32[384,384]{1,0:T(8,128)S(1)}, u32[]{:S(2)}, u32[]{:S(2)}) collective-permute-start(f32[384,384]{1,0:T(8,128)} %refs_5_.1), channel_id=1, source_target_pairs={{0,1},{1,0},{2,3},{3,2},{4,5},{5,4},{6,7},{7,6},{8,9},{9,8},{10,11... | collective-permute-start | bytes 1769480 | tf_op jit(solution)/shard_map/ppermute | solution.py:233
  6.7 1.1 %constant_dynamic-slice_fusion = (f32[64,384]{1,0:T(8,128)S(1)}, f32[64,384]{1,0:T(8,128)S(1)}, f32[64,384]{1,0:T(8,128)S(1)}, f32[64,384]{1,0:T(8,128)S(1)}) fusion(f32[64,1536]{1,0:T(8,128)} %param.5, s32[]{:T(128)S(6)} %select_n.15, s32[]{:T(128)S(6)} %select_n.13, s32[]{:T(128)S(6)} %select_n.12, s32[]{:T(128)S(6)} %select_n.14), kind=kLoop, calls=%fused_computation.1 | loop fusion | bytes 786448 | tf_op jit(solution)/shard_map/dynamic_slice | solution.py:241
  7.8 1.6 %collective-permute-start = (f32[64,384]{1,0:T(8,128)S(1)}, f32[64,384]{1,0:T(8,128)S(1)}, u32[]{:S(2)}, u32[]{:S(2)}) collective-permute-start(f32[64,384]{1,0:T(8,128)S(1)} %get-tuple-element.74), channel_id=1, source_target_pairs={{0,8},{4,12},{8,0},{12,4},{1,9},{5,13},{9,1},{13,5},{2,10},{6,14},... | collective-permute-start | bytes 294920 | tf_op jit(solution)/shard_map/ppermute | solution.py:236
  9.3 0.6 %collective-permute-start.2 = (f32[64,384]{1,0:T(8,128)S(1)}, f32[64,384]{1,0:T(8,128)S(1)}, u32[]{:S(2)}, u32[]{:S(2)}) collective-permute-start(f32[64,384]{1,0:T(8,128)S(1)} %get-tuple-element.73), channel_id=1, source_target_pairs={{0,12},{4,8},{8,4},{12,0},{1,13},{5,9},{9,5},{13,1},{2,14},{6,10},... | collective-permute-start | bytes 294920 | tf_op jit(solution)/shard_map/ppermute | solution.py:236
  10.0 0.1 copy.6.refs_1_
  10.1 0.1 pad_add_fusion.refs_0_
  10.1 0.5 %copy-done.1 = s32[16,16]{1,0:T(8,128)S(1)} copy-done((s32[16,16]{1,0:T(8,128)S(1)}, s32[16,16]{1,0:T(8,128)}, u32[]{:S(2)}) %copy-start.1) | copy-done | bytes 1048
  10.7 2.0 %tables.1 = (f32[8,384]{1,0:T(8,128)S(1)}, f32[8,384]{1,0:T(8,128)S(1)}, f32[4,384]{1,0:T(4,128)S(1)}, f32[16,384]{1,0:T(8,128)S(1)}, f32[4,384]{1,0:T(4,128)S(1...) custom-call(s32[3]{0:T(128)S(1)} %pad_add_fusion.refs_0_, ...), custom_call_target="tpu_custom_call" | custom-call | bytes 212044 | tf_op jit(solution)/shard_map/tables/pallas_call | solution.py:203
  12.7 1.3 %collective-permute-done.2.refs_4_ = f32[64,384]{1,0:T(8,128)S(1)} collective-permute-done((f32[64,384]{1,0:T(8,128)S(1)}, f32[64,384]{1,0:T(8,128)S(1)}, u32[]{:S(2)}, u32[]{:S(2)}) %collective-permute-start.2) | collective-permute-done | bytes 98336 | tf_op jit(solution)/shard_map/ppermute | solution.py:236
  14.1 0.6 %own.1 = (bf16[256,384]{1,0:T(8,128)(2,1)S(1)}, bf16[256,384]{1,0:T(8,128)(2,1)S(1)}, f32[384,384]{1,0:T(8,128)S(1)}, f32[128,384]{1,0:T(8,128)S(1)}, f32[128,384]{1,0:T(8,128)S(1)}) custom-call(f32[8,384]{1,0:T(8,128)S(1)} %get-tuple-element.41.refs_0_, f32[64,384]{1,0:T(8,128)S(1)} %get-tuple-element.75.refs_1_, ...), custom_call_target="tpu_custom_call" | custom-call | flops 226492416 | bytes 2377728 | tf_op jit(solution)/shard_map/own/pallas_call | solution.py:203
  14.6 0.7 %collective-permute-start.4 = (f32[128,384]{1,0:T(8,128)S(1)}, f32[128,384]{1,0:T(8,128)S(1)}, u32[]{:S(2)}, u32[]{:S(2)}) collective-permute-start(f32[128,384]{1,0:T(8,128)S(1)} %get-tuple-element.45), channel_id=1, source_target_pairs={{0,4},{4,0},{8,12},{12,8},{1,5},{5,1},{9,13},{13,9},{2,6},{6,2},{1... | collective-permute-start | bytes 589832 | tf_op jit(solution)/shard_map/ppermute | solution.py:236
  15.3 1.1 %collective-permute-done.4.refs_1_ = f32[128,384]{1,0:T(8,128)S(1)} collective-permute-done((f32[128,384]{1,0:T(8,128)S(1)}, f32[128,384]{1,0:T(8,128)S(1)}, u32[]{:S(2)}, u32[]{:S(2)}) %collective-permute-start.4) | collective-permute-done | bytes 196640 | tf_op jit(solution)/shard_map/ppermute | solution.py:236
  16.5 3.9 %collective-permute-start.5 = (f32[384,384]{1,0:T(8,128)S(1)}, f32[384,384]{1,0:T(8,128)S(1)}, u32[]{:S(2)}, u32[]{:S(2)}) collective-permute-start(f32[384,384]{1,0:T(8,128)S(1)} %pick.1), channel_id=1, source_target_pairs={{0,1},{1,0},{2,3},{3,2},{4,5},{5,4},{6,7},{7,6},{8,9},{9,8},{10,11... | collective-permute-start | bytes 1769480 | tf_op jit(solution)/shard_map/ppermute | solution.py:233
  20.5 0.7 %collective-permute-start.7 = (f32[384,384]{1,0:T(8,128)S(1)}, f32[384,384]{1,0:T(8,128)S(1)}, u32[]{:S(2)}, u32[]{:S(2)}) collective-permute-start(f32[384,384]{1,0:T(8,128)S(1)} %collective-permute-done.6.refs_2_), channel_id=1, source_target_pairs={{0,0},{3,3},{1,2},{2,1},{4,4},{7,7},{5,6},{6,5},{8,8},{11,11},{9,1... | collective-permute-start | bytes 1769480 | tf_op jit(solution)/shard_map/ppermute | solution.py:233
  21.1 0.9 %pair.1 = (f32[128,768]{1,0:T(8,128)S(1)}, f32[128,768]{1,0:T(8,128)S(1)}) custom-call(bf16[256,384]{1,0:T(8,128)(2,1)S(1)} %get-tuple-element.52.refs_0_, bf16[256,384]{1,0:T(8,128)(2,1)S(1)} %get-tuple-element.53.refs_1_, f32[384,384]{1,0:T(8,128)S(1)} %collective-permute-done.6.refs_2_, f32[4,384]{1,0:T(4,128)S(1)} %get-tuple-element.54.refs_3_, ...), custom_call_target="tpu_custom_call" | custom-call | flops 452984832 | bytes 2371584 | tf_op jit(solution)/shard_map/pair/pallas_call | solution.py:203
  22.2 1.6 %collective-permute-start.8 = (f32[64,384]{1,0:T(8,128)S(1)}, f32[64,384]{1,0:T(8,128)S(1)}, u32[]{:S(2)}, u32[]{:S(2)}) collective-permute-start(f32[64,384]{1,0:T(8,128)S(1)} %get-tuple-element.51), channel_id=1, source_target_pairs={{0,8},{4,12},{8,0},{12,4},{1,9},{5,13},{9,1},{13,5},{2,10},{6,14},... | collective-permute-start | bytes 294920 | tf_op jit(solution)/shard_map/ppermute | solution.py:236
  23.7 0.2 collective-permute-done.9.refs_1_
  23.9 1.6 %collective-permute-start.10 = (f32[64,768]{1,0:T(8,128)S(1)}, f32[64,768]{1,0:T(8,128)S(1)}, u32[]{:S(2)}, u32[]{:S(2)}) collective-permute-start(f32[64,768]{1,0:T(8,128)S(1)} %get-tuple-element.59), channel_id=1, source_target_pairs={{0,8},{4,12},{8,0},{12,4},{1,9},{5,13},{9,1},{13,5},{2,10},{6,14},... | collective-permute-start | bytes 589832 | tf_op jit(solution)/shard_map/ppermute | solution.py:236
  25.5 7.4 %collective-permute-done.5.refs_0_ = f32[384,384]{1,0:T(8,128)S(1)} collective-permute-done((f32[384,384]{1,0:T(8,128)S(1)}, f32[384,384]{1,0:T(8,128)S(1)}, u32[]{:S(2)}, u32[]{:S(2)}) %collective-permute-start.5) | collective-permute-done | bytes 589856 | tf_op jit(solution)/shard_map/ppermute | solution.py:233
  32.9 0.1 halves.1
  33.1 0.5 %corner.1 = (f32[128,384]{1,0:T(8,128)S(1)}, f32[128,384]{1,0:T(8,128)S(1)}) custom-call(f32[384,384]{1,0:T(8,128)S(1)} %collective-permute-done.5.refs_0_, bf16[384,384]{1,0:T(8,128)(2,1)S(1)} %get-tuple-element.49.refs_1_.refs_2_, bf16[384,384]{1,0:T(8,128)(2,1)S(1)} %get-tuple-element.50.refs_2_.refs_3_, ...), custom_call_target="tpu_custom_call" | custom-call | flops 226492416 | bytes 1572864 | tf_op jit(solution)/shard_map/corner/pallas_call | solution.py:203
  33.7 0.5 %last.1 = (f32[128,384]{1,0:T(8,128)S(1)}, f32[128,384]{1,0:T(8,128)S(1)}) custom-call(bf16[256,384]{1,0:T(8,128)(2,1)S(1)} %get-tuple-element.52.refs_0_, bf16[256,384]{1,0:T(8,128)(2,1)S(1)} %get-tuple-element.53.refs_1_, bf16[384,384]{1,0:T(8,128)(2,1)S(1)} %get-tuple-element.49.refs_1_.refs_2_, bf16[384,384]{1,0:T(8,128)(2,1)S(1)} %get-tuple-element.50.refs_2_.refs_3_, ...), custom_call_target="tpu_custom_call" | custom-call | flops 226492416 | bytes 1376256 | tf_op jit(solution)/shard_map/last/pallas_call | solution.py:203
  34.2 0.6 %collective-permute-start.14 = (f32[128,384]{1,0:T(8,128)S(1)}, f32[128,384]{1,0:T(8,128)S(1)}, u32[]{:S(2)}, u32[]{:S(2)}) collective-permute-start(f32[128,384]{1,0:T(8,128)S(1)} %get-tuple-element.67), channel_id=1, source_target_pairs={{0,4},{4,0},{8,12},{12,8},{1,5},{5,1},{9,13},{13,9},{2,6},{6,2},{1... | collective-permute-start | bytes 589832 | tf_op jit(solution)/shard_map/ppermute | solution.py:236
  34.8 0.3 collective-permute-done.11.refs_1_
  35.2 1.6 %collective-permute-start.12 = (f32[64,384]{1,0:T(8,128)S(1)}, f32[64,384]{1,0:T(8,128)S(1)}, u32[]{:S(2)}, u32[]{:S(2)}) collective-permute-start(f32[64,384]{1,0:T(8,128)S(1)} %get-tuple-element.63), channel_id=1, source_target_pairs={{0,8},{4,12},{8,0},{12,4},{1,9},{5,13},{9,1},{13,5},{2,10},{6,14},... | collective-permute-start | bytes 294920 | tf_op jit(solution)/shard_map/ppermute | solution.py:236
  36.7 0.7 %collective-permute-start.15 = (f32[64,384]{1,0:T(8,128)S(1)}, f32[64,384]{1,0:T(8,128)S(1)}, u32[]{:S(2)}, u32[]{:S(2)}) collective-permute-start(f32[64,384]{1,0:T(8,128)S(1)} %get-tuple-element.69), channel_id=1, source_target_pairs={{0,8},{4,12},{8,0},{12,4},{1,9},{5,13},{9,1},{13,5},{2,10},{6,14},... | collective-permute-start | bytes 294920 | tf_op jit(solution)/shard_map/ppermute | solution.py:236
  37.5 3.4 %collective-permute-done.12.refs_1_ = f32[64,384]{1,0:T(8,128)S(1)} collective-permute-done((f32[64,384]{1,0:T(8,128)S(1)}, f32[64,384]{1,0:T(8,128)S(1)}, u32[]{:S(2)}, u32[]{:S(2)}) %collective-permute-start.12) | collective-permute-done | bytes 98336 | tf_op jit(solution)/shard_map/ppermute | solution.py:236
  40.9 4.6 %collective-permute-start.13 = (f32[64,384]{1,0:T(8,128)S(1)}, f32[64,384]{1,0:T(8,128)S(1)}, u32[]{:S(2)}, u32[]{:S(2)}) collective-permute-start(f32[64,384]{1,0:T(8,128)S(1)} %add.25), channel_id=1, source_target_pairs={{0,1},{1,0},{2,3},{3,2},{4,5},{5,4},{6,7},{7,6},{8,9},{9,8},{10,11... | collective-permute-start | bytes 294920 | tf_op jit(solution)/shard_map/ppermute | solution.py:233
  45.5 0.5 finish.2.refs_5_
  45.9 2.1 %collective-permute-done.13.refs_1_ = f32[64,384]{1,0:T(8,128)S(1)} collective-permute-done((f32[64,384]{1,0:T(8,128)S(1)}, f32[64,384]{1,0:T(8,128)S(1)}, u32[]{:S(2)}, u32[]{:S(2)}) %collective-permute-start.13) | collective-permute-done | bytes 98336 | tf_op jit(solution)/shard_map/ppermute | solution.py:233
  48.1 1.1 %finish.3 = f32[64,1536]{1,0:T(8,128)} custom-call(f32[16,384]{1,0:T(8,128)S(1)} %get-tuple-element.39.refs_0_, f32[64,384]{1,0:T(8,128)S(1)} %collective-permute-done.13.refs_1_, f32[16,384]{1,0:T(8,128)S(1)} %add.20.refs_2_, f32[64,384]{1,0:T(8,128)S(1)} %get-tuple-element.68.refs_3_, f32[64,384]{1,0:T(8,128)S(1)} %collective-permute-done.15.refs_4_, ...), custom_call_target="tpu_custom_call" | custom-call | flops 393216 | bytes 1130496 | tf_op jit(solution)/shard_map/finish/pallas_call | solution.py:203
  (27 shorter events, 0.4 us)
Async XLA Ops:
  0.0 14.1 %copy-start = (f32[384,384]{1,0:T(8,128)S(1)}, f32[384,384]{1,0:T(8,128)}, u32[]{:S(2)}) copy-start(f32[384,384]{1,0:T(8,128)} %refs_5_.1) | copy-start | bytes 1769476
  0.0 16.4 %collective-permute-start.3 = (f32[384,384]{1,0:T(8,128)}, f32[384,384]{1,0:T(8,128)S(1)}, u32[]{:S(2)}, u32[]{:S(2)}) collective-permute-start(f32[384,384]{1,0:T(8,128)} %refs_5_.1), channel_id=1, source_target_pairs={{0,0},{3,3},{1,2},{2,1},{4,4},{7,7},{5,6},{6,5},{8,8},{11,11},{9,1... | collective-permute-start | bytes 1769480 | tf_op jit(solution)/shard_map/ppermute | solution.py:233
  1.8 18.6 %collective-permute-start.6 = (f32[384,384]{1,0:T(8,128)}, f32[384,384]{1,0:T(8,128)S(1)}, u32[]{:S(2)}, u32[]{:S(2)}) collective-permute-start(f32[384,384]{1,0:T(8,128)} %refs_5_.1), channel_id=1, source_target_pairs={{0,1},{1,0},{2,3},{3,2},{4,5},{5,4},{6,7},{7,6},{8,9},{9,8},{10,11... | collective-permute-start | bytes 1769480 | tf_op jit(solution)/shard_map/ppermute | solution.py:233
  7.8 2.2 %copy-start.3 = (s32[32,16]{0,1:T(8,128)S(1)}, s32[32,16]{0,1:T(8,128)}, u32[]{:S(2)}) copy-start(s32[32,16]{0,1:T(8,128)} %param.7) | copy-start | bytes 6148
  7.8 5.0 %collective-permute-start = (f32[64,384]{1,0:T(8,128)S(1)}, f32[64,384]{1,0:T(8,128)S(1)}, u32[]{:S(2)}, u32[]{:S(2)}) collective-permute-start(f32[64,384]{1,0:T(8,128)S(1)} %get-tuple-element.74), channel_id=1, source_target_pairs={{0,8},{4,12},{8,0},{12,4},{1,9},{5,13},{9,1},{13,5},{2,10},{6,14},... | collective-permute-start | bytes 294920 | tf_op jit(solution)/shard_map/ppermute | solution.py:236
  9.3 3.4 %collective-permute-start.1 = (f32[64,384]{1,0:T(8,128)S(1)}, f32[64,384]{1,0:T(8,128)S(1)}, u32[]{:S(2)}, u32[]{:S(2)}) collective-permute-start(f32[64,384]{1,0:T(8,128)S(1)} %get-tuple-element.76), channel_id=1, source_target_pairs={{0,4},{4,0},{8,12},{12,8},{1,5},{5,1},{9,13},{13,9},{2,6},{6,2},{1... | collective-permute-start | bytes 294920 | tf_op jit(solution)/shard_map/ppermute | solution.py:236
  9.3 4.7 %collective-permute-start.2 = (f32[64,384]{1,0:T(8,128)S(1)}, f32[64,384]{1,0:T(8,128)S(1)}, u32[]{:S(2)}, u32[]{:S(2)}) collective-permute-start(f32[64,384]{1,0:T(8,128)S(1)} %get-tuple-element.73), channel_id=1, source_target_pairs={{0,12},{4,8},{8,4},{12,0},{1,13},{5,9},{9,5},{13,1},{2,14},{6,10},... | collective-permute-start | bytes 294920 | tf_op jit(solution)/shard_map/ppermute | solution.py:236
  10.0 0.7 %copy-start.1 = (s32[16,16]{1,0:T(8,128)S(1)}, s32[16,16]{1,0:T(8,128)}, u32[]{:S(2)}) copy-start(s32[16,16]{1,0:T(8,128)} %refs_2_.1) | copy-start | bytes 3076
  10.1 0.7 %copy-start.2 = (s32[16]{0:T(128)S(1)}, s32[16]{0:T(128)}, u32[]{:S(2)}) copy-start(s32[16]{0:T(128)} %refs_3_.1) | copy-start | bytes 196
  14.6 1.8 %collective-permute-start.4 = (f32[128,384]{1,0:T(8,128)S(1)}, f32[128,384]{1,0:T(8,128)S(1)}, u32[]{:S(2)}, u32[]{:S(2)}) collective-permute-start(f32[128,384]{1,0:T(8,128)S(1)} %get-tuple-element.45), channel_id=1, source_target_pairs={{0,4},{4,0},{8,12},{12,8},{1,5},{5,1},{9,13},{13,9},{2,6},{6,2},{1... | collective-permute-start | bytes 589832 | tf_op jit(solution)/shard_map/ppermute | solution.py:236
  16.5 16.4 %collective-permute-start.5 = (f32[384,384]{1,0:T(8,128)S(1)}, f32[384,384]{1,0:T(8,128)S(1)}, u32[]{:S(2)}, u32[]{:S(2)}) collective-permute-start(f32[384,384]{1,0:T(8,128)S(1)} %pick.1), channel_id=1, source_target_pairs={{0,1},{1,0},{2,3},{3,2},{4,5},{5,4},{6,7},{7,6},{8,9},{9,8},{10,11... | collective-permute-start | bytes 1769480 | tf_op jit(solution)/shard_map/ppermute | solution.py:233
  20.5 12.5 %collective-permute-start.7 = (f32[384,384]{1,0:T(8,128)S(1)}, f32[384,384]{1,0:T(8,128)S(1)}, u32[]{:S(2)}, u32[]{:S(2)}) collective-permute-start(f32[384,384]{1,0:T(8,128)S(1)} %collective-permute-done.6.refs_2_), channel_id=1, source_target_pairs={{0,0},{3,3},{1,2},{2,1},{4,4},{7,7},{5,6},{6,5},{8,8},{11,11},{9,1... | collective-permute-start | bytes 1769480 | tf_op jit(solution)/shard_map/ppermute | solution.py:233
  22.1 1.8 %collective-permute-start.9 = (f32[128,768]{1,0:T(8,128)S(1)}, f32[128,768]{1,0:T(8,128)S(1)}, u32[]{:S(2)}, u32[]{:S(2)}) collective-permute-start(f32[128,768]{1,0:T(8,128)S(1)} %get-tuple-element.57), channel_id=1, source_target_pairs={{0,4},{4,0},{8,12},{12,8},{1,5},{5,1},{9,13},{13,9},{2,6},{6,2},{1... | collective-permute-start | bytes 1179656 | tf_op jit(solution)/shard_map/ppermute | solution.py:236
  22.2 10.9 %collective-permute-start.8 = (f32[64,384]{1,0:T(8,128)S(1)}, f32[64,384]{1,0:T(8,128)S(1)}, u32[]{:S(2)}, u32[]{:S(2)}) collective-permute-start(f32[64,384]{1,0:T(8,128)S(1)} %get-tuple-element.51), channel_id=1, source_target_pairs={{0,8},{4,12},{8,0},{12,4},{1,9},{5,13},{9,1},{13,5},{2,10},{6,14},... | collective-permute-start | bytes 294920 | tf_op jit(solution)/shard_map/ppermute | solution.py:236
  23.9 9.1 %collective-permute-start.10 = (f32[64,768]{1,0:T(8,128)S(1)}, f32[64,768]{1,0:T(8,128)S(1)}, u32[]{:S(2)}, u32[]{:S(2)}) collective-permute-start(f32[64,768]{1,0:T(8,128)S(1)} %get-tuple-element.59), channel_id=1, source_target_pairs={{0,8},{4,12},{8,0},{12,4},{1,9},{5,13},{9,1},{13,5},{2,10},{6,14},... | collective-permute-start | bytes 589832 | tf_op jit(solution)/shard_map/ppermute | solution.py:236
  33.6 1.5 %collective-permute-start.11 = (f32[128,384]{1,0:T(8,128)S(1)}, f32[128,384]{1,0:T(8,128)S(1)}, u32[]{:S(2)}, u32[]{:S(2)}) collective-permute-start(f32[128,384]{1,0:T(8,128)S(1)} %get-tuple-element.61), channel_id=1, source_target_pairs={{0,4},{4,0},{8,12},{12,8},{1,5},{5,1},{9,13},{13,9},{2,6},{6,2},{1... | collective-permute-start | bytes 589832 | tf_op jit(solution)/shard_map/ppermute | solution.py:236
  34.2 2.5 %collective-permute-start.14 = (f32[128,384]{1,0:T(8,128)S(1)}, f32[128,384]{1,0:T(8,128)S(1)}, u32[]{:S(2)}, u32[]{:S(2)}) collective-permute-start(f32[128,384]{1,0:T(8,128)S(1)} %get-tuple-element.67), channel_id=1, source_target_pairs={{0,4},{4,0},{8,12},{12,8},{1,5},{5,1},{9,13},{13,9},{2,6},{6,2},{1... | collective-permute-start | bytes 589832 | tf_op jit(solution)/shard_map/ppermute | solution.py:236
  35.2 5.7 %collective-permute-start.12 = (f32[64,384]{1,0:T(8,128)S(1)}, f32[64,384]{1,0:T(8,128)S(1)}, u32[]{:S(2)}, u32[]{:S(2)}) collective-permute-start(f32[64,384]{1,0:T(8,128)S(1)} %get-tuple-element.63), channel_id=1, source_target_pairs={{0,8},{4,12},{8,0},{12,4},{1,9},{5,13},{9,1},{13,5},{2,10},{6,14},... | collective-permute-start | bytes 294920 | tf_op jit(solution)/shard_map/ppermute | solution.py:236
  36.7 9.2 %collective-permute-start.15 = (f32[64,384]{1,0:T(8,128)S(1)}, f32[64,384]{1,0:T(8,128)S(1)}, u32[]{:S(2)}, u32[]{:S(2)}) collective-permute-start(f32[64,384]{1,0:T(8,128)S(1)} %get-tuple-element.69), channel_id=1, source_target_pairs={{0,8},{4,12},{8,0},{12,4},{1,9},{5,13},{9,1},{13,5},{2,10},{6,14},... | collective-permute-start | bytes 294920 | tf_op jit(solution)/shard_map/ppermute | solution.py:236
  40.9 7.2 %collective-permute-start.13 = (f32[64,384]{1,0:T(8,128)S(1)}, f32[64,384]{1,0:T(8,128)S(1)}, u32[]{:S(2)}, u32[]{:S(2)}) collective-permute-start(f32[64,384]{1,0:T(8,128)S(1)} %add.25), channel_id=1, source_target_pairs={{0,1},{1,0},{2,3},{3,2},{4,5},{5,4},{6,7},{7,6},{8,9},{9,8},{10,11... | collective-permute-start | bytes 294920 | tf_op jit(solution)/shard_map/ppermute | solution.py:233

commit v4 on v3

--- a/solution.py
+++ b/solution.py
@@ -129,6 +129,10 @@
     out[...] = jnp.where(at_end[0:1, :] > 0.5, slab[...], block[...])
 
 
+def pass_kernel(block, out):
+    out[...] = block[...]
+
+
 def halves_kernel(*refs):
     pairs, (high, low) = refs[:-2], refs[-2:]
     high[...], low[...] = masked_halves(list(zip(pairs[::2], pairs[1::2])))
@@ -153,13 +157,6 @@
     for i, out in enumerate(outs):
         at = pl.ds(i * rows, rows)
         out[...] = keep[at, :] + got[at, :]
-
-
-def add_kernel(*refs):
-    total = refs[0][...]
-    for share in refs[1:-1]:
-        total = total + share[...]
-    refs[-1][...] = total
 
 
 def finish_kernel(counts, *refs):
@@ -260,11 +257,18 @@
     masks = dict(zip(kinds + [ends], made[::2]))
     homes = dict(zip(kinds + [ends], made[1::2]))
 
+    def fold(keep, give):
+        shape = f32(rows, keep.shape[1])
+        return call(fold_kernel, "fold", [shape] * (n_row // 2), 0, keep, swap(give, 1))
+
     def exchange(keep, give):
-        got = swap(give, 1)
-        shape = f32(rows, keep.shape[1])
-        pieces = call(fold_kernel, "fold", [shape] * (n_row // 2), 0, keep, got)
+        pieces = fold(keep, give)
         return [pieces[0]] + [swap(pieces[i], 2 * i) for i in range(1, n_row // 2)]
+
+    def next_door(x, d):
+        spots = [(i, j) for i in range(n_row) for j in range(n_col)]
+        to = [((i ^ d) * n_col + (j ^ 1)) for i, j in spots]
+        return lax.ppermute(x, ("row", "col"), [(i * n_col + j, t) for (i, j), t in zip(spots, to)])
 
     def multiply(name, *groups, after=()):
         keep, give = call(
@@ -312,19 +316,21 @@
     slots = [([[(OWN, 0)]], exchange(keep, give))]
     for step in range(1, last + 1):
         if step > 1:
-            going = odd
+            going, through = odd, even
             if corner and step == 2:
+                shape = f32(depth, width)
+                through = call(pass_kernel, "pass", [shape], 0, even)[0]
                 going = call(
                     pick_kernel,
                     "pick",
-                    [f32(depth, width)],
+                    [shape],
                     0,
                     at_end,
                     slab,
                     odd,
-                    after=(slots[0][1][0],),
+                    after=(slots[0][1][0], through),
                 )[0]
-            even, odd = swap_line(going, EVEN), swap_line(even, ODD)
+            odd, even = swap_line(through, ODD), swap_line(going, EVEN)
             if corner and step == 2:
                 end_slab = even
         if 2 * step <= n_col - 1:
@@ -351,8 +357,7 @@
         slots = []
         if corner:
             parts = call(corner_kernel, "corner", sums, 0, end_slab, *b_halves, flops=flops, after=after)
-            summed = call(add_kernel, "add", [f32(rows, width)], 0, *exchange(*parts))[0]
-            slots.append(([[ends]], [swap_line(summed, EVEN)]))
+            slots.append(([[ends]], [next_door(x, 2 * i) for i, x in enumerate(fold(*parts))]))
         parts = call(last_kernel, "last", sums, 0, high, low, *b_halves, flops=flops, after=after)
         slots.append(([[(EVEN, step), (ODD, step)]], exchange(*parts)))
     return finish(slots, out)

time: 49.4 us -> 49 us (level)
  starting transfers between devices: 24.9 us -> 22.2 us
  waiting for transfers between devices: 15.8 us -> 18.1 us
    ppermute x5 -> x4, starting transfers between devices: 16 us -> 10.1 us  [swap_line(): lax.ppermute(x, 'col', ends + [p for p in inner if 0 <= p[1] < n_col])]
    ppermute x0 -> x2, starting transfers between devices: none -> 4.71 us  [next_door(): lax.ppermute(x, ('row', 'col'), [(i * n_col + j, t) for (i, j), t in zip(...]
    ppermute x0 -> x2, waiting for transfers between devices: none -> 4.13 us  [next_door(): lax.ppermute(x, ('row', 'col'), [(i * n_col + j, t) for (i, j), t in zip(...]
    ppermute x11 -> x10, waiting for transfers between devices: 6.27 us -> 4.39 us  [swap(): return lax.ppermute(x, 'row', [(i, i ^ d) for i in range(n_row)])]
    ppermute x11 -> x10, starting transfers between devices: 8.97 us -> 7.32 us  [swap(): return lax.ppermute(x, 'row', [(i, i ^ d) for i in range(n_row)])]
    ppermute x5 -> x4, waiting for transfers between devices: 9.55 us -> 9.56 us  [swap_line(): lax.ppermute(x, 'col', ends + [p for p in inner if 0 <= p[1] < n_col])]
  transfers between devices with their start and end apart: 16 -> 16, of which waited for: 7 -> 9; matrix products, arithmetic and copies ran while one was open for 2% -> 3% of each run, Pallas kernels for 10% -> 10%
where the time goes in v4:
time: 49 us; the launch traced here: 48.7 us
  starting transfers between devices  22.2 us (45%)
  waiting for transfers between devices  18.1 us (37%)
  Pallas kernels  6.52 us (13%)
  local copies, waits for them, and re-layouts  1.73 us (4%)
    ppermute x4, starting transfers between devices, swap_line(): lax.ppermute(x, 'col', ends + [p for p in inner if 0 <= p[1] < n_col])  10.1 us
    ppermute x4, waiting for transfers between devices, swap_line(): lax.ppermute(x, 'col', ends + [p for p in inner if 0 <= p[1] < n_col])  9.56 us
    ppermute x10, starting transfers between devices, swap(): return lax.ppermute(x, 'row', [(i, i ^ d) for i in range(n_row)])  7.32 us
    pallas_call x14, Pallas kernels, call(): pl.pallas_call(body, out_shape=outs, in_specs=[SMEM] * n_smem + [VMEM] *...  6.52 us
    ppermute x2, starting transfers between devices, next_door(): lax.ppermute(x, ('row', 'col'), [(i * n_col + j, t) for (i, j), t in zip(...  4.71 us
    ppermute x10, waiting for transfers between devices, swap(): return lax.ppermute(x, 'row', [(i, i ^ d) for i in range(n_row)])  4.39 us
    ppermute x2, waiting for transfers between devices, next_door(): lax.ppermute(x, ('row', 'col'), [(i * n_col + j, t) for (i, j), t in zip(...  4.13 us
    dynamic_slice x1, local copies, waits for them, and re-layouts, columns(): return lax.dynamic_slice_in_dim(amplitudes, (r ^ d) * depth, depth, 1)  1.06 us
  transfers between devices with their start and end apart: 16, of which 9 were waited for; matrix products, arithmetic and copies ran while one was open for 3% of the time, Pallas kernels for 10%

profile of v4, /device:TPU:0, one launch (start us, length us, event | category | flops | bytes accessed | tf_op | source)
XLA Modules:
  0.0 48.7 jit_solution(11648456670437762679)
XLA Ops:
  0.0 3.0 %collective-permute-start.5 = (f32[384,384]{1,0:T(8,128)}, f32[384,384]{1,0:T(8,128)S(1)}, u32[]{:S(2)}, u32[]{:S(2)}) collective-permute-start(f32[384,384]{1,0:T(8,128)} %refs_5_.1), channel_id=1, source_target_pairs={{0,1},{1,0},{2,3},{3,2},{4,5},{5,4},{6,7},{7,6},{8,9},{9,8},{10,11... | collective-permute-start | bytes 1769480 | tf_op jit(solution)/shard_map/ppermute | solution.py:230
  3.0 1.7 %collective-permute-start.3 = (f32[384,384]{1,0:T(8,128)}, f32[384,384]{1,0:T(8,128)S(1)}, u32[]{:S(2)}, u32[]{:S(2)}) collective-permute-start(f32[384,384]{1,0:T(8,128)} %refs_5_.1), channel_id=1, source_target_pairs={{0,0},{3,3},{1,2},{2,1},{4,4},{7,7},{5,6},{6,5},{8,8},{11,11},{9,1... | collective-permute-start | bytes 1769480 | tf_op jit(solution)/shard_map/ppermute | solution.py:230
  4.7 1.1 %constant_dynamic-slice_fusion = (f32[64,384]{1,0:T(8,128)S(1)}, f32[64,384]{1,0:T(8,128)S(1)}, f32[64,384]{1,0:T(8,128)S(1)}, f32[64,384]{1,0:T(8,128)S(1)}) fusion(f32[64,1536]{1,0:T(8,128)} %param.5, s32[]{:T(128)S(6)} %select_n.15, s32[]{:T(128)S(6)} %select_n.13, s32[]{:T(128)S(6)} %select_n.12, s32[]{:T(128)S(6)} %select_n.14), kind=kLoop, calls=%fused_computation.1 | loop fusion | bytes 786448 | tf_op jit(solution)/shard_map/dynamic_slice | solution.py:238
  5.8 1.6 %collective-permute-start = (f32[64,384]{1,0:T(8,128)S(1)}, f32[64,384]{1,0:T(8,128)S(1)}, u32[]{:S(2)}, u32[]{:S(2)}) collective-permute-start(f32[64,384]{1,0:T(8,128)S(1)} %get-tuple-element.74), channel_id=1, source_target_pairs={{0,8},{4,12},{8,0},{12,4},{1,9},{5,13},{9,1},{13,5},{2,10},{6,14},... | collective-permute-start | bytes 294920 | tf_op jit(solution)/shard_map/ppermute | solution.py:233
  7.4 0.6 %collective-permute-start.2 = (f32[64,384]{1,0:T(8,128)S(1)}, f32[64,384]{1,0:T(8,128)S(1)}, u32[]{:S(2)}, u32[]{:S(2)}) collective-permute-start(f32[64,384]{1,0:T(8,128)S(1)} %get-tuple-element.73), channel_id=1, source_target_pairs={{0,12},{4,8},{8,4},{12,0},{1,13},{5,9},{9,5},{13,1},{2,14},{6,10},... | collective-permute-start | bytes 294920 | tf_op jit(solution)/shard_map/ppermute | solution.py:233
  8.2 0.5 %copy-done.1 = s32[16,16]{1,0:T(8,128)S(1)} copy-done((s32[16,16]{1,0:T(8,128)S(1)}, s32[16,16]{1,0:T(8,128)}, u32[]{:S(2)}) %copy-start.1) | copy-done | bytes 1048
  8.8 2.0 %tables.1 = (f32[8,384]{1,0:T(8,128)S(1)}, f32[8,384]{1,0:T(8,128)S(1)}, f32[4,384]{1,0:T(4,128)S(1)}, f32[16,384]{1,0:T(8,128)S(1)}, f32[4,384]{1,0:T(4,128)S(1...) custom-call(s32[3]{0:T(128)S(1)} %pad_add_fusion.refs_0_, ...), custom_call_target="tpu_custom_call" | custom-call | bytes 212044 | tf_op jit(solution)/shard_map/tables/pallas_call | solution.py:200
  10.8 1.3 %collective-permute-done.2.refs_4_ = f32[64,384]{1,0:T(8,128)S(1)} collective-permute-done((f32[64,384]{1,0:T(8,128)S(1)}, f32[64,384]{1,0:T(8,128)S(1)}, u32[]{:S(2)}, u32[]{:S(2)}) %collective-permute-start.2) | collective-permute-done | bytes 98336 | tf_op jit(solution)/shard_map/ppermute | solution.py:233
  12.1 0.6 %own.1 = (bf16[256,384]{1,0:T(8,128)(2,1)S(1)}, bf16[256,384]{1,0:T(8,128)(2,1)S(1)}, f32[384,384]{1,0:T(8,128)S(1)}, f32[128,384]{1,0:T(8,128)S(1)}, f32[128,384]{1,0:T(8,128)S(1)}) custom-call(f32[8,384]{1,0:T(8,128)S(1)} %get-tuple-element.41.refs_0_, f32[64,384]{1,0:T(8,128)S(1)} %get-tuple-element.75.refs_1_, ...), custom_call_target="tpu_custom_call" | custom-call | flops 226492416 | bytes 2377728 | tf_op jit(solution)/shard_map/own/pallas_call | solution.py:200
  12.7 0.7 %collective-permute-start.4 = (f32[128,384]{1,0:T(8,128)S(1)}, f32[128,384]{1,0:T(8,128)S(1)}, u32[]{:S(2)}, u32[]{:S(2)}) collective-permute-start(f32[128,384]{1,0:T(8,128)S(1)} %get-tuple-element.45), channel_id=1, source_target_pairs={{0,4},{4,0},{8,12},{12,8},{1,5},{5,1},{9,13},{13,9},{2,6},{6,2},{1... | collective-permute-start | bytes 589832 | tf_op jit(solution)/shard_map/ppermute | solution.py:233
  13.4 1.1 %collective-permute-done.4.refs_1_ = f32[128,384]{1,0:T(8,128)S(1)} collective-permute-done((f32[128,384]{1,0:T(8,128)S(1)}, f32[128,384]{1,0:T(8,128)S(1)}, u32[]{:S(2)}, u32[]{:S(2)}) %collective-permute-start.4) | collective-permute-done | bytes 196640 | tf_op jit(solution)/shard_map/ppermute | solution.py:233
  14.5 2.2 %collective-permute-done.5.refs_0_.refs_2_ = f32[384,384]{1,0:T(8,128)S(1)} collective-permute-done((f32[384,384]{1,0:T(8,128)}, f32[384,384]{1,0:T(8,128)S(1)}, u32[]{:S(2)}, u32[]{:S(2)}) %collective-permute-start.5) | collective-permute-done | bytes 589856 | tf_op jit(solution)/shard_map/ppermute | solution.py:230
  16.8 4.7 %collective-permute-start.6 = (f32[384,384]{1,0:T(8,128)S(1)}, f32[384,384]{1,0:T(8,128)S(1)}, u32[]{:S(2)}, u32[]{:S(2)}) collective-permute-start(f32[384,384]{1,0:T(8,128)S(1)} %pick.1), channel_id=1, source_target_pairs={{0,1},{1,0},{2,3},{3,2},{4,5},{5,4},{6,7},{7,6},{8,9},{9,8},{10,11... | collective-permute-start | bytes 1769480 | tf_op jit(solution)/shard_map/ppermute | solution.py:230
  21.5 0.7 %collective-permute-start.7 = (f32[384,384]{1,0:T(8,128)S(1)}, f32[384,384]{1,0:T(8,128)S(1)}, u32[]{:S(2)}, u32[]{:S(2)}) collective-permute-start(f32[384,384]{1,0:T(8,128)S(1)} %pass.1.refs_4_), channel_id=1, source_target_pairs={{0,0},{3,3},{1,2},{2,1},{4,4},{7,7},{5,6},{6,5},{8,8},{11,11},{9,1... | collective-permute-start | bytes 1769480 | tf_op jit(solution)/shard_map/ppermute | solution.py:230
  22.2 1.0 %pair.1 = (f32[128,768]{1,0:T(8,128)S(1)}, f32[128,768]{1,0:T(8,128)S(1)}) custom-call(bf16[256,384]{1,0:T(8,128)(2,1)S(1)} %get-tuple-element.52.refs_0_, bf16[256,384]{1,0:T(8,128)(2,1)S(1)} %get-tuple-element.53.refs_1_, f32[384,384]{1,0:T(8,128)S(1)} %collective-permute-done.5.refs_0_.refs_2_, f32[4,384]{1,0:T(4,128)S(1)} %get-tuple-element.54.refs_3_, ...), custom_call_target="tpu_custom_call" | custom-call | flops 452984832 | bytes 2371584 | tf_op jit(solution)/shard_map/pair/pallas_call | solution.py:200
  23.2 1.6 %collective-permute-start.8 = (f32[64,384]{1,0:T(8,128)S(1)}, f32[64,384]{1,0:T(8,128)S(1)}, u32[]{:S(2)}, u32[]{:S(2)}) collective-permute-start(f32[64,384]{1,0:T(8,128)S(1)} %get-tuple-element.51), channel_id=1, source_target_pairs={{0,8},{4,12},{8,0},{12,4},{1,9},{5,13},{9,1},{13,5},{2,10},{6,14},... | collective-permute-start | bytes 294920 | tf_op jit(solution)/shard_map/ppermute | solution.py:233
  24.8 0.2 collective-permute-done.9.refs_1_
  25.0 1.6 %collective-permute-start.10 = (f32[64,768]{1,0:T(8,128)S(1)}, f32[64,768]{1,0:T(8,128)S(1)}, u32[]{:S(2)}, u32[]{:S(2)}) collective-permute-start(f32[64,768]{1,0:T(8,128)S(1)} %get-tuple-element.59), channel_id=1, source_target_pairs={{0,8},{4,12},{8,0},{12,4},{1,9},{5,13},{9,1},{13,5},{2,10},{6,14},... | collective-permute-start | bytes 589832 | tf_op jit(solution)/shard_map/ppermute | solution.py:233
  26.5 7.4 %collective-permute-done.6.refs_0_ = f32[384,384]{1,0:T(8,128)S(1)} collective-permute-done((f32[384,384]{1,0:T(8,128)S(1)}, f32[384,384]{1,0:T(8,128)S(1)}, u32[]{:S(2)}, u32[]{:S(2)}) %collective-permute-start.6) | collective-permute-done | bytes 589856 | tf_op jit(solution)/shard_map/ppermute | solution.py:230
  33.9 0.1 halves.1
  34.1 0.5 %corner.1 = (f32[128,384]{1,0:T(8,128)S(1)}, f32[128,384]{1,0:T(8,128)S(1)}) custom-call(f32[384,384]{1,0:T(8,128)S(1)} %collective-permute-done.6.refs_0_, bf16[384,384]{1,0:T(8,128)(2,1)S(1)} %get-tuple-element.49.refs_1_.refs_2_, bf16[384,384]{1,0:T(8,128)(2,1)S(1)} %get-tuple-element.50.refs_2_.refs_3_, ...), custom_call_target="tpu_custom_call" | custom-call | flops 226492416 | bytes 1572864 | tf_op jit(solution)/shard_map/corner/pallas_call | solution.py:200
  34.7 0.5 %last.1 = (f32[128,384]{1,0:T(8,128)S(1)}, f32[128,384]{1,0:T(8,128)S(1)}) custom-call(bf16[256,384]{1,0:T(8,128)(2,1)S(1)} %get-tuple-element.52.refs_0_, bf16[256,384]{1,0:T(8,128)(2,1)S(1)} %get-tuple-element.53.refs_1_, bf16[384,384]{1,0:T(8,128)(2,1)S(1)} %get-tuple-element.49.refs_1_.refs_2_, bf16[384,384]{1,0:T(8,128)(2,1)S(1)} %get-tuple-element.50.refs_2_.refs_3_, ...), custom_call_target="tpu_custom_call" | custom-call | flops 226492416 | bytes 1376256 | tf_op jit(solution)/shard_map/last/pallas_call | solution.py:200
  35.3 0.6 %collective-permute-start.14 = (f32[128,384]{1,0:T(8,128)S(1)}, f32[128,384]{1,0:T(8,128)S(1)}, u32[]{:S(2)}, u32[]{:S(2)}) collective-permute-start(f32[128,384]{1,0:T(8,128)S(1)} %get-tuple-element.67), channel_id=1, source_target_pairs={{0,4},{4,0},{8,12},{12,8},{1,5},{5,1},{9,13},{13,9},{2,6},{6,2},{1... | collective-permute-start | bytes 589832 | tf_op jit(solution)/shard_map/ppermute | solution.py:233
  35.8 0.3 collective-permute-done.11.refs_1_
  36.2 3.7 %collective-permute-start.12 = (f32[64,384]{1,0:T(8,128)S(1)}, f32[64,384]{1,0:T(8,128)S(1)}, u32[]{:S(2)}, u32[]{:S(2)}) collective-permute-start(f32[64,384]{1,0:T(8,128)S(1)} %get-tuple-element.62), channel_id=1, source_target_pairs={{0,1},{1,0},{2,3},{3,2},{4,5},{5,4},{6,7},{7,6},{8,9},{9,8},{10,11... | collective-permute-start | bytes 294920 | tf_op jit(solution)/shard_map/ppermute | solution.py:271
  39.9 1.0 %collective-permute-start.13 = (f32[64,384]{1,0:T(8,128)S(1)}, f32[64,384]{1,0:T(8,128)S(1)}, u32[]{:S(2)}, u32[]{:S(2)}) collective-permute-start(f32[64,384]{1,0:T(8,128)S(1)} %get-tuple-element.63), channel_id=1, source_target_pairs={{0,9},{1,8},{2,11},{3,10},{4,13},{5,12},{6,15},{7,14},{8,1},{9,0},... | collective-permute-start | bytes 294920 | tf_op jit(solution)/shard_map/ppermute | solution.py:271
  40.9 0.6 %collective-permute-start.15 = (f32[64,384]{1,0:T(8,128)S(1)}, f32[64,384]{1,0:T(8,128)S(1)}, u32[]{:S(2)}, u32[]{:S(2)}) collective-permute-start(f32[64,384]{1,0:T(8,128)S(1)} %get-tuple-element.69), channel_id=1, source_target_pairs={{0,8},{4,12},{8,0},{12,4},{1,9},{5,13},{9,1},{13,5},{2,10},{6,14},... | collective-permute-start | bytes 294920 | tf_op jit(solution)/shard_map/ppermute | solution.py:233
  41.5 0.5 finish.2.refs_6_
  42.0 1.0 %collective-permute-done.12.refs_1_ = f32[64,384]{1,0:T(8,128)S(1)} collective-permute-done((f32[64,384]{1,0:T(8,128)S(1)}, f32[64,384]{1,0:T(8,128)S(1)}, u32[]{:S(2)}, u32[]{:S(2)}) %collective-permute-start.12) | collective-permute-done | bytes 98336 | tf_op jit(solution)/shard_map/ppermute | solution.py:271
  43.0 3.1 %collective-permute-done.13.refs_2_ = f32[64,384]{1,0:T(8,128)S(1)} collective-permute-done((f32[64,384]{1,0:T(8,128)S(1)}, f32[64,384]{1,0:T(8,128)S(1)}, u32[]{:S(2)}, u32[]{:S(2)}) %collective-permute-start.13) | collective-permute-done | bytes 98336 | tf_op jit(solution)/shard_map/ppermute | solution.py:271
  46.1 1.5 %collective-permute-done.15.refs_5_ = f32[64,384]{1,0:T(8,128)S(1)} collective-permute-done((f32[64,384]{1,0:T(8,128)S(1)}, f32[64,384]{1,0:T(8,128)S(1)}, u32[]{:S(2)}, u32[]{:S(2)}) %collective-permute-start.15) | collective-permute-done | bytes 98336 | tf_op jit(solution)/shard_map/ppermute | solution.py:233
  47.6 1.1 %finish.3 = f32[64,1536]{1,0:T(8,128)} custom-call(f32[16,384]{1,0:T(8,128)S(1)} %get-tuple-element.39.refs_0_, f32[64,384]{1,0:T(8,128)S(1)} %collective-permute-done.12.refs_1_, f32[64,384]{1,0:T(8,128)S(1)} %collective-permute-done.13.refs_2_, f32[16,384]{1,0:T(8,128)S(1)} %add.19.refs_3_, f32[64,384]{1,0:T(8,128)S(1)} %get-tuple-element.68.refs_4_, ...), custom_call_target="tpu_custom_call" | custom-call | flops 393216 | bytes 1228800 | tf_op jit(solution)/shard_map/finish/pallas_call | solution.py:200
  (27 shorter events, 0.6 us)
Async XLA Ops:
  0.0 12.1 %copy-start = (f32[384,384]{1,0:T(8,128)S(1)}, f32[384,384]{1,0:T(8,128)}, u32[]{:S(2)}) copy-start(f32[384,384]{1,0:T(8,128)} %refs_5_.1) | copy-start | bytes 1769476
  0.0 16.6 %collective-permute-start.5 = (f32[384,384]{1,0:T(8,128)}, f32[384,384]{1,0:T(8,128)S(1)}, u32[]{:S(2)}, u32[]{:S(2)}) collective-permute-start(f32[384,384]{1,0:T(8,128)} %refs_5_.1), channel_id=1, source_target_pairs={{0,1},{1,0},{2,3},{3,2},{4,5},{5,4},{6,7},{7,6},{8,9},{9,8},{10,11... | collective-permute-start | bytes 1769480 | tf_op jit(solution)/shard_map/ppermute | solution.py:230
  3.0 13.7 %collective-permute-start.3 = (f32[384,384]{1,0:T(8,128)}, f32[384,384]{1,0:T(8,128)S(1)}, u32[]{:S(2)}, u32[]{:S(2)}) collective-permute-start(f32[384,384]{1,0:T(8,128)} %refs_5_.1), channel_id=1, source_target_pairs={{0,0},{3,3},{1,2},{2,1},{4,4},{7,7},{5,6},{6,5},{8,8},{11,11},{9,1... | collective-permute-start | bytes 1769480 | tf_op jit(solution)/shard_map/ppermute | solution.py:230
  5.8 2.2 %copy-start.3 = (s32[32,16]{0,1:T(8,128)S(1)}, s32[32,16]{0,1:T(8,128)}, u32[]{:S(2)}) copy-start(s32[32,16]{0,1:T(8,128)} %param.7) | copy-start | bytes 6148
  5.8 5.0 %collective-permute-start = (f32[64,384]{1,0:T(8,128)S(1)}, f32[64,384]{1,0:T(8,128)S(1)}, u32[]{:S(2)}, u32[]{:S(2)}) collective-permute-start(f32[64,384]{1,0:T(8,128)S(1)} %get-tuple-element.74), channel_id=1, source_target_pairs={{0,8},{4,12},{8,0},{12,4},{1,9},{5,13},{9,1},{13,5},{2,10},{6,14},... | collective-permute-start | bytes 294920 | tf_op jit(solution)/shard_map/ppermute | solution.py:233
  7.4 3.4 %collective-permute-start.1 = (f32[64,384]{1,0:T(8,128)S(1)}, f32[64,384]{1,0:T(8,128)S(1)}, u32[]{:S(2)}, u32[]{:S(2)}) collective-permute-start(f32[64,384]{1,0:T(8,128)S(1)} %get-tuple-element.76), channel_id=1, source_target_pairs={{0,4},{4,0},{8,12},{12,8},{1,5},{5,1},{9,13},{13,9},{2,6},{6,2},{1... | collective-permute-start | bytes 294920 | tf_op jit(solution)/shard_map/ppermute | solution.py:233
  7.4 4.7 %collective-permute-start.2 = (f32[64,384]{1,0:T(8,128)S(1)}, f32[64,384]{1,0:T(8,128)S(1)}, u32[]{:S(2)}, u32[]{:S(2)}) collective-permute-start(f32[64,384]{1,0:T(8,128)S(1)} %get-tuple-element.73), channel_id=1, source_target_pairs={{0,12},{4,8},{8,4},{12,0},{1,13},{5,9},{9,5},{13,1},{2,14},{6,10},... | collective-permute-start | bytes 294920 | tf_op jit(solution)/shard_map/ppermute | solution.py:233
  8.0 0.7 %copy-start.1 = (s32[16,16]{1,0:T(8,128)S(1)}, s32[16,16]{1,0:T(8,128)}, u32[]{:S(2)}) copy-start(s32[16,16]{1,0:T(8,128)} %refs_2_.1) | copy-start | bytes 3076
  8.1 0.7 %copy-start.2 = (s32[16]{0:T(128)S(1)}, s32[16]{0:T(128)}, u32[]{:S(2)}) copy-start(s32[16]{0:T(128)} %refs_3_.1) | copy-start | bytes 196
  12.7 1.8 %collective-permute-start.4 = (f32[128,384]{1,0:T(8,128)S(1)}, f32[128,384]{1,0:T(8,128)S(1)}, u32[]{:S(2)}, u32[]{:S(2)}) collective-permute-start(f32[128,384]{1,0:T(8,128)S(1)} %get-tuple-element.45), channel_id=1, source_target_pairs={{0,4},{4,0},{8,12},{12,8},{1,5},{5,1},{9,13},{13,9},{2,6},{6,2},{1... | collective-permute-start | bytes 589832 | tf_op jit(solution)/shard_map/ppermute | solution.py:233
  16.8 17.2 %collective-permute-start.6 = (f32[384,384]{1,0:T(8,128)S(1)}, f32[384,384]{1,0:T(8,128)S(1)}, u32[]{:S(2)}, u32[]{:S(2)}) collective-permute-start(f32[384,384]{1,0:T(8,128)S(1)} %pick.1), channel_id=1, source_target_pairs={{0,1},{1,0},{2,3},{3,2},{4,5},{5,4},{6,7},{7,6},{8,9},{9,8},{10,11... | collective-permute-start | bytes 1769480 | tf_op jit(solution)/shard_map/ppermute | solution.py:230
  21.5 12.5 %collective-permute-start.7 = (f32[384,384]{1,0:T(8,128)S(1)}, f32[384,384]{1,0:T(8,128)S(1)}, u32[]{:S(2)}, u32[]{:S(2)}) collective-permute-start(f32[384,384]{1,0:T(8,128)S(1)} %pass.1.refs_4_), channel_id=1, source_target_pairs={{0,0},{3,3},{1,2},{2,1},{4,4},{7,7},{5,6},{6,5},{8,8},{11,11},{9,1... | collective-permute-start | bytes 1769480 | tf_op jit(solution)/shard_map/ppermute | solution.py:230
  23.1 1.8 %collective-permute-start.9 = (f32[128,768]{1,0:T(8,128)S(1)}, f32[128,768]{1,0:T(8,128)S(1)}, u32[]{:S(2)}, u32[]{:S(2)}) collective-permute-start(f32[128,768]{1,0:T(8,128)S(1)} %get-tuple-element.57), channel_id=1, source_target_pairs={{0,4},{4,0},{8,12},{12,8},{1,5},{5,1},{9,13},{13,9},{2,6},{6,2},{1... | collective-permute-start | bytes 1179656 | tf_op jit(solution)/shard_map/ppermute | solution.py:233
  23.2 10.9 %collective-permute-start.8 = (f32[64,384]{1,0:T(8,128)S(1)}, f32[64,384]{1,0:T(8,128)S(1)}, u32[]{:S(2)}, u32[]{:S(2)}) collective-permute-start(f32[64,384]{1,0:T(8,128)S(1)} %get-tuple-element.51), channel_id=1, source_target_pairs={{0,8},{4,12},{8,0},{12,4},{1,9},{5,13},{9,1},{13,5},{2,10},{6,14},... | collective-permute-start | bytes 294920 | tf_op jit(solution)/shard_map/ppermute | solution.py:233
  25.0 9.1 %collective-permute-start.10 = (f32[64,768]{1,0:T(8,128)S(1)}, f32[64,768]{1,0:T(8,128)S(1)}, u32[]{:S(2)}, u32[]{:S(2)}) collective-permute-start(f32[64,768]{1,0:T(8,128)S(1)} %get-tuple-element.59), channel_id=1, source_target_pairs={{0,8},{4,12},{8,0},{12,4},{1,9},{5,13},{9,1},{13,5},{2,10},{6,14},... | collective-permute-start | bytes 589832 | tf_op jit(solution)/shard_map/ppermute | solution.py:233
  34.6 1.5 %collective-permute-start.11 = (f32[128,384]{1,0:T(8,128)S(1)}, f32[128,384]{1,0:T(8,128)S(1)}, u32[]{:S(2)}, u32[]{:S(2)}) collective-permute-start(f32[128,384]{1,0:T(8,128)S(1)} %get-tuple-element.61), channel_id=1, source_target_pairs={{0,4},{4,0},{8,12},{12,8},{1,5},{5,1},{9,13},{13,9},{2,6},{6,2},{1... | collective-permute-start | bytes 589832 | tf_op jit(solution)/shard_map/ppermute | solution.py:233
  35.3 5.6 %collective-permute-start.14 = (f32[128,384]{1,0:T(8,128)S(1)}, f32[128,384]{1,0:T(8,128)S(1)}, u32[]{:S(2)}, u32[]{:S(2)}) collective-permute-start(f32[128,384]{1,0:T(8,128)S(1)} %get-tuple-element.67), channel_id=1, source_target_pairs={{0,4},{4,0},{8,12},{12,8},{1,5},{5,1},{9,13},{13,9},{2,6},{6,2},{1... | collective-permute-start | bytes 589832 | tf_op jit(solution)/shard_map/ppermute | solution.py:233
  36.2 6.9 %collective-permute-start.12 = (f32[64,384]{1,0:T(8,128)S(1)}, f32[64,384]{1,0:T(8,128)S(1)}, u32[]{:S(2)}, u32[]{:S(2)}) collective-permute-start(f32[64,384]{1,0:T(8,128)S(1)} %get-tuple-element.62), channel_id=1, source_target_pairs={{0,1},{1,0},{2,3},{3,2},{4,5},{5,4},{6,7},{7,6},{8,9},{9,8},{10,11... | collective-permute-start | bytes 294920 | tf_op jit(solution)/shard_map/ppermute | solution.py:271
  39.9 6.2 %collective-permute-start.13 = (f32[64,384]{1,0:T(8,128)S(1)}, f32[64,384]{1,0:T(8,128)S(1)}, u32[]{:S(2)}, u32[]{:S(2)}) collective-permute-start(f32[64,384]{1,0:T(8,128)S(1)} %get-tuple-element.63), channel_id=1, source_target_pairs={{0,9},{1,8},{2,11},{3,10},{4,13},{5,12},{6,15},{7,14},{8,1},{9,0},... | collective-permute-start | bytes 294920 | tf_op jit(solution)/shard_map/ppermute | solution.py:271
  40.9 6.7 %collective-permute-start.15 = (f32[64,384]{1,0:T(8,128)S(1)}, f32[64,384]{1,0:T(8,128)S(1)}, u32[]{:S(2)}, u32[]{:S(2)}) collective-permute-start(f32[64,384]{1,0:T(8,128)S(1)} %get-tuple-element.69), channel_id=1, source_target_pairs={{0,8},{4,12},{8,0},{12,4},{1,9},{5,13},{9,1},{13,5},{2,10},{6,14},... | collective-permute-start | bytes 294920 | tf_op jit(solution)/shard_map/ppermute | solution.py:233

commit v5 on v4

--- a/solution.py
+++ b/solution.py
@@ -44,9 +44,11 @@
     return (index >= 0) & (index < n)
 
 
-def tables_kernel(kinds, order, place, amp_mask, int_mask, owner, amp_rows, at_end, *refs):
+def amplitude_tables_kernel(order, place, amp_mask, amp_rows, marks):
     r, c, n_col = place[0], place[1], place[2]
-    at_end[...] = jnp.broadcast_to(((c == 0) | (c == n_col - 1)).astype(jnp.float32), at_end.shape)
+    row = lax.broadcasted_iota(jnp.int32, marks.shape, 0)
+    ends = ((c == 0) | (c == n_col - 1)).astype(jnp.float32)
+    marks[...] = jnp.where(row == 0, ends, (r % 2).astype(jnp.float32))
     count, depth = amp_rows.shape
     occ = count // len(order)
     lane_tile = lax.broadcasted_iota(jnp.int32, (1, depth), 1) // TB
@@ -55,6 +57,10 @@
             row = ((r ^ d) * n_col + c) * occ + o
             bits = [amp_mask[row, r * (depth // TB) + k] for k in range(depth // TB)]
             amp_rows[p * occ + o : p * occ + o + 1, :] = lane_mask(bits, lane_tile)
+
+
+def tables_kernel(kinds, place, int_mask, owner, *refs):
+    r, c, n_col = place[0], place[1], place[2]
     for i, (kind, step) in enumerate(kinds):
         masks, homes = refs[2 * i : 2 * i + 2]
         source = source_of(kind, step, c)
@@ -80,12 +86,25 @@
             homes[pl.ds(g * rows, rows), :] = marks
 
 
+def parted(refs, counts):
+    out, first = [], 0
+    for count in counts:
+        out.append(refs[first : first + count])
+        first += count
+    return out
+
+
 def masked_halves(pairs):
-    k_tiles = pairs[0][1].shape[0]
+    k_tiles = pairs[0][-1].shape[0]
     highs, lows = [], []
     for k in range(k_tiles):
-        at = pl.ds(k * TB, TB)
-        piece = sum(block[at, :] * masks[k : k + 1, :] for block, masks in pairs)
+        piece = 0.0
+        for *parts, masks in pairs:
+            row = k * TB
+            for part in parts:
+                if 0 <= row < part.shape[0]:
+                    piece = piece + part[row : row + TB, :] * masks[k : k + 1, :]
+                row -= part.shape[0]
         h, l = split(piece)
         highs.append(h)
         lows.append(l)
@@ -98,19 +117,18 @@
 
 
 def multiply_kernel(groups, high, low, *refs):
-    pairs, (keep, give) = refs[:-2], refs[-2:]
-    pairs = list(zip(pairs[::2], pairs[1::2]))
+    keep, give = refs[-2:]
     half, width = keep.shape[0], keep.shape[1] // len(groups)
-    for g, count in enumerate(groups):
-        b_high, b_low = masked_halves(pairs[:count])
-        pairs = pairs[count:]
+    for g, counts in enumerate(groups):
+        b_high, b_low = masked_halves(parted(refs, counts))
+        refs = refs[sum(counts) :]
         for out, start in ((give, half), (keep, 0)):
             at = pl.ds(start, half)
             out[:, g * width : (g + 1) * width] = product(high[at, :], low[at, :], b_high, b_low)
 
 
-def own_kernel(n_row, amp_rows, *refs):
-    pieces, (block, masks, high, low, slab, keep, give) = refs[:n_row], refs[n_row:]
+def own_kernel(amp_rows, *refs):
+    pieces, (block, masks, high, low, slab, *sums) = refs[:2], refs[2:]
     rows = pieces[0].shape[0]
     occ = rows // OTB
     for p, piece in enumerate(pieces):
@@ -119,23 +137,35 @@
             at = pl.ds(p * rows + o * OTB, OTB)
             slab[at, :] = masked
             high[at, :], low[at, :] = split(masked)
-    used = n_row * rows
-    if slab.shape[0] > used:
+    used = 2 * rows
+    if used < slab.shape[0]:
         slab[used:, :] = jnp.zeros((slab.shape[0] - used, slab.shape[1]), jnp.float32)
-    multiply_kernel((1,), high, low, block, masks, keep, give)
-
-
-def pick_kernel(at_end, slab, block, out):
-    out[...] = jnp.where(at_end[0:1, :] > 0.5, slab[...], block[...])
+    multiply_kernel(((2,),), high, low, block, masks, *sums)
+
+
+def deal_kernel(marks, *refs):
+    pieces, (keep, give) = refs[:-2], refs[-2:]
+    rows, depth = pieces[0].shape[0], keep.shape[1]
+    second = marks[1:2, :depth] > 0.5
+    for i, piece in enumerate(pieces):
+        at = pl.ds(i * rows, rows)
+        here, there = piece[:, :depth], piece[:, depth:]
+        keep[at, :] = jnp.where(second, there, here)
+        give[at, :] = jnp.where(second, here, there)
+
+
+def pick_kernel(marks, slab, block, out):
+    out[...] = jnp.where(marks[0:1, : out.shape[1]] > 0.5, slab[...], block[...])
 
 
 def pass_kernel(block, out):
-    out[...] = block[...]
-
-
-def halves_kernel(*refs):
-    pairs, (high, low) = refs[:-2], refs[-2:]
-    high[...], low[...] = masked_halves(list(zip(pairs[::2], pairs[1::2])))
+    rows = block.shape[0]
+    out[:rows, :] = block[...]
+    out[rows:, :] = jnp.zeros((out.shape[0] - rows, out.shape[1]), jnp.float32)
+
+
+def halves_kernel(counts, *refs):
+    refs[-2][...], refs[-1][...] = masked_halves(parted(refs[:-2], counts))
 
 
 def last_kernel(high, low, b_high, b_low, keep, give):
@@ -145,10 +175,10 @@
         out[...] = product(high[at, :], low[at, :], b_high[...], b_low[...])
 
 
-def corner_kernel(slab, b_high, b_low, keep, give):
+def corner_kernel(b_high, b_low, slab, keep, give):
     half = keep.shape[0]
     for out, start in ((give, half), (keep, 0)):
-        a_high, a_low = split(slab[pl.ds(start, half), :])
+        a_high, a_low = split(slab[start : start + half, :])
         out[...] = product(a_high, a_low, b_high[...], b_low[...])
 
 
@@ -232,30 +262,51 @@
     def swap(x, d):
         return lax.ppermute(x, "row", [(i, i ^ d) for i in range(n_row)])
 
-    even, odd = swap_line(integrals, EVEN), swap_line(integrals, ODD)
-
-    def columns(d):
-        return lax.dynamic_slice_in_dim(amplitudes, (r ^ d) * depth, depth, 1)
-
-    pieces = [swap(columns(d), d) if d else columns(0) for d in order]
-    corner = n_col >= 4 and total <= depth and depth == width
+    k_tiles, tiles = depth // TB, pairs // TB
+    cut = 0
+    parts = [integrals]
+    even = [swap_line(integrals, EVEN)]
+    odd = [swap_line(x, ODD) for x in parts]
+
+    amp_rows, marks = call(
+        functools.partial(amplitude_tables_kernel, order),
+        "amplitude_tables",
+        [f32(total // OTB, depth), f32(8, max(width, depth))],
+        2,
+        place,
+        amp_mask,
+    )
+
+    def chip_columns(d):
+        start = (r // 2 ^ d) * 2 * depth
+        return lax.dynamic_slice_in_dim(amplitudes, start, 2 * depth, 1)
+
+    pieces = [chip_columns(0)]
+    pieces += [swap(chip_columns(d), 2 * d) for d in range(1, n_row // 2)]
+    keep, give = call(deal_kernel, "deal", [f32(total // 2, depth)] * 2, 0, marks, *pieces)
+    slab_parts = [keep, swap(give, 1)]
+    corner = n_col >= 4 and total <= depth - cut and depth == width
     last = n_col - 2 if corner else n_col - 1
     kinds = [(OWN, 0)] + [(kind, step) for step in range(1, last + 1) for kind in (EVEN, ODD)]
     ends = (CORNER, n_col - 1)
-    k_tiles, tiles = depth // TB, pairs // TB
     per_slot = [f32(k_tiles, width), f32(width // GROUP * tiles, GROUP)]
-    amp_rows, at_end, *made = call(
-        functools.partial(tables_kernel, kinds + [ends], order),
-        "tables",
-        [f32(total // OTB, depth), f32(8, width)] + per_slot * (len(kinds) + 1),
-        4,
-        place,
-        amp_mask,
-        int_mask,
-        owner_map,
-    )
-    masks = dict(zip(kinds + [ends], made[::2]))
-    homes = dict(zip(kinds + [ends], made[1::2]))
+    masks, homes = {}, {}
+
+    def tables(name, kinds):
+        made = call(
+            functools.partial(tables_kernel, kinds),
+            name,
+            per_slot * len(kinds),
+            3,
+            place,
+            int_mask,
+            owner_map,
+        )
+        masks.update(zip(kinds, made[::2]))
+        homes.update(zip(kinds, made[1::2]))
+
+    tables("own_tables", kinds[:1])
+    tables("tables", kinds[1:] + [ends])
 
     def fold(keep, give):
         shape = f32(rows, keep.shape[1])
@@ -266,19 +317,23 @@
         return [pieces[0]] + [swap(pieces[i], 2 * i) for i in range(1, n_row // 2)]
 
     def next_door(x, d):
-        spots = [(i, j) for i in range(n_row) for j in range(n_col)]
-        to = [((i ^ d) * n_col + (j ^ 1)) for i, j in spots]
-        return lax.ppermute(x, ("row", "col"), [(i * n_col + j, t) for (i, j), t in zip(spots, to)])
+        spots = [(i, j) for i in range(n_row) for j in (1, n_col - 2)]
+        return lax.ppermute(
+            x, ("row", "col"), [(i * n_col + j, (i ^ d) * n_col + (j ^ 1)) for i, j in spots]
+        )
 
     def multiply(name, *groups, after=()):
         keep, give = call(
-            functools.partial(multiply_kernel, tuple(len(group) for group in groups)),
+            functools.partial(
+                multiply_kernel,
+                tuple(tuple(len(block) + 1 for _, block in group) for group in groups),
+            ),
             name,
             [f32(total // 2, len(groups) * width)] * 2,
             0,
             high,
             low,
-            *[x for group in groups for slot, block in group for x in (block, masks[slot])],
+            *[x for group in groups for slot, block in group for x in (*block, masks[slot])],
             flops=6 * total * depth * width * len(groups),
             after=after,
         )
@@ -301,14 +356,14 @@
         )[0]
 
     high, low, slab, keep, give = call(
-        functools.partial(own_kernel, n_row),
+        own_kernel,
         "own",
         [jax.ShapeDtypeStruct((total, depth), jnp.bfloat16)] * 2
-        + [f32(depth if corner else total, depth)]
+        + [f32(depth - cut if corner else total, depth)]
         + [f32(total // 2, width)] * 2,
         0,
         amp_rows,
-        *pieces,
+        *slab_parts,
         integrals,
         masks[OWN, 0],
         flops=6 * total * depth * width,
@@ -316,23 +371,24 @@
     slots = [([[(OWN, 0)]], exchange(keep, give))]
     for step in range(1, last + 1):
         if step > 1:
-            going, through = odd, even
+            going, through = list(odd), list(even)
             if corner and step == 2:
-                shape = f32(depth, width)
-                through = call(pass_kernel, "pass", [shape], 0, even)[0]
-                going = call(
+                shape = f32(depth + 8, width)
+                through = [call(pass_kernel, "pass", [shape], 0, x, after=(slab,))[0] for x in even]
+                going[-1] = call(
                     pick_kernel,
                     "pick",
-                    [shape],
+                    [f32(depth - cut, depth)],
                     0,
-                    at_end,
+                    marks,
                     slab,
-                    odd,
-                    after=(slots[0][1][0], through),
+                    odd[-1],
+                    after=through,
                 )[0]
-            odd, even = swap_line(through, ODD), swap_line(going, EVEN)
+            odd = [swap_line(x, ODD) for x in through]
+            even = [swap_line(x, EVEN) for x in going]
             if corner and step == 2:
-                end_slab = even
+                end_slab = even[-1]
         if 2 * step <= n_col - 1:
             slots.append(multiply("pair", [((EVEN, step), even)], [((ODD, step), odd)]))
             continue
@@ -341,13 +397,13 @@
             continue
         out = finish(slots)
         b_halves = call(
-            halves_kernel,
+            functools.partial(halves_kernel, (len(even) + 1, len(odd) + 1)),
             "halves",
             [jax.ShapeDtypeStruct((depth, width), jnp.bfloat16)] * 2,
             0,
-            even,
+            *even,
             masks[EVEN, step],
-            odd,
+            *odd,
             masks[ODD, step],
             flops=WEIGHT,
         )
@@ -356,7 +412,7 @@
         flops = 6 * total * depth * width
         slots = []
         if corner:
-            parts = call(corner_kernel, "corner", sums, 0, end_slab, *b_halves, flops=flops, after=after)
+            parts = call(corner_kernel, "corner", sums, 0, *b_halves, end_slab, flops=flops, after=after)
             slots.append(([[ends]], [next_door(x, 2 * i) for i, x in enumerate(fold(*parts))]))
         parts = call(last_kernel, "last", sums, 0, high, low, *b_halves, flops=flops, after=after)
         slots.append(([[(EVEN, step), (ODD, step)]], exchange(*parts)))

time: 49 us -> 49 us (level)
  starting transfers between devices: 22.2 us -> 19.2 us
  waiting for transfers between devices: 18.1 us -> 19.7 us
  Pallas kernels: 6.52 us -> 7.79 us
    ppermute x10 -> x9, waiting for transfers between devices: 4.39 us -> 7.22 us  [swap(): return lax.ppermute(x, 'row', [(i, i ^ d) for i in range(n_row)])]
    ppermute x4, waiting for transfers between devices: 9.56 us -> 7.42 us  [swap_line(): lax.ppermute(x, 'col', ends + [p for p in inner if 0 <= p[1] < n_col])]
    ppermute x2, starting transfers between devices: 4.71 us -> 2.58 us  [next_door(): lax.ppermute(x, ('row', 'col'), [(i * n_col + j, (i ^ d) * n_col + (j ^ 1...]
    pallas_call x14 -> x17, Pallas kernels: 6.52 us -> 7.79 us  [call(): pl.pallas_call(body, out_shape=outs, in_specs=[SMEM] * n_smem + [VMEM] *...]
    ppermute x2, waiting for transfers between devices: 4.13 us -> 5.1 us  [next_door(): lax.ppermute(x, ('row', 'col'), [(i * n_col + j, (i ^ d) * n_col + (j ^ 1...]
    ppermute x10 -> x9, starting transfers between devices: 7.32 us -> 6.55 us  [swap(): return lax.ppermute(x, 'row', [(i, i ^ d) for i in range(n_row)])]
  transfers between devices with their start and end apart: 16 -> 15, of which waited for: 9 -> 9; matrix products, arithmetic and copies ran while one was open for 3% -> 3% of each run, Pallas kernels for 10% -> 13%
where the time goes in v5:
time: 49 us; the launch traced here: 48.7 us
  waiting for transfers between devices  19.7 us (40%)
  starting transfers between devices  19.2 us (39%)
  Pallas kernels  7.79 us (16%)
  local copies, waits for them, and re-layouts  1.77 us (4%)
    ppermute x4, starting transfers between devices, swap_line(): lax.ppermute(x, 'col', ends + [p for p in inner if 0 <= p[1] < n_col])  10 us
    pallas_call x17, Pallas kernels, call(): pl.pallas_call(body, out_shape=outs, in_specs=[SMEM] * n_smem + [VMEM] *...  7.79 us
    ppermute x4, waiting for transfers between devices, swap_line(): lax.ppermute(x, 'col', ends + [p for p in inner if 0 <= p[1] < n_col])  7.42 us
    ppermute x9, waiting for transfers between devices, swap(): return lax.ppermute(x, 'row', [(i, i ^ d) for i in range(n_row)])  7.22 us
    ppermute x9, starting transfers between devices, swap(): return lax.ppermute(x, 'row', [(i, i ^ d) for i in range(n_row)])  6.55 us
    ppermute x2, waiting for transfers between devices, next_door(): lax.ppermute(x, ('row', 'col'), [(i * n_col + j, (i ^ d) * n_col + (j ^ 1...  5.1 us
    ppermute x2, starting transfers between devices, next_door(): lax.ppermute(x, ('row', 'col'), [(i * n_col + j, (i ^ d) * n_col + (j ^ 1...  2.58 us
    dynamic_slice x1, local copies, waits for them, and re-layouts, chip_columns(): return lax.dynamic_slice_in_dim(amplitudes, start, 2 * depth, 1)  1.11 us
  transfers between devices with their start and end apart: 15, of which 9 were waited for; matrix products, arithmetic and copies ran while one was open for 3% of the time, Pallas kernels for 13%

profile of v5, /device:TPU:0, one launch (start us, length us, event | category | flops | bytes accessed | tf_op | source)
XLA Modules:
  0.0 48.7 jit_solution(7225230257857104212)
XLA Ops:
  0.0 3.0 %collective-permute-start.3 = (f32[384,384]{1,0:T(8,128)}, f32[384,384]{1,0:T(8,128)S(1)}, u32[]{:S(2)}, u32[]{:S(2)}) collective-permute-start(f32[384,384]{1,0:T(8,128)} %refs_3_.1), channel_id=1, source_target_pairs={{0,1},{1,0},{2,3},{3,2},{4,5},{5,4},{6,7},{7,6},{8,9},{9,8},{10,11... | collective-permute-start | bytes 1769480 | tf_op jit(solution)/shard_map/ppermute | solution.py:260
  3.0 1.7 %collective-permute-start.2 = (f32[384,384]{1,0:T(8,128)}, f32[384,384]{1,0:T(8,128)S(1)}, u32[]{:S(2)}, u32[]{:S(2)}) collective-permute-start(f32[384,384]{1,0:T(8,128)} %refs_3_.1), channel_id=1, source_target_pairs={{0,0},{3,3},{1,2},{2,1},{4,4},{7,7},{5,6},{6,5},{8,8},{11,11},{9,1... | collective-permute-start | bytes 1769480 | tf_op jit(solution)/shard_map/ppermute | solution.py:260
  4.7 1.1 %constant_dynamic-slice_fusion = (f32[64,768]{1,0:T(8,128)S(1)}, f32[64,768]{1,0:T(8,128)S(1)}) fusion(f32[64,1536]{1,0:T(8,128)} %param.5, s32[]{:T(128)S(6)} %select_n.14, s32[]{:T(128)S(6)} %select_n.13), kind=kLoop, calls=%fused_computation.2 | loop fusion | bytes 786440 | tf_op jit(solution)/shard_map/dynamic_slice | solution.py:282
  5.9 1.6 %collective-permute-start = (f32[64,768]{1,0:T(8,128)S(1)}, f32[64,768]{1,0:T(8,128)S(1)}, u32[]{:S(2)}, u32[]{:S(2)}) collective-permute-start(f32[64,768]{1,0:T(8,128)S(1)} %get-tuple-element.77), channel_id=1, source_target_pairs={{0,8},{4,12},{8,0},{12,4},{1,9},{5,13},{9,1},{13,5},{2,10},{6,14},... | collective-permute-start | bytes 589832 | tf_op jit(solution)/shard_map/ppermute | solution.py:263
  7.6 0.9 %amplitude_tables.1 = (f32[8,384]{1,0:T(8,128)S(1)}, f32[8,384]{1,0:T(8,128)S(1)}) custom-call(s32[3]{0:T(128)S(1)} %pad_add_fusion.refs_0_, s32[32,16]{1,0:T(8,128)S(1)} %copy.6.refs_1_), custom_call_target="tpu_custom_call" | custom-call | bytes 26636 | tf_op jit(solution)/shard_map/amplitude_tables/pallas_call | solution.py:230
  8.4 3.8 %collective-permute-done.refs_2_ = f32[64,768]{1,0:T(8,128)S(1)} collective-permute-done((f32[64,768]{1,0:T(8,128)S(1)}, f32[64,768]{1,0:T(8,128)S(1)}, u32[]{:S(2)}, u32[]{:S(2)}) %collective-permute-start) | collective-permute-done | bytes 196640 | tf_op jit(solution)/shard_map/ppermute | solution.py:263
  12.4 0.6 %copy-done.1 = s32[16,16]{1,0:T(8,128)S(1)} copy-done((s32[16,16]{1,0:T(8,128)S(1)}, s32[16,16]{1,0:T(8,128)}, u32[]{:S(2)}) %copy-start.1) | copy-done | bytes 1048
  13.0 0.8 %own_tables.1 = (f32[4,384]{1,0:T(4,128)S(1)}, f32[16,384]{1,0:T(8,128)S(1)}) custom-call(s32[3]{0:T(128)S(1)} %pad_add_fusion.refs_0_, s32[16,16]{1,0:T(8,128)S(1)} %copy-done.1, s32[16]{0:T(128)S(1)} %copy-done.2), custom_call_target="tpu_custom_call" | custom-call | bytes 31820 | tf_op jit(solution)/shard_map/own_tables/pallas_call | solution.py:230
  13.8 0.6 %own.1 = (bf16[256,384]{1,0:T(8,128)(2,1)S(1)}, bf16[256,384]{1,0:T(8,128)(2,1)S(1)}, f32[384,384]{1,0:T(8,128)S(1)}, f32[128,384]{1,0:T(8,128)S(1)}, f32[128,384]{1,0:T(8,128)S(1)}) custom-call(f32[8,384]{1,0:T(8,128)S(1)} %get-tuple-element.43.refs_0_, f32[128,384]{1,0:T(8,128)S(1)} %get-tuple-element.44.refs_1_, ...), custom_call_target="tpu_custom_call" | custom-call | flops 226492416 | bytes 2377728 | tf_op jit(solution)/shard_map/own/pallas_call | solution.py:230
  14.4 2.1 %collective-permute-done.3.refs_0_.refs_2_ = f32[384,384]{1,0:T(8,128)S(1)} collective-permute-done((f32[384,384]{1,0:T(8,128)}, f32[384,384]{1,0:T(8,128)S(1)}, u32[]{:S(2)}, u32[]{:S(2)}) %collective-permute-start.3) | collective-permute-done | bytes 589856 | tf_op jit(solution)/shard_map/ppermute | solution.py:260
  16.6 0.7 %collective-permute-start.5 = (f32[392,384]{1,0:T(8,128)S(1)}, f32[392,384]{1,0:T(8,128)S(1)}, u32[]{:S(2)}, u32[]{:S(2)}) collective-permute-start(f32[392,384]{1,0:T(8,128)S(1)} %pass.1.refs_3_), channel_id=1, source_target_pairs={{0,0},{3,3},{1,2},{2,1},{4,4},{7,7},{5,6},{6,5},{8,8},{11,11},{9,1... | collective-permute-start | bytes 1806344 | tf_op jit(solution)/shard_map/ppermute | solution.py:260
  17.4 4.6 %collective-permute-start.4 = (f32[384,384]{1,0:T(8,128)S(1)}, f32[384,384]{1,0:T(8,128)S(1)}, u32[]{:S(2)}, u32[]{:S(2)}) collective-permute-start(f32[384,384]{1,0:T(8,128)S(1)} %pick.1), channel_id=1, source_target_pairs={{0,1},{1,0},{2,3},{3,2},{4,5},{5,4},{6,7},{7,6},{8,9},{9,8},{10,11... | collective-permute-start | bytes 1769480 | tf_op jit(solution)/shard_map/ppermute | solution.py:260
  22.0 1.6 %tables.1 = (f32[4,384]{1,0:T(4,128)S(1)}, f32[16,384]{1,0:T(8,128)S(1)}, f32[4,384]{1,0:T(4,128)S(1)}, f32[16,384]{1,0:T(8,128)S(1)}, f32[4,384]{1,0:T(4,128)S(...) custom-call(s32[3]{0:T(128)S(1)} %pad_add_fusion.refs_0_, ...), custom_call_target="tpu_custom_call" | custom-call | bytes 154700 | tf_op jit(solution)/shard_map/tables/pallas_call | solution.py:230
  23.6 1.0 %pair.1 = (f32[128,768]{1,0:T(8,128)S(1)}, f32[128,768]{1,0:T(8,128)S(1)}) custom-call(bf16[256,384]{1,0:T(8,128)(2,1)S(1)} %get-tuple-element.56.refs_0_, bf16[256,384]{1,0:T(8,128)(2,1)S(1)} %get-tuple-element.57.refs_1_, f32[384,384]{1,0:T(8,128)S(1)} %collective-permute-done.3.refs_0_.refs_2_, f32[4,384]{1,0:T(4,128)S(1)} %get-tuple-element.58.refs_3_, ...), custom_call_target="tpu_custom_call" | custom-call | flops 452984832 | bytes 2371584 | tf_op jit(solution)/shard_map/pair/pallas_call | solution.py:230
  24.7 0.5 %collective-permute-start.6 = (f32[128,384]{1,0:T(8,128)S(1)}, f32[128,384]{1,0:T(8,128)S(1)}, u32[]{:S(2)}, u32[]{:S(2)}) collective-permute-start(f32[128,384]{1,0:T(8,128)S(1)} %get-tuple-element.53), channel_id=1, source_target_pairs={{0,4},{4,0},{8,12},{12,8},{1,5},{5,1},{9,13},{13,9},{2,6},{6,2},{1... | collective-permute-start | bytes 589832 | tf_op jit(solution)/shard_map/ppermute | solution.py:263
  25.2 1.5 %collective-permute-done.6.refs_1_ = f32[128,384]{1,0:T(8,128)S(1)} collective-permute-done((f32[128,384]{1,0:T(8,128)S(1)}, f32[128,384]{1,0:T(8,128)S(1)}, u32[]{:S(2)}, u32[]{:S(2)}) %collective-permute-start.6) | collective-permute-done | bytes 196640 | tf_op jit(solution)/shard_map/ppermute | solution.py:263
  26.7 1.6 %collective-permute-start.7 = (f32[64,384]{1,0:T(8,128)S(1)}, f32[64,384]{1,0:T(8,128)S(1)}, u32[]{:S(2)}, u32[]{:S(2)}) collective-permute-start(f32[64,384]{1,0:T(8,128)S(1)} %get-tuple-element.55), channel_id=1, source_target_pairs={{0,8},{4,12},{8,0},{12,4},{1,9},{5,13},{9,1},{13,5},{2,10},{6,14},... | collective-permute-start | bytes 294920 | tf_op jit(solution)/shard_map/ppermute | solution.py:263
  28.3 0.6 %collective-permute-start.9 = (f32[64,768]{1,0:T(8,128)S(1)}, f32[64,768]{1,0:T(8,128)S(1)}, u32[]{:S(2)}, u32[]{:S(2)}) collective-permute-start(f32[64,768]{1,0:T(8,128)S(1)} %get-tuple-element.63), channel_id=1, source_target_pairs={{0,8},{4,12},{8,0},{12,4},{1,9},{5,13},{9,1},{13,5},{2,10},{6,14},... | collective-permute-start | bytes 589832 | tf_op jit(solution)/shard_map/ppermute | solution.py:263
  28.9 5.3 %collective-permute-done.4.refs_0_.refs_2_ = f32[384,384]{1,0:T(8,128)S(1)} collective-permute-done((f32[384,384]{1,0:T(8,128)S(1)}, f32[384,384]{1,0:T(8,128)S(1)}, u32[]{:S(2)}, u32[]{:S(2)}) %collective-permute-start.4) | collective-permute-done | bytes 589856 | tf_op jit(solution)/shard_map/ppermute | solution.py:260
  34.2 0.1 halves.1
  34.3 1.5 %collective-permute-done.9.refs_6_.refs_7_.refs_5_ = f32[64,768]{1,0:T(8,128)S(1)} collective-permute-done((f32[64,768]{1,0:T(8,128)S(1)}, f32[64,768]{1,0:T(8,128)S(1)}, u32[]{:S(2)}, u32[]{:S(2)}) %collective-permute-start.9) | collective-permute-done | bytes 196640 | tf_op jit(solution)/shard_map/ppermute | solution.py:263
  35.8 0.5 %corner.1 = (f32[128,384]{1,0:T(8,128)S(1)}, f32[128,384]{1,0:T(8,128)S(1)}) custom-call(bf16[384,384]{1,0:T(8,128)(2,1)S(1)} %get-tuple-element.50.refs_0_.refs_2_, bf16[384,384]{1,0:T(8,128)(2,1)S(1)} %get-tuple-element.51.refs_1_.refs_3_, f32[384,384]{1,0:T(8,128)S(1)} %collective-permute-done.4.refs_0_.refs_2_, ...), custom_call_target="tpu_custom_call" | custom-call | flops 226492416 | bytes 1572864 | tf_op jit(solution)/shard_map/corner/pallas_call | solution.py:230
  36.4 0.5 %last.1 = (f32[128,384]{1,0:T(8,128)S(1)}, f32[128,384]{1,0:T(8,128)S(1)}) custom-call(bf16[256,384]{1,0:T(8,128)(2,1)S(1)} %get-tuple-element.56.refs_0_, bf16[256,384]{1,0:T(8,128)(2,1)S(1)} %get-tuple-element.57.refs_1_, bf16[384,384]{1,0:T(8,128)(2,1)S(1)} %get-tuple-element.50.refs_0_.refs_2_, bf16[384,384]{1,0:T(8,128)(2,1)S(1)} %get-tuple-element.51.refs_1_.refs_3_, ...), custom_call_target="tpu_custom_call" | custom-call | flops 226492416 | bytes 1376256 | tf_op jit(solution)/shard_map/last/pallas_call | solution.py:230
  36.9 0.6 %collective-permute-start.13 = (f32[128,384]{1,0:T(8,128)S(1)}, f32[128,384]{1,0:T(8,128)S(1)}, u32[]{:S(2)}, u32[]{:S(2)}) collective-permute-start(f32[128,384]{1,0:T(8,128)S(1)} %get-tuple-element.71), channel_id=1, source_target_pairs={{0,4},{4,0},{8,12},{12,8},{1,5},{5,1},{9,13},{13,9},{2,6},{6,2},{1... | collective-permute-start | bytes 589832 | tf_op jit(solution)/shard_map/ppermute | solution.py:263
  37.5 0.3 collective-permute-done.10.refs_1_
  37.9 1.3 %collective-permute-start.11 = (f32[64,384]{1,0:T(8,128)S(1)}, f32[64,384]{1,0:T(8,128)S(1)}, u32[]{:S(2)}, u32[]{:S(2)}) collective-permute-start(f32[64,384]{1,0:T(8,128)S(1)} %get-tuple-element.66), channel_id=1, source_target_pairs={{1,0},{2,3},{5,4},{6,7},{9,8},{10,11},{13,12},{14,15},{17,16},{18,... | collective-permute-start | bytes 294920 | tf_op jit(solution)/shard_map/ppermute | solution.py:321
  39.2 1.3 %collective-permute-start.12 = (f32[64,384]{1,0:T(8,128)S(1)}, f32[64,384]{1,0:T(8,128)S(1)}, u32[]{:S(2)}, u32[]{:S(2)}) collective-permute-start(f32[64,384]{1,0:T(8,128)S(1)} %get-tuple-element.67), channel_id=1, source_target_pairs={{1,8},{2,11},{5,12},{6,15},{9,0},{10,3},{13,4},{14,7},{17,24},{18,... | collective-permute-start | bytes 294920 | tf_op jit(solution)/shard_map/ppermute | solution.py:321
  40.5 1.6 %collective-permute-start.14 = (f32[64,384]{1,0:T(8,128)S(1)}, f32[64,384]{1,0:T(8,128)S(1)}, u32[]{:S(2)}, u32[]{:S(2)}) collective-permute-start(f32[64,384]{1,0:T(8,128)S(1)} %get-tuple-element.73), channel_id=1, source_target_pairs={{0,8},{4,12},{8,0},{12,4},{1,9},{5,13},{9,1},{13,5},{2,10},{6,14},... | collective-permute-start | bytes 294920 | tf_op jit(solution)/shard_map/ppermute | solution.py:263
  42.1 0.5 finish.2.refs_6_
  42.5 2.1 %collective-permute-done.11.refs_1_ = f32[64,384]{1,0:T(8,128)S(1)} collective-permute-done((f32[64,384]{1,0:T(8,128)S(1)}, f32[64,384]{1,0:T(8,128)S(1)}, u32[]{:S(2)}, u32[]{:S(2)}) %collective-permute-start.11) | collective-permute-done | bytes 98336 | tf_op jit(solution)/shard_map/ppermute | solution.py:321
  44.6 3.0 %collective-permute-done.12.refs_2_ = f32[64,384]{1,0:T(8,128)S(1)} collective-permute-done((f32[64,384]{1,0:T(8,128)S(1)}, f32[64,384]{1,0:T(8,128)S(1)}, u32[]{:S(2)}, u32[]{:S(2)}) %collective-permute-start.12) | collective-permute-done | bytes 98336 | tf_op jit(solution)/shard_map/ppermute | solution.py:321
  47.6 1.1 %finish.3 = f32[64,1536]{1,0:T(8,128)} custom-call(f32[16,384]{1,0:T(8,128)S(1)} %get-tuple-element.41.refs_0_, f32[64,384]{1,0:T(8,128)S(1)} %collective-permute-done.11.refs_1_, f32[64,384]{1,0:T(8,128)S(1)} %collective-permute-done.12.refs_2_, f32[16,384]{1,0:T(8,128)S(1)} %add.12.refs_3_, f32[64,384]{1,0:T(8,128)S(1)} %get-tuple-element.72.refs_4_, ...), custom_call_target="tpu_custom_call" | custom-call | flops 393216 | bytes 1228800 | tf_op jit(solution)/shard_map/finish/pallas_call | solution.py:230
  (28 shorter events, 0.8 us)
Async XLA Ops:
  0.0 16.6 %collective-permute-start.3 = (f32[384,384]{1,0:T(8,128)}, f32[384,384]{1,0:T(8,128)S(1)}, u32[]{:S(2)}, u32[]{:S(2)}) collective-permute-start(f32[384,384]{1,0:T(8,128)} %refs_3_.1), channel_id=1, source_target_pairs={{0,1},{1,0},{2,3},{3,2},{4,5},{5,4},{6,7},{7,6},{8,9},{9,8},{10,11... | collective-permute-start | bytes 1769480 | tf_op jit(solution)/shard_map/ppermute | solution.py:260
  3.0 14.3 %collective-permute-start.2 = (f32[384,384]{1,0:T(8,128)}, f32[384,384]{1,0:T(8,128)S(1)}, u32[]{:S(2)}, u32[]{:S(2)}) collective-permute-start(f32[384,384]{1,0:T(8,128)} %refs_3_.1), channel_id=1, source_target_pairs={{0,0},{3,3},{1,2},{2,1},{4,4},{7,7},{5,6},{6,5},{8,8},{11,11},{9,1... | collective-permute-start | bytes 1769480 | tf_op jit(solution)/shard_map/ppermute | solution.py:260
  4.7 2.7 %copy-start.3 = (s32[32,16]{0,1:T(8,128)S(1)}, s32[32,16]{0,1:T(8,128)}, u32[]{:S(2)}) copy-start(s32[32,16]{0,1:T(8,128)} %param.7) | copy-start | bytes 6148
  4.7 9.1 %copy-start = (f32[384,384]{1,0:T(8,128)S(1)}, f32[384,384]{1,0:T(8,128)}, u32[]{:S(2)}) copy-start(f32[384,384]{1,0:T(8,128)} %refs_3_.1) | copy-start | bytes 1769476
  5.9 6.4 %collective-permute-start = (f32[64,768]{1,0:T(8,128)S(1)}, f32[64,768]{1,0:T(8,128)S(1)}, u32[]{:S(2)}, u32[]{:S(2)}) collective-permute-start(f32[64,768]{1,0:T(8,128)S(1)} %get-tuple-element.77), channel_id=1, source_target_pairs={{0,8},{4,12},{8,0},{12,4},{1,9},{5,13},{9,1},{13,5},{2,10},{6,14},... | collective-permute-start | bytes 589832 | tf_op jit(solution)/shard_map/ppermute | solution.py:263
  12.3 0.7 %copy-start.1 = (s32[16,16]{1,0:T(8,128)S(1)}, s32[16,16]{1,0:T(8,128)}, u32[]{:S(2)}) copy-start(s32[16,16]{1,0:T(8,128)} %refs_1_.4) | copy-start | bytes 3076
  12.3 0.7 %copy-start.2 = (s32[16]{0:T(128)S(1)}, s32[16]{0:T(128)}, u32[]{:S(2)}) copy-start(s32[16]{0:T(128)} %refs_2_.3) | copy-start | bytes 196
  12.3 1.5 %collective-permute-start.1 = (f32[128,384]{1,0:T(8,128)S(1)}, f32[128,384]{1,0:T(8,128)S(1)}, u32[]{:S(2)}, u32[]{:S(2)}) collective-permute-start(f32[128,384]{1,0:T(8,128)S(1)} %get-tuple-element.45), channel_id=1, source_target_pairs={{0,4},{4,0},{8,12},{12,8},{1,5},{5,1},{9,13},{13,9},{2,6},{6,2},{1... | collective-permute-start | bytes 589832 | tf_op jit(solution)/shard_map/ppermute | solution.py:263
  16.6 17.6 %collective-permute-start.5 = (f32[392,384]{1,0:T(8,128)S(1)}, f32[392,384]{1,0:T(8,128)S(1)}, u32[]{:S(2)}, u32[]{:S(2)}) collective-permute-start(f32[392,384]{1,0:T(8,128)S(1)} %pass.1.refs_3_), channel_id=1, source_target_pairs={{0,0},{3,3},{1,2},{2,1},{4,4},{7,7},{5,6},{6,5},{8,8},{11,11},{9,1... | collective-permute-start | bytes 1806344 | tf_op jit(solution)/shard_map/ppermute | solution.py:260
  17.4 16.8 %collective-permute-start.4 = (f32[384,384]{1,0:T(8,128)S(1)}, f32[384,384]{1,0:T(8,128)S(1)}, u32[]{:S(2)}, u32[]{:S(2)}) collective-permute-start(f32[384,384]{1,0:T(8,128)S(1)} %pick.1), channel_id=1, source_target_pairs={{0,1},{1,0},{2,3},{3,2},{4,5},{5,4},{6,7},{7,6},{8,9},{9,8},{10,11... | collective-permute-start | bytes 1769480 | tf_op jit(solution)/shard_map/ppermute | solution.py:260
  24.6 3.7 %collective-permute-start.8 = (f32[128,768]{1,0:T(8,128)S(1)}, f32[128,768]{1,0:T(8,128)S(1)}, u32[]{:S(2)}, u32[]{:S(2)}) collective-permute-start(f32[128,768]{1,0:T(8,128)S(1)} %get-tuple-element.61), channel_id=1, source_target_pairs={{0,4},{4,0},{8,12},{12,8},{1,5},{5,1},{9,13},{13,9},{2,6},{6,2},{1... | collective-permute-start | bytes 1179656 | tf_op jit(solution)/shard_map/ppermute | solution.py:263
  24.7 2.0 %collective-permute-start.6 = (f32[128,384]{1,0:T(8,128)S(1)}, f32[128,384]{1,0:T(8,128)S(1)}, u32[]{:S(2)}, u32[]{:S(2)}) collective-permute-start(f32[128,384]{1,0:T(8,128)S(1)} %get-tuple-element.53), channel_id=1, source_target_pairs={{0,4},{4,0},{8,12},{12,8},{1,5},{5,1},{9,13},{13,9},{2,6},{6,2},{1... | collective-permute-start | bytes 589832 | tf_op jit(solution)/shard_map/ppermute | solution.py:263
  26.7 7.6 %collective-permute-start.7 = (f32[64,384]{1,0:T(8,128)S(1)}, f32[64,384]{1,0:T(8,128)S(1)}, u32[]{:S(2)}, u32[]{:S(2)}) collective-permute-start(f32[64,384]{1,0:T(8,128)S(1)} %get-tuple-element.55), channel_id=1, source_target_pairs={{0,8},{4,12},{8,0},{12,4},{1,9},{5,13},{9,1},{13,5},{2,10},{6,14},... | collective-permute-start | bytes 294920 | tf_op jit(solution)/shard_map/ppermute | solution.py:263
  28.3 7.5 %collective-permute-start.9 = (f32[64,768]{1,0:T(8,128)S(1)}, f32[64,768]{1,0:T(8,128)S(1)}, u32[]{:S(2)}, u32[]{:S(2)}) collective-permute-start(f32[64,768]{1,0:T(8,128)S(1)} %get-tuple-element.63), channel_id=1, source_target_pairs={{0,8},{4,12},{8,0},{12,4},{1,9},{5,13},{9,1},{13,5},{2,10},{6,14},... | collective-permute-start | bytes 589832 | tf_op jit(solution)/shard_map/ppermute | solution.py:263
  36.3 1.5 %collective-permute-start.10 = (f32[128,384]{1,0:T(8,128)S(1)}, f32[128,384]{1,0:T(8,128)S(1)}, u32[]{:S(2)}, u32[]{:S(2)}) collective-permute-start(f32[128,384]{1,0:T(8,128)S(1)} %get-tuple-element.65), channel_id=1, source_target_pairs={{0,4},{4,0},{8,12},{12,8},{1,5},{5,1},{9,13},{13,9},{2,6},{6,2},{1... | collective-permute-start | bytes 589832 | tf_op jit(solution)/shard_map/ppermute | solution.py:263
  36.9 3.5 %collective-permute-start.13 = (f32[128,384]{1,0:T(8,128)S(1)}, f32[128,384]{1,0:T(8,128)S(1)}, u32[]{:S(2)}, u32[]{:S(2)}) collective-permute-start(f32[128,384]{1,0:T(8,128)S(1)} %get-tuple-element.71), channel_id=1, source_target_pairs={{0,4},{4,0},{8,12},{12,8},{1,5},{5,1},{9,13},{13,9},{2,6},{6,2},{1... | collective-permute-start | bytes 589832 | tf_op jit(solution)/shard_map/ppermute | solution.py:263
  37.9 6.7 %collective-permute-start.11 = (f32[64,384]{1,0:T(8,128)S(1)}, f32[64,384]{1,0:T(8,128)S(1)}, u32[]{:S(2)}, u32[]{:S(2)}) collective-permute-start(f32[64,384]{1,0:T(8,128)S(1)} %get-tuple-element.66), channel_id=1, source_target_pairs={{1,0},{2,3},{5,4},{6,7},{9,8},{10,11},{13,12},{14,15},{17,16},{18,... | collective-permute-start | bytes 294920 | tf_op jit(solution)/shard_map/ppermute | solution.py:321
  39.2 8.5 %collective-permute-start.12 = (f32[64,384]{1,0:T(8,128)S(1)}, f32[64,384]{1,0:T(8,128)S(1)}, u32[]{:S(2)}, u32[]{:S(2)}) collective-permute-start(f32[64,384]{1,0:T(8,128)S(1)} %get-tuple-element.67), channel_id=1, source_target_pairs={{1,8},{2,11},{5,12},{6,15},{9,0},{10,3},{13,4},{14,7},{17,24},{18,... | collective-permute-start | bytes 294920 | tf_op jit(solution)/shard_map/ppermute | solution.py:321
  40.5 7.1 %collective-permute-start.14 = (f32[64,384]{1,0:T(8,128)S(1)}, f32[64,384]{1,0:T(8,128)S(1)}, u32[]{:S(2)}, u32[]{:S(2)}) collective-permute-start(f32[64,384]{1,0:T(8,128)S(1)} %get-tuple-element.73), channel_id=1, source_target_pairs={{0,8},{4,12},{8,0},{12,4},{1,9},{5,13},{9,1},{13,5},{2,10},{6,14},... | collective-permute-start | bytes 294920 | tf_op jit(solution)/shard_map/ppermute | solution.py:263

commit v6 on v5

--- a/solution.py
+++ b/solution.py
@@ -137,9 +137,6 @@
             at = pl.ds(p * rows + o * OTB, OTB)
             slab[at, :] = masked
             high[at, :], low[at, :] = split(masked)
-    used = 2 * rows
-    if used < slab.shape[0]:
-        slab[used:, :] = jnp.zeros((slab.shape[0] - used, slab.shape[1]), jnp.float32)
     multiply_kernel(((2,),), high, low, block, masks, *sums)
 
 
@@ -154,31 +151,31 @@
         give[at, :] = jnp.where(second, here, there)
 
 
-def pick_kernel(marks, slab, block, out):
-    out[...] = jnp.where(marks[0:1, : out.shape[1]] > 0.5, slab[...], block[...])
-
-
 def pass_kernel(block, out):
     rows = block.shape[0]
     out[:rows, :] = block[...]
-    out[rows:, :] = jnp.zeros((out.shape[0] - rows, out.shape[1]), jnp.float32)
-
-
-def halves_kernel(counts, *refs):
-    refs[-2][...], refs[-1][...] = masked_halves(parted(refs[:-2], counts))
-
-
-def last_kernel(high, low, b_high, b_low, keep, give):
+    if out.shape[0] > rows:
+        out[rows:, :] = jnp.zeros((out.shape[0] - rows, out.shape[1]), jnp.float32)
+
+
+def halves_kernel(block, masks, high, low):
+    high[...], low[...] = masked_halves([(block, masks)])
+
+
+def last_kernel(high, low, *refs):
+    *halves, keep, give = refs
+    b_high = sum(x[...] for x in halves[::2])
+    b_low = sum(x[...] for x in halves[1::2])
     half = keep.shape[0]
     for out, start in ((give, half), (keep, 0)):
         at = pl.ds(start, half)
-        out[...] = product(high[at, :], low[at, :], b_high[...], b_low[...])
-
-
-def corner_kernel(b_high, b_low, slab, keep, give):
+        out[...] = product(high[at, :], low[at, :], b_high, b_low)
+
+
+def corner_kernel(slab, b_high, b_low, keep, give):
     half = keep.shape[0]
     for out, start in ((give, half), (keep, 0)):
-        a_high, a_low = split(slab[start : start + half, :])
+        a_high, a_low = split(slab[pl.ds(start, half), :])
         out[...] = product(a_high, a_low, b_high[...], b_low[...])
 
 
@@ -187,6 +184,10 @@
     for i, out in enumerate(outs):
         at = pl.ds(i * rows, rows)
         out[...] = keep[at, :] + got[at, :]
+
+
+def add_kernel(*refs):
+    refs[-1][...] = sum(share[...] for share in refs[:-1])
 
 
 def finish_kernel(counts, *refs):
@@ -259,14 +260,17 @@
         inner = [(i, (i + kind ^ 1) - kind) for i in range(n_col)]
         return lax.ppermute(x, "col", ends + [p for p in inner if 0 <= p[1] < n_col])
 
+    def send_in(x):
+        return lax.ppermute(x, "col", [(0, 1), (n_col - 1, n_col - 2)])
+
+    def send_out(x):
+        return lax.ppermute(x, "col", [(1, 0), (n_col - 2, n_col - 1)])
+
     def swap(x, d):
         return lax.ppermute(x, "row", [(i, i ^ d) for i in range(n_row)])
 
     k_tiles, tiles = depth // TB, pairs // TB
-    cut = 0
-    parts = [integrals]
-    even = [swap_line(integrals, EVEN)]
-    odd = [swap_line(x, ODD) for x in parts]
+    even, odd = swap_line(integrals, EVEN), swap_line(integrals, ODD)
 
     amp_rows, marks = call(
         functools.partial(amplitude_tables_kernel, order),
@@ -285,7 +289,7 @@
     pieces += [swap(chip_columns(d), 2 * d) for d in range(1, n_row // 2)]
     keep, give = call(deal_kernel, "deal", [f32(total // 2, depth)] * 2, 0, marks, *pieces)
     slab_parts = [keep, swap(give, 1)]
-    corner = n_col >= 4 and total <= depth - cut and depth == width
+    corner = n_col == 4
     last = n_col - 2 if corner else n_col - 1
     kinds = [(OWN, 0)] + [(kind, step) for step in range(1, last + 1) for kind in (EVEN, ODD)]
     ends = (CORNER, n_col - 1)
@@ -326,14 +330,14 @@
         keep, give = call(
             functools.partial(
                 multiply_kernel,
-                tuple(tuple(len(block) + 1 for _, block in group) for group in groups),
+                tuple((2,) * len(group) for group in groups),
             ),
             name,
             [f32(total // 2, len(groups) * width)] * 2,
             0,
             high,
             low,
-            *[x for group in groups for slot, block in group for x in (*block, masks[slot])],
+            *[x for group in groups for slot, block in group for x in (block, masks[slot])],
             flops=6 * total * depth * width * len(groups),
             after=after,
         )
@@ -359,7 +363,7 @@
         own_kernel,
         "own",
         [jax.ShapeDtypeStruct((total, depth), jnp.bfloat16)] * 2
-        + [f32(depth - cut if corner else total, depth)]
+        + [f32(total, depth)]
         + [f32(total // 2, width)] * 2,
         0,
         amp_rows,
@@ -368,53 +372,54 @@
         masks[OWN, 0],
         flops=6 * total * depth * width,
     )
+    if corner:
+        end_slab = send_in(slab)
     slots = [([[(OWN, 0)]], exchange(keep, give))]
+    moved = ()
+    if corner:
+        shape = f32(depth + 8, width)
+        passed = call(pass_kernel, "pass", [shape], 0, even, after=(slab,))[0]
+        shape = f32(depth, width)
+        turned = call(pass_kernel, "pass", [shape], 0, odd, after=(passed,))[0]
+        moved = (turned,)
     for step in range(1, last + 1):
         if step > 1:
-            going, through = list(odd), list(even)
-            if corner and step == 2:
-                shape = f32(depth + 8, width)
-                through = [call(pass_kernel, "pass", [shape], 0, x, after=(slab,))[0] for x in even]
-                going[-1] = call(
-                    pick_kernel,
-                    "pick",
-                    [f32(depth - cut, depth)],
-                    0,
-                    marks,
-                    slab,
-                    odd[-1],
-                    after=through,
-                )[0]
-            odd = [swap_line(x, ODD) for x in through]
-            even = [swap_line(x, EVEN) for x in going]
-            if corner and step == 2:
-                end_slab = even[-1]
+            if corner:
+                even, odd = send_out(turned), swap_line(passed, ODD)
+            else:
+                even, odd = swap_line(odd, EVEN), swap_line(even, ODD)
         if 2 * step <= n_col - 1:
-            slots.append(multiply("pair", [((EVEN, step), even)], [((ODD, step), odd)]))
+            slots.append(multiply("pair", [((EVEN, step), even)], [((ODD, step), odd)], after=moved))
             continue
         if step < last:
             slots.append(multiply("both", [((EVEN, step), even), ((ODD, step), odd)]))
             continue
         out = finish(slots)
-        b_halves = call(
-            functools.partial(halves_kernel, (len(even) + 1, len(odd) + 1)),
-            "halves",
-            [jax.ShapeDtypeStruct((depth, width), jnp.bfloat16)] * 2,
-            0,
-            *even,
-            masks[EVEN, step],
-            *odd,
-            masks[ODD, step],
-            flops=WEIGHT,
-        )
+        halves = {}
+        for kind, block in ((ODD, odd), (EVEN, even)):
+            halves[kind] = call(
+                halves_kernel,
+                "halves",
+                [jax.ShapeDtypeStruct((depth, width), jnp.bfloat16)] * 2,
+                0,
+                block,
+                masks[kind, step],
+                flops=1*10**9 if kind == ODD else 0,
+            )
         after = tuple(share for _, shares in slots for share in shares)
         sums = [f32(total // 2, width)] * 2
         flops = 6 * total * depth * width
         slots = []
         if corner:
-            parts = call(corner_kernel, "corner", sums, 0, *b_halves, end_slab, flops=flops, after=after)
-            slots.append(([[ends]], [next_door(x, 2 * i) for i, x in enumerate(fold(*parts))]))
-        parts = call(last_kernel, "last", sums, 0, high, low, *b_halves, flops=flops, after=after)
+            args = [end_slab, *halves[ODD]]
+            parts = call(corner_kernel, "corner", sums, 0, *args, flops=flops, after=after)
+            pieces = fold(*parts)
+            shares = [next_door(x, 2 * i) for i, x in enumerate(pieces)]
+            summed = call(add_kernel, "add", [f32(rows, width)], 0, *shares, flops=WEIGHT)
+            slots.append(([[ends]], summed))
+            after = tuple(parts)
+        args = [high, low, *halves[ODD], *halves[EVEN]]
+        parts = call(last_kernel, "last", sums, 0, *args, flops=flops, after=after)
         slots.append(([[(EVEN, step), (ODD, step)]], exchange(*parts)))
     return finish(slots, out)
 

time: 49 us -> 52.5 us (1.071)
  starting transfers between devices: 19.2 us -> 22.2 us
    ppermute x0 -> x2, starting transfers between devices: none -> 7.78 us  [the longest x1 6.49 us: send_in(): return lax.ppermute(x, 'col', [(0, 1), (n_col - 1, n_col - 2)])]
    ppermute x4 -> x3, waiting for transfers between devices: 7.42 us -> 2.16 us  [swap_line(): lax.ppermute(x, 'col', ends + [p for p in inner if 0 <= p[1] < n_col])]
    ppermute x4 -> x3, starting transfers between devices: 10 us -> 5.43 us  [swap_line(): lax.ppermute(x, 'col', ends + [p for p in inner if 0 <= p[1] < n_col])]
    ppermute x9, waiting for transfers between devices: 7.22 us -> 10.6 us  [swap(): return lax.ppermute(x, 'row', [(i, i ^ d) for i in range(n_row)])]
    ppermute x0 -> x2, waiting for transfers between devices: none -> 1.77 us  [the longest x1 1.76 us: send_out(): return lax.ppermute(x, 'col', [(1, 0), (n_col - 2, n_col - 1)])]
    pallas_call x17 -> x19, Pallas kernels: 7.79 us -> 7.86 us  [call(): pl.pallas_call(body, out_shape=outs, in_specs=[SMEM] * n_smem + [VMEM] *...]
  transfers between devices with their start and end apart: 15 -> 16, of which waited for: 9 -> 8; matrix products, arithmetic and copies ran while one was open for 3% -> 2% of each run, Pallas kernels for 13% -> 13%
where the time goes in v6:
time: 52.5 us; the launch traced here: 52.2 us
  starting transfers between devices  22.2 us (42%)
  waiting for transfers between devices  20 us (38%)
  Pallas kernels  7.86 us (15%)
  local copies, waits for them, and re-layouts  1.77 us (3%)
    ppermute x9, waiting for transfers between devices, swap(): return lax.ppermute(x, 'row', [(i, i ^ d) for i in range(n_row)])  10.6 us
    pallas_call x19, Pallas kernels, call(): pl.pallas_call(body, out_shape=outs, in_specs=[SMEM] * n_smem + [VMEM] *...  7.86 us
    ppermute x1, starting transfers between devices, send_in(): return lax.ppermute(x, 'col', [(0, 1), (n_col - 1, n_col - 2)])  6.49 us
    ppermute x9, starting transfers between devices, swap(): return lax.ppermute(x, 'row', [(i, i ^ d) for i in range(n_row)])  6.41 us
    ppermute x2, waiting for transfers between devices, next_door(): lax.ppermute(x, ('row', 'col'), [(i * n_col + j, (i ^ d) * n_col + (j ^ 1...  5.53 us
    ppermute x3, starting transfers between devices, swap_line(): lax.ppermute(x, 'col', ends + [p for p in inner if 0 <= p[1] < n_col])  5.43 us
    ppermute x2, starting transfers between devices, next_door(): lax.ppermute(x, ('row', 'col'), [(i * n_col + j, (i ^ d) * n_col + (j ^ 1...  2.58 us
    ppermute x3, waiting for transfers between devices, swap_line(): lax.ppermute(x, 'col', ends + [p for p in inner if 0 <= p[1] < n_col])  2.16 us
  transfers between devices with their start and end apart: 16, of which 8 were waited for; matrix products, arithmetic and copies ran while one was open for 2% of the time, Pallas kernels for 13%

profile of v6, /device:TPU:0, one launch (start us, length us, event | category | flops | bytes accessed | tf_op | source)
XLA Modules:
  0.0 52.2 jit_solution(16864672487458662730)
XLA Ops:
  0.0 3.0 %collective-permute-start.3 = (f32[384,384]{1,0:T(8,128)}, f32[384,384]{1,0:T(8,128)S(1)}, u32[]{:S(2)}, u32[]{:S(2)}) collective-permute-start(f32[384,384]{1,0:T(8,128)} %refs_3_.1), channel_id=1, source_target_pairs={{0,1},{1,0},{2,3},{3,2},{4,5},{5,4},{6,7},{7,6},{8,9},{9,8},{10,11... | collective-permute-start | bytes 1769480 | tf_op jit(solution)/shard_map/ppermute | solution.py:261
  3.0 1.7 %collective-permute-start.7 = (f32[384,384]{1,0:T(8,128)}, f32[384,384]{1,0:T(8,128)S(1)}, u32[]{:S(2)}, u32[]{:S(2)}) collective-permute-start(f32[384,384]{1,0:T(8,128)} %refs_3_.1), channel_id=1, source_target_pairs={{0,0},{3,3},{1,2},{2,1},{4,4},{7,7},{5,6},{6,5},{8,8},{11,11},{9,1... | collective-permute-start | bytes 1769480 | tf_op jit(solution)/shard_map/ppermute | solution.py:261
  4.7 1.1 %constant_dynamic-slice_fusion = (f32[64,768]{1,0:T(8,128)S(1)}, f32[64,768]{1,0:T(8,128)S(1)}) fusion(f32[64,1536]{1,0:T(8,128)} %param.5, s32[]{:T(128)S(6)} %select_n.14, s32[]{:T(128)S(6)} %select_n.13), kind=kLoop, calls=%fused_computation.2 | loop fusion | bytes 786440 | tf_op jit(solution)/shard_map/dynamic_slice | solution.py:286
  5.9 1.6 %collective-permute-start = (f32[64,768]{1,0:T(8,128)S(1)}, f32[64,768]{1,0:T(8,128)S(1)}, u32[]{:S(2)}, u32[]{:S(2)}) collective-permute-start(f32[64,768]{1,0:T(8,128)S(1)} %get-tuple-element.81), channel_id=1, source_target_pairs={{0,8},{4,12},{8,0},{12,4},{1,9},{5,13},{9,1},{13,5},{2,10},{6,14},... | collective-permute-start | bytes 589832 | tf_op jit(solution)/shard_map/ppermute | solution.py:270
  7.6 0.9 %amplitude_tables.1 = (f32[8,384]{1,0:T(8,128)S(1)}, f32[8,384]{1,0:T(8,128)S(1)}) custom-call(s32[3]{0:T(128)S(1)} %pad_add_fusion.refs_0_, s32[32,16]{1,0:T(8,128)S(1)} %copy.6.refs_1_), custom_call_target="tpu_custom_call" | custom-call | bytes 26636 | tf_op jit(solution)/shard_map/amplitude_tables/pallas_call | solution.py:231
  8.4 3.8 %collective-permute-done.refs_2_ = f32[64,768]{1,0:T(8,128)S(1)} collective-permute-done((f32[64,768]{1,0:T(8,128)S(1)}, f32[64,768]{1,0:T(8,128)S(1)}, u32[]{:S(2)}, u32[]{:S(2)}) %collective-permute-start) | collective-permute-done | bytes 196640 | tf_op jit(solution)/shard_map/ppermute | solution.py:270
  12.4 0.6 %copy-done.1 = s32[16,16]{1,0:T(8,128)S(1)} copy-done((s32[16,16]{1,0:T(8,128)S(1)}, s32[16,16]{1,0:T(8,128)}, u32[]{:S(2)}) %copy-start.1) | copy-done | bytes 1048
  13.0 0.8 %own_tables.1 = (f32[4,384]{1,0:T(4,128)S(1)}, f32[16,384]{1,0:T(8,128)S(1)}) custom-call(s32[3]{0:T(128)S(1)} %pad_add_fusion.refs_0_, s32[16,16]{1,0:T(8,128)S(1)} %copy-done.1, s32[16]{0:T(128)S(1)} %copy-done.2), custom_call_target="tpu_custom_call" | custom-call | bytes 31820 | tf_op jit(solution)/shard_map/own_tables/pallas_call | solution.py:231
  13.8 0.6 %own.1 = (bf16[256,384]{1,0:T(8,128)(2,1)S(1)}, bf16[256,384]{1,0:T(8,128)(2,1)S(1)}, f32[256,384]{1,0:T(8,128)S(1)}, f32[128,384]{1,0:T(8,128)S(1)}, f32[128,384]{1,0:T(8,128)S(1)}) custom-call(f32[8,384]{1,0:T(8,128)S(1)} %get-tuple-element.44.refs_0_, f32[128,384]{1,0:T(8,128)S(1)} %get-tuple-element.46.refs_1_, ...), custom_call_target="tpu_custom_call" | custom-call | flops 226492416 | bytes 2181120 | tf_op jit(solution)/shard_map/own/pallas_call | solution.py:231
  14.4 2.2 %collective-permute-done.3.refs_0_.refs_2_ = f32[384,384]{1,0:T(8,128)S(1)} collective-permute-done((f32[384,384]{1,0:T(8,128)}, f32[384,384]{1,0:T(8,128)S(1)}, u32[]{:S(2)}, u32[]{:S(2)}) %collective-permute-start.3) | collective-permute-done | bytes 589856 | tf_op jit(solution)/shard_map/ppermute | solution.py:261
  16.6 0.7 %collective-permute-start.4 = (f32[392,384]{1,0:T(8,128)S(1)}, f32[392,384]{1,0:T(8,128)S(1)}, u32[]{:S(2)}, u32[]{:S(2)}) collective-permute-start(f32[392,384]{1,0:T(8,128)S(1)} %pass.2.refs_1_), channel_id=1, source_target_pairs={{0,0},{3,3},{1,2},{2,1},{4,4},{7,7},{5,6},{6,5},{8,8},{11,11},{9,1... | collective-permute-start | bytes 1806344 | tf_op jit(solution)/shard_map/ppermute | solution.py:261
  17.3 1.6 %tables.1 = (f32[4,384]{1,0:T(4,128)S(1)}, f32[16,384]{1,0:T(8,128)S(1)}, f32[4,384]{1,0:T(4,128)S(1)}, f32[16,384]{1,0:T(8,128)S(1)}, f32[4,384]{1,0:T(4,128)S(...) custom-call(s32[3]{0:T(128)S(1)} %pad_add_fusion.refs_0_, ...), custom_call_target="tpu_custom_call" | custom-call | bytes 154700 | tf_op jit(solution)/shard_map/tables/pallas_call | solution.py:231
  19.0 1.0 %pair.1 = (f32[128,768]{1,0:T(8,128)S(1)}, f32[128,768]{1,0:T(8,128)S(1)}) custom-call(bf16[256,384]{1,0:T(8,128)(2,1)S(1)} %get-tuple-element.57.refs_0_, bf16[256,384]{1,0:T(8,128)(2,1)S(1)} %get-tuple-element.58.refs_1_, f32[384,384]{1,0:T(8,128)S(1)} %collective-permute-done.3.refs_0_.refs_2_, f32[4,384]{1,0:T(4,128)S(1)} %get-tuple-element.59.refs_3_, ...), custom_call_target="tpu_custom_call" | custom-call | flops 452984832 | bytes 2371584 | tf_op jit(solution)/shard_map/pair/pallas_call | solution.py:231
  20.1 1.3 %collective-permute-start.13 = (f32[384,384]{1,0:T(8,128)S(1)}, f32[384,384]{1,0:T(8,128)S(1)}, u32[]{:S(2)}, u32[]{:S(2)}) collective-permute-start(f32[384,384]{1,0:T(8,128)S(1)} %pass.3.refs_6_), channel_id=1, source_target_pairs={{1,0},{2,3},{5,4},{6,7},{9,8},{10,11},{13,12},{14,15},{17,16},{18,... | collective-permute-start | bytes 1769480 | tf_op jit(solution)/shard_map/ppermute | solution.py:267
  21.4 6.5 %collective-permute-start.2 = (f32[256,384]{1,0:T(8,128)S(1)}, f32[256,384]{1,0:T(8,128)S(1)}, u32[]{:S(2)}, u32[]{:S(2)}) collective-permute-start(f32[256,384]{1,0:T(8,128)S(1)} %get-tuple-element.49.refs_1_), channel_id=1, source_target_pairs={{0,1},{3,2},{4,5},{7,6},{8,9},{11,10},{12,13},{15,14},{16,17},{19,... | collective-permute-start | bytes 1179656 | tf_op jit(solution)/shard_map/ppermute | solution.py:264
  27.9 0.3 collective-permute-start.5
  28.2 1.6 %collective-permute-start.9 = (f32[64,768]{1,0:T(8,128)S(1)}, f32[64,768]{1,0:T(8,128)S(1)}, u32[]{:S(2)}, u32[]{:S(2)}) collective-permute-start(f32[64,768]{1,0:T(8,128)S(1)} %get-tuple-element.64), channel_id=1, source_target_pairs={{0,8},{4,12},{8,0},{12,4},{1,9},{5,13},{9,1},{13,5},{2,10},{6,14},... | collective-permute-start | bytes 589832 | tf_op jit(solution)/shard_map/ppermute | solution.py:270
  29.8 1.2 %collective-permute-start.6 = (f32[64,384]{1,0:T(8,128)S(1)}, f32[64,384]{1,0:T(8,128)S(1)}, u32[]{:S(2)}, u32[]{:S(2)}) collective-permute-start(f32[64,384]{1,0:T(8,128)S(1)} %get-tuple-element.56), channel_id=1, source_target_pairs={{0,8},{4,12},{8,0},{12,4},{1,9},{5,13},{9,1},{13,5},{2,10},{6,14},... | collective-permute-start | bytes 294920 | tf_op jit(solution)/shard_map/ppermute | solution.py:270
  30.9 0.1 halves.2
  31.1 6.4 %collective-permute-done.6.refs_4_.refs_2_ = f32[64,384]{1,0:T(8,128)S(1)} collective-permute-done((f32[64,384]{1,0:T(8,128)S(1)}, f32[64,384]{1,0:T(8,128)S(1)}, u32[]{:S(2)}, u32[]{:S(2)}) %collective-permute-start.6) | collective-permute-done | bytes 98336 | tf_op jit(solution)/shard_map/ppermute | solution.py:270
  37.5 0.5 corner.1
  38.1 1.8 %collective-permute-done.13.refs_0_ = f32[384,384]{1,0:T(8,128)S(1)} collective-permute-done((f32[384,384]{1,0:T(8,128)S(1)}, f32[384,384]{1,0:T(8,128)S(1)}, u32[]{:S(2)}, u32[]{:S(2)}) %collective-permute-start.13) | collective-permute-done | bytes 589856 | tf_op jit(solution)/shard_map/ppermute | solution.py:267
  39.8 0.1 halves.3
  40.0 0.5 %last.1 = (f32[128,384]{1,0:T(8,128)S(1)}, f32[128,384]{1,0:T(8,128)S(1)}) custom-call(bf16[256,384]{1,0:T(8,128)(2,1)S(1)} %get-tuple-element.57.refs_0_, bf16[256,384]{1,0:T(8,128)(2,1)S(1)} %get-tuple-element.58.refs_1_, bf16[384,384]{1,0:T(8,128)(2,1)S(1)} %get-tuple-element.51.refs_1_.refs_2_, bf16[384,384]{1,0:T(8,128)(2,1)S(1)} %get-tuple-element.52.refs_2_.refs_3_, ...), custom_call_target="tpu_custom_call" | custom-call | flops 226492416 | bytes 1966080 | tf_op jit(solution)/shard_map/last/pallas_call | solution.py:231
  40.6 1.3 %collective-permute-start.11 = (f32[64,384]{1,0:T(8,128)S(1)}, f32[64,384]{1,0:T(8,128)S(1)}, u32[]{:S(2)}, u32[]{:S(2)}) collective-permute-start(f32[64,384]{1,0:T(8,128)S(1)} %get-tuple-element.67), channel_id=1, source_target_pairs={{1,0},{2,3},{5,4},{6,7},{9,8},{10,11},{13,12},{14,15},{17,16},{18,... | collective-permute-start | bytes 294920 | tf_op jit(solution)/shard_map/ppermute | solution.py:325
  41.9 1.3 %collective-permute-start.12 = (f32[64,384]{1,0:T(8,128)S(1)}, f32[64,384]{1,0:T(8,128)S(1)}, u32[]{:S(2)}, u32[]{:S(2)}) collective-permute-start(f32[64,384]{1,0:T(8,128)S(1)} %get-tuple-element.68), channel_id=1, source_target_pairs={{1,8},{2,11},{5,12},{6,15},{9,0},{10,3},{13,4},{14,7},{17,24},{18,... | collective-permute-start | bytes 294920 | tf_op jit(solution)/shard_map/ppermute | solution.py:325
  43.3 0.5 finish.2.refs_5_
  43.8 1.6 %collective-permute-start.15 = (f32[64,384]{1,0:T(8,128)S(1)}, f32[64,384]{1,0:T(8,128)S(1)}, u32[]{:S(2)}, u32[]{:S(2)}) collective-permute-start(f32[64,384]{1,0:T(8,128)S(1)} %get-tuple-element.77), channel_id=1, source_target_pairs={{0,8},{4,12},{8,0},{12,4},{1,9},{5,13},{9,1},{13,5},{2,10},{6,14},... | collective-permute-start | bytes 294920 | tf_op jit(solution)/shard_map/ppermute | solution.py:270
  45.3 2.4 %collective-permute-done.11.refs_0_ = f32[64,384]{1,0:T(8,128)S(1)} collective-permute-done((f32[64,384]{1,0:T(8,128)S(1)}, f32[64,384]{1,0:T(8,128)S(1)}, u32[]{:S(2)}, u32[]{:S(2)}) %collective-permute-start.11) | collective-permute-done | bytes 98336 | tf_op jit(solution)/shard_map/ppermute | solution.py:325
  47.7 3.1 %collective-permute-done.12.refs_1_ = f32[64,384]{1,0:T(8,128)S(1)} collective-permute-done((f32[64,384]{1,0:T(8,128)S(1)}, f32[64,384]{1,0:T(8,128)S(1)}, u32[]{:S(2)}, u32[]{:S(2)}) %collective-permute-start.12) | collective-permute-done | bytes 98336 | tf_op jit(solution)/shard_map/ppermute | solution.py:325
  50.9 0.2 collective-permute-done.15.refs_4_
  51.1 1.1 %finish.3 = f32[64,1536]{1,0:T(8,128)} custom-call(f32[16,384]{1,0:T(8,128)S(1)} %get-tuple-element.43.refs_0_, f32[64,384]{1,0:T(8,128)S(1)} %add.18.refs_1_, f32[16,384]{1,0:T(8,128)S(1)} %add.13.refs_2_, f32[64,384]{1,0:T(8,128)S(1)} %get-tuple-element.76.refs_3_, f32[64,384]{1,0:T(8,128)S(1)} %collective-permute-done.15.refs_4_, ...), custom_call_target="tpu_custom_call" | custom-call | flops 393216 | bytes 1130496 | tf_op jit(solution)/shard_map/finish/pallas_call | solution.py:231
  (32 shorter events, 0.8 us)
Async XLA Ops:
  0.0 16.6 %collective-permute-start.3 = (f32[384,384]{1,0:T(8,128)}, f32[384,384]{1,0:T(8,128)S(1)}, u32[]{:S(2)}, u32[]{:S(2)}) collective-permute-start(f32[384,384]{1,0:T(8,128)} %refs_3_.1), channel_id=1, source_target_pairs={{0,1},{1,0},{2,3},{3,2},{4,5},{5,4},{6,7},{7,6},{8,9},{9,8},{10,11... | collective-permute-start | bytes 1769480 | tf_op jit(solution)/shard_map/ppermute | solution.py:261
  3.0 15.9 %collective-permute-start.7 = (f32[384,384]{1,0:T(8,128)}, f32[384,384]{1,0:T(8,128)S(1)}, u32[]{:S(2)}, u32[]{:S(2)}) collective-permute-start(f32[384,384]{1,0:T(8,128)} %refs_3_.1), channel_id=1, source_target_pairs={{0,0},{3,3},{1,2},{2,1},{4,4},{7,7},{5,6},{6,5},{8,8},{11,11},{9,1... | collective-permute-start | bytes 1769480 | tf_op jit(solution)/shard_map/ppermute | solution.py:261
  4.7 2.7 %copy-start.3 = (s32[32,16]{0,1:T(8,128)S(1)}, s32[32,16]{0,1:T(8,128)}, u32[]{:S(2)}) copy-start(s32[32,16]{0,1:T(8,128)} %param.7) | copy-start | bytes 6148
  4.7 9.1 %copy-start = (f32[384,384]{1,0:T(8,128)S(1)}, f32[384,384]{1,0:T(8,128)}, u32[]{:S(2)}) copy-start(f32[384,384]{1,0:T(8,128)} %refs_3_.1) | copy-start | bytes 1769476
  5.9 6.4 %collective-permute-start = (f32[64,768]{1,0:T(8,128)S(1)}, f32[64,768]{1,0:T(8,128)S(1)}, u32[]{:S(2)}, u32[]{:S(2)}) collective-permute-start(f32[64,768]{1,0:T(8,128)S(1)} %get-tuple-element.81), channel_id=1, source_target_pairs={{0,8},{4,12},{8,0},{12,4},{1,9},{5,13},{9,1},{13,5},{2,10},{6,14},... | collective-permute-start | bytes 589832 | tf_op jit(solution)/shard_map/ppermute | solution.py:270
  12.3 0.7 %copy-start.1 = (s32[16,16]{1,0:T(8,128)S(1)}, s32[16,16]{1,0:T(8,128)}, u32[]{:S(2)}) copy-start(s32[16,16]{1,0:T(8,128)} %refs_1_.4) | copy-start | bytes 3076
  12.3 0.7 %copy-start.2 = (s32[16]{0:T(128)S(1)}, s32[16]{0:T(128)}, u32[]{:S(2)}) copy-start(s32[16]{0:T(128)} %refs_2_.3) | copy-start | bytes 196
  12.3 1.5 %collective-permute-start.1 = (f32[128,384]{1,0:T(8,128)S(1)}, f32[128,384]{1,0:T(8,128)S(1)}, u32[]{:S(2)}, u32[]{:S(2)}) collective-permute-start(f32[128,384]{1,0:T(8,128)S(1)} %get-tuple-element.47), channel_id=1, source_target_pairs={{0,4},{4,0},{8,12},{12,8},{1,5},{5,1},{9,13},{13,9},{2,6},{6,2},{1... | collective-permute-start | bytes 589832 | tf_op jit(solution)/shard_map/ppermute | solution.py:270
  16.6 14.3 %collective-permute-start.4 = (f32[392,384]{1,0:T(8,128)S(1)}, f32[392,384]{1,0:T(8,128)S(1)}, u32[]{:S(2)}, u32[]{:S(2)}) collective-permute-start(f32[392,384]{1,0:T(8,128)S(1)} %pass.2.refs_1_), channel_id=1, source_target_pairs={{0,0},{3,3},{1,2},{2,1},{4,4},{7,7},{5,6},{6,5},{8,8},{11,11},{9,1... | collective-permute-start | bytes 1806344 | tf_op jit(solution)/shard_map/ppermute | solution.py:261
  20.0 8.2 %collective-permute-start.8 = (f32[128,768]{1,0:T(8,128)S(1)}, f32[128,768]{1,0:T(8,128)S(1)}, u32[]{:S(2)}, u32[]{:S(2)}) collective-permute-start(f32[128,768]{1,0:T(8,128)S(1)} %get-tuple-element.62), channel_id=1, source_target_pairs={{0,4},{4,0},{8,12},{12,8},{1,5},{5,1},{9,13},{13,9},{2,6},{6,2},{1... | collective-permute-start | bytes 1179656 | tf_op jit(solution)/shard_map/ppermute | solution.py:270
  20.1 19.8 %collective-permute-start.13 = (f32[384,384]{1,0:T(8,128)S(1)}, f32[384,384]{1,0:T(8,128)S(1)}, u32[]{:S(2)}, u32[]{:S(2)}) collective-permute-start(f32[384,384]{1,0:T(8,128)S(1)} %pass.3.refs_6_), channel_id=1, source_target_pairs={{1,0},{2,3},{5,4},{6,7},{9,8},{10,11},{13,12},{14,15},{17,16},{18,... | collective-permute-start | bytes 1769480 | tf_op jit(solution)/shard_map/ppermute | solution.py:267
  21.4 16.1 %collective-permute-start.2 = (f32[256,384]{1,0:T(8,128)S(1)}, f32[256,384]{1,0:T(8,128)S(1)}, u32[]{:S(2)}, u32[]{:S(2)}) collective-permute-start(f32[256,384]{1,0:T(8,128)S(1)} %get-tuple-element.49.refs_1_), channel_id=1, source_target_pairs={{0,1},{3,2},{4,5},{7,6},{8,9},{11,10},{12,13},{15,14},{16,17},{19,... | collective-permute-start | bytes 1179656 | tf_op jit(solution)/shard_map/ppermute | solution.py:264
  27.9 1.9 %collective-permute-start.5 = (f32[128,384]{1,0:T(8,128)S(1)}, f32[128,384]{1,0:T(8,128)S(1)}, u32[]{:S(2)}, u32[]{:S(2)}) collective-permute-start(f32[128,384]{1,0:T(8,128)S(1)} %get-tuple-element.54), channel_id=1, source_target_pairs={{0,4},{4,0},{8,12},{12,8},{1,5},{5,1},{9,13},{13,9},{2,6},{6,2},{1... | collective-permute-start | bytes 589832 | tf_op jit(solution)/shard_map/ppermute | solution.py:270
  28.2 9.3 %collective-permute-start.9 = (f32[64,768]{1,0:T(8,128)S(1)}, f32[64,768]{1,0:T(8,128)S(1)}, u32[]{:S(2)}, u32[]{:S(2)}) collective-permute-start(f32[64,768]{1,0:T(8,128)S(1)} %get-tuple-element.64), channel_id=1, source_target_pairs={{0,8},{4,12},{8,0},{12,4},{1,9},{5,13},{9,1},{13,5},{2,10},{6,14},... | collective-permute-start | bytes 589832 | tf_op jit(solution)/shard_map/ppermute | solution.py:270
  29.8 7.7 %collective-permute-start.6 = (f32[64,384]{1,0:T(8,128)S(1)}, f32[64,384]{1,0:T(8,128)S(1)}, u32[]{:S(2)}, u32[]{:S(2)}) collective-permute-start(f32[64,384]{1,0:T(8,128)S(1)} %get-tuple-element.56), channel_id=1, source_target_pairs={{0,8},{4,12},{8,0},{12,4},{1,9},{5,13},{9,1},{13,5},{2,10},{6,14},... | collective-permute-start | bytes 294920 | tf_op jit(solution)/shard_map/ppermute | solution.py:270
  38.0 2.6 %collective-permute-start.10 = (f32[128,384]{1,0:T(8,128)S(1)}, f32[128,384]{1,0:T(8,128)S(1)}, u32[]{:S(2)}, u32[]{:S(2)}) collective-permute-start(f32[128,384]{1,0:T(8,128)S(1)} %get-tuple-element.66.refs_7_), channel_id=1, source_target_pairs={{0,4},{4,0},{8,12},{12,8},{1,5},{5,1},{9,13},{13,9},{2,6},{6,2},{1... | collective-permute-start | bytes 589832 | tf_op jit(solution)/shard_map/ppermute | solution.py:270
  40.5 3.2 %collective-permute-start.14 = (f32[128,384]{1,0:T(8,128)S(1)}, f32[128,384]{1,0:T(8,128)S(1)}, u32[]{:S(2)}, u32[]{:S(2)}) collective-permute-start(f32[128,384]{1,0:T(8,128)S(1)} %get-tuple-element.75), channel_id=1, source_target_pairs={{0,4},{4,0},{8,12},{12,8},{1,5},{5,1},{9,13},{13,9},{2,6},{6,2},{1... | collective-permute-start | bytes 589832 | tf_op jit(solution)/shard_map/ppermute | solution.py:270
  40.6 7.1 %collective-permute-start.11 = (f32[64,384]{1,0:T(8,128)S(1)}, f32[64,384]{1,0:T(8,128)S(1)}, u32[]{:S(2)}, u32[]{:S(2)}) collective-permute-start(f32[64,384]{1,0:T(8,128)S(1)} %get-tuple-element.67), channel_id=1, source_target_pairs={{1,0},{2,3},{5,4},{6,7},{9,8},{10,11},{13,12},{14,15},{17,16},{18,... | collective-permute-start | bytes 294920 | tf_op jit(solution)/shard_map/ppermute | solution.py:325
  41.9 8.9 %collective-permute-start.12 = (f32[64,384]{1,0:T(8,128)S(1)}, f32[64,384]{1,0:T(8,128)S(1)}, u32[]{:S(2)}, u32[]{:S(2)}) collective-permute-start(f32[64,384]{1,0:T(8,128)S(1)} %get-tuple-element.68), channel_id=1, source_target_pairs={{1,8},{2,11},{5,12},{6,15},{9,0},{10,3},{13,4},{14,7},{17,24},{18,... | collective-permute-start | bytes 294920 | tf_op jit(solution)/shard_map/ppermute | solution.py:325
  43.8 7.4 %collective-permute-start.15 = (f32[64,384]{1,0:T(8,128)S(1)}, f32[64,384]{1,0:T(8,128)S(1)}, u32[]{:S(2)}, u32[]{:S(2)}) collective-permute-start(f32[64,384]{1,0:T(8,128)S(1)} %get-tuple-element.77), channel_id=1, source_target_pairs={{0,8},{4,12},{8,0},{12,4},{1,9},{5,13},{9,1},{13,5},{2,10},{6,14},... | collective-permute-start | bytes 294920 | tf_op jit(solution)/shard_map/ppermute | solution.py:270

commit v7 on v5

--- a/solution.py
+++ b/solution.py
@@ -44,7 +44,7 @@
     return (index >= 0) & (index < n)
 
 
-def amplitude_tables_kernel(order, place, amp_mask, amp_rows, marks):
+def tables_kernel(order, kinds, place, amp_mask, int_mask, owner, amp_rows, marks, *refs):
     r, c, n_col = place[0], place[1], place[2]
     row = lax.broadcasted_iota(jnp.int32, marks.shape, 0)
     ends = ((c == 0) | (c == n_col - 1)).astype(jnp.float32)
@@ -57,10 +57,6 @@
             row = ((r ^ d) * n_col + c) * occ + o
             bits = [amp_mask[row, r * (depth // TB) + k] for k in range(depth // TB)]
             amp_rows[p * occ + o : p * occ + o + 1, :] = lane_mask(bits, lane_tile)
-
-
-def tables_kernel(kinds, place, int_mask, owner, *refs):
-    r, c, n_col = place[0], place[1], place[2]
     for i, (kind, step) in enumerate(kinds):
         masks, homes = refs[2 * i : 2 * i + 2]
         source = source_of(kind, step, c)
@@ -263,19 +259,25 @@
         return lax.ppermute(x, "row", [(i, i ^ d) for i in range(n_row)])
 
     k_tiles, tiles = depth // TB, pairs // TB
-    cut = 0
-    parts = [integrals]
     even = [swap_line(integrals, EVEN)]
-    odd = [swap_line(x, ODD) for x in parts]
-
-    amp_rows, marks = call(
-        functools.partial(amplitude_tables_kernel, order),
-        "amplitude_tables",
-        [f32(total // OTB, depth), f32(8, max(width, depth))],
-        2,
+    odd = [swap_line(integrals, ODD)]
+    corner = n_col == 4 and total <= depth and depth == width
+    last = n_col - 2 if corner else n_col - 1
+    kinds = [(OWN, 0)] + [(kind, step) for step in range(1, last + 1) for kind in (EVEN, ODD)]
+    ends = (CORNER, n_col - 1)
+    per_slot = [f32(k_tiles, width), f32(width // GROUP * tiles, GROUP)]
+    amp_rows, marks, *made = call(
+        functools.partial(tables_kernel, order, kinds + [ends]),
+        "tables",
+        [f32(total // OTB, depth), f32(8, max(width, depth))] + per_slot * (len(kinds) + 1),
+        4,
         place,
         amp_mask,
+        int_mask,
+        owner_map,
     )
+    masks = dict(zip(kinds + [ends], made[::2]))
+    homes = dict(zip(kinds + [ends], made[1::2]))
 
     def chip_columns(d):
         start = (r // 2 ^ d) * 2 * depth
@@ -285,29 +287,6 @@
     pieces += [swap(chip_columns(d), 2 * d) for d in range(1, n_row // 2)]
     keep, give = call(deal_kernel, "deal", [f32(total // 2, depth)] * 2, 0, marks, *pieces)
     slab_parts = [keep, swap(give, 1)]
-    corner = n_col >= 4 and total <= depth - cut and depth == width
-    last = n_col - 2 if corner else n_col - 1
-    kinds = [(OWN, 0)] + [(kind, step) for step in range(1, last + 1) for kind in (EVEN, ODD)]
-    ends = (CORNER, n_col - 1)
-    per_slot = [f32(k_tiles, width), f32(width // GROUP * tiles, GROUP)]
-    masks, homes = {}, {}
-
-    def tables(name, kinds):
-        made = call(
-            functools.partial(tables_kernel, kinds),
-            name,
-            per_slot * len(kinds),
-            3,
-            place,
-            int_mask,
-            owner_map,
-        )
-        masks.update(zip(kinds, made[::2]))
-        homes.update(zip(kinds, made[1::2]))
-
-    tables("own_tables", kinds[:1])
-    tables("tables", kinds[1:] + [ends])
-
     def fold(keep, give):
         shape = f32(rows, keep.shape[1])
         return call(fold_kernel, "fold", [shape] * (n_row // 2), 0, keep, swap(give, 1))
@@ -317,7 +296,7 @@
         return [pieces[0]] + [swap(pieces[i], 2 * i) for i in range(1, n_row // 2)]
 
     def next_door(x, d):
-        spots = [(i, j) for i in range(n_row) for j in (1, n_col - 2)]
+        spots = [(i, j) for i in range(n_row) for j in range(n_col)]
         return lax.ppermute(
             x, ("row", "col"), [(i * n_col + j, (i ^ d) * n_col + (j ^ 1)) for i, j in spots]
         )
@@ -359,7 +338,7 @@
         own_kernel,
         "own",
         [jax.ShapeDtypeStruct((total, depth), jnp.bfloat16)] * 2
-        + [f32(depth - cut if corner else total, depth)]
+        + [f32(depth if corner else total, depth)]
         + [f32(total // 2, width)] * 2,
         0,
         amp_rows,
@@ -378,7 +357,7 @@
                 going[-1] = call(
                     pick_kernel,
                     "pick",
-                    [f32(depth - cut, depth)],
+                    [f32(depth, width)],
                     0,
                     marks,
                     slab,

time: 49 us -> 47.2 us (0.963)
  Pallas kernels: 7.79 us -> 6.57 us
  starting transfers between devices: 19.2 us -> 18.6 us
    ppermute x4, waiting for transfers between devices: 7.42 us -> 9.05 us  [swap_line(): lax.ppermute(x, 'col', ends + [p for p in inner if 0 <= p[1] < n_col])]
    pallas_call x17 -> x15, Pallas kernels: 7.79 us -> 6.57 us  [call(): pl.pallas_call(body, out_shape=outs, in_specs=[SMEM] * n_smem + [VMEM] *...]
    ppermute x2, waiting for transfers between devices: 5.1 us -> 3.92 us  [next_door(): lax.ppermute(x, ('row', 'col'), [(i * n_col + j, (i ^ d) * n_col + (j ^ 1...]
    ppermute x9, starting transfers between devices: 6.55 us -> 5.58 us  [swap(): return lax.ppermute(x, 'row', [(i, i ^ d) for i in range(n_row)])]
  transfers between devices with their start and end apart: 15 -> 15, of which waited for: 9 -> 9; matrix products, arithmetic and copies ran while one was open for 3% -> 3% of each run, Pallas kernels for 13% -> 11%
where the time goes in v7:
time: 47.2 us; the launch traced here: 46.9 us
  waiting for transfers between devices  19.7 us (42%)
  starting transfers between devices  18.6 us (39%)
  Pallas kernels  6.57 us (14%)
  local copies, waits for them, and re-layouts  1.77 us (4%)
    ppermute x4, starting transfers between devices, swap_line(): lax.ppermute(x, 'col', ends + [p for p in inner if 0 <= p[1] < n_col])  10 us
    ppermute x4, waiting for transfers between devices, swap_line(): lax.ppermute(x, 'col', ends + [p for p in inner if 0 <= p[1] < n_col])  9.05 us
    ppermute x9, waiting for transfers between devices, swap(): return lax.ppermute(x, 'row', [(i, i ^ d) for i in range(n_row)])  6.76 us
    pallas_call x15, Pallas kernels, call(): pl.pallas_call(body, out_shape=outs, in_specs=[SMEM] * n_smem + [VMEM] *...  6.57 us
    ppermute x9, starting transfers between devices, swap(): return lax.ppermute(x, 'row', [(i, i ^ d) for i in range(n_row)])  5.58 us
    ppermute x2, waiting for transfers between devices, next_door(): lax.ppermute(x, ('row', 'col'), [(i * n_col + j, (i ^ d) * n_col + (j ^ 1...  3.92 us
    ppermute x2, starting transfers between devices, next_door(): lax.ppermute(x, ('row', 'col'), [(i * n_col + j, (i ^ d) * n_col + (j ^ 1...  3.02 us
    dynamic_slice x1, local copies, waits for them, and re-layouts, chip_columns(): return lax.dynamic_slice_in_dim(amplitudes, start, 2 * depth, 1)  1.11 us
  transfers between devices with their start and end apart: 15, of which 9 were waited for; matrix products, arithmetic and copies ran while one was open for 3% of the time, Pallas kernels for 11%

profile of v7, /device:TPU:0, one launch (start us, length us, event | category | flops | bytes accessed | tf_op | source)
XLA Modules:
  0.0 46.9 jit_solution(6027746571782273702)
XLA Ops:
  0.0 3.0 %collective-permute-start.3 = (f32[384,384]{1,0:T(8,128)}, f32[384,384]{1,0:T(8,128)S(1)}, u32[]{:S(2)}, u32[]{:S(2)}) collective-permute-start(f32[384,384]{1,0:T(8,128)} %refs_3_.3), channel_id=1, source_target_pairs={{0,1},{1,0},{2,3},{3,2},{4,5},{5,4},{6,7},{7,6},{8,9},{9,8},{10,11... | collective-permute-start | bytes 1769480 | tf_op jit(solution)/shard_map/ppermute | solution.py:256
  3.0 1.7 %collective-permute-start.2 = (f32[384,384]{1,0:T(8,128)}, f32[384,384]{1,0:T(8,128)S(1)}, u32[]{:S(2)}, u32[]{:S(2)}) collective-permute-start(f32[384,384]{1,0:T(8,128)} %refs_3_.3), channel_id=1, source_target_pairs={{0,0},{3,3},{1,2},{2,1},{4,4},{7,7},{5,6},{6,5},{8,8},{11,11},{9,1... | collective-permute-start | bytes 1769480 | tf_op jit(solution)/shard_map/ppermute | solution.py:256
  4.7 1.1 %constant_dynamic-slice_fusion = (f32[64,768]{1,0:T(8,128)S(1)}, f32[64,768]{1,0:T(8,128)S(1)}) fusion(f32[64,1536]{1,0:T(8,128)} %param.5, s32[]{:T(128)S(6)} %select_n.14, s32[]{:T(128)S(6)} %select_n.13), kind=kLoop, calls=%fused_computation.2 | loop fusion | bytes 786440 | tf_op jit(solution)/shard_map/dynamic_slice | solution.py:284
  5.9 1.6 %collective-permute-start = (f32[64,768]{1,0:T(8,128)S(1)}, f32[64,768]{1,0:T(8,128)S(1)}, u32[]{:S(2)}, u32[]{:S(2)}) collective-permute-start(f32[64,768]{1,0:T(8,128)S(1)} %get-tuple-element.77), channel_id=1, source_target_pairs={{0,8},{4,12},{8,0},{12,4},{1,9},{5,13},{9,1},{13,5},{2,10},{6,14},... | collective-permute-start | bytes 589832 | tf_op jit(solution)/shard_map/ppermute | solution.py:259
  7.5 0.1 pad_add_fusion.refs_0_
  7.6 0.5 %copy-done.1 = s32[16,16]{1,0:T(8,128)S(1)} copy-done((s32[16,16]{1,0:T(8,128)S(1)}, s32[16,16]{1,0:T(8,128)}, u32[]{:S(2)}) %copy-start.1) | copy-done | bytes 1048
  8.1 2.0 %tables.1 = (f32[8,384]{1,0:T(8,128)S(1)}, f32[8,384]{1,0:T(8,128)S(1)}, f32[4,384]{1,0:T(4,128)S(1)}, f32[16,384]{1,0:T(8,128)S(1)}, f32[4,384]{1,0:T(4,128)S(1...) custom-call(s32[3]{0:T(128)S(1)} %pad_add_fusion.refs_0_, ...), custom_call_target="tpu_custom_call" | custom-call | bytes 212044 | tf_op jit(solution)/shard_map/tables/pallas_call | solution.py:226
  10.2 2.1 %collective-permute-done.refs_2_ = f32[64,768]{1,0:T(8,128)S(1)} collective-permute-done((f32[64,768]{1,0:T(8,128)S(1)}, f32[64,768]{1,0:T(8,128)S(1)}, u32[]{:S(2)}, u32[]{:S(2)}) %collective-permute-start) | collective-permute-done | bytes 196640 | tf_op jit(solution)/shard_map/ppermute | solution.py:259
  12.4 1.4 %collective-permute-done.1.refs_2_ = f32[128,384]{1,0:T(8,128)S(1)} collective-permute-done((f32[128,384]{1,0:T(8,128)S(1)}, f32[128,384]{1,0:T(8,128)S(1)}, u32[]{:S(2)}, u32[]{:S(2)}) %collective-permute-start.1) | collective-permute-done | bytes 196640 | tf_op jit(solution)/shard_map/ppermute | solution.py:259
  13.8 0.6 %own.1 = (bf16[256,384]{1,0:T(8,128)(2,1)S(1)}, bf16[256,384]{1,0:T(8,128)(2,1)S(1)}, f32[384,384]{1,0:T(8,128)S(1)}, f32[128,384]{1,0:T(8,128)S(1)}, f32[128,384]{1,0:T(8,128)S(1)}) custom-call(f32[8,384]{1,0:T(8,128)S(1)} %get-tuple-element.43.refs_0_, f32[128,384]{1,0:T(8,128)S(1)} %get-tuple-element.44.refs_1_, ...), custom_call_target="tpu_custom_call" | custom-call | flops 226492416 | bytes 2377728 | tf_op jit(solution)/shard_map/own/pallas_call | solution.py:226
  14.4 2.2 %collective-permute-done.3.refs_0_.refs_2_ = f32[384,384]{1,0:T(8,128)S(1)} collective-permute-done((f32[384,384]{1,0:T(8,128)}, f32[384,384]{1,0:T(8,128)S(1)}, u32[]{:S(2)}, u32[]{:S(2)}) %collective-permute-start.3) | collective-permute-done | bytes 589856 | tf_op jit(solution)/shard_map/ppermute | solution.py:256
  16.6 0.7 %collective-permute-start.5 = (f32[392,384]{1,0:T(8,128)S(1)}, f32[392,384]{1,0:T(8,128)S(1)}, u32[]{:S(2)}, u32[]{:S(2)}) collective-permute-start(f32[392,384]{1,0:T(8,128)S(1)} %pass.1.refs_3_), channel_id=1, source_target_pairs={{0,0},{3,3},{1,2},{2,1},{4,4},{7,7},{5,6},{6,5},{8,8},{11,11},{9,1... | collective-permute-start | bytes 1806344 | tf_op jit(solution)/shard_map/ppermute | solution.py:256
  17.4 4.6 %collective-permute-start.4 = (f32[384,384]{1,0:T(8,128)S(1)}, f32[384,384]{1,0:T(8,128)S(1)}, u32[]{:S(2)}, u32[]{:S(2)}) collective-permute-start(f32[384,384]{1,0:T(8,128)S(1)} %pick.1), channel_id=1, source_target_pairs={{0,1},{1,0},{2,3},{3,2},{4,5},{5,4},{6,7},{7,6},{8,9},{9,8},{10,11... | collective-permute-start | bytes 1769480 | tf_op jit(solution)/shard_map/ppermute | solution.py:256
  22.0 1.0 %pair.1 = (f32[128,768]{1,0:T(8,128)S(1)}, f32[128,768]{1,0:T(8,128)S(1)}) custom-call(bf16[256,384]{1,0:T(8,128)(2,1)S(1)} %get-tuple-element.56.refs_0_, bf16[256,384]{1,0:T(8,128)(2,1)S(1)} %get-tuple-element.57.refs_1_, f32[384,384]{1,0:T(8,128)S(1)} %collective-permute-done.3.refs_0_.refs_2_, f32[4,384]{1,0:T(4,128)S(1)} %get-tuple-element.58.refs_3_, ...), custom_call_target="tpu_custom_call" | custom-call | flops 452984832 | bytes 2371584 | tf_op jit(solution)/shard_map/pair/pallas_call | solution.py:226
  23.0 0.5 %collective-permute-start.6 = (f32[128,384]{1,0:T(8,128)S(1)}, f32[128,384]{1,0:T(8,128)S(1)}, u32[]{:S(2)}, u32[]{:S(2)}) collective-permute-start(f32[128,384]{1,0:T(8,128)S(1)} %get-tuple-element.53), channel_id=1, source_target_pairs={{0,4},{4,0},{8,12},{12,8},{1,5},{5,1},{9,13},{13,9},{2,6},{6,2},{1... | collective-permute-start | bytes 589832 | tf_op jit(solution)/shard_map/ppermute | solution.py:259
  23.5 1.5 %collective-permute-done.6.refs_1_ = f32[128,384]{1,0:T(8,128)S(1)} collective-permute-done((f32[128,384]{1,0:T(8,128)S(1)}, f32[128,384]{1,0:T(8,128)S(1)}, u32[]{:S(2)}, u32[]{:S(2)}) %collective-permute-start.6) | collective-permute-done | bytes 196640 | tf_op jit(solution)/shard_map/ppermute | solution.py:259
  25.1 1.6 %collective-permute-start.7 = (f32[64,384]{1,0:T(8,128)S(1)}, f32[64,384]{1,0:T(8,128)S(1)}, u32[]{:S(2)}, u32[]{:S(2)}) collective-permute-start(f32[64,384]{1,0:T(8,128)S(1)} %get-tuple-element.55), channel_id=1, source_target_pairs={{0,8},{4,12},{8,0},{12,4},{1,9},{5,13},{9,1},{13,5},{2,10},{6,14},... | collective-permute-start | bytes 294920 | tf_op jit(solution)/shard_map/ppermute | solution.py:259
  26.7 0.6 %collective-permute-start.9 = (f32[64,768]{1,0:T(8,128)S(1)}, f32[64,768]{1,0:T(8,128)S(1)}, u32[]{:S(2)}, u32[]{:S(2)}) collective-permute-start(f32[64,768]{1,0:T(8,128)S(1)} %get-tuple-element.63), channel_id=1, source_target_pairs={{0,8},{4,12},{8,0},{12,4},{1,9},{5,13},{9,1},{13,5},{2,10},{6,14},... | collective-permute-start | bytes 589832 | tf_op jit(solution)/shard_map/ppermute | solution.py:259
  27.3 6.9 %collective-permute-done.4.refs_0_.refs_2_ = f32[384,384]{1,0:T(8,128)S(1)} collective-permute-done((f32[384,384]{1,0:T(8,128)S(1)}, f32[384,384]{1,0:T(8,128)S(1)}, u32[]{:S(2)}, u32[]{:S(2)}) %collective-permute-start.4) | collective-permute-done | bytes 589856 | tf_op jit(solution)/shard_map/ppermute | solution.py:256
  34.2 0.1 halves.1
  34.3 0.5 %corner.1 = (f32[128,384]{1,0:T(8,128)S(1)}, f32[128,384]{1,0:T(8,128)S(1)}) custom-call(bf16[384,384]{1,0:T(8,128)(2,1)S(1)} %get-tuple-element.50.refs_0_.refs_2_, bf16[384,384]{1,0:T(8,128)(2,1)S(1)} %get-tuple-element.51.refs_1_.refs_3_, f32[384,384]{1,0:T(8,128)S(1)} %collective-permute-done.4.refs_0_.refs_2_, ...), custom_call_target="tpu_custom_call" | custom-call | flops 226492416 | bytes 1572864 | tf_op jit(solution)/shard_map/corner/pallas_call | solution.py:226
  35.0 0.5 %last.1 = (f32[128,384]{1,0:T(8,128)S(1)}, f32[128,384]{1,0:T(8,128)S(1)}) custom-call(bf16[256,384]{1,0:T(8,128)(2,1)S(1)} %get-tuple-element.56.refs_0_, bf16[256,384]{1,0:T(8,128)(2,1)S(1)} %get-tuple-element.57.refs_1_, bf16[384,384]{1,0:T(8,128)(2,1)S(1)} %get-tuple-element.50.refs_0_.refs_2_, bf16[384,384]{1,0:T(8,128)(2,1)S(1)} %get-tuple-element.51.refs_1_.refs_3_, ...), custom_call_target="tpu_custom_call" | custom-call | flops 226492416 | bytes 1376256 | tf_op jit(solution)/shard_map/last/pallas_call | solution.py:226
  35.5 0.6 %collective-permute-start.13 = (f32[128,384]{1,0:T(8,128)S(1)}, f32[128,384]{1,0:T(8,128)S(1)}, u32[]{:S(2)}, u32[]{:S(2)}) collective-permute-start(f32[128,384]{1,0:T(8,128)S(1)} %get-tuple-element.71), channel_id=1, source_target_pairs={{0,4},{4,0},{8,12},{12,8},{1,5},{5,1},{9,13},{13,9},{2,6},{6,2},{1... | collective-permute-start | bytes 589832 | tf_op jit(solution)/shard_map/ppermute | solution.py:259
  36.1 0.3 collective-permute-done.10.refs_1_
  36.4 1.8 %collective-permute-start.11 = (f32[64,384]{1,0:T(8,128)S(1)}, f32[64,384]{1,0:T(8,128)S(1)}, u32[]{:S(2)}, u32[]{:S(2)}) collective-permute-start(f32[64,384]{1,0:T(8,128)S(1)} %get-tuple-element.66), channel_id=1, source_target_pairs={{0,1},{1,0},{2,3},{3,2},{4,5},{5,4},{6,7},{7,6},{8,9},{9,8},{10,11... | collective-permute-start | bytes 294920 | tf_op jit(solution)/shard_map/ppermute | solution.py:300
  38.2 1.2 %collective-permute-start.12 = (f32[64,384]{1,0:T(8,128)S(1)}, f32[64,384]{1,0:T(8,128)S(1)}, u32[]{:S(2)}, u32[]{:S(2)}) collective-permute-start(f32[64,384]{1,0:T(8,128)S(1)} %get-tuple-element.67), channel_id=1, source_target_pairs={{0,9},{1,8},{2,11},{3,10},{4,13},{5,12},{6,15},{7,14},{8,1},{9,0},... | collective-permute-start | bytes 294920 | tf_op jit(solution)/shard_map/ppermute | solution.py:300
  39.5 0.6 %collective-permute-start.14 = (f32[64,384]{1,0:T(8,128)S(1)}, f32[64,384]{1,0:T(8,128)S(1)}, u32[]{:S(2)}, u32[]{:S(2)}) collective-permute-start(f32[64,384]{1,0:T(8,128)S(1)} %get-tuple-element.73), channel_id=1, source_target_pairs={{0,8},{4,12},{8,0},{12,4},{1,9},{5,13},{9,1},{13,5},{2,10},{6,14},... | collective-permute-start | bytes 294920 | tf_op jit(solution)/shard_map/ppermute | solution.py:259
  40.1 0.5 finish.2.refs_6_
  40.5 0.8 %collective-permute-done.11.refs_1_ = f32[64,384]{1,0:T(8,128)S(1)} collective-permute-done((f32[64,384]{1,0:T(8,128)S(1)}, f32[64,384]{1,0:T(8,128)S(1)}, u32[]{:S(2)}, u32[]{:S(2)}) %collective-permute-start.11) | collective-permute-done | bytes 98336 | tf_op jit(solution)/shard_map/ppermute | solution.py:300
  41.4 3.1 %collective-permute-done.12.refs_2_ = f32[64,384]{1,0:T(8,128)S(1)} collective-permute-done((f32[64,384]{1,0:T(8,128)S(1)}, f32[64,384]{1,0:T(8,128)S(1)}, u32[]{:S(2)}, u32[]{:S(2)}) %collective-permute-start.12) | collective-permute-done | bytes 98336 | tf_op jit(solution)/shard_map/ppermute | solution.py:300
  44.5 1.4 %collective-permute-done.14.refs_5_ = f32[64,384]{1,0:T(8,128)S(1)} collective-permute-done((f32[64,384]{1,0:T(8,128)S(1)}, f32[64,384]{1,0:T(8,128)S(1)}, u32[]{:S(2)}, u32[]{:S(2)}) %collective-permute-start.14) | collective-permute-done | bytes 98336 | tf_op jit(solution)/shard_map/ppermute | solution.py:259
  45.8 1.1 %finish.3 = f32[64,1536]{1,0:T(8,128)} custom-call(f32[16,384]{1,0:T(8,128)S(1)} %get-tuple-element.41.refs_0_, f32[64,384]{1,0:T(8,128)S(1)} %collective-permute-done.11.refs_1_, f32[64,384]{1,0:T(8,128)S(1)} %collective-permute-done.12.refs_2_, f32[16,384]{1,0:T(8,128)S(1)} %add.12.refs_3_, f32[64,384]{1,0:T(8,128)S(1)} %get-tuple-element.72.refs_4_, ...), custom_call_target="tpu_custom_call" | custom-call | flops 393216 | bytes 1228800 | tf_op jit(solution)/shard_map/finish/pallas_call | solution.py:226
  (26 shorter events, 0.6 us)
Async XLA Ops:
  0.0 16.6 %collective-permute-start.3 = (f32[384,384]{1,0:T(8,128)}, f32[384,384]{1,0:T(8,128)S(1)}, u32[]{:S(2)}, u32[]{:S(2)}) collective-permute-start(f32[384,384]{1,0:T(8,128)} %refs_3_.3), channel_id=1, source_target_pairs={{0,1},{1,0},{2,3},{3,2},{4,5},{5,4},{6,7},{7,6},{8,9},{9,8},{10,11... | collective-permute-start | bytes 1769480 | tf_op jit(solution)/shard_map/ppermute | solution.py:256
  3.0 14.3 %collective-permute-start.2 = (f32[384,384]{1,0:T(8,128)}, f32[384,384]{1,0:T(8,128)S(1)}, u32[]{:S(2)}, u32[]{:S(2)}) collective-permute-start(f32[384,384]{1,0:T(8,128)} %refs_3_.3), channel_id=1, source_target_pairs={{0,0},{3,3},{1,2},{2,1},{4,4},{7,7},{5,6},{6,5},{8,8},{11,11},{9,1... | collective-permute-start | bytes 1769480 | tf_op jit(solution)/shard_map/ppermute | solution.py:256
  4.7 2.7 %copy-start.3 = (s32[32,16]{0,1:T(8,128)S(1)}, s32[32,16]{0,1:T(8,128)}, u32[]{:S(2)}) copy-start(s32[32,16]{0,1:T(8,128)} %param.7) | copy-start | bytes 6148
  4.7 9.1 %copy-start = (f32[384,384]{1,0:T(8,128)S(1)}, f32[384,384]{1,0:T(8,128)}, u32[]{:S(2)}) copy-start(f32[384,384]{1,0:T(8,128)} %refs_3_.3) | copy-start | bytes 1769476
  5.9 6.4 %collective-permute-start = (f32[64,768]{1,0:T(8,128)S(1)}, f32[64,768]{1,0:T(8,128)S(1)}, u32[]{:S(2)}, u32[]{:S(2)}) collective-permute-start(f32[64,768]{1,0:T(8,128)S(1)} %get-tuple-element.77), channel_id=1, source_target_pairs={{0,8},{4,12},{8,0},{12,4},{1,9},{5,13},{9,1},{13,5},{2,10},{6,14},... | collective-permute-start | bytes 589832 | tf_op jit(solution)/shard_map/ppermute | solution.py:259
  7.4 0.7 %copy-start.1 = (s32[16,16]{1,0:T(8,128)S(1)}, s32[16,16]{1,0:T(8,128)}, u32[]{:S(2)}) copy-start(s32[16,16]{1,0:T(8,128)} %refs_2_.1) | copy-start | bytes 3076
  7.5 0.7 %copy-start.2 = (s32[16]{0:T(128)S(1)}, s32[16]{0:T(128)}, u32[]{:S(2)}) copy-start(s32[16]{0:T(128)} %refs_3_.2) | copy-start | bytes 196
  12.3 1.5 %collective-permute-start.1 = (f32[128,384]{1,0:T(8,128)S(1)}, f32[128,384]{1,0:T(8,128)S(1)}, u32[]{:S(2)}, u32[]{:S(2)}) collective-permute-start(f32[128,384]{1,0:T(8,128)S(1)} %get-tuple-element.45), channel_id=1, source_target_pairs={{0,4},{4,0},{8,12},{12,8},{1,5},{5,1},{9,13},{13,9},{2,6},{6,2},{1... | collective-permute-start | bytes 589832 | tf_op jit(solution)/shard_map/ppermute | solution.py:259
  16.6 17.6 %collective-permute-start.5 = (f32[392,384]{1,0:T(8,128)S(1)}, f32[392,384]{1,0:T(8,128)S(1)}, u32[]{:S(2)}, u32[]{:S(2)}) collective-permute-start(f32[392,384]{1,0:T(8,128)S(1)} %pass.1.refs_3_), channel_id=1, source_target_pairs={{0,0},{3,3},{1,2},{2,1},{4,4},{7,7},{5,6},{6,5},{8,8},{11,11},{9,1... | collective-permute-start | bytes 1806344 | tf_op jit(solution)/shard_map/ppermute | solution.py:256
  17.4 16.8 %collective-permute-start.4 = (f32[384,384]{1,0:T(8,128)S(1)}, f32[384,384]{1,0:T(8,128)S(1)}, u32[]{:S(2)}, u32[]{:S(2)}) collective-permute-start(f32[384,384]{1,0:T(8,128)S(1)} %pick.1), channel_id=1, source_target_pairs={{0,1},{1,0},{2,3},{3,2},{4,5},{5,4},{6,7},{7,6},{8,9},{9,8},{10,11... | collective-permute-start | bytes 1769480 | tf_op jit(solution)/shard_map/ppermute | solution.py:256
  23.0 3.7 %collective-permute-start.8 = (f32[128,768]{1,0:T(8,128)S(1)}, f32[128,768]{1,0:T(8,128)S(1)}, u32[]{:S(2)}, u32[]{:S(2)}) collective-permute-start(f32[128,768]{1,0:T(8,128)S(1)} %get-tuple-element.61), channel_id=1, source_target_pairs={{0,4},{4,0},{8,12},{12,8},{1,5},{5,1},{9,13},{13,9},{2,6},{6,2},{1... | collective-permute-start | bytes 1179656 | tf_op jit(solution)/shard_map/ppermute | solution.py:259
  23.0 2.0 %collective-permute-start.6 = (f32[128,384]{1,0:T(8,128)S(1)}, f32[128,384]{1,0:T(8,128)S(1)}, u32[]{:S(2)}, u32[]{:S(2)}) collective-permute-start(f32[128,384]{1,0:T(8,128)S(1)} %get-tuple-element.53), channel_id=1, source_target_pairs={{0,4},{4,0},{8,12},{12,8},{1,5},{5,1},{9,13},{13,9},{2,6},{6,2},{1... | collective-permute-start | bytes 589832 | tf_op jit(solution)/shard_map/ppermute | solution.py:259
  25.1 9.3 %collective-permute-start.7 = (f32[64,384]{1,0:T(8,128)S(1)}, f32[64,384]{1,0:T(8,128)S(1)}, u32[]{:S(2)}, u32[]{:S(2)}) collective-permute-start(f32[64,384]{1,0:T(8,128)S(1)} %get-tuple-element.55), channel_id=1, source_target_pairs={{0,8},{4,12},{8,0},{12,4},{1,9},{5,13},{9,1},{13,5},{2,10},{6,14},... | collective-permute-start | bytes 294920 | tf_op jit(solution)/shard_map/ppermute | solution.py:259
  26.7 7.7 %collective-permute-start.9 = (f32[64,768]{1,0:T(8,128)S(1)}, f32[64,768]{1,0:T(8,128)S(1)}, u32[]{:S(2)}, u32[]{:S(2)}) collective-permute-start(f32[64,768]{1,0:T(8,128)S(1)} %get-tuple-element.63), channel_id=1, source_target_pairs={{0,8},{4,12},{8,0},{12,4},{1,9},{5,13},{9,1},{13,5},{2,10},{6,14},... | collective-permute-start | bytes 589832 | tf_op jit(solution)/shard_map/ppermute | solution.py:259
  34.9 1.5 %collective-permute-start.10 = (f32[128,384]{1,0:T(8,128)S(1)}, f32[128,384]{1,0:T(8,128)S(1)}, u32[]{:S(2)}, u32[]{:S(2)}) collective-permute-start(f32[128,384]{1,0:T(8,128)S(1)} %get-tuple-element.65), channel_id=1, source_target_pairs={{0,4},{4,0},{8,12},{12,8},{1,5},{5,1},{9,13},{13,9},{2,6},{6,2},{1... | collective-permute-start | bytes 589832 | tf_op jit(solution)/shard_map/ppermute | solution.py:259
  35.5 3.9 %collective-permute-start.13 = (f32[128,384]{1,0:T(8,128)S(1)}, f32[128,384]{1,0:T(8,128)S(1)}, u32[]{:S(2)}, u32[]{:S(2)}) collective-permute-start(f32[128,384]{1,0:T(8,128)S(1)} %get-tuple-element.71), channel_id=1, source_target_pairs={{0,4},{4,0},{8,12},{12,8},{1,5},{5,1},{9,13},{13,9},{2,6},{6,2},{1... | collective-permute-start | bytes 589832 | tf_op jit(solution)/shard_map/ppermute | solution.py:259
  36.4 5.0 %collective-permute-start.11 = (f32[64,384]{1,0:T(8,128)S(1)}, f32[64,384]{1,0:T(8,128)S(1)}, u32[]{:S(2)}, u32[]{:S(2)}) collective-permute-start(f32[64,384]{1,0:T(8,128)S(1)} %get-tuple-element.66), channel_id=1, source_target_pairs={{0,1},{1,0},{2,3},{3,2},{4,5},{5,4},{6,7},{7,6},{8,9},{9,8},{10,11... | collective-permute-start | bytes 294920 | tf_op jit(solution)/shard_map/ppermute | solution.py:300
  38.2 6.2 %collective-permute-start.12 = (f32[64,384]{1,0:T(8,128)S(1)}, f32[64,384]{1,0:T(8,128)S(1)}, u32[]{:S(2)}, u32[]{:S(2)}) collective-permute-start(f32[64,384]{1,0:T(8,128)S(1)} %get-tuple-element.67), channel_id=1, source_target_pairs={{0,9},{1,8},{2,11},{3,10},{4,13},{5,12},{6,15},{7,14},{8,1},{9,0},... | collective-permute-start | bytes 294920 | tf_op jit(solution)/shard_map/ppermute | solution.py:300
  39.5 6.4 %collective-permute-start.14 = (f32[64,384]{1,0:T(8,128)S(1)}, f32[64,384]{1,0:T(8,128)S(1)}, u32[]{:S(2)}, u32[]{:S(2)}) collective-permute-start(f32[64,384]{1,0:T(8,128)S(1)} %get-tuple-element.73), channel_id=1, source_target_pairs={{0,8},{4,12},{8,0},{12,4},{1,9},{5,13},{9,1},{13,5},{2,10},{6,14},... | collective-permute-start | bytes 294920 | tf_op jit(solution)/shard_map/ppermute | solution.py:259

commit v8 on v7

--- a/solution.py
+++ b/solution.py
@@ -251,9 +251,12 @@
     order = list(range(0, n_row, 2)) + list(range(1, n_row, 2))
 
     def swap_line(x, kind):
-        ends = [(i, i) for i in range(n_col) if not 0 <= (i + kind ^ 1) - kind < n_col]
-        inner = [(i, (i + kind ^ 1) - kind) for i in range(n_col)]
-        return lax.ppermute(x, "col", ends + [p for p in inner if 0 <= p[1] < n_col])
+        pairs_ = []
+        for i in range(n_row):
+            for j in range(n_col):
+                to = ((j + kind) ^ 1) - kind
+                pairs_.append((i * n_col + j, i * n_col + to if 0 <= to < n_col else (i ^ 1) * n_col + j))
+        return lax.ppermute(x, ("row", "col"), pairs_)
 
     def swap(x, d):
         return lax.ppermute(x, "row", [(i, i ^ d) for i in range(n_row)])
@@ -296,7 +299,7 @@
         return [pieces[0]] + [swap(pieces[i], 2 * i) for i in range(1, n_row // 2)]
 
     def next_door(x, d):
-        spots = [(i, j) for i in range(n_row) for j in range(n_col)]
+        spots = [(i, j) for i in range(n_row) for j in (1, n_col - 2)]
         return lax.ppermute(
             x, ("row", "col"), [(i * n_col + j, (i ^ d) * n_col + (j ^ 1)) for i, j in spots]
         )

time: 47.2 us -> 46.1 us (0.977)
  starting transfers between devices: 18.6 us -> 15.7 us
  waiting for transfers between devices: 19.7 us -> 21.5 us
    ppermute x4, starting transfers between devices: 10 us -> 6.46 us  [swap_line(): return lax.ppermute(x, ('row', 'col'), pairs_)]
    ppermute x2, waiting for transfers between devices: 3.92 us -> 5.1 us  [next_door(): lax.ppermute(x, ('row', 'col'), [(i * n_col + j, (i ^ d) * n_col + (j ^ 1...]
    ppermute x9, starting transfers between devices: 5.58 us -> 6.7 us  [swap(): return lax.ppermute(x, 'row', [(i, i ^ d) for i in range(n_row)])]
    ppermute x4, waiting for transfers between devices: 9.05 us -> 10.1 us  [swap_line(): return lax.ppermute(x, ('row', 'col'), pairs_)]
  transfers between devices with their start and end apart: 15 -> 15, of which waited for: 9 -> 8; matrix products, arithmetic and copies ran while one was open for 3% -> 3% of each run, Pallas kernels for 11% -> 11%
where the time goes in v8:
time: 46.1 us; the launch traced here: 45.8 us
  waiting for transfers between devices  21.5 us (47%)
  starting transfers between devices  15.7 us (34%)
  Pallas kernels  6.57 us (14%)
  local copies, waits for them, and re-layouts  1.77 us (4%)
    ppermute x4, waiting for transfers between devices, swap_line(): return lax.ppermute(x, ('row', 'col'), pairs_)  10.1 us
    ppermute x9, starting transfers between devices, swap(): return lax.ppermute(x, 'row', [(i, i ^ d) for i in range(n_row)])  6.7 us
    pallas_call x15, Pallas kernels, call(): pl.pallas_call(body, out_shape=outs, in_specs=[SMEM] * n_smem + [VMEM] *...  6.57 us
    ppermute x4, starting transfers between devices, swap_line(): return lax.ppermute(x, ('row', 'col'), pairs_)  6.46 us
    ppermute x9, waiting for transfers between devices, swap(): return lax.ppermute(x, 'row', [(i, i ^ d) for i in range(n_row)])  6.33 us
    ppermute x2, waiting for transfers between devices, next_door(): lax.ppermute(x, ('row', 'col'), [(i * n_col + j, (i ^ d) * n_col + (j ^ 1...  5.1 us
    ppermute x2, starting transfers between devices, next_door(): lax.ppermute(x, ('row', 'col'), [(i * n_col + j, (i ^ d) * n_col + (j ^ 1...  2.58 us
    dynamic_slice x1, local copies, waits for them, and re-layouts, chip_columns(): return lax.dynamic_slice_in_dim(amplitudes, start, 2 * depth, 1)  1.11 us
  transfers between devices with their start and end apart: 15, of which 8 were waited for; matrix products, arithmetic and copies ran while one was open for 3% of the time, Pallas kernels for 11%

profile of v8, /device:TPU:0, one launch (start us, length us, event | category | flops | bytes accessed | tf_op | source)
XLA Modules:
  0.0 45.8 jit_solution(4773274516795647930)
XLA Ops:
  0.0 3.0 %collective-permute-start.3 = (f32[384,384]{1,0:T(8,128)}, f32[384,384]{1,0:T(8,128)S(1)}, u32[]{:S(2)}, u32[]{:S(2)}) collective-permute-start(f32[384,384]{1,0:T(8,128)} %refs_3_.3), channel_id=1, source_target_pairs={{0,1},{1,0},{2,3},{3,2},{4,5},{5,4},{6,7},{7,6},{8,9},{9,8},{10,11... | collective-permute-start | bytes 1769480 | tf_op jit(solution)/shard_map/ppermute | solution.py:259
  3.0 1.1 %constant_dynamic-slice_fusion = (f32[64,768]{1,0:T(8,128)S(1)}, f32[64,768]{1,0:T(8,128)S(1)}) fusion(f32[64,1536]{1,0:T(8,128)} %param.5, s32[]{:T(128)S(6)} %select_n.14, s32[]{:T(128)S(6)} %select_n.13), kind=kLoop, calls=%fused_computation.2 | loop fusion | bytes 786440 | tf_op jit(solution)/shard_map/dynamic_slice | solution.py:287
  4.1 1.6 %collective-permute-start = (f32[64,768]{1,0:T(8,128)S(1)}, f32[64,768]{1,0:T(8,128)S(1)}, u32[]{:S(2)}, u32[]{:S(2)}) collective-permute-start(f32[64,768]{1,0:T(8,128)S(1)} %get-tuple-element.77), channel_id=1, source_target_pairs={{0,8},{4,12},{8,0},{12,4},{1,9},{5,13},{9,1},{13,5},{2,10},{6,14},... | collective-permute-start | bytes 589832 | tf_op jit(solution)/shard_map/ppermute | solution.py:262
  5.7 0.1 copy.6.refs_1_
  5.8 0.1 pad_add_fusion.refs_0_
  5.9 0.5 %copy-done.1 = s32[16,16]{1,0:T(8,128)S(1)} copy-done((s32[16,16]{1,0:T(8,128)S(1)}, s32[16,16]{1,0:T(8,128)}, u32[]{:S(2)}) %copy-start.1) | copy-done | bytes 1048
  6.4 2.0 %tables.1 = (f32[8,384]{1,0:T(8,128)S(1)}, f32[8,384]{1,0:T(8,128)S(1)}, f32[4,384]{1,0:T(4,128)S(1)}, f32[16,384]{1,0:T(8,128)S(1)}, f32[4,384]{1,0:T(4,128)S(1...) custom-call(s32[3]{0:T(128)S(1)} %pad_add_fusion.refs_0_, ...), custom_call_target="tpu_custom_call" | custom-call | bytes 212044 | tf_op jit(solution)/shard_map/tables/pallas_call | solution.py:226
  8.5 3.1 %collective-permute-done.refs_2_ = f32[64,768]{1,0:T(8,128)S(1)} collective-permute-done((f32[64,768]{1,0:T(8,128)S(1)}, f32[64,768]{1,0:T(8,128)S(1)}, u32[]{:S(2)}, u32[]{:S(2)}) %collective-permute-start) | collective-permute-done | bytes 196640 | tf_op jit(solution)/shard_map/ppermute | solution.py:262
  11.6 0.1 collective-permute-start.1
  11.6 1.4 %collective-permute-done.1.refs_2_ = f32[128,384]{1,0:T(8,128)S(1)} collective-permute-done((f32[128,384]{1,0:T(8,128)S(1)}, f32[128,384]{1,0:T(8,128)S(1)}, u32[]{:S(2)}, u32[]{:S(2)}) %collective-permute-start.1) | collective-permute-done | bytes 196640 | tf_op jit(solution)/shard_map/ppermute | solution.py:262
  13.1 0.6 %own.1 = (bf16[256,384]{1,0:T(8,128)(2,1)S(1)}, bf16[256,384]{1,0:T(8,128)(2,1)S(1)}, f32[384,384]{1,0:T(8,128)S(1)}, f32[128,384]{1,0:T(8,128)S(1)}, f32[128,384]{1,0:T(8,128)S(1)}) custom-call(f32[8,384]{1,0:T(8,128)S(1)} %get-tuple-element.43.refs_0_, f32[128,384]{1,0:T(8,128)S(1)} %get-tuple-element.44.refs_1_, ...), custom_call_target="tpu_custom_call" | custom-call | flops 226492416 | bytes 2377728 | tf_op jit(solution)/shard_map/own/pallas_call | solution.py:226
  13.7 2.9 %collective-permute-done.3.refs_0_.refs_2_ = f32[384,384]{1,0:T(8,128)S(1)} collective-permute-done((f32[384,384]{1,0:T(8,128)}, f32[384,384]{1,0:T(8,128)S(1)}, u32[]{:S(2)}, u32[]{:S(2)}) %collective-permute-start.3) | collective-permute-done | bytes 589856 | tf_op jit(solution)/shard_map/ppermute | solution.py:259
  16.6 0.1 collective-permute-start.5
  16.8 3.4 %collective-permute-start.4 = (f32[384,384]{1,0:T(8,128)S(1)}, f32[384,384]{1,0:T(8,128)S(1)}, u32[]{:S(2)}, u32[]{:S(2)}) collective-permute-start(f32[384,384]{1,0:T(8,128)S(1)} %pick.1), channel_id=1, source_target_pairs={{0,1},{1,0},{2,3},{3,2},{4,5},{5,4},{6,7},{7,6},{8,9},{9,8},{10,11... | collective-permute-start | bytes 1769480 | tf_op jit(solution)/shard_map/ppermute | solution.py:259
  20.1 1.0 %pair.1 = (f32[128,768]{1,0:T(8,128)S(1)}, f32[128,768]{1,0:T(8,128)S(1)}) custom-call(bf16[256,384]{1,0:T(8,128)(2,1)S(1)} %get-tuple-element.56.refs_0_, bf16[256,384]{1,0:T(8,128)(2,1)S(1)} %get-tuple-element.57.refs_1_, f32[384,384]{1,0:T(8,128)S(1)} %collective-permute-done.3.refs_0_.refs_2_, f32[4,384]{1,0:T(4,128)S(1)} %get-tuple-element.58.refs_3_, ...), custom_call_target="tpu_custom_call" | custom-call | flops 452984832 | bytes 2371584 | tf_op jit(solution)/shard_map/pair/pallas_call | solution.py:226
  21.2 0.5 %collective-permute-start.6 = (f32[128,384]{1,0:T(8,128)S(1)}, f32[128,384]{1,0:T(8,128)S(1)}, u32[]{:S(2)}, u32[]{:S(2)}) collective-permute-start(f32[128,384]{1,0:T(8,128)S(1)} %get-tuple-element.53), channel_id=1, source_target_pairs={{0,4},{4,0},{8,12},{12,8},{1,5},{5,1},{9,13},{13,9},{2,6},{6,2},{1... | collective-permute-start | bytes 589832 | tf_op jit(solution)/shard_map/ppermute | solution.py:262
  21.7 1.5 %collective-permute-done.6.refs_1_ = f32[128,384]{1,0:T(8,128)S(1)} collective-permute-done((f32[128,384]{1,0:T(8,128)S(1)}, f32[128,384]{1,0:T(8,128)S(1)}, u32[]{:S(2)}, u32[]{:S(2)}) %collective-permute-start.6) | collective-permute-done | bytes 196640 | tf_op jit(solution)/shard_map/ppermute | solution.py:262
  23.2 1.6 %collective-permute-start.7 = (f32[64,384]{1,0:T(8,128)S(1)}, f32[64,384]{1,0:T(8,128)S(1)}, u32[]{:S(2)}, u32[]{:S(2)}) collective-permute-start(f32[64,384]{1,0:T(8,128)S(1)} %get-tuple-element.55), channel_id=1, source_target_pairs={{0,8},{4,12},{8,0},{12,4},{1,9},{5,13},{9,1},{13,5},{2,10},{6,14},... | collective-permute-start | bytes 294920 | tf_op jit(solution)/shard_map/ppermute | solution.py:262
  24.8 0.6 %collective-permute-start.9 = (f32[64,768]{1,0:T(8,128)S(1)}, f32[64,768]{1,0:T(8,128)S(1)}, u32[]{:S(2)}, u32[]{:S(2)}) collective-permute-start(f32[64,768]{1,0:T(8,128)S(1)} %get-tuple-element.63), channel_id=1, source_target_pairs={{0,8},{4,12},{8,0},{12,4},{1,9},{5,13},{9,1},{13,5},{2,10},{6,14},... | collective-permute-start | bytes 589832 | tf_op jit(solution)/shard_map/ppermute | solution.py:262
  25.4 7.1 %collective-permute-done.4.refs_0_.refs_2_ = f32[384,384]{1,0:T(8,128)S(1)} collective-permute-done((f32[384,384]{1,0:T(8,128)S(1)}, f32[384,384]{1,0:T(8,128)S(1)}, u32[]{:S(2)}, u32[]{:S(2)}) %collective-permute-start.4) | collective-permute-done | bytes 589856 | tf_op jit(solution)/shard_map/ppermute | solution.py:259
  32.6 0.1 halves.1
  32.7 0.5 %corner.1 = (f32[128,384]{1,0:T(8,128)S(1)}, f32[128,384]{1,0:T(8,128)S(1)}) custom-call(bf16[384,384]{1,0:T(8,128)(2,1)S(1)} %get-tuple-element.50.refs_0_.refs_2_, bf16[384,384]{1,0:T(8,128)(2,1)S(1)} %get-tuple-element.51.refs_1_.refs_3_, f32[384,384]{1,0:T(8,128)S(1)} %collective-permute-done.4.refs_0_.refs_2_, ...), custom_call_target="tpu_custom_call" | custom-call | flops 226492416 | bytes 1572864 | tf_op jit(solution)/shard_map/corner/pallas_call | solution.py:226
  33.3 0.5 %last.1 = (f32[128,384]{1,0:T(8,128)S(1)}, f32[128,384]{1,0:T(8,128)S(1)}) custom-call(bf16[256,384]{1,0:T(8,128)(2,1)S(1)} %get-tuple-element.56.refs_0_, bf16[256,384]{1,0:T(8,128)(2,1)S(1)} %get-tuple-element.57.refs_1_, bf16[384,384]{1,0:T(8,128)(2,1)S(1)} %get-tuple-element.50.refs_0_.refs_2_, bf16[384,384]{1,0:T(8,128)(2,1)S(1)} %get-tuple-element.51.refs_1_.refs_3_, ...), custom_call_target="tpu_custom_call" | custom-call | flops 226492416 | bytes 1376256 | tf_op jit(solution)/shard_map/last/pallas_call | solution.py:226
  33.9 0.6 %collective-permute-start.13 = (f32[128,384]{1,0:T(8,128)S(1)}, f32[128,384]{1,0:T(8,128)S(1)}, u32[]{:S(2)}, u32[]{:S(2)}) collective-permute-start(f32[128,384]{1,0:T(8,128)S(1)} %get-tuple-element.71), channel_id=1, source_target_pairs={{0,4},{4,0},{8,12},{12,8},{1,5},{5,1},{9,13},{13,9},{2,6},{6,2},{1... | collective-permute-start | bytes 589832 | tf_op jit(solution)/shard_map/ppermute | solution.py:262
  34.4 0.3 collective-permute-done.10.refs_1_
  34.8 1.3 %collective-permute-start.11 = (f32[64,384]{1,0:T(8,128)S(1)}, f32[64,384]{1,0:T(8,128)S(1)}, u32[]{:S(2)}, u32[]{:S(2)}) collective-permute-start(f32[64,384]{1,0:T(8,128)S(1)} %get-tuple-element.66), channel_id=1, source_target_pairs={{1,0},{2,3},{5,4},{6,7},{9,8},{10,11},{13,12},{14,15},{17,16},{18,... | collective-permute-start | bytes 294920 | tf_op jit(solution)/shard_map/ppermute | solution.py:303
  36.1 1.3 %collective-permute-start.12 = (f32[64,384]{1,0:T(8,128)S(1)}, f32[64,384]{1,0:T(8,128)S(1)}, u32[]{:S(2)}, u32[]{:S(2)}) collective-permute-start(f32[64,384]{1,0:T(8,128)S(1)} %get-tuple-element.67), channel_id=1, source_target_pairs={{1,8},{2,11},{5,12},{6,15},{9,0},{10,3},{13,4},{14,7},{17,24},{18,... | collective-permute-start | bytes 294920 | tf_op jit(solution)/shard_map/ppermute | solution.py:303
  37.4 1.7 %collective-permute-start.14 = (f32[64,384]{1,0:T(8,128)S(1)}, f32[64,384]{1,0:T(8,128)S(1)}, u32[]{:S(2)}, u32[]{:S(2)}) collective-permute-start(f32[64,384]{1,0:T(8,128)S(1)} %get-tuple-element.73), channel_id=1, source_target_pairs={{0,8},{4,12},{8,0},{12,4},{1,9},{5,13},{9,1},{13,5},{2,10},{6,14},... | collective-permute-start | bytes 294920 | tf_op jit(solution)/shard_map/ppermute | solution.py:262
  39.2 0.5 %finish.2.refs_6_ = f32[64,1536]{1,0:T(8,128)S(1)} custom-call(f32[16,384]{1,0:T(8,128)S(1)} %get-tuple-element.74.refs_0_, f32[64,384]{1,0:T(8,128)S(1)} %get-tuple-element.54.refs_3_.refs_4_.refs_1_, f32[64,384]{1,0:T(8,128)S(1)} %collective-permute-done.7.refs_4_.refs_5_.refs_2_, f32[32,384]{1,0:T(8,128)S(1)} %pad_maximum_fusion.refs_3_, ...), custom_call_target="tpu_custom_call" | custom-call | flops 393216 | bytes 1056768 | tf_op jit(solution)/shard_map/finish/pallas_call | solution.py:226
  39.6 1.9 %collective-permute-done.11.refs_1_ = f32[64,384]{1,0:T(8,128)S(1)} collective-permute-done((f32[64,384]{1,0:T(8,128)S(1)}, f32[64,384]{1,0:T(8,128)S(1)}, u32[]{:S(2)}, u32[]{:S(2)}) %collective-permute-start.11) | collective-permute-done | bytes 98336 | tf_op jit(solution)/shard_map/ppermute | solution.py:303
  41.5 3.2 %collective-permute-done.12.refs_2_ = f32[64,384]{1,0:T(8,128)S(1)} collective-permute-done((f32[64,384]{1,0:T(8,128)S(1)}, f32[64,384]{1,0:T(8,128)S(1)}, u32[]{:S(2)}, u32[]{:S(2)}) %collective-permute-start.12) | collective-permute-done | bytes 98336 | tf_op jit(solution)/shard_map/ppermute | solution.py:303
  44.7 1.1 %finish.3 = f32[64,1536]{1,0:T(8,128)} custom-call(f32[16,384]{1,0:T(8,128)S(1)} %get-tuple-element.41.refs_0_, f32[64,384]{1,0:T(8,128)S(1)} %collective-permute-done.11.refs_1_, f32[64,384]{1,0:T(8,128)S(1)} %collective-permute-done.12.refs_2_, f32[16,384]{1,0:T(8,128)S(1)} %add.12.refs_3_, f32[64,384]{1,0:T(8,128)S(1)} %get-tuple-element.72.refs_4_, ...), custom_call_target="tpu_custom_call" | custom-call | flops 393216 | bytes 1228800 | tf_op jit(solution)/shard_map/finish/pallas_call | solution.py:226
  (26 shorter events, 0.5 us)
Async XLA Ops:
  0.0 16.6 %collective-permute-start.3 = (f32[384,384]{1,0:T(8,128)}, f32[384,384]{1,0:T(8,128)S(1)}, u32[]{:S(2)}, u32[]{:S(2)}) collective-permute-start(f32[384,384]{1,0:T(8,128)} %refs_3_.3), channel_id=1, source_target_pairs={{0,1},{1,0},{2,3},{3,2},{4,5},{5,4},{6,7},{7,6},{8,9},{9,8},{10,11... | collective-permute-start | bytes 1769480 | tf_op jit(solution)/shard_map/ppermute | solution.py:259
  3.0 13.7 %collective-permute-start.2 = (f32[384,384]{1,0:T(8,128)}, f32[384,384]{1,0:T(8,128)S(1)}, u32[]{:S(2)}, u32[]{:S(2)}) collective-permute-start(f32[384,384]{1,0:T(8,128)} %refs_3_.3), channel_id=1, source_target_pairs={{0,4},{1,2},{2,1},{3,7},{4,0},{5,6},{6,5},{7,3},{8,12},{9,10},{10,... | collective-permute-start | bytes 1769480 | tf_op jit(solution)/shard_map/ppermute | solution.py:259
  3.0 2.7 %copy-start.3 = (s32[32,16]{0,1:T(8,128)S(1)}, s32[32,16]{0,1:T(8,128)}, u32[]{:S(2)}) copy-start(s32[32,16]{0,1:T(8,128)} %param.7) | copy-start | bytes 6148
  3.0 10.0 %copy-start = (f32[384,384]{1,0:T(8,128)S(1)}, f32[384,384]{1,0:T(8,128)}, u32[]{:S(2)}) copy-start(f32[384,384]{1,0:T(8,128)} %refs_3_.3) | copy-start | bytes 1769476
  4.1 7.4 %collective-permute-start = (f32[64,768]{1,0:T(8,128)S(1)}, f32[64,768]{1,0:T(8,128)S(1)}, u32[]{:S(2)}, u32[]{:S(2)}) collective-permute-start(f32[64,768]{1,0:T(8,128)S(1)} %get-tuple-element.77), channel_id=1, source_target_pairs={{0,8},{4,12},{8,0},{12,4},{1,9},{5,13},{9,1},{13,5},{2,10},{6,14},... | collective-permute-start | bytes 589832 | tf_op jit(solution)/shard_map/ppermute | solution.py:262
  5.7 0.7 %copy-start.1 = (s32[16,16]{1,0:T(8,128)S(1)}, s32[16,16]{1,0:T(8,128)}, u32[]{:S(2)}) copy-start(s32[16,16]{1,0:T(8,128)} %refs_2_.1) | copy-start | bytes 3076
  5.8 0.7 %copy-start.2 = (s32[16]{0:T(128)S(1)}, s32[16]{0:T(128)}, u32[]{:S(2)}) copy-start(s32[16]{0:T(128)} %refs_3_.2) | copy-start | bytes 196
  11.6 1.5 %collective-permute-start.1 = (f32[128,384]{1,0:T(8,128)S(1)}, f32[128,384]{1,0:T(8,128)S(1)}, u32[]{:S(2)}, u32[]{:S(2)}) collective-permute-start(f32[128,384]{1,0:T(8,128)S(1)} %get-tuple-element.45), channel_id=1, source_target_pairs={{0,4},{4,0},{8,12},{12,8},{1,5},{5,1},{9,13},{13,9},{2,6},{6,2},{1... | collective-permute-start | bytes 589832 | tf_op jit(solution)/shard_map/ppermute | solution.py:262
  16.6 15.9 %collective-permute-start.5 = (f32[392,384]{1,0:T(8,128)S(1)}, f32[392,384]{1,0:T(8,128)S(1)}, u32[]{:S(2)}, u32[]{:S(2)}) collective-permute-start(f32[392,384]{1,0:T(8,128)S(1)} %pass.1.refs_3_), channel_id=1, source_target_pairs={{0,4},{1,2},{2,1},{3,7},{4,0},{5,6},{6,5},{7,3},{8,12},{9,10},{10,... | collective-permute-start | bytes 1806344 | tf_op jit(solution)/shard_map/ppermute | solution.py:259
  16.8 15.8 %collective-permute-start.4 = (f32[384,384]{1,0:T(8,128)S(1)}, f32[384,384]{1,0:T(8,128)S(1)}, u32[]{:S(2)}, u32[]{:S(2)}) collective-permute-start(f32[384,384]{1,0:T(8,128)S(1)} %pick.1), channel_id=1, source_target_pairs={{0,1},{1,0},{2,3},{3,2},{4,5},{5,4},{6,7},{7,6},{8,9},{9,8},{10,11... | collective-permute-start | bytes 1769480 | tf_op jit(solution)/shard_map/ppermute | solution.py:259
  21.1 3.7 %collective-permute-start.8 = (f32[128,768]{1,0:T(8,128)S(1)}, f32[128,768]{1,0:T(8,128)S(1)}, u32[]{:S(2)}, u32[]{:S(2)}) collective-permute-start(f32[128,768]{1,0:T(8,128)S(1)} %get-tuple-element.61), channel_id=1, source_target_pairs={{0,4},{4,0},{8,12},{12,8},{1,5},{5,1},{9,13},{13,9},{2,6},{6,2},{1... | collective-permute-start | bytes 1179656 | tf_op jit(solution)/shard_map/ppermute | solution.py:262
  21.2 2.0 %collective-permute-start.6 = (f32[128,384]{1,0:T(8,128)S(1)}, f32[128,384]{1,0:T(8,128)S(1)}, u32[]{:S(2)}, u32[]{:S(2)}) collective-permute-start(f32[128,384]{1,0:T(8,128)S(1)} %get-tuple-element.53), channel_id=1, source_target_pairs={{0,4},{4,0},{8,12},{12,8},{1,5},{5,1},{9,13},{13,9},{2,6},{6,2},{1... | collective-permute-start | bytes 589832 | tf_op jit(solution)/shard_map/ppermute | solution.py:262
  23.2 9.5 %collective-permute-start.7 = (f32[64,384]{1,0:T(8,128)S(1)}, f32[64,384]{1,0:T(8,128)S(1)}, u32[]{:S(2)}, u32[]{:S(2)}) collective-permute-start(f32[64,384]{1,0:T(8,128)S(1)} %get-tuple-element.55), channel_id=1, source_target_pairs={{0,8},{4,12},{8,0},{12,4},{1,9},{5,13},{9,1},{13,5},{2,10},{6,14},... | collective-permute-start | bytes 294920 | tf_op jit(solution)/shard_map/ppermute | solution.py:262
  24.8 7.9 %collective-permute-start.9 = (f32[64,768]{1,0:T(8,128)S(1)}, f32[64,768]{1,0:T(8,128)S(1)}, u32[]{:S(2)}, u32[]{:S(2)}) collective-permute-start(f32[64,768]{1,0:T(8,128)S(1)} %get-tuple-element.63), channel_id=1, source_target_pairs={{0,8},{4,12},{8,0},{12,4},{1,9},{5,13},{9,1},{13,5},{2,10},{6,14},... | collective-permute-start | bytes 589832 | tf_op jit(solution)/shard_map/ppermute | solution.py:262
  33.3 1.5 %collective-permute-start.10 = (f32[128,384]{1,0:T(8,128)S(1)}, f32[128,384]{1,0:T(8,128)S(1)}, u32[]{:S(2)}, u32[]{:S(2)}) collective-permute-start(f32[128,384]{1,0:T(8,128)S(1)} %get-tuple-element.65), channel_id=1, source_target_pairs={{0,4},{4,0},{8,12},{12,8},{1,5},{5,1},{9,13},{13,9},{2,6},{6,2},{1... | collective-permute-start | bytes 589832 | tf_op jit(solution)/shard_map/ppermute | solution.py:262
  33.9 3.5 %collective-permute-start.13 = (f32[128,384]{1,0:T(8,128)S(1)}, f32[128,384]{1,0:T(8,128)S(1)}, u32[]{:S(2)}, u32[]{:S(2)}) collective-permute-start(f32[128,384]{1,0:T(8,128)S(1)} %get-tuple-element.71), channel_id=1, source_target_pairs={{0,4},{4,0},{8,12},{12,8},{1,5},{5,1},{9,13},{13,9},{2,6},{6,2},{1... | collective-permute-start | bytes 589832 | tf_op jit(solution)/shard_map/ppermute | solution.py:262
  34.8 6.7 %collective-permute-start.11 = (f32[64,384]{1,0:T(8,128)S(1)}, f32[64,384]{1,0:T(8,128)S(1)}, u32[]{:S(2)}, u32[]{:S(2)}) collective-permute-start(f32[64,384]{1,0:T(8,128)S(1)} %get-tuple-element.66), channel_id=1, source_target_pairs={{1,0},{2,3},{5,4},{6,7},{9,8},{10,11},{13,12},{14,15},{17,16},{18,... | collective-permute-start | bytes 294920 | tf_op jit(solution)/shard_map/ppermute | solution.py:303
  36.1 8.6 %collective-permute-start.12 = (f32[64,384]{1,0:T(8,128)S(1)}, f32[64,384]{1,0:T(8,128)S(1)}, u32[]{:S(2)}, u32[]{:S(2)}) collective-permute-start(f32[64,384]{1,0:T(8,128)S(1)} %get-tuple-element.67), channel_id=1, source_target_pairs={{1,8},{2,11},{5,12},{6,15},{9,0},{10,3},{13,4},{14,7},{17,24},{18,... | collective-permute-start | bytes 294920 | tf_op jit(solution)/shard_map/ppermute | solution.py:303
  37.4 7.3 %collective-permute-start.14 = (f32[64,384]{1,0:T(8,128)S(1)}, f32[64,384]{1,0:T(8,128)S(1)}, u32[]{:S(2)}, u32[]{:S(2)}) collective-permute-start(f32[64,384]{1,0:T(8,128)S(1)} %get-tuple-element.73), channel_id=1, source_target_pairs={{0,8},{4,12},{8,0},{12,4},{1,9},{5,13},{9,1},{13,5},{2,10},{6,14},... | collective-permute-start | bytes 294920 | tf_op jit(solution)/shard_map/ppermute | solution.py:262

commit v9 on v8

--- a/solution.py
+++ b/solution.py
@@ -299,9 +299,11 @@
         return [pieces[0]] + [swap(pieces[i], 2 * i) for i in range(1, n_row // 2)]
 
     def next_door(x, d):
-        spots = [(i, j) for i in range(n_row) for j in (1, n_col - 2)]
+        spots = [(i, j, j ^ 1) for i in range(n_row) for j in range(n_col)]
         return lax.ppermute(
-            x, ("row", "col"), [(i * n_col + j, (i ^ d) * n_col + (j ^ 1)) for i, j in spots]
+            x,
+            ("row", "col"),
+            [(i * n_col + j, (i ^ (d if 0 < j < n_col - 1 else 0)) * n_col + to) for i, j, to in spots],
         )
 
     def multiply(name, *groups, after=()):

time: 46.1 us -> 44.7 us (0.970)
  waiting for transfers between devices: 21.5 us -> 20.7 us
    ppermute x2, waiting for transfers between devices: 5.1 us -> 3.89 us  [next_door(): lax.ppermute(x, ('row', 'col'), [(i * n_col + j, (i ^ (d if 0 < j < n_col...]
    ppermute x2, starting transfers between devices: 2.58 us -> 2.09 us  [next_door(): lax.ppermute(x, ('row', 'col'), [(i * n_col + j, (i ^ (d if 0 < j < n_col...]
  transfers between devices with their start and end apart: 15 -> 15, of which waited for: 8 -> 9; matrix products, arithmetic and copies ran while one was open for 3% -> 3% of each run, Pallas kernels for 11% -> 11%
where the time goes in v9:
time: 44.7 us; the launch traced here: 44.5 us
  waiting for transfers between devices  20.7 us (46%)
  starting transfers between devices  15.3 us (34%)
  Pallas kernels  6.57 us (15%)
  local copies, waits for them, and re-layouts  1.77 us (4%)
    ppermute x4, waiting for transfers between devices, swap_line(): return lax.ppermute(x, ('row', 'col'), pairs_)  10.1 us
    ppermute x9, waiting for transfers between devices, swap(): return lax.ppermute(x, 'row', [(i, i ^ d) for i in range(n_row)])  6.75 us
    ppermute x9, starting transfers between devices, swap(): return lax.ppermute(x, 'row', [(i, i ^ d) for i in range(n_row)])  6.7 us
    pallas_call x15, Pallas kernels, call(): pl.pallas_call(body, out_shape=outs, in_specs=[SMEM] * n_smem + [VMEM] *...  6.57 us
    ppermute x4, starting transfers between devices, swap_line(): return lax.ppermute(x, ('row', 'col'), pairs_)  6.46 us
    ppermute x2, waiting for transfers between devices, next_door(): lax.ppermute(x, ('row', 'col'), [(i * n_col + j, (i ^ (d if 0 < j < n_col...  3.89 us
    ppermute x2, starting transfers between devices, next_door(): lax.ppermute(x, ('row', 'col'), [(i * n_col + j, (i ^ (d if 0 < j < n_col...  2.09 us
    dynamic_slice x1, local copies, waits for them, and re-layouts, chip_columns(): return lax.dynamic_slice_in_dim(amplitudes, start, 2 * depth, 1)  1.11 us
  transfers between devices with their start and end apart: 15, of which 9 were waited for; matrix products, arithmetic and copies ran while one was open for 3% of the time, Pallas kernels for 11%

profile of v9, /device:TPU:0, one launch (start us, length us, event | category | flops | bytes accessed | tf_op | source)
XLA Modules:
  0.0 44.5 jit_solution(12309908357672764311)
XLA Ops:
  0.0 3.0 %collective-permute-start.3 = (f32[384,384]{1,0:T(8,128)}, f32[384,384]{1,0:T(8,128)S(1)}, u32[]{:S(2)}, u32[]{:S(2)}) collective-permute-start(f32[384,384]{1,0:T(8,128)} %refs_3_.3), channel_id=1, source_target_pairs={{0,1},{1,0},{2,3},{3,2},{4,5},{5,4},{6,7},{7,6},{8,9},{9,8},{10,11... | collective-permute-start | bytes 1769480 | tf_op jit(solution)/shard_map/ppermute | solution.py:259
  3.0 1.1 %constant_dynamic-slice_fusion = (f32[64,768]{1,0:T(8,128)S(1)}, f32[64,768]{1,0:T(8,128)S(1)}) fusion(f32[64,1536]{1,0:T(8,128)} %param.5, s32[]{:T(128)S(6)} %select_n.14, s32[]{:T(128)S(6)} %select_n.13), kind=kLoop, calls=%fused_computation.2 | loop fusion | bytes 786440 | tf_op jit(solution)/shard_map/dynamic_slice | solution.py:287
  4.1 1.6 %collective-permute-start = (f32[64,768]{1,0:T(8,128)S(1)}, f32[64,768]{1,0:T(8,128)S(1)}, u32[]{:S(2)}, u32[]{:S(2)}) collective-permute-start(f32[64,768]{1,0:T(8,128)S(1)} %get-tuple-element.77), channel_id=1, source_target_pairs={{0,8},{4,12},{8,0},{12,4},{1,9},{5,13},{9,1},{13,5},{2,10},{6,14},... | collective-permute-start | bytes 589832 | tf_op jit(solution)/shard_map/ppermute | solution.py:262
  5.7 0.1 copy.6.refs_1_
  5.8 0.1 pad_add_fusion.refs_0_
  5.9 0.5 %copy-done.1 = s32[16,16]{1,0:T(8,128)S(1)} copy-done((s32[16,16]{1,0:T(8,128)S(1)}, s32[16,16]{1,0:T(8,128)}, u32[]{:S(2)}) %copy-start.1) | copy-done | bytes 1048
  6.4 2.0 %tables.1 = (f32[8,384]{1,0:T(8,128)S(1)}, f32[8,384]{1,0:T(8,128)S(1)}, f32[4,384]{1,0:T(4,128)S(1)}, f32[16,384]{1,0:T(8,128)S(1)}, f32[4,384]{1,0:T(4,128)S(1...) custom-call(s32[3]{0:T(128)S(1)} %pad_add_fusion.refs_0_, ...), custom_call_target="tpu_custom_call" | custom-call | bytes 212044 | tf_op jit(solution)/shard_map/tables/pallas_call | solution.py:226
  8.5 3.1 %collective-permute-done.refs_2_ = f32[64,768]{1,0:T(8,128)S(1)} collective-permute-done((f32[64,768]{1,0:T(8,128)S(1)}, f32[64,768]{1,0:T(8,128)S(1)}, u32[]{:S(2)}, u32[]{:S(2)}) %collective-permute-start) | collective-permute-done | bytes 196640 | tf_op jit(solution)/shard_map/ppermute | solution.py:262
  11.6 1.4 %collective-permute-done.1.refs_2_ = f32[128,384]{1,0:T(8,128)S(1)} collective-permute-done((f32[128,384]{1,0:T(8,128)S(1)}, f32[128,384]{1,0:T(8,128)S(1)}, u32[]{:S(2)}, u32[]{:S(2)}) %collective-permute-start.1) | collective-permute-done | bytes 196640 | tf_op jit(solution)/shard_map/ppermute | solution.py:262
  13.1 0.6 %own.1 = (bf16[256,384]{1,0:T(8,128)(2,1)S(1)}, bf16[256,384]{1,0:T(8,128)(2,1)S(1)}, f32[384,384]{1,0:T(8,128)S(1)}, f32[128,384]{1,0:T(8,128)S(1)}, f32[128,384]{1,0:T(8,128)S(1)}) custom-call(f32[8,384]{1,0:T(8,128)S(1)} %get-tuple-element.43.refs_0_, f32[128,384]{1,0:T(8,128)S(1)} %get-tuple-element.44.refs_1_, ...), custom_call_target="tpu_custom_call" | custom-call | flops 226492416 | bytes 2377728 | tf_op jit(solution)/shard_map/own/pallas_call | solution.py:226
  13.7 2.9 %collective-permute-done.3.refs_0_.refs_2_ = f32[384,384]{1,0:T(8,128)S(1)} collective-permute-done((f32[384,384]{1,0:T(8,128)}, f32[384,384]{1,0:T(8,128)S(1)}, u32[]{:S(2)}, u32[]{:S(2)}) %collective-permute-start.3) | collective-permute-done | bytes 589856 | tf_op jit(solution)/shard_map/ppermute | solution.py:259
  16.6 0.1 collective-permute-start.5
  16.8 3.4 %collective-permute-start.4 = (f32[384,384]{1,0:T(8,128)S(1)}, f32[384,384]{1,0:T(8,128)S(1)}, u32[]{:S(2)}, u32[]{:S(2)}) collective-permute-start(f32[384,384]{1,0:T(8,128)S(1)} %pick.1), channel_id=1, source_target_pairs={{0,1},{1,0},{2,3},{3,2},{4,5},{5,4},{6,7},{7,6},{8,9},{9,8},{10,11... | collective-permute-start | bytes 1769480 | tf_op jit(solution)/shard_map/ppermute | solution.py:259
  20.1 1.0 %pair.1 = (f32[128,768]{1,0:T(8,128)S(1)}, f32[128,768]{1,0:T(8,128)S(1)}) custom-call(bf16[256,384]{1,0:T(8,128)(2,1)S(1)} %get-tuple-element.56.refs_0_, bf16[256,384]{1,0:T(8,128)(2,1)S(1)} %get-tuple-element.57.refs_1_, f32[384,384]{1,0:T(8,128)S(1)} %collective-permute-done.3.refs_0_.refs_2_, f32[4,384]{1,0:T(4,128)S(1)} %get-tuple-element.58.refs_3_, ...), custom_call_target="tpu_custom_call" | custom-call | flops 452984832 | bytes 2371584 | tf_op jit(solution)/shard_map/pair/pallas_call | solution.py:226
  21.2 0.5 %collective-permute-start.6 = (f32[128,384]{1,0:T(8,128)S(1)}, f32[128,384]{1,0:T(8,128)S(1)}, u32[]{:S(2)}, u32[]{:S(2)}) collective-permute-start(f32[128,384]{1,0:T(8,128)S(1)} %get-tuple-element.53), channel_id=1, source_target_pairs={{0,4},{4,0},{8,12},{12,8},{1,5},{5,1},{9,13},{13,9},{2,6},{6,2},{1... | collective-permute-start | bytes 589832 | tf_op jit(solution)/shard_map/ppermute | solution.py:262
  21.7 1.5 %collective-permute-done.6.refs_1_ = f32[128,384]{1,0:T(8,128)S(1)} collective-permute-done((f32[128,384]{1,0:T(8,128)S(1)}, f32[128,384]{1,0:T(8,128)S(1)}, u32[]{:S(2)}, u32[]{:S(2)}) %collective-permute-start.6) | collective-permute-done | bytes 196640 | tf_op jit(solution)/shard_map/ppermute | solution.py:262
  23.2 1.6 %collective-permute-start.7 = (f32[64,384]{1,0:T(8,128)S(1)}, f32[64,384]{1,0:T(8,128)S(1)}, u32[]{:S(2)}, u32[]{:S(2)}) collective-permute-start(f32[64,384]{1,0:T(8,128)S(1)} %get-tuple-element.55), channel_id=1, source_target_pairs={{0,8},{4,12},{8,0},{12,4},{1,9},{5,13},{9,1},{13,5},{2,10},{6,14},... | collective-permute-start | bytes 294920 | tf_op jit(solution)/shard_map/ppermute | solution.py:262
  24.8 0.6 %collective-permute-start.9 = (f32[64,768]{1,0:T(8,128)S(1)}, f32[64,768]{1,0:T(8,128)S(1)}, u32[]{:S(2)}, u32[]{:S(2)}) collective-permute-start(f32[64,768]{1,0:T(8,128)S(1)} %get-tuple-element.63), channel_id=1, source_target_pairs={{0,8},{4,12},{8,0},{12,4},{1,9},{5,13},{9,1},{13,5},{2,10},{6,14},... | collective-permute-start | bytes 589832 | tf_op jit(solution)/shard_map/ppermute | solution.py:262
  25.4 7.1 %collective-permute-done.4.refs_0_.refs_2_ = f32[384,384]{1,0:T(8,128)S(1)} collective-permute-done((f32[384,384]{1,0:T(8,128)S(1)}, f32[384,384]{1,0:T(8,128)S(1)}, u32[]{:S(2)}, u32[]{:S(2)}) %collective-permute-start.4) | collective-permute-done | bytes 589856 | tf_op jit(solution)/shard_map/ppermute | solution.py:259
  32.6 0.1 halves.1
  32.7 0.5 %corner.1 = (f32[128,384]{1,0:T(8,128)S(1)}, f32[128,384]{1,0:T(8,128)S(1)}) custom-call(bf16[384,384]{1,0:T(8,128)(2,1)S(1)} %get-tuple-element.50.refs_0_.refs_2_, bf16[384,384]{1,0:T(8,128)(2,1)S(1)} %get-tuple-element.51.refs_1_.refs_3_, f32[384,384]{1,0:T(8,128)S(1)} %collective-permute-done.4.refs_0_.refs_2_, ...), custom_call_target="tpu_custom_call" | custom-call | flops 226492416 | bytes 1572864 | tf_op jit(solution)/shard_map/corner/pallas_call | solution.py:226
  33.3 0.5 %last.1 = (f32[128,384]{1,0:T(8,128)S(1)}, f32[128,384]{1,0:T(8,128)S(1)}) custom-call(bf16[256,384]{1,0:T(8,128)(2,1)S(1)} %get-tuple-element.56.refs_0_, bf16[256,384]{1,0:T(8,128)(2,1)S(1)} %get-tuple-element.57.refs_1_, bf16[384,384]{1,0:T(8,128)(2,1)S(1)} %get-tuple-element.50.refs_0_.refs_2_, bf16[384,384]{1,0:T(8,128)(2,1)S(1)} %get-tuple-element.51.refs_1_.refs_3_, ...), custom_call_target="tpu_custom_call" | custom-call | flops 226492416 | bytes 1376256 | tf_op jit(solution)/shard_map/last/pallas_call | solution.py:226
  33.9 0.6 %collective-permute-start.13 = (f32[128,384]{1,0:T(8,128)S(1)}, f32[128,384]{1,0:T(8,128)S(1)}, u32[]{:S(2)}, u32[]{:S(2)}) collective-permute-start(f32[128,384]{1,0:T(8,128)S(1)} %get-tuple-element.71), channel_id=1, source_target_pairs={{0,4},{4,0},{8,12},{12,8},{1,5},{5,1},{9,13},{13,9},{2,6},{6,2},{1... | collective-permute-start | bytes 589832 | tf_op jit(solution)/shard_map/ppermute | solution.py:262
  34.4 0.3 collective-permute-done.10.refs_1_
  34.8 1.6 %collective-permute-start.11 = (f32[64,384]{1,0:T(8,128)S(1)}, f32[64,384]{1,0:T(8,128)S(1)}, u32[]{:S(2)}, u32[]{:S(2)}) collective-permute-start(f32[64,384]{1,0:T(8,128)S(1)} %get-tuple-element.66), channel_id=1, source_target_pairs={{0,1},{1,0},{2,3},{3,2},{4,5},{5,4},{6,7},{7,6},{8,9},{9,8},{10,11... | collective-permute-start | bytes 294920 | tf_op jit(solution)/shard_map/ppermute | solution.py:303
  36.4 0.5 %collective-permute-start.12 = (f32[64,384]{1,0:T(8,128)S(1)}, f32[64,384]{1,0:T(8,128)S(1)}, u32[]{:S(2)}, u32[]{:S(2)}) collective-permute-start(f32[64,384]{1,0:T(8,128)S(1)} %get-tuple-element.67), channel_id=1, source_target_pairs={{0,1},{1,8},{2,11},{3,2},{4,5},{5,12},{6,15},{7,6},{8,9},{9,0},{10... | collective-permute-start | bytes 294920 | tf_op jit(solution)/shard_map/ppermute | solution.py:303
  36.9 1.7 %collective-permute-start.14 = (f32[64,384]{1,0:T(8,128)S(1)}, f32[64,384]{1,0:T(8,128)S(1)}, u32[]{:S(2)}, u32[]{:S(2)}) collective-permute-start(f32[64,384]{1,0:T(8,128)S(1)} %get-tuple-element.73), channel_id=1, source_target_pairs={{0,8},{4,12},{8,0},{12,4},{1,9},{5,13},{9,1},{13,5},{2,10},{6,14},... | collective-permute-start | bytes 294920 | tf_op jit(solution)/shard_map/ppermute | solution.py:262
  38.6 0.5 %finish.2.refs_6_ = f32[64,1536]{1,0:T(8,128)S(1)} custom-call(f32[16,384]{1,0:T(8,128)S(1)} %get-tuple-element.74.refs_0_, f32[64,384]{1,0:T(8,128)S(1)} %get-tuple-element.54.refs_3_.refs_4_.refs_1_, f32[64,384]{1,0:T(8,128)S(1)} %collective-permute-done.7.refs_4_.refs_5_.refs_2_, f32[32,384]{1,0:T(8,128)S(1)} %pad_maximum_fusion.refs_3_, ...), custom_call_target="tpu_custom_call" | custom-call | flops 393216 | bytes 1056768 | tf_op jit(solution)/shard_map/finish/pallas_call | solution.py:226
  39.1 0.6 %collective-permute-done.11.refs_1_ = f32[64,384]{1,0:T(8,128)S(1)} collective-permute-done((f32[64,384]{1,0:T(8,128)S(1)}, f32[64,384]{1,0:T(8,128)S(1)}, u32[]{:S(2)}, u32[]{:S(2)}) %collective-permute-start.11) | collective-permute-done | bytes 98336 | tf_op jit(solution)/shard_map/ppermute | solution.py:303
  39.7 3.3 %collective-permute-done.12.refs_2_ = f32[64,384]{1,0:T(8,128)S(1)} collective-permute-done((f32[64,384]{1,0:T(8,128)S(1)}, f32[64,384]{1,0:T(8,128)S(1)}, u32[]{:S(2)}, u32[]{:S(2)}) %collective-permute-start.12) | collective-permute-done | bytes 98336 | tf_op jit(solution)/shard_map/ppermute | solution.py:303
  43.0 0.4 collective-permute-done.14.refs_5_
  43.4 1.1 %finish.3 = f32[64,1536]{1,0:T(8,128)} custom-call(f32[16,384]{1,0:T(8,128)S(1)} %get-tuple-element.41.refs_0_, f32[64,384]{1,0:T(8,128)S(1)} %collective-permute-done.11.refs_1_, f32[64,384]{1,0:T(8,128)S(1)} %collective-permute-done.12.refs_2_, f32[16,384]{1,0:T(8,128)S(1)} %add.12.refs_3_, f32[64,384]{1,0:T(8,128)S(1)} %get-tuple-element.72.refs_4_, ...), custom_call_target="tpu_custom_call" | custom-call | flops 393216 | bytes 1228800 | tf_op jit(solution)/shard_map/finish/pallas_call | solution.py:226
  (26 shorter events, 0.5 us)
Async XLA Ops:
  0.0 16.6 %collective-permute-start.3 = (f32[384,384]{1,0:T(8,128)}, f32[384,384]{1,0:T(8,128)S(1)}, u32[]{:S(2)}, u32[]{:S(2)}) collective-permute-start(f32[384,384]{1,0:T(8,128)} %refs_3_.3), channel_id=1, source_target_pairs={{0,1},{1,0},{2,3},{3,2},{4,5},{5,4},{6,7},{7,6},{8,9},{9,8},{10,11... | collective-permute-start | bytes 1769480 | tf_op jit(solution)/shard_map/ppermute | solution.py:259
  3.0 13.7 %collective-permute-start.2 = (f32[384,384]{1,0:T(8,128)}, f32[384,384]{1,0:T(8,128)S(1)}, u32[]{:S(2)}, u32[]{:S(2)}) collective-permute-start(f32[384,384]{1,0:T(8,128)} %refs_3_.3), channel_id=1, source_target_pairs={{0,4},{1,2},{2,1},{3,7},{4,0},{5,6},{6,5},{7,3},{8,12},{9,10},{10,... | collective-permute-start | bytes 1769480 | tf_op jit(solution)/shard_map/ppermute | solution.py:259
  3.0 2.7 %copy-start.3 = (s32[32,16]{0,1:T(8,128)S(1)}, s32[32,16]{0,1:T(8,128)}, u32[]{:S(2)}) copy-start(s32[32,16]{0,1:T(8,128)} %param.7) | copy-start | bytes 6148
  3.0 10.0 %copy-start = (f32[384,384]{1,0:T(8,128)S(1)}, f32[384,384]{1,0:T(8,128)}, u32[]{:S(2)}) copy-start(f32[384,384]{1,0:T(8,128)} %refs_3_.3) | copy-start | bytes 1769476
  4.1 7.4 %collective-permute-start = (f32[64,768]{1,0:T(8,128)S(1)}, f32[64,768]{1,0:T(8,128)S(1)}, u32[]{:S(2)}, u32[]{:S(2)}) collective-permute-start(f32[64,768]{1,0:T(8,128)S(1)} %get-tuple-element.77), channel_id=1, source_target_pairs={{0,8},{4,12},{8,0},{12,4},{1,9},{5,13},{9,1},{13,5},{2,10},{6,14},... | collective-permute-start | bytes 589832 | tf_op jit(solution)/shard_map/ppermute | solution.py:262
  5.7 0.7 %copy-start.1 = (s32[16,16]{1,0:T(8,128)S(1)}, s32[16,16]{1,0:T(8,128)}, u32[]{:S(2)}) copy-start(s32[16,16]{1,0:T(8,128)} %refs_2_.1) | copy-start | bytes 3076
  5.8 0.7 %copy-start.2 = (s32[16]{0:T(128)S(1)}, s32[16]{0:T(128)}, u32[]{:S(2)}) copy-start(s32[16]{0:T(128)} %refs_3_.2) | copy-start | bytes 196
  11.6 1.5 %collective-permute-start.1 = (f32[128,384]{1,0:T(8,128)S(1)}, f32[128,384]{1,0:T(8,128)S(1)}, u32[]{:S(2)}, u32[]{:S(2)}) collective-permute-start(f32[128,384]{1,0:T(8,128)S(1)} %get-tuple-element.45), channel_id=1, source_target_pairs={{0,4},{4,0},{8,12},{12,8},{1,5},{5,1},{9,13},{13,9},{2,6},{6,2},{1... | collective-permute-start | bytes 589832 | tf_op jit(solution)/shard_map/ppermute | solution.py:262
  16.6 15.9 %collective-permute-start.5 = (f32[392,384]{1,0:T(8,128)S(1)}, f32[392,384]{1,0:T(8,128)S(1)}, u32[]{:S(2)}, u32[]{:S(2)}) collective-permute-start(f32[392,384]{1,0:T(8,128)S(1)} %pass.1.refs_3_), channel_id=1, source_target_pairs={{0,4},{1,2},{2,1},{3,7},{4,0},{5,6},{6,5},{7,3},{8,12},{9,10},{10,... | collective-permute-start | bytes 1806344 | tf_op jit(solution)/shard_map/ppermute | solution.py:259
  16.8 15.8 %collective-permute-start.4 = (f32[384,384]{1,0:T(8,128)S(1)}, f32[384,384]{1,0:T(8,128)S(1)}, u32[]{:S(2)}, u32[]{:S(2)}) collective-permute-start(f32[384,384]{1,0:T(8,128)S(1)} %pick.1), channel_id=1, source_target_pairs={{0,1},{1,0},{2,3},{3,2},{4,5},{5,4},{6,7},{7,6},{8,9},{9,8},{10,11... | collective-permute-start | bytes 1769480 | tf_op jit(solution)/shard_map/ppermute | solution.py:259
  21.1 3.7 %collective-permute-start.8 = (f32[128,768]{1,0:T(8,128)S(1)}, f32[128,768]{1,0:T(8,128)S(1)}, u32[]{:S(2)}, u32[]{:S(2)}) collective-permute-start(f32[128,768]{1,0:T(8,128)S(1)} %get-tuple-element.61), channel_id=1, source_target_pairs={{0,4},{4,0},{8,12},{12,8},{1,5},{5,1},{9,13},{13,9},{2,6},{6,2},{1... | collective-permute-start | bytes 1179656 | tf_op jit(solution)/shard_map/ppermute | solution.py:262
  21.2 2.0 %collective-permute-start.6 = (f32[128,384]{1,0:T(8,128)S(1)}, f32[128,384]{1,0:T(8,128)S(1)}, u32[]{:S(2)}, u32[]{:S(2)}) collective-permute-start(f32[128,384]{1,0:T(8,128)S(1)} %get-tuple-element.53), channel_id=1, source_target_pairs={{0,4},{4,0},{8,12},{12,8},{1,5},{5,1},{9,13},{13,9},{2,6},{6,2},{1... | collective-permute-start | bytes 589832 | tf_op jit(solution)/shard_map/ppermute | solution.py:262
  23.2 9.5 %collective-permute-start.7 = (f32[64,384]{1,0:T(8,128)S(1)}, f32[64,384]{1,0:T(8,128)S(1)}, u32[]{:S(2)}, u32[]{:S(2)}) collective-permute-start(f32[64,384]{1,0:T(8,128)S(1)} %get-tuple-element.55), channel_id=1, source_target_pairs={{0,8},{4,12},{8,0},{12,4},{1,9},{5,13},{9,1},{13,5},{2,10},{6,14},... | collective-permute-start | bytes 294920 | tf_op jit(solution)/shard_map/ppermute | solution.py:262
  24.8 7.9 %collective-permute-start.9 = (f32[64,768]{1,0:T(8,128)S(1)}, f32[64,768]{1,0:T(8,128)S(1)}, u32[]{:S(2)}, u32[]{:S(2)}) collective-permute-start(f32[64,768]{1,0:T(8,128)S(1)} %get-tuple-element.63), channel_id=1, source_target_pairs={{0,8},{4,12},{8,0},{12,4},{1,9},{5,13},{9,1},{13,5},{2,10},{6,14},... | collective-permute-start | bytes 589832 | tf_op jit(solution)/shard_map/ppermute | solution.py:262
  33.3 1.5 %collective-permute-start.10 = (f32[128,384]{1,0:T(8,128)S(1)}, f32[128,384]{1,0:T(8,128)S(1)}, u32[]{:S(2)}, u32[]{:S(2)}) collective-permute-start(f32[128,384]{1,0:T(8,128)S(1)} %get-tuple-element.65), channel_id=1, source_target_pairs={{0,4},{4,0},{8,12},{12,8},{1,5},{5,1},{9,13},{13,9},{2,6},{6,2},{1... | collective-permute-start | bytes 589832 | tf_op jit(solution)/shard_map/ppermute | solution.py:262
  33.9 3.0 %collective-permute-start.13 = (f32[128,384]{1,0:T(8,128)S(1)}, f32[128,384]{1,0:T(8,128)S(1)}, u32[]{:S(2)}, u32[]{:S(2)}) collective-permute-start(f32[128,384]{1,0:T(8,128)S(1)} %get-tuple-element.71), channel_id=1, source_target_pairs={{0,4},{4,0},{8,12},{12,8},{1,5},{5,1},{9,13},{13,9},{2,6},{6,2},{1... | collective-permute-start | bytes 589832 | tf_op jit(solution)/shard_map/ppermute | solution.py:262
  34.8 4.9 %collective-permute-start.11 = (f32[64,384]{1,0:T(8,128)S(1)}, f32[64,384]{1,0:T(8,128)S(1)}, u32[]{:S(2)}, u32[]{:S(2)}) collective-permute-start(f32[64,384]{1,0:T(8,128)S(1)} %get-tuple-element.66), channel_id=1, source_target_pairs={{0,1},{1,0},{2,3},{3,2},{4,5},{5,4},{6,7},{7,6},{8,9},{9,8},{10,11... | collective-permute-start | bytes 294920 | tf_op jit(solution)/shard_map/ppermute | solution.py:303
  36.4 6.6 %collective-permute-start.12 = (f32[64,384]{1,0:T(8,128)S(1)}, f32[64,384]{1,0:T(8,128)S(1)}, u32[]{:S(2)}, u32[]{:S(2)}) collective-permute-start(f32[64,384]{1,0:T(8,128)S(1)} %get-tuple-element.67), channel_id=1, source_target_pairs={{0,1},{1,8},{2,11},{3,2},{4,5},{5,12},{6,15},{7,6},{8,9},{9,0},{10... | collective-permute-start | bytes 294920 | tf_op jit(solution)/shard_map/ppermute | solution.py:303
  36.9 6.5 %collective-permute-start.14 = (f32[64,384]{1,0:T(8,128)S(1)}, f32[64,384]{1,0:T(8,128)S(1)}, u32[]{:S(2)}, u32[]{:S(2)}) collective-permute-start(f32[64,384]{1,0:T(8,128)S(1)} %get-tuple-element.73), channel_id=1, source_target_pairs={{0,8},{4,12},{8,0},{12,4},{1,9},{5,13},{9,1},{13,5},{2,10},{6,14},... | collective-permute-start | bytes 294920 | tf_op jit(solution)/shard_map/ppermute | solution.py:262

commit v10 on v9

--- a/solution.py
+++ b/solution.py
@@ -397,7 +397,8 @@
         slots = []
         if corner:
             parts = call(corner_kernel, "corner", sums, 0, *b_halves, end_slab, flops=flops, after=after)
-            slots.append(([[ends]], [next_door(x, 2 * i) for i, x in enumerate(fold(*parts))]))
+            pieces = list(enumerate(fold(*parts)))
+            slots.append(([[ends]], [next_door(x, 2 * i) for i, x in reversed(pieces)]))
         parts = call(last_kernel, "last", sums, 0, high, low, *b_halves, flops=flops, after=after)
         slots.append(([[(EVEN, step), (ODD, step)]], exchange(*parts)))
     return finish(slots, out)

time: 44.7 us -> 44.2 us (0.989)
    ppermute x9, starting transfers between devices: 6.7 us -> 5.41 us  [swap(): return lax.ppermute(x, 'row', [(i, i ^ d) for i in range(n_row)])]
    ppermute x2, starting transfers between devices: 2.09 us -> 3.17 us  [next_door(): lax.ppermute(x, ('row', 'col'), [(i * n_col + j, (i ^ (d if 0 < j < n_col...]
  transfers between devices with their start and end apart: 15 -> 15, of which waited for: 9 -> 8; matrix products, arithmetic and copies ran while one was open for 3% -> 3% of each run, Pallas kernels for 11% -> 11%
where the time goes in v10:
time: 44.2 us; the launch traced here: 44 us
  waiting for transfers between devices  20.4 us (46%)
  starting transfers between devices  15 us (34%)
  Pallas kernels  6.57 us (15%)
  local copies, waits for them, and re-layouts  1.77 us (4%)
    ppermute x4, waiting for transfers between devices, swap_line(): return lax.ppermute(x, ('row', 'col'), pairs_)  10.1 us
    pallas_call x15, Pallas kernels, call(): pl.pallas_call(body, out_shape=outs, in_specs=[SMEM] * n_smem + [VMEM] *...  6.57 us
    ppermute x4, starting transfers between devices, swap_line(): return lax.ppermute(x, ('row', 'col'), pairs_)  6.46 us
    ppermute x9, waiting for transfers between devices, swap(): return lax.ppermute(x, 'row', [(i, i ^ d) for i in range(n_row)])  6.35 us
    ppermute x9, starting transfers between devices, swap(): return lax.ppermute(x, 'row', [(i, i ^ d) for i in range(n_row)])  5.41 us
    ppermute x2, waiting for transfers between devices, next_door(): lax.ppermute(x, ('row', 'col'), [(i * n_col + j, (i ^ (d if 0 < j < n_col...  3.98 us
    ppermute x2, starting transfers between devices, next_door(): lax.ppermute(x, ('row', 'col'), [(i * n_col + j, (i ^ (d if 0 < j < n_col...  3.17 us
    dynamic_slice x1, local copies, waits for them, and re-layouts, chip_columns(): return lax.dynamic_slice_in_dim(amplitudes, start, 2 * depth, 1)  1.11 us
  transfers between devices with their start and end apart: 15, of which 8 were waited for; matrix products, arithmetic and copies ran while one was open for 3% of the time, Pallas kernels for 11%

profile of v10, /device:TPU:0, one launch (start us, length us, event | category | flops | bytes accessed | tf_op | source)
XLA Modules:
  0.0 44.0 jit_solution(6266527289698411799)
XLA Ops:
  0.0 3.0 %collective-permute-start.3 = (f32[384,384]{1,0:T(8,128)}, f32[384,384]{1,0:T(8,128)S(1)}, u32[]{:S(2)}, u32[]{:S(2)}) collective-permute-start(f32[384,384]{1,0:T(8,128)} %refs_3_.3), channel_id=1, source_target_pairs={{0,1},{1,0},{2,3},{3,2},{4,5},{5,4},{6,7},{7,6},{8,9},{9,8},{10,11... | collective-permute-start | bytes 1769480 | tf_op jit(solution)/shard_map/ppermute | solution.py:259
  3.0 1.1 %constant_dynamic-slice_fusion = (f32[64,768]{1,0:T(8,128)S(1)}, f32[64,768]{1,0:T(8,128)S(1)}) fusion(f32[64,1536]{1,0:T(8,128)} %param.5, s32[]{:T(128)S(6)} %select_n.14, s32[]{:T(128)S(6)} %select_n.13), kind=kLoop, calls=%fused_computation.2 | loop fusion | bytes 786440 | tf_op jit(solution)/shard_map/dynamic_slice | solution.py:287
  4.1 1.6 %collective-permute-start = (f32[64,768]{1,0:T(8,128)S(1)}, f32[64,768]{1,0:T(8,128)S(1)}, u32[]{:S(2)}, u32[]{:S(2)}) collective-permute-start(f32[64,768]{1,0:T(8,128)S(1)} %get-tuple-element.77), channel_id=1, source_target_pairs={{0,8},{4,12},{8,0},{12,4},{1,9},{5,13},{9,1},{13,5},{2,10},{6,14},... | collective-permute-start | bytes 589832 | tf_op jit(solution)/shard_map/ppermute | solution.py:262
  5.7 0.1 copy.6.refs_1_
  5.8 0.1 pad_add_fusion.refs_0_
  5.9 0.5 %copy-done.1 = s32[16,16]{1,0:T(8,128)S(1)} copy-done((s32[16,16]{1,0:T(8,128)S(1)}, s32[16,16]{1,0:T(8,128)}, u32[]{:S(2)}) %copy-start.1) | copy-done | bytes 1048
  6.4 2.0 %tables.1 = (f32[8,384]{1,0:T(8,128)S(1)}, f32[8,384]{1,0:T(8,128)S(1)}, f32[4,384]{1,0:T(4,128)S(1)}, f32[16,384]{1,0:T(8,128)S(1)}, f32[4,384]{1,0:T(4,128)S(1...) custom-call(s32[3]{0:T(128)S(1)} %pad_add_fusion.refs_0_, ...), custom_call_target="tpu_custom_call" | custom-call | bytes 212044 | tf_op jit(solution)/shard_map/tables/pallas_call | solution.py:226
  8.5 3.1 %collective-permute-done.refs_2_ = f32[64,768]{1,0:T(8,128)S(1)} collective-permute-done((f32[64,768]{1,0:T(8,128)S(1)}, f32[64,768]{1,0:T(8,128)S(1)}, u32[]{:S(2)}, u32[]{:S(2)}) %collective-permute-start) | collective-permute-done | bytes 196640 | tf_op jit(solution)/shard_map/ppermute | solution.py:262
  11.6 0.1 collective-permute-start.1
  11.6 1.4 %collective-permute-done.1.refs_2_ = f32[128,384]{1,0:T(8,128)S(1)} collective-permute-done((f32[128,384]{1,0:T(8,128)S(1)}, f32[128,384]{1,0:T(8,128)S(1)}, u32[]{:S(2)}, u32[]{:S(2)}) %collective-permute-start.1) | collective-permute-done | bytes 196640 | tf_op jit(solution)/shard_map/ppermute | solution.py:262
  13.1 0.6 %own.1 = (bf16[256,384]{1,0:T(8,128)(2,1)S(1)}, bf16[256,384]{1,0:T(8,128)(2,1)S(1)}, f32[384,384]{1,0:T(8,128)S(1)}, f32[128,384]{1,0:T(8,128)S(1)}, f32[128,384]{1,0:T(8,128)S(1)}) custom-call(f32[8,384]{1,0:T(8,128)S(1)} %get-tuple-element.43.refs_0_, f32[128,384]{1,0:T(8,128)S(1)} %get-tuple-element.44.refs_1_, ...), custom_call_target="tpu_custom_call" | custom-call | flops 226492416 | bytes 2377728 | tf_op jit(solution)/shard_map/own/pallas_call | solution.py:226
  13.7 2.9 %collective-permute-done.3.refs_0_.refs_2_ = f32[384,384]{1,0:T(8,128)S(1)} collective-permute-done((f32[384,384]{1,0:T(8,128)}, f32[384,384]{1,0:T(8,128)S(1)}, u32[]{:S(2)}, u32[]{:S(2)}) %collective-permute-start.3) | collective-permute-done | bytes 589856 | tf_op jit(solution)/shard_map/ppermute | solution.py:259
  16.6 0.1 collective-permute-start.5
  16.8 3.4 %collective-permute-start.4 = (f32[384,384]{1,0:T(8,128)S(1)}, f32[384,384]{1,0:T(8,128)S(1)}, u32[]{:S(2)}, u32[]{:S(2)}) collective-permute-start(f32[384,384]{1,0:T(8,128)S(1)} %pick.1), channel_id=1, source_target_pairs={{0,1},{1,0},{2,3},{3,2},{4,5},{5,4},{6,7},{7,6},{8,9},{9,8},{10,11... | collective-permute-start | bytes 1769480 | tf_op jit(solution)/shard_map/ppermute | solution.py:259
  20.1 1.0 %pair.1 = (f32[128,768]{1,0:T(8,128)S(1)}, f32[128,768]{1,0:T(8,128)S(1)}) custom-call(bf16[256,384]{1,0:T(8,128)(2,1)S(1)} %get-tuple-element.56.refs_0_, bf16[256,384]{1,0:T(8,128)(2,1)S(1)} %get-tuple-element.57.refs_1_, f32[384,384]{1,0:T(8,128)S(1)} %collective-permute-done.3.refs_0_.refs_2_, f32[4,384]{1,0:T(4,128)S(1)} %get-tuple-element.58.refs_3_, ...), custom_call_target="tpu_custom_call" | custom-call | flops 452984832 | bytes 2371584 | tf_op jit(solution)/shard_map/pair/pallas_call | solution.py:226
  21.2 0.5 %collective-permute-start.6 = (f32[128,384]{1,0:T(8,128)S(1)}, f32[128,384]{1,0:T(8,128)S(1)}, u32[]{:S(2)}, u32[]{:S(2)}) collective-permute-start(f32[128,384]{1,0:T(8,128)S(1)} %get-tuple-element.53), channel_id=1, source_target_pairs={{0,4},{4,0},{8,12},{12,8},{1,5},{5,1},{9,13},{13,9},{2,6},{6,2},{1... | collective-permute-start | bytes 589832 | tf_op jit(solution)/shard_map/ppermute | solution.py:262
  21.7 1.5 %collective-permute-done.6.refs_1_ = f32[128,384]{1,0:T(8,128)S(1)} collective-permute-done((f32[128,384]{1,0:T(8,128)S(1)}, f32[128,384]{1,0:T(8,128)S(1)}, u32[]{:S(2)}, u32[]{:S(2)}) %collective-permute-start.6) | collective-permute-done | bytes 196640 | tf_op jit(solution)/shard_map/ppermute | solution.py:262
  23.2 1.6 %collective-permute-start.7 = (f32[64,384]{1,0:T(8,128)S(1)}, f32[64,384]{1,0:T(8,128)S(1)}, u32[]{:S(2)}, u32[]{:S(2)}) collective-permute-start(f32[64,384]{1,0:T(8,128)S(1)} %get-tuple-element.55), channel_id=1, source_target_pairs={{0,8},{4,12},{8,0},{12,4},{1,9},{5,13},{9,1},{13,5},{2,10},{6,14},... | collective-permute-start | bytes 294920 | tf_op jit(solution)/shard_map/ppermute | solution.py:262
  24.8 0.6 %collective-permute-start.9 = (f32[64,768]{1,0:T(8,128)S(1)}, f32[64,768]{1,0:T(8,128)S(1)}, u32[]{:S(2)}, u32[]{:S(2)}) collective-permute-start(f32[64,768]{1,0:T(8,128)S(1)} %get-tuple-element.63), channel_id=1, source_target_pairs={{0,8},{4,12},{8,0},{12,4},{1,9},{5,13},{9,1},{13,5},{2,10},{6,14},... | collective-permute-start | bytes 589832 | tf_op jit(solution)/shard_map/ppermute | solution.py:262
  25.4 7.1 %collective-permute-done.4.refs_0_.refs_2_ = f32[384,384]{1,0:T(8,128)S(1)} collective-permute-done((f32[384,384]{1,0:T(8,128)S(1)}, f32[384,384]{1,0:T(8,128)S(1)}, u32[]{:S(2)}, u32[]{:S(2)}) %collective-permute-start.4) | collective-permute-done | bytes 589856 | tf_op jit(solution)/shard_map/ppermute | solution.py:259
  32.6 0.1 halves.1
  32.7 0.5 %corner.1 = (f32[128,384]{1,0:T(8,128)S(1)}, f32[128,384]{1,0:T(8,128)S(1)}) custom-call(bf16[384,384]{1,0:T(8,128)(2,1)S(1)} %get-tuple-element.50.refs_0_.refs_2_, bf16[384,384]{1,0:T(8,128)(2,1)S(1)} %get-tuple-element.51.refs_1_.refs_3_, f32[384,384]{1,0:T(8,128)S(1)} %collective-permute-done.4.refs_0_.refs_2_, ...), custom_call_target="tpu_custom_call" | custom-call | flops 226492416 | bytes 1572864 | tf_op jit(solution)/shard_map/corner/pallas_call | solution.py:226
  33.3 0.5 %last.1 = (f32[128,384]{1,0:T(8,128)S(1)}, f32[128,384]{1,0:T(8,128)S(1)}) custom-call(bf16[256,384]{1,0:T(8,128)(2,1)S(1)} %get-tuple-element.56.refs_0_, bf16[256,384]{1,0:T(8,128)(2,1)S(1)} %get-tuple-element.57.refs_1_, bf16[384,384]{1,0:T(8,128)(2,1)S(1)} %get-tuple-element.50.refs_0_.refs_2_, bf16[384,384]{1,0:T(8,128)(2,1)S(1)} %get-tuple-element.51.refs_1_.refs_3_, ...), custom_call_target="tpu_custom_call" | custom-call | flops 226492416 | bytes 1376256 | tf_op jit(solution)/shard_map/last/pallas_call | solution.py:226
  33.9 0.6 %collective-permute-start.13 = (f32[128,384]{1,0:T(8,128)S(1)}, f32[128,384]{1,0:T(8,128)S(1)}, u32[]{:S(2)}, u32[]{:S(2)}) collective-permute-start(f32[128,384]{1,0:T(8,128)S(1)} %get-tuple-element.71), channel_id=1, source_target_pairs={{0,4},{4,0},{8,12},{12,8},{1,5},{5,1},{9,13},{13,9},{2,6},{6,2},{1... | collective-permute-start | bytes 589832 | tf_op jit(solution)/shard_map/ppermute | solution.py:262
  34.4 0.3 collective-permute-done.10.refs_1_
  34.8 1.5 %collective-permute-start.11 = (f32[64,384]{1,0:T(8,128)S(1)}, f32[64,384]{1,0:T(8,128)S(1)}, u32[]{:S(2)}, u32[]{:S(2)}) collective-permute-start(f32[64,384]{1,0:T(8,128)S(1)} %get-tuple-element.66), channel_id=1, source_target_pairs={{0,1},{1,8},{2,11},{3,2},{4,5},{5,12},{6,15},{7,6},{8,9},{9,0},{10... | collective-permute-start | bytes 294920 | tf_op jit(solution)/shard_map/ppermute | solution.py:303
  36.3 1.6 %collective-permute-start.12 = (f32[64,384]{1,0:T(8,128)S(1)}, f32[64,384]{1,0:T(8,128)S(1)}, u32[]{:S(2)}, u32[]{:S(2)}) collective-permute-start(f32[64,384]{1,0:T(8,128)S(1)} %get-tuple-element.67), channel_id=1, source_target_pairs={{0,1},{1,0},{2,3},{3,2},{4,5},{5,4},{6,7},{7,6},{8,9},{9,8},{10,11... | collective-permute-start | bytes 294920 | tf_op jit(solution)/shard_map/ppermute | solution.py:303
  38.0 0.4 collective-permute-start.14
  38.4 0.5 %finish.2.refs_6_ = f32[64,1536]{1,0:T(8,128)S(1)} custom-call(f32[16,384]{1,0:T(8,128)S(1)} %get-tuple-element.74.refs_0_, f32[64,384]{1,0:T(8,128)S(1)} %get-tuple-element.54.refs_3_.refs_4_.refs_1_, f32[64,384]{1,0:T(8,128)S(1)} %collective-permute-done.7.refs_4_.refs_5_.refs_2_, f32[32,384]{1,0:T(8,128)S(1)} %pad_maximum_fusion.refs_3_, ...), custom_call_target="tpu_custom_call" | custom-call | flops 393216 | bytes 1056768 | tf_op jit(solution)/shard_map/finish/pallas_call | solution.py:226
  38.9 2.5 %collective-permute-done.11.refs_1_ = f32[64,384]{1,0:T(8,128)S(1)} collective-permute-done((f32[64,384]{1,0:T(8,128)S(1)}, f32[64,384]{1,0:T(8,128)S(1)}, u32[]{:S(2)}, u32[]{:S(2)}) %collective-permute-start.11) | collective-permute-done | bytes 98336 | tf_op jit(solution)/shard_map/ppermute | solution.py:303
  41.4 1.5 %collective-permute-done.12.refs_2_ = f32[64,384]{1,0:T(8,128)S(1)} collective-permute-done((f32[64,384]{1,0:T(8,128)S(1)}, f32[64,384]{1,0:T(8,128)S(1)}, u32[]{:S(2)}, u32[]{:S(2)}) %collective-permute-start.12) | collective-permute-done | bytes 98336 | tf_op jit(solution)/shard_map/ppermute | solution.py:303
  42.9 1.1 %finish.3 = f32[64,1536]{1,0:T(8,128)} custom-call(f32[16,384]{1,0:T(8,128)S(1)} %get-tuple-element.41.refs_0_, f32[64,384]{1,0:T(8,128)S(1)} %collective-permute-done.11.refs_1_, f32[64,384]{1,0:T(8,128)S(1)} %collective-permute-done.12.refs_2_, f32[16,384]{1,0:T(8,128)S(1)} %add.12.refs_3_, f32[64,384]{1,0:T(8,128)S(1)} %get-tuple-element.72.refs_4_, ...), custom_call_target="tpu_custom_call" | custom-call | flops 393216 | bytes 1228800 | tf_op jit(solution)/shard_map/finish/pallas_call | solution.py:226
  (26 shorter events, 0.5 us)
Async XLA Ops:
  0.0 16.6 %collective-permute-start.3 = (f32[384,384]{1,0:T(8,128)}, f32[384,384]{1,0:T(8,128)S(1)}, u32[]{:S(2)}, u32[]{:S(2)}) collective-permute-start(f32[384,384]{1,0:T(8,128)} %refs_3_.3), channel_id=1, source_target_pairs={{0,1},{1,0},{2,3},{3,2},{4,5},{5,4},{6,7},{7,6},{8,9},{9,8},{10,11... | collective-permute-start | bytes 1769480 | tf_op jit(solution)/shard_map/ppermute | solution.py:259
  3.0 13.7 %collective-permute-start.2 = (f32[384,384]{1,0:T(8,128)}, f32[384,384]{1,0:T(8,128)S(1)}, u32[]{:S(2)}, u32[]{:S(2)}) collective-permute-start(f32[384,384]{1,0:T(8,128)} %refs_3_.3), channel_id=1, source_target_pairs={{0,4},{1,2},{2,1},{3,7},{4,0},{5,6},{6,5},{7,3},{8,12},{9,10},{10,... | collective-permute-start | bytes 1769480 | tf_op jit(solution)/shard_map/ppermute | solution.py:259
  3.0 2.7 %copy-start.3 = (s32[32,16]{0,1:T(8,128)S(1)}, s32[32,16]{0,1:T(8,128)}, u32[]{:S(2)}) copy-start(s32[32,16]{0,1:T(8,128)} %param.7) | copy-start | bytes 6148
  3.0 10.0 %copy-start = (f32[384,384]{1,0:T(8,128)S(1)}, f32[384,384]{1,0:T(8,128)}, u32[]{:S(2)}) copy-start(f32[384,384]{1,0:T(8,128)} %refs_3_.3) | copy-start | bytes 1769476
  4.1 7.4 %collective-permute-start = (f32[64,768]{1,0:T(8,128)S(1)}, f32[64,768]{1,0:T(8,128)S(1)}, u32[]{:S(2)}, u32[]{:S(2)}) collective-permute-start(f32[64,768]{1,0:T(8,128)S(1)} %get-tuple-element.77), channel_id=1, source_target_pairs={{0,8},{4,12},{8,0},{12,4},{1,9},{5,13},{9,1},{13,5},{2,10},{6,14},... | collective-permute-start | bytes 589832 | tf_op jit(solution)/shard_map/ppermute | solution.py:262
  5.7 0.7 %copy-start.1 = (s32[16,16]{1,0:T(8,128)S(1)}, s32[16,16]{1,0:T(8,128)}, u32[]{:S(2)}) copy-start(s32[16,16]{1,0:T(8,128)} %refs_2_.1) | copy-start | bytes 3076
  5.8 0.7 %copy-start.2 = (s32[16]{0:T(128)S(1)}, s32[16]{0:T(128)}, u32[]{:S(2)}) copy-start(s32[16]{0:T(128)} %refs_3_.2) | copy-start | bytes 196
  11.6 1.5 %collective-permute-start.1 = (f32[128,384]{1,0:T(8,128)S(1)}, f32[128,384]{1,0:T(8,128)S(1)}, u32[]{:S(2)}, u32[]{:S(2)}) collective-permute-start(f32[128,384]{1,0:T(8,128)S(1)} %get-tuple-element.45), channel_id=1, source_target_pairs={{0,4},{4,0},{8,12},{12,8},{1,5},{5,1},{9,13},{13,9},{2,6},{6,2},{1... | collective-permute-start | bytes 589832 | tf_op jit(solution)/shard_map/ppermute | solution.py:262
  16.6 15.9 %collective-permute-start.5 = (f32[392,384]{1,0:T(8,128)S(1)}, f32[392,384]{1,0:T(8,128)S(1)}, u32[]{:S(2)}, u32[]{:S(2)}) collective-permute-start(f32[392,384]{1,0:T(8,128)S(1)} %pass.1.refs_3_), channel_id=1, source_target_pairs={{0,4},{1,2},{2,1},{3,7},{4,0},{5,6},{6,5},{7,3},{8,12},{9,10},{10,... | collective-permute-start | bytes 1806344 | tf_op jit(solution)/shard_map/ppermute | solution.py:259
  16.8 15.8 %collective-permute-start.4 = (f32[384,384]{1,0:T(8,128)S(1)}, f32[384,384]{1,0:T(8,128)S(1)}, u32[]{:S(2)}, u32[]{:S(2)}) collective-permute-start(f32[384,384]{1,0:T(8,128)S(1)} %pick.1), channel_id=1, source_target_pairs={{0,1},{1,0},{2,3},{3,2},{4,5},{5,4},{6,7},{7,6},{8,9},{9,8},{10,11... | collective-permute-start | bytes 1769480 | tf_op jit(solution)/shard_map/ppermute | solution.py:259
  21.1 3.7 %collective-permute-start.8 = (f32[128,768]{1,0:T(8,128)S(1)}, f32[128,768]{1,0:T(8,128)S(1)}, u32[]{:S(2)}, u32[]{:S(2)}) collective-permute-start(f32[128,768]{1,0:T(8,128)S(1)} %get-tuple-element.61), channel_id=1, source_target_pairs={{0,4},{4,0},{8,12},{12,8},{1,5},{5,1},{9,13},{13,9},{2,6},{6,2},{1... | collective-permute-start | bytes 1179656 | tf_op jit(solution)/shard_map/ppermute | solution.py:262
  21.2 2.0 %collective-permute-start.6 = (f32[128,384]{1,0:T(8,128)S(1)}, f32[128,384]{1,0:T(8,128)S(1)}, u32[]{:S(2)}, u32[]{:S(2)}) collective-permute-start(f32[128,384]{1,0:T(8,128)S(1)} %get-tuple-element.53), channel_id=1, source_target_pairs={{0,4},{4,0},{8,12},{12,8},{1,5},{5,1},{9,13},{13,9},{2,6},{6,2},{1... | collective-permute-start | bytes 589832 | tf_op jit(solution)/shard_map/ppermute | solution.py:262
  23.2 9.5 %collective-permute-start.7 = (f32[64,384]{1,0:T(8,128)S(1)}, f32[64,384]{1,0:T(8,128)S(1)}, u32[]{:S(2)}, u32[]{:S(2)}) collective-permute-start(f32[64,384]{1,0:T(8,128)S(1)} %get-tuple-element.55), channel_id=1, source_target_pairs={{0,8},{4,12},{8,0},{12,4},{1,9},{5,13},{9,1},{13,5},{2,10},{6,14},... | collective-permute-start | bytes 294920 | tf_op jit(solution)/shard_map/ppermute | solution.py:262
  24.8 7.9 %collective-permute-start.9 = (f32[64,768]{1,0:T(8,128)S(1)}, f32[64,768]{1,0:T(8,128)S(1)}, u32[]{:S(2)}, u32[]{:S(2)}) collective-permute-start(f32[64,768]{1,0:T(8,128)S(1)} %get-tuple-element.63), channel_id=1, source_target_pairs={{0,8},{4,12},{8,0},{12,4},{1,9},{5,13},{9,1},{13,5},{2,10},{6,14},... | collective-permute-start | bytes 589832 | tf_op jit(solution)/shard_map/ppermute | solution.py:262
  33.3 1.5 %collective-permute-start.10 = (f32[128,384]{1,0:T(8,128)S(1)}, f32[128,384]{1,0:T(8,128)S(1)}, u32[]{:S(2)}, u32[]{:S(2)}) collective-permute-start(f32[128,384]{1,0:T(8,128)S(1)} %get-tuple-element.65), channel_id=1, source_target_pairs={{0,4},{4,0},{8,12},{12,8},{1,5},{5,1},{9,13},{13,9},{2,6},{6,2},{1... | collective-permute-start | bytes 589832 | tf_op jit(solution)/shard_map/ppermute | solution.py:262
  33.9 4.1 %collective-permute-start.13 = (f32[128,384]{1,0:T(8,128)S(1)}, f32[128,384]{1,0:T(8,128)S(1)}, u32[]{:S(2)}, u32[]{:S(2)}) collective-permute-start(f32[128,384]{1,0:T(8,128)S(1)} %get-tuple-element.71), channel_id=1, source_target_pairs={{0,4},{4,0},{8,12},{12,8},{1,5},{5,1},{9,13},{13,9},{2,6},{6,2},{1... | collective-permute-start | bytes 589832 | tf_op jit(solution)/shard_map/ppermute | solution.py:262
  34.8 6.6 %collective-permute-start.11 = (f32[64,384]{1,0:T(8,128)S(1)}, f32[64,384]{1,0:T(8,128)S(1)}, u32[]{:S(2)}, u32[]{:S(2)}) collective-permute-start(f32[64,384]{1,0:T(8,128)S(1)} %get-tuple-element.66), channel_id=1, source_target_pairs={{0,1},{1,8},{2,11},{3,2},{4,5},{5,12},{6,15},{7,6},{8,9},{9,0},{10... | collective-permute-start | bytes 294920 | tf_op jit(solution)/shard_map/ppermute | solution.py:303
  36.3 6.5 %collective-permute-start.12 = (f32[64,384]{1,0:T(8,128)S(1)}, f32[64,384]{1,0:T(8,128)S(1)}, u32[]{:S(2)}, u32[]{:S(2)}) collective-permute-start(f32[64,384]{1,0:T(8,128)S(1)} %get-tuple-element.67), channel_id=1, source_target_pairs={{0,1},{1,0},{2,3},{3,2},{4,5},{5,4},{6,7},{7,6},{8,9},{9,8},{10,11... | collective-permute-start | bytes 294920 | tf_op jit(solution)/shard_map/ppermute | solution.py:303
  38.0 4.9 %collective-permute-start.14 = (f32[64,384]{1,0:T(8,128)S(1)}, f32[64,384]{1,0:T(8,128)S(1)}, u32[]{:S(2)}, u32[]{:S(2)}) collective-permute-start(f32[64,384]{1,0:T(8,128)S(1)} %get-tuple-element.73), channel_id=1, source_target_pairs={{0,8},{4,12},{8,0},{12,4},{1,9},{5,13},{9,1},{13,5},{2,10},{6,14},... | collective-permute-start | bytes 294920 | tf_op jit(solution)/shard_map/ppermute | solution.py:262

commit v11 on v10

--- a/solution.py
+++ b/solution.py
@@ -15,6 +15,7 @@
 VMEM = pl.BlockSpec(memory_space=pltpu.VMEM)
 SMEM = pl.BlockSpec(memory_space=pltpu.SMEM)
 EVEN, ODD, OWN, CORNER = 0, 1, 2, 3
+PARTS = 2
 WEIGHT = 10**10
 
 
@@ -96,11 +97,9 @@
     for k in range(k_tiles):
         piece = 0.0
         for *parts, masks in pairs:
-            row = k * TB
-            for part in parts:
-                if 0 <= row < part.shape[0]:
-                    piece = piece + part[row : row + TB, :] * masks[k : k + 1, :]
-                row -= part.shape[0]
+            per = k_tiles // len(parts)
+            row = k % per * TB
+            piece = piece + parts[k // per][row : row + TB, :] * masks[k : k + 1, :]
         h, l = split(piece)
         highs.append(h)
         lows.append(l)
@@ -113,29 +112,31 @@
 
 
 def multiply_kernel(groups, high, low, *refs):
-    keep, give = refs[-2:]
-    half, width = keep.shape[0], keep.shape[1] // len(groups)
+    keep, *gives = refs[-1 - len(groups) :]
+    half, width = gives[0].shape
     for g, counts in enumerate(groups):
         b_high, b_low = masked_halves(parted(refs, counts))
         refs = refs[sum(counts) :]
-        for out, start in ((give, half), (keep, 0)):
-            at = pl.ds(start, half)
-            out[:, g * width : (g + 1) * width] = product(high[at, :], low[at, :], b_high, b_low)
+        gives[g][...] = product(high[half:, :], low[half:, :], b_high, b_low)
+        keep[:, g * width : (g + 1) * width] = product(high[:half, :], low[:half, :], b_high, b_low)
 
 
 def own_kernel(amp_rows, *refs):
-    pieces, (block, masks, high, low, slab, *sums) = refs[:2], refs[2:]
+    pieces, (block, masks, high, low), slabs, sums = refs[:2], refs[2:6], refs[6:-2], refs[-2:]
     rows = pieces[0].shape[0]
     occ = rows // OTB
+    per = slabs[0].shape[0]
     for p, piece in enumerate(pieces):
         for o in range(occ):
             masked = piece[o * OTB : (o + 1) * OTB, :] * amp_rows[p * occ + o : p * occ + o + 1, :]
-            at = pl.ds(p * rows + o * OTB, OTB)
-            slab[at, :] = masked
+            start = p * rows + o * OTB
+            at = pl.ds(start, OTB)
+            slabs[start // per][pl.ds(start % per, OTB), :] = masked
             high[at, :], low[at, :] = split(masked)
-    used = 2 * rows
-    if used < slab.shape[0]:
-        slab[used:, :] = jnp.zeros((slab.shape[0] - used, slab.shape[1]), jnp.float32)
+    for i, slab in enumerate(slabs):
+        left = max(2 * rows - i * per, 0)
+        if left < per:
+            slab[left:, :] = jnp.zeros((per - left, slab.shape[1]), jnp.float32)
     multiply_kernel(((2,),), high, low, block, masks, *sums)
 
 
@@ -171,18 +172,23 @@
         out[...] = product(high[at, :], low[at, :], b_high[...], b_low[...])
 
 
-def corner_kernel(b_high, b_low, slab, keep, give):
+def corner_kernel(b_high, b_low, *refs):
+    slabs, (keep, give) = refs[:-2], refs[-2:]
+    slab = jnp.concatenate([part[...] for part in slabs], axis=0)
     half = keep.shape[0]
     for out, start in ((give, half), (keep, 0)):
         a_high, a_low = split(slab[start : start + half, :])
         out[...] = product(a_high, a_low, b_high[...], b_low[...])
 
 
-def fold_kernel(keep, got, *outs):
-    rows = outs[0].shape[0]
+def fold_kernel(count, keep, *refs):
+    gots, outs = refs[:count], refs[count:]
+    rows, width = outs[0].shape[0], gots[0].shape[1]
     for i, out in enumerate(outs):
         at = pl.ds(i * rows, rows)
-        out[...] = keep[at, :] + got[at, :]
+        for g, got in enumerate(gots):
+            columns = pl.ds(g * width, width)
+            out[:, columns] = keep[at, columns] + got[at, :]
 
 
 def finish_kernel(counts, *refs):
@@ -262,8 +268,10 @@
         return lax.ppermute(x, "row", [(i, i ^ d) for i in range(n_row)])
 
     k_tiles, tiles = depth // TB, pairs // TB
-    even = [swap_line(integrals, EVEN)]
-    odd = [swap_line(integrals, ODD)]
+    part = depth // PARTS
+    parts = [integrals[i * part : (i + 1) * part, :] for i in range(PARTS)]
+    even = [swap_line(x, EVEN) for x in parts]
+    odd = [swap_line(x, ODD) for x in parts]
     corner = n_col == 4 and total <= depth and depth == width
     last = n_col - 2 if corner else n_col - 1
     kinds = [(OWN, 0)] + [(kind, step) for step in range(1, last + 1) for kind in (EVEN, ODD)]
@@ -278,6 +286,7 @@
         amp_mask,
         int_mask,
         owner_map,
+        flops=10**9,
     )
     masks = dict(zip(kinds + [ends], made[::2]))
     homes = dict(zip(kinds + [ends], made[1::2]))
@@ -290,12 +299,13 @@
     pieces += [swap(chip_columns(d), 2 * d) for d in range(1, n_row // 2)]
     keep, give = call(deal_kernel, "deal", [f32(total // 2, depth)] * 2, 0, marks, *pieces)
     slab_parts = [keep, swap(give, 1)]
-    def fold(keep, give):
+    def fold(keep, *gives):
         shape = f32(rows, keep.shape[1])
-        return call(fold_kernel, "fold", [shape] * (n_row // 2), 0, keep, swap(give, 1))
-
-    def exchange(keep, give):
-        pieces = fold(keep, give)
+        kernel = functools.partial(fold_kernel, len(gives))
+        return call(kernel, "fold", [shape] * (n_row // 2), 0, keep, *[swap(x, 1) for x in gives])
+
+    def exchange(keep, *gives):
+        pieces = fold(keep, *gives)
         return [pieces[0]] + [swap(pieces[i], 2 * i) for i in range(1, n_row // 2)]
 
     def next_door(x, d):
@@ -307,13 +317,13 @@
         )
 
     def multiply(name, *groups, after=()):
-        keep, give = call(
+        sums = call(
             functools.partial(
                 multiply_kernel,
                 tuple(tuple(len(block) + 1 for _, block in group) for group in groups),
             ),
             name,
-            [f32(total // 2, len(groups) * width)] * 2,
+            [f32(total // 2, len(groups) * width)] + [f32(total // 2, width)] * len(groups),
             0,
             high,
             low,
@@ -321,7 +331,7 @@
             flops=6 * total * depth * width * len(groups),
             after=after,
         )
-        return [[slot for slot, _ in group] for group in groups], exchange(keep, give)
+        return [[slot for slot, _ in group] for group in groups], exchange(*sums)
 
     def finish(slots, *so_far):
         args, counts = [], []
@@ -339,11 +349,11 @@
             flops=rows * pairs * n_row,
         )[0]
 
-    high, low, slab, keep, give = call(
+    high, low, *slabs, keep, give = call(
         own_kernel,
         "own",
         [jax.ShapeDtypeStruct((total, depth), jnp.bfloat16)] * 2
-        + [f32(depth if corner else total, depth)]
+        + ([f32(part, depth)] * PARTS if corner else [f32(total, depth)])
         + [f32(total // 2, width)] * 2,
         0,
         amp_rows,
@@ -353,28 +363,22 @@
         flops=6 * total * depth * width,
     )
     slots = [([[(OWN, 0)]], exchange(keep, give))]
+    going, through = odd, even
+    if corner:
+        shape = f32(part + 8, width)
+        through = [call(pass_kernel, "pass", [shape], 0, x, after=slabs)[0] for x in even]
+        going = [
+            call(pick_kernel, "pick", [f32(part, width)], 0, marks, *x, after=through)[0]
+            for x in zip(slabs, odd)
+        ]
     for step in range(1, last + 1):
         if step > 1:
-            going, through = list(odd), list(even)
-            if corner and step == 2:
-                shape = f32(depth + 8, width)
-                through = [call(pass_kernel, "pass", [shape], 0, x, after=(slab,))[0] for x in even]
-                going[-1] = call(
-                    pick_kernel,
-                    "pick",
-                    [f32(depth, width)],
-                    0,
-                    marks,
-                    slab,
-                    odd[-1],
-                    after=through,
-                )[0]
-            odd = [swap_line(x, ODD) for x in through]
-            even = [swap_line(x, EVEN) for x in going]
-            if corner and step == 2:
-                end_slab = even[-1]
+            odd, even = [swap_line(x, ODD) for x in through], [swap_line(x, EVEN) for x in going]
+            going, through = odd, even
         if 2 * step <= n_col - 1:
-            slots.append(multiply("pair", [((EVEN, step), even)], [((ODD, step), odd)]))
+            slots.append(
+                multiply("pair", [((EVEN, step), even)], [((ODD, step), odd)], after=going)
+            )
             continue
         if step < last:
             slots.append(multiply("both", [((EVEN, step), even), ((ODD, step), odd)]))
@@ -396,7 +400,7 @@
         flops = 6 * total * depth * width
         slots = []
         if corner:
-            parts = call(corner_kernel, "corner", sums, 0, *b_halves, end_slab, flops=flops, after=after)
+            parts = call(corner_kernel, "corner", sums, 0, *b_halves, *even, flops=flops, after=after)
             pieces = list(enumerate(fold(*parts)))
             slots.append(([[ends]], [next_door(x, 2 * i) for i, x in reversed(pieces)]))
         parts = call(last_kernel, "last", sums, 0, high, low, *b_halves, flops=flops, after=after)

time: 44.2 us -> 49 us (1.11)
  starting transfers between devices: 15 us -> 17.8 us
  waiting for transfers between devices: 20.4 us -> 22.3 us
    ppermute x4 -> x8, starting transfers between devices: 6.46 us -> 8.57 us  [swap_line(): return lax.ppermute(x, ('row', 'col'), pairs_)]
    ppermute x4 -> x8, waiting for transfers between devices: 10.1 us -> 12 us  [swap_line(): return lax.ppermute(x, ('row', 'col'), pairs_)]
    slice x0 -> x1, local copies, waits for them, and re-layouts: none -> 1.14 us  [on_device(): parts = [integrals[i * part:(i + 1) * part, :] for i in range(PARTS)]]
    dynamic_slice x1, local copies, waits for them, and re-layouts: 1.11 us -> 0.03 us  [chip_columns(): return lax.dynamic_slice_in_dim(amplitudes, start, 2 * depth, 1)]
    ppermute x9 -> x10, starting transfers between devices: 5.41 us -> 6.24 us  [swap(): return lax.ppermute(x, 'row', [(i, i ^ d) for i in range(n_row)])]
    ppermute x9 -> x10, waiting for transfers between devices: 6.35 us -> 6.48 us  [swap(): return lax.ppermute(x, 'row', [(i, i ^ d) for i in range(n_row)])]
    pallas_call x15 -> x17, Pallas kernels: 6.57 us -> 6.62 us  [call(): pl.pallas_call(body, out_shape=outs, in_specs=[SMEM] * n_smem + [VMEM] *...]
  transfers between devices with their start and end apart: 15 -> 20, of which waited for: 8 -> 10; matrix products, arithmetic and copies ran while one was open for 3% -> 0% of each run, Pallas kernels for 11% -> 10%
where the time goes in v11:
time: 49 us; the launch traced here: 48.8 us
  waiting for transfers between devices  22.3 us (46%)
  starting transfers between devices  17.8 us (36%)
  Pallas kernels  6.62 us (14%)
  local copies, waits for them, and re-layouts  1.84 us (4%)
    ppermute x8, waiting for transfers between devices, swap_line(): return lax.ppermute(x, ('row', 'col'), pairs_)  12 us
    ppermute x8, starting transfers between devices, swap_line(): return lax.ppermute(x, ('row', 'col'), pairs_)  8.57 us
    pallas_call x17, Pallas kernels, call(): pl.pallas_call(body, out_shape=outs, in_specs=[SMEM] * n_smem + [VMEM] *...  6.62 us
    ppermute x10, waiting for transfers between devices, swap(): return lax.ppermute(x, 'row', [(i, i ^ d) for i in range(n_row)])  6.48 us
    ppermute x10, starting transfers between devices, swap(): return lax.ppermute(x, 'row', [(i, i ^ d) for i in range(n_row)])  6.24 us
    ppermute x2, waiting for transfers between devices, next_door(): lax.ppermute(x, ('row', 'col'), [(i * n_col + j, (i ^ (d if 0 < j < n_col...  3.74 us
    ppermute x2, starting transfers between devices, next_door(): lax.ppermute(x, ('row', 'col'), [(i * n_col + j, (i ^ (d if 0 < j < n_col...  3 us
    slice x1, local copies, waits for them, and re-layouts, on_device(): parts = [integrals[i * part:(i + 1) * part, :] for i in range(PARTS)]  1.14 us
  transfers between devices with their start and end apart: 20, of which 10 were waited for; matrix products, arithmetic and copies ran while one was open for 0% of the time, Pallas kernels for 10%

profile of v11, /device:TPU:0, one launch (start us, length us, event | category | flops | bytes accessed | tf_op | source)
XLA Modules:
  0.0 48.8 jit_solution(9385521393783215974)
XLA Ops:
  0.0 1.1 %fusion = (f32[192,384]{1,0:T(8,128)S(1)}, f32[192,384]{1,0:T(8,128)S(1)}) fusion(f32[384,384]{1,0:T(8,128)} %refs_3_.3), kind=kLoop, calls=%fused_computation.4 | loop fusion | bytes 1179648 | tf_op jit(solution)/shard_map/slice | solution.py:272
  1.1 0.5 %collective-permute-start.6 = (f32[192,384]{1,0:T(8,128)S(1)}, f32[192,384]{1,0:T(8,128)S(1)}, u32[]{:S(2)}, u32[]{:S(2)}) collective-permute-start(f32[192,384]{1,0:T(8,128)S(1)} %get-tuple-element.81), channel_id=1, source_target_pairs={{0,4},{1,2},{2,1},{3,7},{4,0},{5,6},{6,5},{7,3},{8,12},{9,10},{10,... | collective-permute-start | bytes 884744 | tf_op jit(solution)/shard_map/ppermute | solution.py:265
  1.7 4.1 %collective-permute-start.4 = (f32[192,384]{1,0:T(8,128)S(1)}, f32[192,384]{1,0:T(8,128)S(1)}, u32[]{:S(2)}, u32[]{:S(2)}) collective-permute-start(f32[192,384]{1,0:T(8,128)S(1)} %get-tuple-element.81), channel_id=1, source_target_pairs={{0,1},{1,0},{2,3},{3,2},{4,5},{5,4},{6,7},{7,6},{8,9},{9,8},{10,11... | collective-permute-start | bytes 884744 | tf_op jit(solution)/shard_map/ppermute | solution.py:265
  5.9 1.6 %collective-permute-start = (f32[64,768]{1,0:T(8,128)S(1)}, f32[64,768]{1,0:T(8,128)S(1)}, u32[]{:S(2)}, u32[]{:S(2)}) collective-permute-start(f32[64,768]{1,0:T(8,128)S(1)} %get-tuple-element.83), channel_id=1, source_target_pairs={{0,8},{4,12},{8,0},{12,4},{1,9},{5,13},{9,1},{13,5},{2,10},{6,14},... | collective-permute-start | bytes 589832 | tf_op jit(solution)/shard_map/ppermute | solution.py:268
  7.6 0.5 %copy-done.1 = s32[16,16]{1,0:T(8,128)S(1)} copy-done((s32[16,16]{1,0:T(8,128)S(1)}, s32[16,16]{1,0:T(8,128)}, u32[]{:S(2)}) %copy-start.1) | copy-done | bytes 1048
  8.2 2.0 %tables.1 = (f32[8,384]{1,0:T(8,128)S(1)}, f32[8,384]{1,0:T(8,128)S(1)}, f32[4,384]{1,0:T(4,128)S(1)}, f32[16,384]{1,0:T(8,128)S(1)}, f32[4,384]{1,0:T(4,128)S(1...) custom-call(s32[3]{0:T(128)S(1)} %pad_add_fusion.refs_0_, ...), custom_call_target="tpu_custom_call" | custom-call | flops 1000000000 | bytes 212044 | tf_op jit(solution)/shard_map/tables/pallas_call | solution.py:232
  10.2 3.1 %collective-permute-done.refs_2_ = f32[64,768]{1,0:T(8,128)S(1)} collective-permute-done((f32[64,768]{1,0:T(8,128)S(1)}, f32[64,768]{1,0:T(8,128)S(1)}, u32[]{:S(2)}, u32[]{:S(2)}) %collective-permute-start) | collective-permute-done | bytes 196640 | tf_op jit(solution)/shard_map/ppermute | solution.py:268
  13.4 1.4 %collective-permute-done.1.refs_2_ = f32[128,384]{1,0:T(8,128)S(1)} collective-permute-done((f32[128,384]{1,0:T(8,128)S(1)}, f32[128,384]{1,0:T(8,128)S(1)}, u32[]{:S(2)}, u32[]{:S(2)}) %collective-permute-start.1) | collective-permute-done | bytes 196640 | tf_op jit(solution)/shard_map/ppermute | solution.py:268
  14.8 0.6 %own.1 = (bf16[256,384]{1,0:T(8,128)(2,1)S(1)}, bf16[256,384]{1,0:T(8,128)(2,1)S(1)}, f32[192,384]{1,0:T(8,128)S(1)}, f32[192,384]{1,0:T(8,128)S(1)}, f32[128,384]{1,0:T(8,128)S(1)}, /*index=5*/f32[128,384]{1,0:T(8,128)S(1)}) custom-call(f32[8,384]{1,0:T(8,128)S(1)} %get-tuple-element.45.refs_0_, f32[128,384]{1,0:T(8,128)S(1)} %get-tuple-element.46.refs_1_, ...), custom_call_target="tpu_custom_call" | custom-call | flops 226492416 | bytes 2377728 | tf_op jit(solution)/shard_map/own/pallas_call | solution.py:232
  15.4 0.2 collective-permute-start.10
  15.6 3.2 %collective-permute-done.3.refs_0_.refs_2_ = f32[192,384]{1,0:T(8,128)S(1)} collective-permute-done((f32[192,384]{1,0:T(8,128)S(1)}, f32[192,384]{1,0:T(8,128)S(1)}, u32[]{:S(2)}, u32[]{:S(2)}) %collective-permute-start.3) | collective-permute-done | bytes 294944 | tf_op jit(solution)/shard_map/ppermute | solution.py:265
  19.0 1.0 %pair.1 = (f32[128,768]{1,0:T(8,128)S(1)}, f32[128,384]{1,0:T(8,128)S(1)}, f32[128,384]{1,0:T(8,128)S(1)}) custom-call(bf16[256,384]{1,0:T(8,128)(2,1)S(1)} %get-tuple-element.59.refs_0_, bf16[256,384]{1,0:T(8,128)(2,1)S(1)} %get-tuple-element.60.refs_1_, f32[192,384]{1,0:T(8,128)S(1)} %collective-permute-done.3.refs_0_.refs_2_, ...), custom_call_target="tpu_custom_call" | custom-call | flops 452984832 | bytes 2371584 | tf_op jit(solution)/shard_map/pair/pallas_call | solution.py:232
  20.1 0.5 %collective-permute-start.8 = (f32[200,384]{1,0:T(8,128)S(1)}, f32[200,384]{1,0:T(8,128)S(1)}, u32[]{:S(2)}, u32[]{:S(2)}) collective-permute-start(f32[200,384]{1,0:T(8,128)S(1)} %pass.2.refs_3_), channel_id=1, source_target_pairs={{0,4},{1,2},{2,1},{3,7},{4,0},{5,6},{6,5},{7,3},{8,12},{9,10},{10,... | collective-permute-start | bytes 921608 | tf_op jit(solution)/shard_map/ppermute | solution.py:265
  20.6 3.3 %collective-permute-start.5 = (f32[192,384]{1,0:T(8,128)S(1)}, f32[192,384]{1,0:T(8,128)S(1)}, u32[]{:S(2)}, u32[]{:S(2)}) collective-permute-start(f32[192,384]{1,0:T(8,128)S(1)} %pick.2.refs_8_), channel_id=1, source_target_pairs={{0,1},{1,0},{2,3},{3,2},{4,5},{5,4},{6,7},{7,6},{8,9},{9,8},{10,11... | collective-permute-start | bytes 884744 | tf_op jit(solution)/shard_map/ppermute | solution.py:265
  24.0 1.4 %collective-permute-done.13.refs_2_ = f32[128,384]{1,0:T(8,128)S(1)} collective-permute-done((f32[128,384]{1,0:T(8,128)S(1)}, f32[128,384]{1,0:T(8,128)S(1)}, u32[]{:S(2)}, u32[]{:S(2)}) %collective-permute-start.13) | collective-permute-done | bytes 196640 | tf_op jit(solution)/shard_map/ppermute | solution.py:268
  25.4 1.5 %collective-permute-start.11 = (f32[64,384]{1,0:T(8,128)S(1)}, f32[64,384]{1,0:T(8,128)S(1)}, u32[]{:S(2)}, u32[]{:S(2)}) collective-permute-start(f32[64,384]{1,0:T(8,128)S(1)} %get-tuple-element.58), channel_id=1, source_target_pairs={{0,8},{4,12},{8,0},{12,4},{1,9},{5,13},{9,1},{13,5},{2,10},{6,14},... | collective-permute-start | bytes 294920 | tf_op jit(solution)/shard_map/ppermute | solution.py:268
  27.0 4.8 %collective-permute-done.5.refs_0_.refs_2_ = f32[192,384]{1,0:T(8,128)S(1)} collective-permute-done((f32[192,384]{1,0:T(8,128)S(1)}, f32[192,384]{1,0:T(8,128)S(1)}, u32[]{:S(2)}, u32[]{:S(2)}) %collective-permute-start.5) | collective-permute-done | bytes 294944 | tf_op jit(solution)/shard_map/ppermute | solution.py:265
  31.7 1.5 %collective-permute-start.14 = (f32[64,768]{1,0:T(8,128)S(1)}, f32[64,768]{1,0:T(8,128)S(1)}, u32[]{:S(2)}, u32[]{:S(2)}) collective-permute-start(f32[64,768]{1,0:T(8,128)S(1)} %get-tuple-element.67), channel_id=1, source_target_pairs={{0,8},{4,12},{8,0},{12,4},{1,9},{5,13},{9,1},{13,5},{2,10},{6,14},... | collective-permute-start | bytes 589832 | tf_op jit(solution)/shard_map/ppermute | solution.py:268
  33.2 4.1 %collective-permute-done.7.refs_1_.refs_3_ = f32[192,384]{1,0:T(8,128)S(1)} collective-permute-done((f32[192,384]{1,0:T(8,128)S(1)}, f32[192,384]{1,0:T(8,128)S(1)}, u32[]{:S(2)}, u32[]{:S(2)}) %collective-permute-start.7) | collective-permute-done | bytes 294944 | tf_op jit(solution)/shard_map/ppermute | solution.py:265
  37.3 0.2 halves.1
  37.5 0.5 %corner.1 = (f32[128,384]{1,0:T(8,128)S(1)}, f32[128,384]{1,0:T(8,128)S(1)}) custom-call(bf16[384,384]{1,0:T(8,128)(2,1)S(1)} %get-tuple-element.53.refs_0_.refs_2_, bf16[384,384]{1,0:T(8,128)(2,1)S(1)} %get-tuple-element.54.refs_1_.refs_3_, f32[192,384]{1,0:T(8,128)S(1)} %collective-permute-done.5.refs_0_.refs_2_, ...), custom_call_target="tpu_custom_call" | custom-call | flops 226492416 | bytes 1572864 | tf_op jit(solution)/shard_map/corner/pallas_call | solution.py:232
  38.1 0.5 %last.1 = (f32[128,384]{1,0:T(8,128)S(1)}, f32[128,384]{1,0:T(8,128)S(1)}) custom-call(bf16[256,384]{1,0:T(8,128)(2,1)S(1)} %get-tuple-element.59.refs_0_, bf16[256,384]{1,0:T(8,128)(2,1)S(1)} %get-tuple-element.60.refs_1_, bf16[384,384]{1,0:T(8,128)(2,1)S(1)} %get-tuple-element.53.refs_0_.refs_2_, bf16[384,384]{1,0:T(8,128)(2,1)S(1)} %get-tuple-element.54.refs_1_.refs_3_, ...), custom_call_target="tpu_custom_call" | custom-call | flops 226492416 | bytes 1376256 | tf_op jit(solution)/shard_map/last/pallas_call | solution.py:232
  38.6 0.6 %collective-permute-start.18 = (f32[128,384]{1,0:T(8,128)S(1)}, f32[128,384]{1,0:T(8,128)S(1)}, u32[]{:S(2)}, u32[]{:S(2)}) collective-permute-start(f32[128,384]{1,0:T(8,128)S(1)} %get-tuple-element.75), channel_id=1, source_target_pairs={{0,4},{4,0},{8,12},{12,8},{1,5},{5,1},{9,13},{13,9},{2,6},{6,2},{1... | collective-permute-start | bytes 589832 | tf_op jit(solution)/shard_map/ppermute | solution.py:268
  39.2 0.3 collective-permute-done.15.refs_1_
  39.5 2.1 %collective-permute-start.16 = (f32[64,384]{1,0:T(8,128)S(1)}, f32[64,384]{1,0:T(8,128)S(1)}, u32[]{:S(2)}, u32[]{:S(2)}) collective-permute-start(f32[64,384]{1,0:T(8,128)S(1)} %get-tuple-element.70), channel_id=1, source_target_pairs={{0,1},{1,8},{2,11},{3,2},{4,5},{5,12},{6,15},{7,6},{8,9},{9,0},{10... | collective-permute-start | bytes 294920 | tf_op jit(solution)/shard_map/ppermute | solution.py:313
  41.6 1.0 %collective-permute-start.17 = (f32[64,384]{1,0:T(8,128)S(1)}, f32[64,384]{1,0:T(8,128)S(1)}, u32[]{:S(2)}, u32[]{:S(2)}) collective-permute-start(f32[64,384]{1,0:T(8,128)S(1)} %get-tuple-element.71), channel_id=1, source_target_pairs={{0,1},{1,0},{2,3},{3,2},{4,5},{5,4},{6,7},{7,6},{8,9},{9,8},{10,11... | collective-permute-start | bytes 294920 | tf_op jit(solution)/shard_map/ppermute | solution.py:313
  42.6 0.7 %collective-permute-start.19 = (f32[64,384]{1,0:T(8,128)S(1)}, f32[64,384]{1,0:T(8,128)S(1)}, u32[]{:S(2)}, u32[]{:S(2)}) collective-permute-start(f32[64,384]{1,0:T(8,128)S(1)} %get-tuple-element.77), channel_id=1, source_target_pairs={{0,8},{4,12},{8,0},{12,4},{1,9},{5,13},{9,1},{13,5},{2,10},{6,14},... | collective-permute-start | bytes 294920 | tf_op jit(solution)/shard_map/ppermute | solution.py:268
  43.2 0.5 finish.2.refs_6_
  43.7 2.4 %collective-permute-done.16.refs_1_ = f32[64,384]{1,0:T(8,128)S(1)} collective-permute-done((f32[64,384]{1,0:T(8,128)S(1)}, f32[64,384]{1,0:T(8,128)S(1)}, u32[]{:S(2)}, u32[]{:S(2)}) %collective-permute-start.16) | collective-permute-done | bytes 98336 | tf_op jit(solution)/shard_map/ppermute | solution.py:313
  46.1 1.4 %collective-permute-done.17.refs_2_ = f32[64,384]{1,0:T(8,128)S(1)} collective-permute-done((f32[64,384]{1,0:T(8,128)S(1)}, f32[64,384]{1,0:T(8,128)S(1)}, u32[]{:S(2)}, u32[]{:S(2)}) %collective-permute-start.17) | collective-permute-done | bytes 98336 | tf_op jit(solution)/shard_map/ppermute | solution.py:313
  47.4 0.3 collective-permute-done.19.refs_5_
  47.7 1.1 %finish.3 = f32[64,1536]{1,0:T(8,128)} custom-call(f32[16,384]{1,0:T(8,128)S(1)} %get-tuple-element.43.refs_0_, f32[64,384]{1,0:T(8,128)S(1)} %collective-permute-done.16.refs_1_, f32[64,384]{1,0:T(8,128)S(1)} %collective-permute-done.17.refs_2_, f32[16,384]{1,0:T(8,128)S(1)} %add.12.refs_3_, f32[64,384]{1,0:T(8,128)S(1)} %get-tuple-element.76.refs_4_, ...), custom_call_target="tpu_custom_call" | custom-call | flops 393216 | bytes 1228800 | tf_op jit(solution)/shard_map/finish/pallas_call | solution.py:232
  (41 shorter events, 1.0 us)
Async XLA Ops:
  0.0 5.9 %copy-start.3 = (f32[64,1536]{1,0:T(8,128)S(1)}, f32[64,1536]{1,0:T(8,128)}, u32[]{:S(2)}) copy-start(f32[64,1536]{1,0:T(8,128)} %param.5) | copy-start | bytes 1179652
  1.1 17.7 %collective-permute-start.6 = (f32[192,384]{1,0:T(8,128)S(1)}, f32[192,384]{1,0:T(8,128)S(1)}, u32[]{:S(2)}, u32[]{:S(2)}) collective-permute-start(f32[192,384]{1,0:T(8,128)S(1)} %get-tuple-element.81), channel_id=1, source_target_pairs={{0,4},{1,2},{2,1},{3,7},{4,0},{5,6},{6,5},{7,3},{8,12},{9,10},{10,... | collective-permute-start | bytes 884744 | tf_op jit(solution)/shard_map/ppermute | solution.py:265
  1.7 13.9 %collective-permute-start.4 = (f32[192,384]{1,0:T(8,128)S(1)}, f32[192,384]{1,0:T(8,128)S(1)}, u32[]{:S(2)}, u32[]{:S(2)}) collective-permute-start(f32[192,384]{1,0:T(8,128)S(1)} %get-tuple-element.81), channel_id=1, source_target_pairs={{0,1},{1,0},{2,3},{3,2},{4,5},{5,4},{6,7},{7,6},{8,9},{9,8},{10,11... | collective-permute-start | bytes 884744 | tf_op jit(solution)/shard_map/ppermute | solution.py:265
  5.8 13.0 %collective-permute-start.3 = (f32[192,384]{1,0:T(8,128)S(1)}, f32[192,384]{1,0:T(8,128)S(1)}, u32[]{:S(2)}, u32[]{:S(2)}) collective-permute-start(f32[192,384]{1,0:T(8,128)S(1)} %get-tuple-element.82), channel_id=1, source_target_pairs={{0,1},{1,0},{2,3},{3,2},{4,5},{5,4},{6,7},{7,6},{8,9},{9,8},{10,11... | collective-permute-start | bytes 884744 | tf_op jit(solution)/shard_map/ppermute | solution.py:265
  5.8 13.1 %collective-permute-start.2 = (f32[192,384]{1,0:T(8,128)S(1)}, f32[192,384]{1,0:T(8,128)S(1)}, u32[]{:S(2)}, u32[]{:S(2)}) collective-permute-start(f32[192,384]{1,0:T(8,128)S(1)} %get-tuple-element.82), channel_id=1, source_target_pairs={{0,4},{1,2},{2,1},{3,7},{4,0},{5,6},{6,5},{7,3},{8,12},{9,10},{10,... | collective-permute-start | bytes 884744 | tf_op jit(solution)/shard_map/ppermute | solution.py:265
  5.9 1.6 %copy-start.4 = (s32[32,16]{0,1:T(8,128)S(1)}, s32[32,16]{0,1:T(8,128)}, u32[]{:S(2)}) copy-start(s32[32,16]{0,1:T(8,128)} %param.7) | copy-start | bytes 6148
  5.9 7.4 %collective-permute-start = (f32[64,768]{1,0:T(8,128)S(1)}, f32[64,768]{1,0:T(8,128)S(1)}, u32[]{:S(2)}, u32[]{:S(2)}) collective-permute-start(f32[64,768]{1,0:T(8,128)S(1)} %get-tuple-element.83), channel_id=1, source_target_pairs={{0,8},{4,12},{8,0},{12,4},{1,9},{5,13},{9,1},{13,5},{2,10},{6,14},... | collective-permute-start | bytes 589832 | tf_op jit(solution)/shard_map/ppermute | solution.py:268
  7.5 0.7 %copy-start.1 = (s32[16,16]{1,0:T(8,128)S(1)}, s32[16,16]{1,0:T(8,128)}, u32[]{:S(2)}) copy-start(s32[16,16]{1,0:T(8,128)} %refs_2_.1) | copy-start | bytes 3076
  7.5 0.7 %copy-start.2 = (s32[16]{0:T(128)S(1)}, s32[16]{0:T(128)}, u32[]{:S(2)}) copy-start(s32[16]{0:T(128)} %refs_3_.2) | copy-start | bytes 196
  8.2 6.6 %copy-start = (f32[384,384]{1,0:T(8,128)S(1)}, f32[384,384]{1,0:T(8,128)}, u32[]{:S(2)}) copy-start(f32[384,384]{1,0:T(8,128)} %refs_3_.3) | copy-start | bytes 1769476
  13.3 1.5 %collective-permute-start.1 = (f32[128,384]{1,0:T(8,128)S(1)}, f32[128,384]{1,0:T(8,128)S(1)}, u32[]{:S(2)}, u32[]{:S(2)}) collective-permute-start(f32[128,384]{1,0:T(8,128)S(1)} %get-tuple-element.47), channel_id=1, source_target_pairs={{0,4},{4,0},{8,12},{12,8},{1,5},{5,1},{9,13},{13,9},{2,6},{6,2},{1... | collective-permute-start | bytes 589832 | tf_op jit(solution)/shard_map/ppermute | solution.py:268
  15.4 8.5 %collective-permute-start.10 = (f32[128,384]{1,0:T(8,128)S(1)}, f32[128,384]{1,0:T(8,128)S(1)}, u32[]{:S(2)}, u32[]{:S(2)}) collective-permute-start(f32[128,384]{1,0:T(8,128)S(1)} %get-tuple-element.56), channel_id=1, source_target_pairs={{0,4},{4,0},{8,12},{12,8},{1,5},{5,1},{9,13},{13,9},{2,6},{6,2},{1... | collective-permute-start | bytes 589832 | tf_op jit(solution)/shard_map/ppermute | solution.py:268
  20.0 4.0 %collective-permute-start.12 = (f32[128,384]{1,0:T(8,128)S(1)}, f32[128,384]{1,0:T(8,128)S(1)}, u32[]{:S(2)}, u32[]{:S(2)}) collective-permute-start(f32[128,384]{1,0:T(8,128)S(1)} %get-tuple-element.64), channel_id=1, source_target_pairs={{0,4},{4,0},{8,12},{12,8},{1,5},{5,1},{9,13},{13,9},{2,6},{6,2},{1... | collective-permute-start | bytes 589832 | tf_op jit(solution)/shard_map/ppermute | solution.py:268
  20.1 17.2 %collective-permute-start.8 = (f32[200,384]{1,0:T(8,128)S(1)}, f32[200,384]{1,0:T(8,128)S(1)}, u32[]{:S(2)}, u32[]{:S(2)}) collective-permute-start(f32[200,384]{1,0:T(8,128)S(1)} %pass.2.refs_3_), channel_id=1, source_target_pairs={{0,4},{1,2},{2,1},{3,7},{4,0},{5,6},{6,5},{7,3},{8,12},{9,10},{10,... | collective-permute-start | bytes 921608 | tf_op jit(solution)/shard_map/ppermute | solution.py:265
  20.6 16.7 %collective-permute-start.9 = (f32[200,384]{1,0:T(8,128)S(1)}, f32[200,384]{1,0:T(8,128)S(1)}, u32[]{:S(2)}, u32[]{:S(2)}) collective-permute-start(f32[200,384]{1,0:T(8,128)S(1)} %pass.3.refs_4_), channel_id=1, source_target_pairs={{0,4},{1,2},{2,1},{3,7},{4,0},{5,6},{6,5},{7,3},{8,12},{9,10},{10,... | collective-permute-start | bytes 921608 | tf_op jit(solution)/shard_map/ppermute | solution.py:265
  20.6 11.1 %collective-permute-start.5 = (f32[192,384]{1,0:T(8,128)S(1)}, f32[192,384]{1,0:T(8,128)S(1)}, u32[]{:S(2)}, u32[]{:S(2)}) collective-permute-start(f32[192,384]{1,0:T(8,128)S(1)} %pick.2.refs_8_), channel_id=1, source_target_pairs={{0,1},{1,0},{2,3},{3,2},{4,5},{5,4},{6,7},{7,6},{8,9},{9,8},{10,11... | collective-permute-start | bytes 884744 | tf_op jit(solution)/shard_map/ppermute | solution.py:265
  23.9 13.4 %collective-permute-start.7 = (f32[192,384]{1,0:T(8,128)S(1)}, f32[192,384]{1,0:T(8,128)S(1)}, u32[]{:S(2)}, u32[]{:S(2)}) collective-permute-start(f32[192,384]{1,0:T(8,128)S(1)} %pick.3.refs_9_), channel_id=1, source_target_pairs={{0,1},{1,0},{2,3},{3,2},{4,5},{5,4},{6,7},{7,6},{8,9},{9,8},{10,11... | collective-permute-start | bytes 884744 | tf_op jit(solution)/shard_map/ppermute | solution.py:265
  23.9 1.5 %collective-permute-start.13 = (f32[128,384]{1,0:T(8,128)S(1)}, f32[128,384]{1,0:T(8,128)S(1)}, u32[]{:S(2)}, u32[]{:S(2)}) collective-permute-start(f32[128,384]{1,0:T(8,128)S(1)} %get-tuple-element.65), channel_id=1, source_target_pairs={{0,4},{4,0},{8,12},{12,8},{1,5},{5,1},{9,13},{13,9},{2,6},{6,2},{1... | collective-permute-start | bytes 589832 | tf_op jit(solution)/shard_map/ppermute | solution.py:268
  25.4 12.0 %collective-permute-start.11 = (f32[64,384]{1,0:T(8,128)S(1)}, f32[64,384]{1,0:T(8,128)S(1)}, u32[]{:S(2)}, u32[]{:S(2)}) collective-permute-start(f32[64,384]{1,0:T(8,128)S(1)} %get-tuple-element.58), channel_id=1, source_target_pairs={{0,8},{4,12},{8,0},{12,4},{1,9},{5,13},{9,1},{13,5},{2,10},{6,14},... | collective-permute-start | bytes 294920 | tf_op jit(solution)/shard_map/ppermute | solution.py:268
  31.7 5.7 %collective-permute-start.14 = (f32[64,768]{1,0:T(8,128)S(1)}, f32[64,768]{1,0:T(8,128)S(1)}, u32[]{:S(2)}, u32[]{:S(2)}) collective-permute-start(f32[64,768]{1,0:T(8,128)S(1)} %get-tuple-element.67), channel_id=1, source_target_pairs={{0,8},{4,12},{8,0},{12,4},{1,9},{5,13},{9,1},{13,5},{2,10},{6,14},... | collective-permute-start | bytes 589832 | tf_op jit(solution)/shard_map/ppermute | solution.py:268
  38.0 1.5 %collective-permute-start.15 = (f32[128,384]{1,0:T(8,128)S(1)}, f32[128,384]{1,0:T(8,128)S(1)}, u32[]{:S(2)}, u32[]{:S(2)}) collective-permute-start(f32[128,384]{1,0:T(8,128)S(1)} %get-tuple-element.69), channel_id=1, source_target_pairs={{0,4},{4,0},{8,12},{12,8},{1,5},{5,1},{9,13},{13,9},{2,6},{6,2},{1... | collective-permute-start | bytes 589832 | tf_op jit(solution)/shard_map/ppermute | solution.py:268
  38.6 3.9 %collective-permute-start.18 = (f32[128,384]{1,0:T(8,128)S(1)}, f32[128,384]{1,0:T(8,128)S(1)}, u32[]{:S(2)}, u32[]{:S(2)}) collective-permute-start(f32[128,384]{1,0:T(8,128)S(1)} %get-tuple-element.75), channel_id=1, source_target_pairs={{0,4},{4,0},{8,12},{12,8},{1,5},{5,1},{9,13},{13,9},{2,6},{6,2},{1... | collective-permute-start | bytes 589832 | tf_op jit(solution)/shard_map/ppermute | solution.py:268
  39.5 6.6 %collective-permute-start.16 = (f32[64,384]{1,0:T(8,128)S(1)}, f32[64,384]{1,0:T(8,128)S(1)}, u32[]{:S(2)}, u32[]{:S(2)}) collective-permute-start(f32[64,384]{1,0:T(8,128)S(1)} %get-tuple-element.70), channel_id=1, source_target_pairs={{0,1},{1,8},{2,11},{3,2},{4,5},{5,12},{6,15},{7,6},{8,9},{9,0},{10... | collective-permute-start | bytes 294920 | tf_op jit(solution)/shard_map/ppermute | solution.py:313
  41.6 5.9 %collective-permute-start.17 = (f32[64,384]{1,0:T(8,128)S(1)}, f32[64,384]{1,0:T(8,128)S(1)}, u32[]{:S(2)}, u32[]{:S(2)}) collective-permute-start(f32[64,384]{1,0:T(8,128)S(1)} %get-tuple-element.71), channel_id=1, source_target_pairs={{0,1},{1,0},{2,3},{3,2},{4,5},{5,4},{6,7},{7,6},{8,9},{9,8},{10,11... | collective-permute-start | bytes 294920 | tf_op jit(solution)/shard_map/ppermute | solution.py:313
  42.6 5.2 %collective-permute-start.19 = (f32[64,384]{1,0:T(8,128)S(1)}, f32[64,384]{1,0:T(8,128)S(1)}, u32[]{:S(2)}, u32[]{:S(2)}) collective-permute-start(f32[64,384]{1,0:T(8,128)S(1)} %get-tuple-element.77), channel_id=1, source_target_pairs={{0,8},{4,12},{8,0},{12,4},{1,9},{5,13},{9,1},{13,5},{2,10},{6,14},... | collective-permute-start | bytes 294920 | tf_op jit(solution)/shard_map/ppermute | solution.py:268

commit v12 on v10

--- a/solution.py
+++ b/solution.py
@@ -186,6 +186,10 @@
 
 
 def finish_kernel(counts, *refs):
+    sems = None
+    if refs[-1].dtype != jnp.float32:
+        *refs, final, out, sems = refs
+        refs = (*refs, out)
     out = refs[-1]
     n_in = sum(counts) + len(counts)
     rows = out.shape[0]
@@ -203,6 +207,7 @@
             part = total[:, g * GROUP : (g + 1) * GROUP]
             turned = [part] + [pltpu.roll(part, t * TB, 1) for t in range(1, PER)]
             totals.append((homes, g * n_home * PER, turned))
+    copies = []
     for home in range(n_home):
         to = pl.ds(home * GROUP, GROUP)
         if len(refs) - 1 > n_in:
@@ -214,9 +219,14 @@
                 row = base + home * PER + t
                 value = jnp.where(homes[row : row + 1, :] > 0.5, turned[t], value)
         out[:, to] = value
-
-
-def call(kernel, name, outs, n_smem, *args, flops=0, after=()):
+        if sems is not None:
+            copies.append(pltpu.make_async_copy(out.at[:, to], final.at[:, to], sems.at[home]))
+            copies[-1].start()
+    for copy in copies:
+        copy.wait()
+
+
+def call(kernel, name, outs, n_smem, *args, flops=0, after=(), scratch=(), out_space=pltpu.VMEM):
     moved = sum(x.size * x.dtype.itemsize for x in list(args) + list(outs))
     n_args, n_after = len(args), len(after)
 
@@ -229,7 +239,8 @@
         in_specs=[SMEM] * n_smem
         + [VMEM] * (len(args) - n_smem)
         + [pl.BlockSpec(memory_space=pl.ANY)] * n_after,
-        out_specs=[VMEM] * len(outs),
+        out_specs=[pl.BlockSpec(memory_space=out_space)] * len(outs),
+        scratch_shapes=scratch,
         compiler_params=pltpu.CompilerParams(vmem_limit_bytes=40 * 2**20),
         cost_estimate=pl.CostEstimate(
             flops=int(flops), bytes_accessed=int(moved), transcendentals=0
@@ -324,7 +335,10 @@
         return [[slot for slot, _ in group] for group in groups], exchange(keep, give)
 
     def finish(slots, *so_far):
-        args, counts = [], []
+        args, counts, place_ = [], [], {}
+        if so_far:
+            buffers = [pltpu.VMEM((rows, pairs), jnp.float32), pltpu.SemaphoreType.DMA((pairs // GROUP,))]
+            place_ = dict(scratch=buffers, out_space=pl.ANY)
         for groups, shares in slots:
             args.append(jnp.concatenate([sum(homes[name] for name in names) for names in groups]))
             args.extend(shares)
@@ -337,6 +351,7 @@
             *args,
             *so_far,
             flops=rows * pairs * n_row,
+            **place_,
         )[0]
 
     high, low, slab, keep, give = call(
@@ -355,24 +370,13 @@
     slots = [([[(OWN, 0)]], exchange(keep, give))]
     for step in range(1, last + 1):
         if step > 1:
-            going, through = list(odd), list(even)
-            if corner and step == 2:
-                shape = f32(depth + 8, width)
-                through = [call(pass_kernel, "pass", [shape], 0, x, after=(slab,))[0] for x in even]
-                going[-1] = call(
-                    pick_kernel,
-                    "pick",
-                    [f32(depth, width)],
-                    0,
-                    marks,
-                    slab,
-                    odd[-1],
-                    after=through,
-                )[0]
-            odd = [swap_line(x, ODD) for x in through]
-            even = [swap_line(x, EVEN) for x in going]
-            if corner and step == 2:
-                end_slab = even[-1]
+            going = list(odd)
+            if corner:
+                shape = f32(depth, width)
+                going = [call(pick_kernel, "pick", [shape], 0, marks, slab, odd[0])[0]]
+            odd, even = [swap_line(x, ODD) for x in even], [swap_line(x, EVEN) for x in going]
+            if corner:
+                end_slab = even[0]
         if 2 * step <= n_col - 1:
             slots.append(multiply("pair", [((EVEN, step), even)], [((ODD, step), odd)]))
             continue

time: 44.2 us -> 43.2 us (0.977)
  waiting for transfers between devices: 20.4 us -> 16.2 us
  starting transfers between devices: 15 us -> 18.3 us
    ppermute x4, waiting for transfers between devices: 10.1 us -> 7.06 us  [swap_line(): return lax.ppermute(x, ('row', 'col'), pairs_)]
    ppermute x4, starting transfers between devices: 6.46 us -> 8.97 us  [swap_line(): return lax.ppermute(x, ('row', 'col'), pairs_)]
    ppermute x9, starting transfers between devices: 5.41 us -> 6.34 us  [swap(): return lax.ppermute(x, 'row', [(i, i ^ d) for i in range(n_row)])]
    ppermute x2, waiting for transfers between devices: 3.98 us -> 3.16 us  [next_door(): lax.ppermute(x, ('row', 'col'), [(i * n_col + j, (i ^ (d if 0 < j < n_col...]
    pallas_call x15 -> x14, Pallas kernels: 6.57 us -> 6.48 us  [call(): pl.pallas_call(body, out_shape=outs, in_specs=[SMEM] * n_smem + [VMEM] *...]
where the time goes in v12:
time: 43.2 us; the launch traced here: 43 us
  starting transfers between devices  18.3 us (42%)
  waiting for transfers between devices  16.2 us (38%)
  Pallas kernels  6.48 us (15%)
  local copies, waits for them, and re-layouts  1.77 us (4%)
    ppermute x4, starting transfers between devices, swap_line(): return lax.ppermute(x, ('row', 'col'), pairs_)  8.97 us
    ppermute x4, waiting for transfers between devices, swap_line(): return lax.ppermute(x, ('row', 'col'), pairs_)  7.06 us
    pallas_call x14, Pallas kernels, call(): pl.pallas_call(body, out_shape=outs, in_specs=[SMEM] * n_smem + [VMEM] *...  6.48 us
    ppermute x9, starting transfers between devices, swap(): return lax.ppermute(x, 'row', [(i, i ^ d) for i in range(n_row)])  6.34 us
    ppermute x9, waiting for transfers between devices, swap(): return lax.ppermute(x, 'row', [(i, i ^ d) for i in range(n_row)])  6 us
    ppermute x2, waiting for transfers between devices, next_door(): lax.ppermute(x, ('row', 'col'), [(i * n_col + j, (i ^ (d if 0 < j < n_col...  3.16 us
    ppermute x2, starting transfers between devices, next_door(): lax.ppermute(x, ('row', 'col'), [(i * n_col + j, (i ^ (d if 0 < j < n_col...  3.01 us
    dynamic_slice x1, local copies, waits for them, and re-layouts, chip_columns(): return lax.dynamic_slice_in_dim(amplitudes, start, 2 * depth, 1)  1.11 us
  transfers between devices with their start and end apart: 15, of which 8 were waited for; matrix products, arithmetic and copies ran while one was open for 3% of the time, Pallas kernels for 11%

profile of v12, /device:TPU:0, one launch (start us, length us, event | category | flops | bytes accessed | tf_op | source)
XLA Modules:
  0.0 43.0 jit_solution(12076905017007317670)
XLA Ops:
  0.0 0.5 %collective-permute-start.2 = (f32[384,384]{1,0:T(8,128)}, f32[384,384]{1,0:T(8,128)S(1)}, u32[]{:S(2)}, u32[]{:S(2)}) collective-permute-start(f32[384,384]{1,0:T(8,128)} %refs_3_.3), channel_id=1, source_target_pairs={{0,4},{1,2},{2,1},{3,7},{4,0},{5,6},{6,5},{7,3},{8,12},{9,10},{10,... | collective-permute-start | bytes 1769480 | tf_op jit(solution)/shard_map/ppermute | solution.py:270
  0.5 4.1 %collective-permute-start.4 = (f32[384,384]{1,0:T(8,128)}, f32[384,384]{1,0:T(8,128)S(1)}, u32[]{:S(2)}, u32[]{:S(2)}) collective-permute-start(f32[384,384]{1,0:T(8,128)} %refs_3_.3), channel_id=1, source_target_pairs={{0,1},{1,0},{2,3},{3,2},{4,5},{5,4},{6,7},{7,6},{8,9},{9,8},{10,11... | collective-permute-start | bytes 1769480 | tf_op jit(solution)/shard_map/ppermute | solution.py:270
  4.6 1.1 %constant_dynamic-slice_fusion = (f32[64,768]{1,0:T(8,128)S(1)}, f32[64,768]{1,0:T(8,128)S(1)}) fusion(f32[64,1536]{1,0:T(8,128)} %param.5, s32[]{:T(128)S(6)} %select_n.14, s32[]{:T(128)S(6)} %select_n.13), kind=kLoop, calls=%fused_computation.2 | loop fusion | bytes 786440 | tf_op jit(solution)/shard_map/dynamic_slice | solution.py:298
  5.7 1.6 %collective-permute-start = (f32[64,768]{1,0:T(8,128)S(1)}, f32[64,768]{1,0:T(8,128)S(1)}, u32[]{:S(2)}, u32[]{:S(2)}) collective-permute-start(f32[64,768]{1,0:T(8,128)S(1)} %get-tuple-element.77), channel_id=1, source_target_pairs={{0,8},{4,12},{8,0},{12,4},{1,9},{5,13},{9,1},{13,5},{2,10},{6,14},... | collective-permute-start | bytes 589832 | tf_op jit(solution)/shard_map/ppermute | solution.py:273
  7.3 0.1 copy.6.refs_1_
  7.4 0.1 pad_add_fusion.refs_0_
  7.4 0.5 %copy-done.1 = s32[16,16]{1,0:T(8,128)S(1)} copy-done((s32[16,16]{1,0:T(8,128)S(1)}, s32[16,16]{1,0:T(8,128)}, u32[]{:S(2)}) %copy-start.1) | copy-done | bytes 1048
  8.0 2.0 %tables.1 = (f32[8,384]{1,0:T(8,128)S(1)}, f32[8,384]{1,0:T(8,128)S(1)}, f32[4,384]{1,0:T(4,128)S(1)}, f32[16,384]{1,0:T(8,128)S(1)}, f32[4,384]{1,0:T(4,128)S(1...) custom-call(s32[3]{0:T(128)S(1)} %pad_add_fusion.refs_0_, ...), custom_call_target="tpu_custom_call" | custom-call | bytes 212044 | tf_op jit(solution)/shard_map/tables/pallas_call | solution.py:236
  10.0 1.8 %collective-permute-done.refs_2_ = f32[64,768]{1,0:T(8,128)S(1)} collective-permute-done((f32[64,768]{1,0:T(8,128)S(1)}, f32[64,768]{1,0:T(8,128)S(1)}, u32[]{:S(2)}, u32[]{:S(2)}) %collective-permute-start) | collective-permute-done | bytes 196640 | tf_op jit(solution)/shard_map/ppermute | solution.py:273
  12.0 1.4 %collective-permute-done.1.refs_2_ = f32[128,384]{1,0:T(8,128)S(1)} collective-permute-done((f32[128,384]{1,0:T(8,128)S(1)}, f32[128,384]{1,0:T(8,128)S(1)}, u32[]{:S(2)}, u32[]{:S(2)}) %collective-permute-start.1) | collective-permute-done | bytes 196640 | tf_op jit(solution)/shard_map/ppermute | solution.py:273
  13.4 0.6 %own.1 = (bf16[256,384]{1,0:T(8,128)(2,1)S(1)}, bf16[256,384]{1,0:T(8,128)(2,1)S(1)}, f32[384,384]{1,0:T(8,128)S(1)}, f32[128,384]{1,0:T(8,128)S(1)}, f32[128,384]{1,0:T(8,128)S(1)}) custom-call(f32[8,384]{1,0:T(8,128)S(1)} %get-tuple-element.43.refs_0_, f32[128,384]{1,0:T(8,128)S(1)} %get-tuple-element.44.refs_1_, ...), custom_call_target="tpu_custom_call" | custom-call | flops 226492416 | bytes 2377728 | tf_op jit(solution)/shard_map/own/pallas_call | solution.py:236
  14.1 4.4 %collective-permute-start.3 = (f32[384,384]{1,0:T(8,128)S(1)}, f32[384,384]{1,0:T(8,128)S(1)}, u32[]{:S(2)}, u32[]{:S(2)}) collective-permute-start(f32[384,384]{1,0:T(8,128)S(1)} %pick.1), channel_id=1, source_target_pairs={{0,1},{1,0},{2,3},{3,2},{4,5},{5,4},{6,7},{7,6},{8,9},{9,8},{10,11... | collective-permute-start | bytes 1769480 | tf_op jit(solution)/shard_map/ppermute | solution.py:270
  18.4 0.9 %pair.1 = (f32[128,768]{1,0:T(8,128)S(1)}, f32[128,768]{1,0:T(8,128)S(1)}) custom-call(bf16[256,384]{1,0:T(8,128)(2,1)S(1)} %get-tuple-element.56.refs_0_, bf16[256,384]{1,0:T(8,128)(2,1)S(1)} %get-tuple-element.57.refs_1_, f32[384,384]{1,0:T(8,128)S(1)} %collective-permute-done.4.refs_2_, f32[4,384]{1,0:T(4,128)S(1)} %get-tuple-element.58.refs_3_, ...), custom_call_target="tpu_custom_call" | custom-call | flops 452984832 | bytes 2371584 | tf_op jit(solution)/shard_map/pair/pallas_call | solution.py:236
  19.4 0.6 %collective-permute-start.8 = (f32[128,768]{1,0:T(8,128)S(1)}, f32[128,768]{1,0:T(8,128)S(1)}, u32[]{:S(2)}, u32[]{:S(2)}) collective-permute-start(f32[128,768]{1,0:T(8,128)S(1)} %get-tuple-element.61), channel_id=1, source_target_pairs={{0,4},{4,0},{8,12},{12,8},{1,5},{5,1},{9,13},{13,9},{2,6},{6,2},{1... | collective-permute-start | bytes 1179656 | tf_op jit(solution)/shard_map/ppermute | solution.py:273
  20.0 0.1 collective-permute-start.6
  20.0 1.6 %collective-permute-done.6.refs_1_ = f32[128,384]{1,0:T(8,128)S(1)} collective-permute-done((f32[128,384]{1,0:T(8,128)S(1)}, f32[128,384]{1,0:T(8,128)S(1)}, u32[]{:S(2)}, u32[]{:S(2)}) %collective-permute-start.6) | collective-permute-done | bytes 196640 | tf_op jit(solution)/shard_map/ppermute | solution.py:273
  21.6 1.6 %collective-permute-start.7 = (f32[64,384]{1,0:T(8,128)S(1)}, f32[64,384]{1,0:T(8,128)S(1)}, u32[]{:S(2)}, u32[]{:S(2)}) collective-permute-start(f32[64,384]{1,0:T(8,128)S(1)} %get-tuple-element.55), channel_id=1, source_target_pairs={{0,8},{4,12},{8,0},{12,4},{1,9},{5,13},{9,1},{13,5},{2,10},{6,14},... | collective-permute-start | bytes 294920 | tf_op jit(solution)/shard_map/ppermute | solution.py:273
  23.2 0.6 %collective-permute-start.9 = (f32[64,768]{1,0:T(8,128)S(1)}, f32[64,768]{1,0:T(8,128)S(1)}, u32[]{:S(2)}, u32[]{:S(2)}) collective-permute-start(f32[64,768]{1,0:T(8,128)S(1)} %get-tuple-element.63), channel_id=1, source_target_pairs={{0,8},{4,12},{8,0},{12,4},{1,9},{5,13},{9,1},{13,5},{2,10},{6,14},... | collective-permute-start | bytes 589832 | tf_op jit(solution)/shard_map/ppermute | solution.py:273
  23.8 7.1 %collective-permute-done.3.refs_0_.refs_2_ = f32[384,384]{1,0:T(8,128)S(1)} collective-permute-done((f32[384,384]{1,0:T(8,128)S(1)}, f32[384,384]{1,0:T(8,128)S(1)}, u32[]{:S(2)}, u32[]{:S(2)}) %collective-permute-start.3) | collective-permute-done | bytes 589856 | tf_op jit(solution)/shard_map/ppermute | solution.py:270
  30.9 0.1 halves.1
  31.1 0.5 %corner.1 = (f32[128,384]{1,0:T(8,128)S(1)}, f32[128,384]{1,0:T(8,128)S(1)}) custom-call(bf16[384,384]{1,0:T(8,128)(2,1)S(1)} %get-tuple-element.50.refs_0_.refs_2_, bf16[384,384]{1,0:T(8,128)(2,1)S(1)} %get-tuple-element.51.refs_1_.refs_3_, f32[384,384]{1,0:T(8,128)S(1)} %collective-permute-done.3.refs_0_.refs_2_, ...), custom_call_target="tpu_custom_call" | custom-call | flops 226492416 | bytes 1572864 | tf_op jit(solution)/shard_map/corner/pallas_call | solution.py:236
  31.7 0.5 %last.1 = (f32[128,384]{1,0:T(8,128)S(1)}, f32[128,384]{1,0:T(8,128)S(1)}) custom-call(bf16[256,384]{1,0:T(8,128)(2,1)S(1)} %get-tuple-element.56.refs_0_, bf16[256,384]{1,0:T(8,128)(2,1)S(1)} %get-tuple-element.57.refs_1_, bf16[384,384]{1,0:T(8,128)(2,1)S(1)} %get-tuple-element.50.refs_0_.refs_2_, bf16[384,384]{1,0:T(8,128)(2,1)S(1)} %get-tuple-element.51.refs_1_.refs_3_, ...), custom_call_target="tpu_custom_call" | custom-call | flops 226492416 | bytes 1376256 | tf_op jit(solution)/shard_map/last/pallas_call | solution.py:236
  32.2 0.6 %collective-permute-start.13 = (f32[128,384]{1,0:T(8,128)S(1)}, f32[128,384]{1,0:T(8,128)S(1)}, u32[]{:S(2)}, u32[]{:S(2)}) collective-permute-start(f32[128,384]{1,0:T(8,128)S(1)} %get-tuple-element.71), channel_id=1, source_target_pairs={{0,4},{4,0},{8,12},{12,8},{1,5},{5,1},{9,13},{13,9},{2,6},{6,2},{1... | collective-permute-start | bytes 589832 | tf_op jit(solution)/shard_map/ppermute | solution.py:273
  32.8 0.3 collective-permute-done.10.refs_1_
  33.1 2.6 %collective-permute-start.11 = (f32[64,384]{1,0:T(8,128)S(1)}, f32[64,384]{1,0:T(8,128)S(1)}, u32[]{:S(2)}, u32[]{:S(2)}) collective-permute-start(f32[64,384]{1,0:T(8,128)S(1)} %get-tuple-element.66), channel_id=1, source_target_pairs={{0,1},{1,8},{2,11},{3,2},{4,5},{5,12},{6,15},{7,6},{8,9},{9,0},{10... | collective-permute-start | bytes 294920 | tf_op jit(solution)/shard_map/ppermute | solution.py:314
  35.8 0.4 collective-permute-start.12
  36.2 1.3 %collective-permute-start.14 = (f32[64,384]{1,0:T(8,128)S(1)}, f32[64,384]{1,0:T(8,128)S(1)}, u32[]{:S(2)}, u32[]{:S(2)}) collective-permute-start(f32[64,384]{1,0:T(8,128)S(1)} %get-tuple-element.73), channel_id=1, source_target_pairs={{0,8},{4,12},{8,0},{12,4},{1,9},{5,13},{9,1},{13,5},{2,10},{6,14},... | collective-permute-start | bytes 294920 | tf_op jit(solution)/shard_map/ppermute | solution.py:273
  37.4 0.5 %finish.2.refs_6_ = f32[64,1536]{1,0:T(8,128)S(1)} custom-call(f32[16,384]{1,0:T(8,128)S(1)} %get-tuple-element.74.refs_0_, f32[64,384]{1,0:T(8,128)S(1)} %get-tuple-element.54.refs_3_.refs_4_.refs_1_, f32[64,384]{1,0:T(8,128)S(1)} %collective-permute-done.7.refs_4_.refs_5_.refs_2_, f32[32,384]{1,0:T(8,128)S(1)} %pad_maximum_fusion.refs_3_, ...), custom_call_target="tpu_custom_call" | custom-call | flops 393216 | bytes 1056768 | tf_op jit(solution)/shard_map/finish/pallas_call | solution.py:236
  37.9 2.4 %collective-permute-done.11.refs_1_ = f32[64,384]{1,0:T(8,128)S(1)} collective-permute-done((f32[64,384]{1,0:T(8,128)S(1)}, f32[64,384]{1,0:T(8,128)S(1)}, u32[]{:S(2)}, u32[]{:S(2)}) %collective-permute-start.11) | collective-permute-done | bytes 98336 | tf_op jit(solution)/shard_map/ppermute | solution.py:314
  40.3 0.8 %collective-permute-done.12.refs_2_ = f32[64,384]{1,0:T(8,128)S(1)} collective-permute-done((f32[64,384]{1,0:T(8,128)S(1)}, f32[64,384]{1,0:T(8,128)S(1)}, u32[]{:S(2)}, u32[]{:S(2)}) %collective-permute-start.12) | collective-permute-done | bytes 98336 | tf_op jit(solution)/shard_map/ppermute | solution.py:314
  41.1 0.8 %collective-permute-done.14.refs_5_ = f32[64,384]{1,0:T(8,128)S(1)} collective-permute-done((f32[64,384]{1,0:T(8,128)S(1)}, f32[64,384]{1,0:T(8,128)S(1)}, u32[]{:S(2)}, u32[]{:S(2)}) %collective-permute-start.14) | collective-permute-done | bytes 98336 | tf_op jit(solution)/shard_map/ppermute | solution.py:273
  41.9 1.1 %finish.3 = f32[64,1536]{1,0:T(8,128)} custom-call(f32[16,384]{1,0:T(8,128)S(1)} %get-tuple-element.41.refs_0_, f32[64,384]{1,0:T(8,128)S(1)} %collective-permute-done.11.refs_1_, f32[64,384]{1,0:T(8,128)S(1)} %collective-permute-done.12.refs_2_, f32[16,384]{1,0:T(8,128)S(1)} %add.12.refs_3_, f32[64,384]{1,0:T(8,128)S(1)} %get-tuple-element.72.refs_4_, ...), custom_call_target="tpu_custom_call" | custom-call | flops 393216 | bytes 1228800 | tf_op jit(solution)/shard_map/finish/pallas_call | solution.py:236
  (25 shorter events, 0.4 us)
Async XLA Ops:
  0.0 14.0 %collective-permute-start.2 = (f32[384,384]{1,0:T(8,128)}, f32[384,384]{1,0:T(8,128)S(1)}, u32[]{:S(2)}, u32[]{:S(2)}) collective-permute-start(f32[384,384]{1,0:T(8,128)} %refs_3_.3), channel_id=1, source_target_pairs={{0,4},{1,2},{2,1},{3,7},{4,0},{5,6},{6,5},{7,3},{8,12},{9,10},{10,... | collective-permute-start | bytes 1769480 | tf_op jit(solution)/shard_map/ppermute | solution.py:270
  0.5 18.0 %collective-permute-start.4 = (f32[384,384]{1,0:T(8,128)}, f32[384,384]{1,0:T(8,128)S(1)}, u32[]{:S(2)}, u32[]{:S(2)}) collective-permute-start(f32[384,384]{1,0:T(8,128)} %refs_3_.3), channel_id=1, source_target_pairs={{0,1},{1,0},{2,3},{3,2},{4,5},{5,4},{6,7},{7,6},{8,9},{9,8},{10,11... | collective-permute-start | bytes 1769480 | tf_op jit(solution)/shard_map/ppermute | solution.py:270
  4.6 2.7 %copy-start.3 = (s32[32,16]{0,1:T(8,128)S(1)}, s32[32,16]{0,1:T(8,128)}, u32[]{:S(2)}) copy-start(s32[32,16]{0,1:T(8,128)} %param.7) | copy-start | bytes 6148
  4.6 8.8 %copy-start = (f32[384,384]{1,0:T(8,128)S(1)}, f32[384,384]{1,0:T(8,128)}, u32[]{:S(2)}) copy-start(f32[384,384]{1,0:T(8,128)} %refs_3_.3) | copy-start | bytes 1769476
  5.7 6.1 %collective-permute-start = (f32[64,768]{1,0:T(8,128)S(1)}, f32[64,768]{1,0:T(8,128)S(1)}, u32[]{:S(2)}, u32[]{:S(2)}) collective-permute-start(f32[64,768]{1,0:T(8,128)S(1)} %get-tuple-element.77), channel_id=1, source_target_pairs={{0,8},{4,12},{8,0},{12,4},{1,9},{5,13},{9,1},{13,5},{2,10},{6,14},... | collective-permute-start | bytes 589832 | tf_op jit(solution)/shard_map/ppermute | solution.py:273
  7.3 0.7 %copy-start.1 = (s32[16,16]{1,0:T(8,128)S(1)}, s32[16,16]{1,0:T(8,128)}, u32[]{:S(2)}) copy-start(s32[16,16]{1,0:T(8,128)} %refs_2_.1) | copy-start | bytes 3076
  7.4 0.7 %copy-start.2 = (s32[16]{0:T(128)S(1)}, s32[16]{0:T(128)}, u32[]{:S(2)}) copy-start(s32[16]{0:T(128)} %refs_3_.2) | copy-start | bytes 196
  11.9 1.5 %collective-permute-start.1 = (f32[128,384]{1,0:T(8,128)S(1)}, f32[128,384]{1,0:T(8,128)S(1)}, u32[]{:S(2)}, u32[]{:S(2)}) collective-permute-start(f32[128,384]{1,0:T(8,128)S(1)} %get-tuple-element.45), channel_id=1, source_target_pairs={{0,4},{4,0},{8,12},{12,8},{1,5},{5,1},{9,13},{13,9},{2,6},{6,2},{1... | collective-permute-start | bytes 589832 | tf_op jit(solution)/shard_map/ppermute | solution.py:273
  14.1 16.8 %collective-permute-start.3 = (f32[384,384]{1,0:T(8,128)S(1)}, f32[384,384]{1,0:T(8,128)S(1)}, u32[]{:S(2)}, u32[]{:S(2)}) collective-permute-start(f32[384,384]{1,0:T(8,128)S(1)} %pick.1), channel_id=1, source_target_pairs={{0,1},{1,0},{2,3},{3,2},{4,5},{5,4},{6,7},{7,6},{8,9},{9,8},{10,11... | collective-permute-start | bytes 1769480 | tf_op jit(solution)/shard_map/ppermute | solution.py:270
  18.4 12.5 %collective-permute-start.5 = (f32[384,384]{1,0:T(8,128)S(1)}, f32[384,384]{1,0:T(8,128)S(1)}, u32[]{:S(2)}, u32[]{:S(2)}) collective-permute-start(f32[384,384]{1,0:T(8,128)S(1)} %collective-permute-done.4.refs_2_), channel_id=1, source_target_pairs={{0,4},{1,2},{2,1},{3,7},{4,0},{5,6},{6,5},{7,3},{8,12},{9,10},{10,... | collective-permute-start | bytes 1769480 | tf_op jit(solution)/shard_map/ppermute | solution.py:270
  19.4 3.8 %collective-permute-start.8 = (f32[128,768]{1,0:T(8,128)S(1)}, f32[128,768]{1,0:T(8,128)S(1)}, u32[]{:S(2)}, u32[]{:S(2)}) collective-permute-start(f32[128,768]{1,0:T(8,128)S(1)} %get-tuple-element.61), channel_id=1, source_target_pairs={{0,4},{4,0},{8,12},{12,8},{1,5},{5,1},{9,13},{13,9},{2,6},{6,2},{1... | collective-permute-start | bytes 1179656 | tf_op jit(solution)/shard_map/ppermute | solution.py:273
  20.0 1.6 %collective-permute-start.6 = (f32[128,384]{1,0:T(8,128)S(1)}, f32[128,384]{1,0:T(8,128)S(1)}, u32[]{:S(2)}, u32[]{:S(2)}) collective-permute-start(f32[128,384]{1,0:T(8,128)S(1)} %get-tuple-element.53), channel_id=1, source_target_pairs={{0,4},{4,0},{8,12},{12,8},{1,5},{5,1},{9,13},{13,9},{2,6},{6,2},{1... | collective-permute-start | bytes 589832 | tf_op jit(solution)/shard_map/ppermute | solution.py:273
  21.6 9.4 %collective-permute-start.7 = (f32[64,384]{1,0:T(8,128)S(1)}, f32[64,384]{1,0:T(8,128)S(1)}, u32[]{:S(2)}, u32[]{:S(2)}) collective-permute-start(f32[64,384]{1,0:T(8,128)S(1)} %get-tuple-element.55), channel_id=1, source_target_pairs={{0,8},{4,12},{8,0},{12,4},{1,9},{5,13},{9,1},{13,5},{2,10},{6,14},... | collective-permute-start | bytes 294920 | tf_op jit(solution)/shard_map/ppermute | solution.py:273
  23.2 7.8 %collective-permute-start.9 = (f32[64,768]{1,0:T(8,128)S(1)}, f32[64,768]{1,0:T(8,128)S(1)}, u32[]{:S(2)}, u32[]{:S(2)}) collective-permute-start(f32[64,768]{1,0:T(8,128)S(1)} %get-tuple-element.63), channel_id=1, source_target_pairs={{0,8},{4,12},{8,0},{12,4},{1,9},{5,13},{9,1},{13,5},{2,10},{6,14},... | collective-permute-start | bytes 589832 | tf_op jit(solution)/shard_map/ppermute | solution.py:273
  31.6 1.5 %collective-permute-start.10 = (f32[128,384]{1,0:T(8,128)S(1)}, f32[128,384]{1,0:T(8,128)S(1)}, u32[]{:S(2)}, u32[]{:S(2)}) collective-permute-start(f32[128,384]{1,0:T(8,128)S(1)} %get-tuple-element.65), channel_id=1, source_target_pairs={{0,4},{4,0},{8,12},{12,8},{1,5},{5,1},{9,13},{13,9},{2,6},{6,2},{1... | collective-permute-start | bytes 589832 | tf_op jit(solution)/shard_map/ppermute | solution.py:273
  32.2 3.9 %collective-permute-start.13 = (f32[128,384]{1,0:T(8,128)S(1)}, f32[128,384]{1,0:T(8,128)S(1)}, u32[]{:S(2)}, u32[]{:S(2)}) collective-permute-start(f32[128,384]{1,0:T(8,128)S(1)} %get-tuple-element.71), channel_id=1, source_target_pairs={{0,4},{4,0},{8,12},{12,8},{1,5},{5,1},{9,13},{13,9},{2,6},{6,2},{1... | collective-permute-start | bytes 589832 | tf_op jit(solution)/shard_map/ppermute | solution.py:273
  33.1 7.1 %collective-permute-start.11 = (f32[64,384]{1,0:T(8,128)S(1)}, f32[64,384]{1,0:T(8,128)S(1)}, u32[]{:S(2)}, u32[]{:S(2)}) collective-permute-start(f32[64,384]{1,0:T(8,128)S(1)} %get-tuple-element.66), channel_id=1, source_target_pairs={{0,1},{1,8},{2,11},{3,2},{4,5},{5,12},{6,15},{7,6},{8,9},{9,0},{10... | collective-permute-start | bytes 294920 | tf_op jit(solution)/shard_map/ppermute | solution.py:314
  35.8 5.3 %collective-permute-start.12 = (f32[64,384]{1,0:T(8,128)S(1)}, f32[64,384]{1,0:T(8,128)S(1)}, u32[]{:S(2)}, u32[]{:S(2)}) collective-permute-start(f32[64,384]{1,0:T(8,128)S(1)} %get-tuple-element.67), channel_id=1, source_target_pairs={{0,1},{1,0},{2,3},{3,2},{4,5},{5,4},{6,7},{7,6},{8,9},{9,8},{10,11... | collective-permute-start | bytes 294920 | tf_op jit(solution)/shard_map/ppermute | solution.py:314
  36.2 5.7 %collective-permute-start.14 = (f32[64,384]{1,0:T(8,128)S(1)}, f32[64,384]{1,0:T(8,128)S(1)}, u32[]{:S(2)}, u32[]{:S(2)}) collective-permute-start(f32[64,384]{1,0:T(8,128)S(1)} %get-tuple-element.73), channel_id=1, source_target_pairs={{0,8},{4,12},{8,0},{12,4},{1,9},{5,13},{9,1},{13,5},{2,10},{6,14},... | collective-permute-start | bytes 294920 | tf_op jit(solution)/shard_map/ppermute | solution.py:273

commit v13 on v12

--- a/solution.py
+++ b/solution.py
@@ -14,7 +14,7 @@
 
 VMEM = pl.BlockSpec(memory_space=pltpu.VMEM)
 SMEM = pl.BlockSpec(memory_space=pltpu.SMEM)
-EVEN, ODD, OWN, CORNER = 0, 1, 2, 3
+EVEN, ODD, OWN, RING, ACROSS = 0, 1, 2, 3, 4
 WEIGHT = 10**10
 
 
@@ -34,8 +34,10 @@
 def source_of(kind, step, c):
     if kind == OWN:
         return c
-    if kind == CORNER:
-        return jnp.where(c == 0, step, jnp.where(c == step, 0, -1))
+    if kind == ACROSS:
+        return c ^ step
+    if kind == RING:
+        return jnp.where(c % 2 == 1, (c + 1) % step, (c + step - 1) % step)
     up = (c % 2) == kind
     return jnp.where(up, c + step, c - step)
 
@@ -261,11 +263,14 @@
     place = jnp.stack([r, c, jnp.int32(n_col)]).astype(jnp.int32)
     order = list(range(0, n_row, 2)) + list(range(1, n_row, 2))
 
+    ring = n_col == 4
+
     def swap_line(x, kind):
         pairs_ = []
         for i in range(n_row):
             for j in range(n_col):
                 to = ((j + kind) ^ 1) - kind
+                to = to % n_col if ring else to
                 pairs_.append((i * n_col + j, i * n_col + to if 0 <= to < n_col else (i ^ 1) * n_col + j))
         return lax.ppermute(x, ("row", "col"), pairs_)
 
@@ -275,10 +280,12 @@
     k_tiles, tiles = depth // TB, pairs // TB
     even = [swap_line(integrals, EVEN)]
     odd = [swap_line(integrals, ODD)]
-    corner = n_col == 4 and total <= depth and depth == width
-    last = n_col - 2 if corner else n_col - 1
+    corner = False
+    last = n_col - 1
     kinds = [(OWN, 0)] + [(kind, step) for step in range(1, last + 1) for kind in (EVEN, ODD)]
-    ends = (CORNER, n_col - 1)
+    if ring:
+        kinds = [(OWN, 0), (EVEN, 1), (RING, n_col), (ACROSS, 2)]
+    ends = kinds[0]
     per_slot = [f32(k_tiles, width), f32(width // GROUP * tiles, GROUP)]
     amp_rows, marks, *made = call(
         functools.partial(tables_kernel, order, kinds + [ends]),
@@ -368,6 +375,12 @@
         flops=6 * total * depth * width,
     )
     slots = [([[(OWN, 0)]], exchange(keep, give))]
+    if ring:
+        slots.append(multiply("pair", [((EVEN, 1), even)], [((RING, n_col), odd)]))
+        part = depth // 2
+        parts = [swap_line(odd[0][:part, :], EVEN), swap_line(even[0][part:, :], ODD)]
+        slots.append(multiply("across", [((ACROSS, 2), parts)]))
+        return finish(slots)
     for step in range(1, last + 1):
         if step > 1:
             going = list(odd)

time: 43.2 us -> 59.6 us (1.38)
  waiting for transfers between devices: 16.2 us -> 26.7 us
  starting transfers between devices: 18.3 us -> 24.7 us
    ppermute x4, starting transfers between devices: 8.97 us -> 18.7 us  [swap_line(): return lax.ppermute(x, ('row', 'col'), pairs_)]
    ppermute x4, waiting for transfers between devices: 7.06 us -> 15.3 us  [swap_line(): return lax.ppermute(x, ('row', 'col'), pairs_)]
    ppermute x9 -> x8, waiting for transfers between devices: 6 us -> 11.4 us  [swap(): return lax.ppermute(x, 'row', [(i, i ^ d) for i in range(n_row)])]
    ppermute x2 -> x0, waiting for transfers between devices: 3.16 us -> none  [next_door(): lax.ppermute(x, ('row', 'col'), [(i * n_col + j, (i ^ (d if 0 < j < n_col...]
    ppermute x2 -> x0, starting transfers between devices: 3.01 us -> none  [next_door(): lax.ppermute(x, ('row', 'col'), [(i * n_col + j, (i ^ (d if 0 < j < n_col...]
    pallas_call x14 -> x9, Pallas kernels: 6.48 us -> 6.03 us  [call(): pl.pallas_call(body, out_shape=outs, in_specs=[SMEM] * n_smem + [VMEM] *...]
    ppermute x9 -> x8, starting transfers between devices: 6.34 us -> 5.98 us  [swap(): return lax.ppermute(x, 'row', [(i, i ^ d) for i in range(n_row)])]
  transfers between devices with their start and end apart: 15 -> 12, of which waited for: 8 -> 8; matrix products, arithmetic and copies ran while one was open for 3% -> 2% of each run, Pallas kernels for 11% -> 8%
where the time goes in v13:
time: 59.6 us; the launch traced here: 59.4 us
  waiting for transfers between devices  26.7 us (45%)
  starting transfers between devices  24.7 us (41%)
  Pallas kernels  6.03 us (10%)
  local copies, waits for them, and re-layouts  1.81 us (3%)
    ppermute x4, starting transfers between devices, swap_line(): return lax.ppermute(x, ('row', 'col'), pairs_)  18.7 us
    ppermute x4, waiting for transfers between devices, swap_line(): return lax.ppermute(x, ('row', 'col'), pairs_)  15.3 us
    ppermute x8, waiting for transfers between devices, swap(): return lax.ppermute(x, 'row', [(i, i ^ d) for i in range(n_row)])  11.4 us
    pallas_call x9, Pallas kernels, call(): pl.pallas_call(body, out_shape=outs, in_specs=[SMEM] * n_smem + [VMEM] *...  6.03 us
    ppermute x8, starting transfers between devices, swap(): return lax.ppermute(x, 'row', [(i, i ^ d) for i in range(n_row)])  5.98 us
  transfers between devices with their start and end apart: 12, of which 8 were waited for; matrix products, arithmetic and copies ran while one was open for 2% of the time, Pallas kernels for 8%

profile of v13, /device:TPU:0, one launch (start us, length us, event | category | flops | bytes accessed | tf_op | source)
XLA Modules:
  0.0 59.4 jit_solution(13257601431040078046)
XLA Ops:
  0.0 5.0 %collective-permute-start.5 = (f32[384,384]{1,0:T(8,128)}, f32[384,384]{1,0:T(8,128)S(1)}, u32[]{:S(2)}, u32[]{:S(2)}) collective-permute-start(f32[384,384]{1,0:T(8,128)} %refs_3_.3), channel_id=1, source_target_pairs={{0,3},{1,2},{2,1},{3,0},{4,7},{5,6},{6,5},{7,4},{8,11},{9,10},{10,... | collective-permute-start | bytes 1769480 | tf_op jit(solution)/shard_map/ppermute | solution.py:275
  5.0 0.0 collective-permute-start.4
  5.1 1.1 %constant_dynamic-slice_fusion = (f32[64,768]{1,0:T(8,128)S(1)}, f32[64,768]{1,0:T(8,128)S(1)}) fusion(f32[64,1536]{1,0:T(8,128)} %param.5, s32[]{:T(128)S(6)} %select_n.14, s32[]{:T(128)S(6)} %select_n.13), kind=kLoop, calls=%fused_computation.2 | loop fusion | bytes 786440 | tf_op jit(solution)/shard_map/dynamic_slice | solution.py:305
  6.2 1.6 %collective-permute-start = (f32[64,768]{1,0:T(8,128)S(1)}, f32[64,768]{1,0:T(8,128)S(1)}, u32[]{:S(2)}, u32[]{:S(2)}) collective-permute-start(f32[64,768]{1,0:T(8,128)S(1)} %get-tuple-element.57), channel_id=1, source_target_pairs={{0,8},{4,12},{8,0},{12,4},{1,9},{5,13},{9,1},{13,5},{2,10},{6,14},... | collective-permute-start | bytes 589832 | tf_op jit(solution)/shard_map/ppermute | solution.py:278
  7.7 0.1 copy.6.refs_1_
  7.8 0.1 pad_add_fusion.refs_0_
  7.9 0.5 copy-done.1
  8.4 0.0 copy-done.2
  8.5 2.0 %tables.1 = (f32[8,384]{1,0:T(8,128)S(1)}, f32[8,384]{1,0:T(8,128)S(1)}, f32[4,384]{1,0:T(4,128)}, f32[16,384]{1,0:T(8,128)}, f32[4,384]{1,0:T(4,128)S(1)}, /*in...) custom-call(s32[3]{0:T(128)S(1)} %pad_add_fusion.refs_0_, ...), custom_call_target="tpu_custom_call" | custom-call | bytes 181324 | tf_op jit(solution)/shard_map/tables/pallas_call | solution.py:238
  10.4 2.2 %collective-permute-done.refs_2_ = f32[64,768]{1,0:T(8,128)S(1)} collective-permute-done((f32[64,768]{1,0:T(8,128)S(1)}, f32[64,768]{1,0:T(8,128)S(1)}, u32[]{:S(2)}, u32[]{:S(2)}) %collective-permute-start) | collective-permute-done | bytes 196640 | tf_op jit(solution)/shard_map/ppermute | solution.py:278
  12.6 0.1 collective-permute-start.1
  12.7 1.4 %collective-permute-done.1.refs_2_ = f32[128,384]{1,0:T(8,128)S(1)} collective-permute-done((f32[128,384]{1,0:T(8,128)S(1)}, f32[128,384]{1,0:T(8,128)S(1)}, u32[]{:S(2)}, u32[]{:S(2)}) %collective-permute-start.1) | collective-permute-done | bytes 196640 | tf_op jit(solution)/shard_map/ppermute | solution.py:278
  14.1 1.1 %own.1 = (bf16[256,384]{1,0:T(8,128)(2,1)S(1)}, bf16[256,384]{1,0:T(8,128)(2,1)S(1)}, f32[256,384]{1,0:T(8,128)}, f32[128,384]{1,0:T(8,128)S(1)}, f32[128,384]{1,0:T(8,128)S(1)}) custom-call(f32[8,384]{1,0:T(8,128)S(1)} %get-tuple-element.32.refs_0_, f32[128,384]{1,0:T(8,128)S(1)} %get-tuple-element.34.refs_1_, ...), custom_call_target="tpu_custom_call" | custom-call | flops 226492416 | bytes 2181120 | tf_op jit(solution)/shard_map/own/pallas_call | solution.py:238
  15.3 4.2 %collective-permute-done.5.refs_4_ = f32[384,384]{1,0:T(8,128)S(1)} collective-permute-done((f32[384,384]{1,0:T(8,128)}, f32[384,384]{1,0:T(8,128)S(1)}, u32[]{:S(2)}, u32[]{:S(2)}) %collective-permute-start.5) | collective-permute-done | bytes 589856 | tf_op jit(solution)/shard_map/ppermute | solution.py:275
  19.5 11.5 %collective-permute-start.8 = (f32[192,384]{1,0:T(8,128)S(1)}, f32[192,384]{1,0:T(8,128)S(1)}, u32[]{:S(2)}, u32[]{:S(2)}) collective-permute-start(f32[192,384]{1,0:T(8,128)S(1)} %slice.8), channel_id=1, source_target_pairs={{0,1},{1,0},{2,3},{3,2},{4,5},{5,4},{6,7},{7,6},{8,9},{9,8},{10,11... | collective-permute-start | bytes 884744 | tf_op jit(solution)/shard_map/ppermute | solution.py:275
  31.0 0.4 collective-permute-done.4.refs_2_
  31.4 2.2 %collective-permute-start.9 = (f32[192,384]{1,0:T(8,128)S(1)}, f32[192,384]{1,0:T(8,128)S(1)}, u32[]{:S(2)}, u32[]{:S(2)}) collective-permute-start(f32[192,384]{1,0:T(8,128)S(1)} %slice.9), channel_id=1, source_target_pairs={{0,3},{1,2},{2,1},{3,0},{4,7},{5,6},{6,5},{7,4},{8,11},{9,10},{10,... | collective-permute-start | bytes 884744 | tf_op jit(solution)/shard_map/ppermute | solution.py:275
  33.6 0.9 %pair.1 = (f32[128,768]{1,0:T(8,128)S(1)}, f32[128,768]{1,0:T(8,128)S(1)}) custom-call(bf16[256,384]{1,0:T(8,128)(2,1)S(1)} %get-tuple-element.43.refs_0_, bf16[256,384]{1,0:T(8,128)(2,1)S(1)} %get-tuple-element.44.refs_1_, f32[384,384]{1,0:T(8,128)S(1)} %collective-permute-done.4.refs_2_, f32[4,384]{1,0:T(4,128)S(1)} %get-tuple-element.45.refs_3_, ...), custom_call_target="tpu_custom_call" | custom-call | flops 452984832 | bytes 2371584 | tf_op jit(solution)/shard_map/pair/pallas_call | solution.py:238
  34.5 0.1 collective-permute-start.6
  34.6 0.5 collective-permute-start.2
  35.1 3.4 %collective-permute-done.8.refs_2_ = f32[192,384]{1,0:T(8,128)S(1)} collective-permute-done((f32[192,384]{1,0:T(8,128)S(1)}, f32[192,384]{1,0:T(8,128)S(1)}, u32[]{:S(2)}, u32[]{:S(2)}) %collective-permute-start.8) | collective-permute-done | bytes 294944 | tf_op jit(solution)/shard_map/ppermute | solution.py:275
  38.5 7.3 %collective-permute-done.9.refs_3_ = f32[192,384]{1,0:T(8,128)S(1)} collective-permute-done((f32[192,384]{1,0:T(8,128)S(1)}, f32[192,384]{1,0:T(8,128)S(1)}, u32[]{:S(2)}, u32[]{:S(2)}) %collective-permute-start.9) | collective-permute-done | bytes 294944 | tf_op jit(solution)/shard_map/ppermute | solution.py:275
  45.8 0.5 across.1
  46.3 0.1 collective-permute-start.10
  46.4 0.0 collective-permute-done.6.refs_1_
  46.5 1.6 %collective-permute-start.7 = (f32[64,768]{1,0:T(8,128)S(1)}, f32[64,768]{1,0:T(8,128)S(1)}, u32[]{:S(2)}, u32[]{:S(2)}) collective-permute-start(f32[64,768]{1,0:T(8,128)S(1)} %get-tuple-element.50), channel_id=1, source_target_pairs={{0,8},{4,12},{8,0},{12,4},{1,9},{5,13},{9,1},{13,5},{2,10},{6,14},... | collective-permute-start | bytes 589832 | tf_op jit(solution)/shard_map/ppermute | solution.py:278
  48.1 0.6 %collective-permute-start.3 = (f32[64,384]{1,0:T(8,128)S(1)}, f32[64,384]{1,0:T(8,128)S(1)}, u32[]{:S(2)}, u32[]{:S(2)}) collective-permute-start(f32[64,384]{1,0:T(8,128)S(1)} %get-tuple-element.40), channel_id=1, source_target_pairs={{0,8},{4,12},{8,0},{12,4},{1,9},{5,13},{9,1},{13,5},{2,10},{6,14},... | collective-permute-start | bytes 294920 | tf_op jit(solution)/shard_map/ppermute | solution.py:278
  48.7 1.6 %collective-permute-start.11 = (f32[64,384]{1,0:T(8,128)S(1)}, f32[64,384]{1,0:T(8,128)S(1)}, u32[]{:S(2)}, u32[]{:S(2)}) collective-permute-start(f32[64,384]{1,0:T(8,128)S(1)} %get-tuple-element.56), channel_id=1, source_target_pairs={{0,8},{4,12},{8,0},{12,4},{1,9},{5,13},{9,1},{13,5},{2,10},{6,14},... | collective-permute-start | bytes 294920 | tf_op jit(solution)/shard_map/ppermute | solution.py:278
  50.2 6.1 %collective-permute-done.3.refs_2_ = f32[64,384]{1,0:T(8,128)S(1)} collective-permute-done((f32[64,384]{1,0:T(8,128)S(1)}, f32[64,384]{1,0:T(8,128)S(1)}, u32[]{:S(2)}, u32[]{:S(2)}) %collective-permute-start.3) | collective-permute-done | bytes 98336 | tf_op jit(solution)/shard_map/ppermute | solution.py:278
  56.3 0.0 collective-permute-done.7.refs_5_
  56.3 1.7 %collective-permute-done.11.refs_8_ = f32[64,384]{1,0:T(8,128)S(1)} collective-permute-done((f32[64,384]{1,0:T(8,128)S(1)}, f32[64,384]{1,0:T(8,128)S(1)}, u32[]{:S(2)}, u32[]{:S(2)}) %collective-permute-start.11) | collective-permute-done | bytes 98336 | tf_op jit(solution)/shard_map/ppermute | solution.py:278
  58.0 1.3 %finish.1 = f32[64,1536]{1,0:T(8,128)} custom-call(f32[16,384]{1,0:T(8,128)S(1)} %get-tuple-element.31.refs_0_, f32[64,384]{1,0:T(8,128)S(1)} %get-tuple-element.39.refs_1_, f32[64,384]{1,0:T(8,128)S(1)} %collective-permute-done.3.refs_2_, f32[32,384]{1,0:T(8,128)S(1)} %pad_maximum_fusion.refs_3_, f32[64,768]{1,0:T(8,128)S(1)} %get-tuple-element.49.refs_4_, ...), custom_call_target="tpu_custom_call" | custom-call | flops 393216 | bytes 1277952 | tf_op jit(solution)/shard_map/finish/pallas_call | solution.py:238
  (15 shorter events, 0.2 us)
Async XLA Ops:
  0.0 19.5 %collective-permute-start.5 = (f32[384,384]{1,0:T(8,128)}, f32[384,384]{1,0:T(8,128)S(1)}, u32[]{:S(2)}, u32[]{:S(2)}) collective-permute-start(f32[384,384]{1,0:T(8,128)} %refs_3_.3), channel_id=1, source_target_pairs={{0,3},{1,2},{2,1},{3,0},{4,7},{5,6},{6,5},{7,4},{8,11},{9,10},{10,... | collective-permute-start | bytes 1769480 | tf_op jit(solution)/shard_map/ppermute | solution.py:275
  5.0 26.4 %collective-permute-start.4 = (f32[384,384]{1,0:T(8,128)}, f32[384,384]{1,0:T(8,128)S(1)}, u32[]{:S(2)}, u32[]{:S(2)}) collective-permute-start(f32[384,384]{1,0:T(8,128)} %refs_3_.3), channel_id=1, source_target_pairs={{0,1},{1,0},{2,3},{3,2},{4,5},{5,4},{6,7},{7,6},{8,9},{9,8},{10,11... | collective-permute-start | bytes 1769480 | tf_op jit(solution)/shard_map/ppermute | solution.py:275
  5.1 2.7 %copy-start.3 = (s32[32,16]{0,1:T(8,128)S(1)}, s32[32,16]{0,1:T(8,128)}, u32[]{:S(2)}) copy-start(s32[32,16]{0,1:T(8,128)} %param.7) | copy-start | bytes 6148
  5.1 9.1 %copy-start = (f32[384,384]{1,0:T(8,128)S(1)}, f32[384,384]{1,0:T(8,128)}, u32[]{:S(2)}) copy-start(f32[384,384]{1,0:T(8,128)} %refs_3_.3) | copy-start | bytes 1769476
  6.2 6.4 %collective-permute-start = (f32[64,768]{1,0:T(8,128)S(1)}, f32[64,768]{1,0:T(8,128)S(1)}, u32[]{:S(2)}, u32[]{:S(2)}) collective-permute-start(f32[64,768]{1,0:T(8,128)S(1)} %get-tuple-element.57), channel_id=1, source_target_pairs={{0,8},{4,12},{8,0},{12,4},{1,9},{5,13},{9,1},{13,5},{2,10},{6,14},... | collective-permute-start | bytes 589832 | tf_op jit(solution)/shard_map/ppermute | solution.py:278
  7.7 0.7 %copy-start.1 = (s32[16,16]{1,0:T(8,128)S(1)}, s32[16,16]{1,0:T(8,128)}, u32[]{:S(2)}) copy-start(s32[16,16]{1,0:T(8,128)} %refs_2_.1) | copy-start | bytes 3076
  7.8 0.7 %copy-start.2 = (s32[16]{0:T(128)S(1)}, s32[16]{0:T(128)}, u32[]{:S(2)}) copy-start(s32[16]{0:T(128)} %refs_3_.2) | copy-start | bytes 196
  12.6 1.5 %collective-permute-start.1 = (f32[128,384]{1,0:T(8,128)S(1)}, f32[128,384]{1,0:T(8,128)S(1)}, u32[]{:S(2)}, u32[]{:S(2)}) collective-permute-start(f32[128,384]{1,0:T(8,128)S(1)} %get-tuple-element.35), channel_id=1, source_target_pairs={{0,4},{4,0},{8,12},{12,8},{1,5},{5,1},{9,13},{13,9},{2,6},{6,2},{1... | collective-permute-start | bytes 589832 | tf_op jit(solution)/shard_map/ppermute | solution.py:278
  19.5 19.0 %collective-permute-start.8 = (f32[192,384]{1,0:T(8,128)S(1)}, f32[192,384]{1,0:T(8,128)S(1)}, u32[]{:S(2)}, u32[]{:S(2)}) collective-permute-start(f32[192,384]{1,0:T(8,128)S(1)} %slice.8), channel_id=1, source_target_pairs={{0,1},{1,0},{2,3},{3,2},{4,5},{5,4},{6,7},{7,6},{8,9},{9,8},{10,11... | collective-permute-start | bytes 884744 | tf_op jit(solution)/shard_map/ppermute | solution.py:275
  31.4 14.3 %collective-permute-start.9 = (f32[192,384]{1,0:T(8,128)S(1)}, f32[192,384]{1,0:T(8,128)S(1)}, u32[]{:S(2)}, u32[]{:S(2)}) collective-permute-start(f32[192,384]{1,0:T(8,128)S(1)} %slice.9), channel_id=1, source_target_pairs={{0,3},{1,2},{2,1},{3,0},{4,7},{5,6},{6,5},{7,4},{8,11},{9,10},{10,... | collective-permute-start | bytes 884744 | tf_op jit(solution)/shard_map/ppermute | solution.py:275
  34.5 11.9 %collective-permute-start.6 = (f32[128,768]{1,0:T(8,128)S(1)}, f32[128,768]{1,0:T(8,128)S(1)}, u32[]{:S(2)}, u32[]{:S(2)}) collective-permute-start(f32[128,768]{1,0:T(8,128)S(1)} %get-tuple-element.48), channel_id=1, source_target_pairs={{0,4},{4,0},{8,12},{12,8},{1,5},{5,1},{9,13},{13,9},{2,6},{6,2},{1... | collective-permute-start | bytes 1179656 | tf_op jit(solution)/shard_map/ppermute | solution.py:278
  34.6 13.4 %collective-permute-start.2 = (f32[128,384]{1,0:T(8,128)S(1)}, f32[128,384]{1,0:T(8,128)S(1)}, u32[]{:S(2)}, u32[]{:S(2)}) collective-permute-start(f32[128,384]{1,0:T(8,128)S(1)} %get-tuple-element.38), channel_id=1, source_target_pairs={{0,4},{4,0},{8,12},{12,8},{1,5},{5,1},{9,13},{13,9},{2,6},{6,2},{1... | collective-permute-start | bytes 589832 | tf_op jit(solution)/shard_map/ppermute | solution.py:278
  46.3 2.3 %collective-permute-start.10 = (f32[128,384]{1,0:T(8,128)S(1)}, f32[128,384]{1,0:T(8,128)S(1)}, u32[]{:S(2)}, u32[]{:S(2)}) collective-permute-start(f32[128,384]{1,0:T(8,128)S(1)} %get-tuple-element.54), channel_id=1, source_target_pairs={{0,4},{4,0},{8,12},{12,8},{1,5},{5,1},{9,13},{13,9},{2,6},{6,2},{1... | collective-permute-start | bytes 589832 | tf_op jit(solution)/shard_map/ppermute | solution.py:278
  46.5 9.9 %collective-permute-start.7 = (f32[64,768]{1,0:T(8,128)S(1)}, f32[64,768]{1,0:T(8,128)S(1)}, u32[]{:S(2)}, u32[]{:S(2)}) collective-permute-start(f32[64,768]{1,0:T(8,128)S(1)} %get-tuple-element.50), channel_id=1, source_target_pairs={{0,8},{4,12},{8,0},{12,4},{1,9},{5,13},{9,1},{13,5},{2,10},{6,14},... | collective-permute-start | bytes 589832 | tf_op jit(solution)/shard_map/ppermute | solution.py:278
  48.1 8.3 %collective-permute-start.3 = (f32[64,384]{1,0:T(8,128)S(1)}, f32[64,384]{1,0:T(8,128)S(1)}, u32[]{:S(2)}, u32[]{:S(2)}) collective-permute-start(f32[64,384]{1,0:T(8,128)S(1)} %get-tuple-element.40), channel_id=1, source_target_pairs={{0,8},{4,12},{8,0},{12,4},{1,9},{5,13},{9,1},{13,5},{2,10},{6,14},... | collective-permute-start | bytes 294920 | tf_op jit(solution)/shard_map/ppermute | solution.py:278
  48.7 9.4 %collective-permute-start.11 = (f32[64,384]{1,0:T(8,128)S(1)}, f32[64,384]{1,0:T(8,128)S(1)}, u32[]{:S(2)}, u32[]{:S(2)}) collective-permute-start(f32[64,384]{1,0:T(8,128)S(1)} %get-tuple-element.56), channel_id=1, source_target_pairs={{0,8},{4,12},{8,0},{12,4},{1,9},{5,13},{9,1},{13,5},{2,10},{6,14},... | collective-permute-start | bytes 294920 | tf_op jit(solution)/shard_map/ppermute | solution.py:278

commit v14 on v12

--- a/solution.py
+++ b/solution.py
@@ -152,12 +152,6 @@
 
 def pick_kernel(marks, slab, block, out):
     out[...] = jnp.where(marks[0:1, : out.shape[1]] > 0.5, slab[...], block[...])
-
-
-def pass_kernel(block, out):
-    rows = block.shape[0]
-    out[:rows, :] = block[...]
-    out[rows:, :] = jnp.zeros((out.shape[0] - rows, out.shape[1]), jnp.float32)
 
 
 def halves_kernel(counts, *refs):
@@ -301,12 +295,12 @@
     pieces += [swap(chip_columns(d), 2 * d) for d in range(1, n_row // 2)]
     keep, give = call(deal_kernel, "deal", [f32(total // 2, depth)] * 2, 0, marks, *pieces)
     slab_parts = [keep, swap(give, 1)]
-    def fold(keep, give):
+    def fold(keep, give, after=()):
         shape = f32(rows, keep.shape[1])
-        return call(fold_kernel, "fold", [shape] * (n_row // 2), 0, keep, swap(give, 1))
-
-    def exchange(keep, give):
-        pieces = fold(keep, give)
+        return call(fold_kernel, "fold", [shape] * (n_row // 2), 0, keep, swap(give, 1), after=after)
+
+    def exchange(keep, give, after=()):
+        pieces = fold(keep, give, after)
         return [pieces[0]] + [swap(pieces[i], 2 * i) for i in range(1, n_row // 2)]
 
     def next_door(x, d):
@@ -334,9 +328,9 @@
         )
         return [[slot for slot, _ in group] for group in groups], exchange(keep, give)
 
-    def finish(slots, *so_far):
+    def finish(slots, *so_far, final=False):
         args, counts, place_ = [], [], {}
-        if so_far:
+        if final:
             buffers = [pltpu.VMEM((rows, pairs), jnp.float32), pltpu.SemaphoreType.DMA((pairs // GROUP,))]
             place_ = dict(scratch=buffers, out_space=pl.ANY)
         for groups, shares in slots:
@@ -398,14 +392,17 @@
         after = tuple(share for _, shares in slots for share in shares)
         sums = [f32(total // 2, width)] * 2
         flops = 6 * total * depth * width
-        slots = []
+        slots, folded = [], ()
         if corner:
             parts = call(corner_kernel, "corner", sums, 0, *b_halves, end_slab, flops=flops, after=after)
-            pieces = list(enumerate(fold(*parts)))
+            folded = fold(*parts)
+            after, pieces = (parts[0],), list(enumerate(folded))
             slots.append(([[ends]], [next_door(x, 2 * i) for i, x in reversed(pieces)]))
         parts = call(last_kernel, "last", sums, 0, high, low, *b_halves, flops=flops, after=after)
-        slots.append(([[(EVEN, step), (ODD, step)]], exchange(*parts)))
-    return finish(slots, out)
+        if slots:
+            out = finish(slots, out)
+        slots = [([[(EVEN, step), (ODD, step)]], exchange(*parts, after=folded))]
+    return finish(slots, out, final=True)
 
 
 def solution(mesh):

time: 43.2 us -> 43.1 us (level)
    pallas_call x14 -> x15, Pallas kernels: 6.48 us -> 6.52 us  [call(): pl.pallas_call(body, out_shape=outs, in_specs=[SMEM] * n_smem + [VMEM] *...]
  transfers between devices with their start and end apart: 15 -> 15, of which waited for: 8 -> 8; matrix products, arithmetic and copies ran while one was open for 3% -> 3% of each run, Pallas kernels for 11% -> 12%
where the time goes in v14:
time: 43.1 us; the launch traced here: 42.9 us
  starting transfers between devices  18.3 us (42%)
  waiting for transfers between devices  16 us (37%)
  Pallas kernels  6.52 us (15%)
  local copies, waits for them, and re-layouts  1.77 us (4%)
    ppermute x4, starting transfers between devices, swap_line(): return lax.ppermute(x, ('row', 'col'), pairs_)  8.97 us
    ppermute x4, waiting for transfers between devices, swap_line(): return lax.ppermute(x, ('row', 'col'), pairs_)  7.07 us
    pallas_call x15, Pallas kernels, call(): pl.pallas_call(body, out_shape=outs, in_specs=[SMEM] * n_smem + [VMEM] *...  6.52 us
    ppermute x9, starting transfers between devices, swap(): return lax.ppermute(x, 'row', [(i, i ^ d) for i in range(n_row)])  6.34 us
    ppermute x9, waiting for transfers between devices, swap(): return lax.ppermute(x, 'row', [(i, i ^ d) for i in range(n_row)])  5.81 us
    ppermute x2, waiting for transfers between devices, next_door(): lax.ppermute(x, ('row', 'col'), [(i * n_col + j, (i ^ (d if 0 < j < n_col...  3.15 us
    ppermute x2, starting transfers between devices, next_door(): lax.ppermute(x, ('row', 'col'), [(i * n_col + j, (i ^ (d if 0 < j < n_col...  3 us
    dynamic_slice x1, local copies, waits for them, and re-layouts, chip_columns(): return lax.dynamic_slice_in_dim(amplitudes, start, 2 * depth, 1)  1.11 us
  transfers between devices with their start and end apart: 15, of which 8 were waited for; matrix products, arithmetic and copies ran while one was open for 3% of the time, Pallas kernels for 12%

profile of v14, /device:TPU:0, one launch (start us, length us, event | category | flops | bytes accessed | tf_op | source)
XLA Modules:
  0.0 42.9 jit_solution(7134699727259277616)
XLA Ops:
  0.0 0.5 %collective-permute-start.2 = (f32[384,384]{1,0:T(8,128)}, f32[384,384]{1,0:T(8,128)S(1)}, u32[]{:S(2)}, u32[]{:S(2)}) collective-permute-start(f32[384,384]{1,0:T(8,128)} %refs_3_.3), channel_id=1, source_target_pairs={{0,4},{1,2},{2,1},{3,7},{4,0},{5,6},{6,5},{7,3},{8,12},{9,10},{10,... | collective-permute-start | bytes 1769480 | tf_op jit(solution)/shard_map/ppermute | solution.py:264
  0.5 4.1 %collective-permute-start.4 = (f32[384,384]{1,0:T(8,128)}, f32[384,384]{1,0:T(8,128)S(1)}, u32[]{:S(2)}, u32[]{:S(2)}) collective-permute-start(f32[384,384]{1,0:T(8,128)} %refs_3_.3), channel_id=1, source_target_pairs={{0,1},{1,0},{2,3},{3,2},{4,5},{5,4},{6,7},{7,6},{8,9},{9,8},{10,11... | collective-permute-start | bytes 1769480 | tf_op jit(solution)/shard_map/ppermute | solution.py:264
  4.6 1.1 %constant_dynamic-slice_fusion = (f32[64,768]{1,0:T(8,128)S(1)}, f32[64,768]{1,0:T(8,128)S(1)}) fusion(f32[64,1536]{1,0:T(8,128)} %param.5, s32[]{:T(128)S(6)} %select_n.14, s32[]{:T(128)S(6)} %select_n.13), kind=kLoop, calls=%fused_computation.2 | loop fusion | bytes 786440 | tf_op jit(solution)/shard_map/dynamic_slice | solution.py:292
  5.7 1.6 %collective-permute-start = (f32[64,768]{1,0:T(8,128)S(1)}, f32[64,768]{1,0:T(8,128)S(1)}, u32[]{:S(2)}, u32[]{:S(2)}) collective-permute-start(f32[64,768]{1,0:T(8,128)S(1)} %get-tuple-element.77), channel_id=1, source_target_pairs={{0,8},{4,12},{8,0},{12,4},{1,9},{5,13},{9,1},{13,5},{2,10},{6,14},... | collective-permute-start | bytes 589832 | tf_op jit(solution)/shard_map/ppermute | solution.py:267
  7.4 0.1 pad_add_fusion.refs_0_
  7.4 0.5 %copy-done.1 = s32[16,16]{1,0:T(8,128)S(1)} copy-done((s32[16,16]{1,0:T(8,128)S(1)}, s32[16,16]{1,0:T(8,128)}, u32[]{:S(2)}) %copy-start.1) | copy-done | bytes 1048
  8.0 2.0 %tables.1 = (f32[8,384]{1,0:T(8,128)S(1)}, f32[8,384]{1,0:T(8,128)S(1)}, f32[4,384]{1,0:T(4,128)S(1)}, f32[16,384]{1,0:T(8,128)S(1)}, f32[4,384]{1,0:T(4,128)S(1...) custom-call(s32[3]{0:T(128)S(1)} %pad_add_fusion.refs_0_, ...), custom_call_target="tpu_custom_call" | custom-call | bytes 212044 | tf_op jit(solution)/shard_map/tables/pallas_call | solution.py:230
  10.0 1.8 %collective-permute-done.refs_2_ = f32[64,768]{1,0:T(8,128)S(1)} collective-permute-done((f32[64,768]{1,0:T(8,128)S(1)}, f32[64,768]{1,0:T(8,128)S(1)}, u32[]{:S(2)}, u32[]{:S(2)}) %collective-permute-start) | collective-permute-done | bytes 196640 | tf_op jit(solution)/shard_map/ppermute | solution.py:267
  12.0 1.4 %collective-permute-done.1.refs_2_ = f32[128,384]{1,0:T(8,128)S(1)} collective-permute-done((f32[128,384]{1,0:T(8,128)S(1)}, f32[128,384]{1,0:T(8,128)S(1)}, u32[]{:S(2)}, u32[]{:S(2)}) %collective-permute-start.1) | collective-permute-done | bytes 196640 | tf_op jit(solution)/shard_map/ppermute | solution.py:267
  13.4 0.6 %own.1 = (bf16[256,384]{1,0:T(8,128)(2,1)S(1)}, bf16[256,384]{1,0:T(8,128)(2,1)S(1)}, f32[384,384]{1,0:T(8,128)S(1)}, f32[128,384]{1,0:T(8,128)S(1)}, f32[128,384]{1,0:T(8,128)S(1)}) custom-call(f32[8,384]{1,0:T(8,128)S(1)} %get-tuple-element.43.refs_0_, f32[128,384]{1,0:T(8,128)S(1)} %get-tuple-element.45.refs_1_, ...), custom_call_target="tpu_custom_call" | custom-call | flops 226492416 | bytes 2377728 | tf_op jit(solution)/shard_map/own/pallas_call | solution.py:230
  14.1 4.4 %collective-permute-start.3 = (f32[384,384]{1,0:T(8,128)S(1)}, f32[384,384]{1,0:T(8,128)S(1)}, u32[]{:S(2)}, u32[]{:S(2)}) collective-permute-start(f32[384,384]{1,0:T(8,128)S(1)} %pick.1), channel_id=1, source_target_pairs={{0,1},{1,0},{2,3},{3,2},{4,5},{5,4},{6,7},{7,6},{8,9},{9,8},{10,11... | collective-permute-start | bytes 1769480 | tf_op jit(solution)/shard_map/ppermute | solution.py:264
  18.4 0.9 %pair.1 = (f32[128,768]{1,0:T(8,128)S(1)}, f32[128,768]{1,0:T(8,128)S(1)}) custom-call(bf16[256,384]{1,0:T(8,128)(2,1)S(1)} %get-tuple-element.48.refs_0_, bf16[256,384]{1,0:T(8,128)(2,1)S(1)} %get-tuple-element.49.refs_1_, f32[384,384]{1,0:T(8,128)S(1)} %collective-permute-done.4.refs_2_, f32[4,384]{1,0:T(4,128)S(1)} %get-tuple-element.59.refs_3_, ...), custom_call_target="tpu_custom_call" | custom-call | flops 452984832 | bytes 2371584 | tf_op jit(solution)/shard_map/pair/pallas_call | solution.py:230
  19.4 0.6 %collective-permute-start.8 = (f32[128,768]{1,0:T(8,128)S(1)}, f32[128,768]{1,0:T(8,128)S(1)}, u32[]{:S(2)}, u32[]{:S(2)}) collective-permute-start(f32[128,768]{1,0:T(8,128)S(1)} %get-tuple-element.62), channel_id=1, source_target_pairs={{0,4},{4,0},{8,12},{12,8},{1,5},{5,1},{9,13},{13,9},{2,6},{6,2},{1... | collective-permute-start | bytes 1179656 | tf_op jit(solution)/shard_map/ppermute | solution.py:267
  20.0 0.1 collective-permute-start.6
  20.0 1.6 %collective-permute-done.6.refs_1_ = f32[128,384]{1,0:T(8,128)S(1)} collective-permute-done((f32[128,384]{1,0:T(8,128)S(1)}, f32[128,384]{1,0:T(8,128)S(1)}, u32[]{:S(2)}, u32[]{:S(2)}) %collective-permute-start.6) | collective-permute-done | bytes 196640 | tf_op jit(solution)/shard_map/ppermute | solution.py:267
  21.6 1.6 %collective-permute-start.7 = (f32[64,384]{1,0:T(8,128)S(1)}, f32[64,384]{1,0:T(8,128)S(1)}, u32[]{:S(2)}, u32[]{:S(2)}) collective-permute-start(f32[64,384]{1,0:T(8,128)S(1)} %get-tuple-element.58), channel_id=1, source_target_pairs={{0,8},{4,12},{8,0},{12,4},{1,9},{5,13},{9,1},{13,5},{2,10},{6,14},... | collective-permute-start | bytes 294920 | tf_op jit(solution)/shard_map/ppermute | solution.py:267
  23.2 0.6 %collective-permute-start.9 = (f32[64,768]{1,0:T(8,128)S(1)}, f32[64,768]{1,0:T(8,128)S(1)}, u32[]{:S(2)}, u32[]{:S(2)}) collective-permute-start(f32[64,768]{1,0:T(8,128)S(1)} %get-tuple-element.64), channel_id=1, source_target_pairs={{0,8},{4,12},{8,0},{12,4},{1,9},{5,13},{9,1},{13,5},{2,10},{6,14},... | collective-permute-start | bytes 589832 | tf_op jit(solution)/shard_map/ppermute | solution.py:267
  23.8 7.1 %collective-permute-done.3.refs_0_.refs_2_ = f32[384,384]{1,0:T(8,128)S(1)} collective-permute-done((f32[384,384]{1,0:T(8,128)S(1)}, f32[384,384]{1,0:T(8,128)S(1)}, u32[]{:S(2)}, u32[]{:S(2)}) %collective-permute-start.3) | collective-permute-done | bytes 589856 | tf_op jit(solution)/shard_map/ppermute | solution.py:264
  30.9 0.1 halves.1
  31.1 0.5 %corner.1 = (f32[128,384]{1,0:T(8,128)S(1)}, f32[128,384]{1,0:T(8,128)S(1)}) custom-call(bf16[384,384]{1,0:T(8,128)(2,1)S(1)} %get-tuple-element.53.refs_0_.refs_2_, bf16[384,384]{1,0:T(8,128)(2,1)S(1)} %get-tuple-element.54.refs_1_.refs_3_, f32[384,384]{1,0:T(8,128)S(1)} %collective-permute-done.3.refs_0_.refs_2_, ...), custom_call_target="tpu_custom_call" | custom-call | flops 226492416 | bytes 1572864 | tf_op jit(solution)/shard_map/corner/pallas_call | solution.py:230
  31.7 0.5 %last.1 = (f32[128,384]{1,0:T(8,128)S(1)}, f32[128,384]{1,0:T(8,128)S(1)}) custom-call(bf16[256,384]{1,0:T(8,128)(2,1)S(1)} %get-tuple-element.48.refs_0_, bf16[256,384]{1,0:T(8,128)(2,1)S(1)} %get-tuple-element.49.refs_1_, bf16[384,384]{1,0:T(8,128)(2,1)S(1)} %get-tuple-element.53.refs_0_.refs_2_, bf16[384,384]{1,0:T(8,128)(2,1)S(1)} %get-tuple-element.54.refs_1_.refs_3_, ...), custom_call_target="tpu_custom_call" | custom-call | flops 226492416 | bytes 1376256 | tf_op jit(solution)/shard_map/last/pallas_call | solution.py:230
  32.2 0.6 %collective-permute-start.10 = (f32[128,384]{1,0:T(8,128)S(1)}, f32[128,384]{1,0:T(8,128)S(1)}, u32[]{:S(2)}, u32[]{:S(2)}) collective-permute-start(f32[128,384]{1,0:T(8,128)S(1)} %get-tuple-element.67), channel_id=1, source_target_pairs={{0,4},{4,0},{8,12},{12,8},{1,5},{5,1},{9,13},{13,9},{2,6},{6,2},{1... | collective-permute-start | bytes 589832 | tf_op jit(solution)/shard_map/ppermute | solution.py:267
  32.8 0.3 collective-permute-done.11.refs_1_
  33.1 2.6 %collective-permute-start.13 = (f32[64,384]{1,0:T(8,128)S(1)}, f32[64,384]{1,0:T(8,128)S(1)}, u32[]{:S(2)}, u32[]{:S(2)}) collective-permute-start(f32[64,384]{1,0:T(8,128)S(1)} %get-tuple-element.70.refs_3_), channel_id=1, source_target_pairs={{0,1},{1,8},{2,11},{3,2},{4,5},{5,12},{6,15},{7,6},{8,9},{9,0},{10... | collective-permute-start | bytes 294920 | tf_op jit(solution)/shard_map/ppermute | solution.py:308
  35.8 0.4 collective-permute-start.14
  36.2 1.3 %collective-permute-start.12 = (f32[64,384]{1,0:T(8,128)S(1)}, f32[64,384]{1,0:T(8,128)S(1)}, u32[]{:S(2)}, u32[]{:S(2)}) collective-permute-start(f32[64,384]{1,0:T(8,128)S(1)} %get-tuple-element.72), channel_id=1, source_target_pairs={{0,8},{4,12},{8,0},{12,4},{1,9},{5,13},{9,1},{13,5},{2,10},{6,14},... | collective-permute-start | bytes 294920 | tf_op jit(solution)/shard_map/ppermute | solution.py:267
  37.4 0.5 %finish.3.refs_3_ = f32[64,1536]{1,0:T(8,128)S(1)} custom-call(f32[16,384]{1,0:T(8,128)S(1)} %get-tuple-element.74.refs_0_, f32[64,384]{1,0:T(8,128)S(1)} %get-tuple-element.57.refs_3_.refs_1_, f32[64,384]{1,0:T(8,128)S(1)} %collective-permute-done.7.refs_4_.refs_2_, f32[32,384]{1,0:T(8,128)S(1)} %pad_maximum_fusion.refs_3_, ...), custom_call_target="tpu_custom_call" | custom-call | flops 393216 | bytes 1056768 | tf_op jit(solution)/shard_map/finish/pallas_call | solution.py:230
  37.9 2.4 %collective-permute-done.13.refs_1_ = f32[64,384]{1,0:T(8,128)S(1)} collective-permute-done((f32[64,384]{1,0:T(8,128)S(1)}, f32[64,384]{1,0:T(8,128)S(1)}, u32[]{:S(2)}, u32[]{:S(2)}) %collective-permute-start.13) | collective-permute-done | bytes 98336 | tf_op jit(solution)/shard_map/ppermute | solution.py:308
  40.3 0.8 %collective-permute-done.14.refs_2_ = f32[64,384]{1,0:T(8,128)S(1)} collective-permute-done((f32[64,384]{1,0:T(8,128)S(1)}, f32[64,384]{1,0:T(8,128)S(1)}, u32[]{:S(2)}, u32[]{:S(2)}) %collective-permute-start.14) | collective-permute-done | bytes 98336 | tf_op jit(solution)/shard_map/ppermute | solution.py:308
  41.1 0.2 finish.4.refs_3_
  41.2 0.7 %collective-permute-done.12.refs_2_ = f32[64,384]{1,0:T(8,128)S(1)} collective-permute-done((f32[64,384]{1,0:T(8,128)S(1)}, f32[64,384]{1,0:T(8,128)S(1)}, u32[]{:S(2)}, u32[]{:S(2)}) %collective-permute-start.12) | collective-permute-done | bytes 98336 | tf_op jit(solution)/shard_map/ppermute | solution.py:267
  41.9 1.0 %finish.5 = f32[64,1536]{1,0:T(8,128)} custom-call(f32[16,384]{1,0:T(8,128)S(1)} %add.10.refs_0_, f32[64,384]{1,0:T(8,128)S(1)} %get-tuple-element.71.refs_1_, f32[64,384]{1,0:T(8,128)S(1)} %collective-permute-done.12.refs_2_, f32[64,1536]{1,0:T(8,128)S(1)} %finish.4.refs_3_), custom_call_target="tpu_custom_call" | custom-call | flops 393216 | bytes 1007616 | tf_op jit(solution)/shard_map/finish/pallas_call | solution.py:230
  (26 shorter events, 0.5 us)
Async XLA Ops:
  0.0 14.0 %collective-permute-start.2 = (f32[384,384]{1,0:T(8,128)}, f32[384,384]{1,0:T(8,128)S(1)}, u32[]{:S(2)}, u32[]{:S(2)}) collective-permute-start(f32[384,384]{1,0:T(8,128)} %refs_3_.3), channel_id=1, source_target_pairs={{0,4},{1,2},{2,1},{3,7},{4,0},{5,6},{6,5},{7,3},{8,12},{9,10},{10,... | collective-permute-start | bytes 1769480 | tf_op jit(solution)/shard_map/ppermute | solution.py:264
  0.5 18.0 %collective-permute-start.4 = (f32[384,384]{1,0:T(8,128)}, f32[384,384]{1,0:T(8,128)S(1)}, u32[]{:S(2)}, u32[]{:S(2)}) collective-permute-start(f32[384,384]{1,0:T(8,128)} %refs_3_.3), channel_id=1, source_target_pairs={{0,1},{1,0},{2,3},{3,2},{4,5},{5,4},{6,7},{7,6},{8,9},{9,8},{10,11... | collective-permute-start | bytes 1769480 | tf_op jit(solution)/shard_map/ppermute | solution.py:264
  4.6 2.7 %copy-start.3 = (s32[32,16]{0,1:T(8,128)S(1)}, s32[32,16]{0,1:T(8,128)}, u32[]{:S(2)}) copy-start(s32[32,16]{0,1:T(8,128)} %param.7) | copy-start | bytes 6148
  4.6 8.8 %copy-start = (f32[384,384]{1,0:T(8,128)S(1)}, f32[384,384]{1,0:T(8,128)}, u32[]{:S(2)}) copy-start(f32[384,384]{1,0:T(8,128)} %refs_3_.3) | copy-start | bytes 1769476
  5.7 6.1 %collective-permute-start = (f32[64,768]{1,0:T(8,128)S(1)}, f32[64,768]{1,0:T(8,128)S(1)}, u32[]{:S(2)}, u32[]{:S(2)}) collective-permute-start(f32[64,768]{1,0:T(8,128)S(1)} %get-tuple-element.77), channel_id=1, source_target_pairs={{0,8},{4,12},{8,0},{12,4},{1,9},{5,13},{9,1},{13,5},{2,10},{6,14},... | collective-permute-start | bytes 589832 | tf_op jit(solution)/shard_map/ppermute | solution.py:267
  7.3 0.7 %copy-start.1 = (s32[16,16]{1,0:T(8,128)S(1)}, s32[16,16]{1,0:T(8,128)}, u32[]{:S(2)}) copy-start(s32[16,16]{1,0:T(8,128)} %refs_2_.1) | copy-start | bytes 3076
  7.4 0.7 %copy-start.2 = (s32[16]{0:T(128)S(1)}, s32[16]{0:T(128)}, u32[]{:S(2)}) copy-start(s32[16]{0:T(128)} %refs_3_.2) | copy-start | bytes 196
  11.9 1.5 %collective-permute-start.1 = (f32[128,384]{1,0:T(8,128)S(1)}, f32[128,384]{1,0:T(8,128)S(1)}, u32[]{:S(2)}, u32[]{:S(2)}) collective-permute-start(f32[128,384]{1,0:T(8,128)S(1)} %get-tuple-element.46), channel_id=1, source_target_pairs={{0,4},{4,0},{8,12},{12,8},{1,5},{5,1},{9,13},{13,9},{2,6},{6,2},{1... | collective-permute-start | bytes 589832 | tf_op jit(solution)/shard_map/ppermute | solution.py:267
  14.1 16.8 %collective-permute-start.3 = (f32[384,384]{1,0:T(8,128)S(1)}, f32[384,384]{1,0:T(8,128)S(1)}, u32[]{:S(2)}, u32[]{:S(2)}) collective-permute-start(f32[384,384]{1,0:T(8,128)S(1)} %pick.1), channel_id=1, source_target_pairs={{0,1},{1,0},{2,3},{3,2},{4,5},{5,4},{6,7},{7,6},{8,9},{9,8},{10,11... | collective-permute-start | bytes 1769480 | tf_op jit(solution)/shard_map/ppermute | solution.py:264
  18.4 12.5 %collective-permute-start.5 = (f32[384,384]{1,0:T(8,128)S(1)}, f32[384,384]{1,0:T(8,128)S(1)}, u32[]{:S(2)}, u32[]{:S(2)}) collective-permute-start(f32[384,384]{1,0:T(8,128)S(1)} %collective-permute-done.4.refs_2_), channel_id=1, source_target_pairs={{0,4},{1,2},{2,1},{3,7},{4,0},{5,6},{6,5},{7,3},{8,12},{9,10},{10,... | collective-permute-start | bytes 1769480 | tf_op jit(solution)/shard_map/ppermute | solution.py:264
  19.4 3.8 %collective-permute-start.8 = (f32[128,768]{1,0:T(8,128)S(1)}, f32[128,768]{1,0:T(8,128)S(1)}, u32[]{:S(2)}, u32[]{:S(2)}) collective-permute-start(f32[128,768]{1,0:T(8,128)S(1)} %get-tuple-element.62), channel_id=1, source_target_pairs={{0,4},{4,0},{8,12},{12,8},{1,5},{5,1},{9,13},{13,9},{2,6},{6,2},{1... | collective-permute-start | bytes 1179656 | tf_op jit(solution)/shard_map/ppermute | solution.py:267
  20.0 1.6 %collective-permute-start.6 = (f32[128,384]{1,0:T(8,128)S(1)}, f32[128,384]{1,0:T(8,128)S(1)}, u32[]{:S(2)}, u32[]{:S(2)}) collective-permute-start(f32[128,384]{1,0:T(8,128)S(1)} %get-tuple-element.56), channel_id=1, source_target_pairs={{0,4},{4,0},{8,12},{12,8},{1,5},{5,1},{9,13},{13,9},{2,6},{6,2},{1... | collective-permute-start | bytes 589832 | tf_op jit(solution)/shard_map/ppermute | solution.py:267
  21.6 9.4 %collective-permute-start.7 = (f32[64,384]{1,0:T(8,128)S(1)}, f32[64,384]{1,0:T(8,128)S(1)}, u32[]{:S(2)}, u32[]{:S(2)}) collective-permute-start(f32[64,384]{1,0:T(8,128)S(1)} %get-tuple-element.58), channel_id=1, source_target_pairs={{0,8},{4,12},{8,0},{12,4},{1,9},{5,13},{9,1},{13,5},{2,10},{6,14},... | collective-permute-start | bytes 294920 | tf_op jit(solution)/shard_map/ppermute | solution.py:267
  23.2 7.8 %collective-permute-start.9 = (f32[64,768]{1,0:T(8,128)S(1)}, f32[64,768]{1,0:T(8,128)S(1)}, u32[]{:S(2)}, u32[]{:S(2)}) collective-permute-start(f32[64,768]{1,0:T(8,128)S(1)} %get-tuple-element.64), channel_id=1, source_target_pairs={{0,8},{4,12},{8,0},{12,4},{1,9},{5,13},{9,1},{13,5},{2,10},{6,14},... | collective-permute-start | bytes 589832 | tf_op jit(solution)/shard_map/ppermute | solution.py:267
  31.6 1.5 %collective-permute-start.11 = (f32[128,384]{1,0:T(8,128)S(1)}, f32[128,384]{1,0:T(8,128)S(1)}, u32[]{:S(2)}, u32[]{:S(2)}) collective-permute-start(f32[128,384]{1,0:T(8,128)S(1)} %get-tuple-element.68), channel_id=1, source_target_pairs={{0,4},{4,0},{8,12},{12,8},{1,5},{5,1},{9,13},{13,9},{2,6},{6,2},{1... | collective-permute-start | bytes 589832 | tf_op jit(solution)/shard_map/ppermute | solution.py:267
  32.2 3.9 %collective-permute-start.10 = (f32[128,384]{1,0:T(8,128)S(1)}, f32[128,384]{1,0:T(8,128)S(1)}, u32[]{:S(2)}, u32[]{:S(2)}) collective-permute-start(f32[128,384]{1,0:T(8,128)S(1)} %get-tuple-element.67), channel_id=1, source_target_pairs={{0,4},{4,0},{8,12},{12,8},{1,5},{5,1},{9,13},{13,9},{2,6},{6,2},{1... | collective-permute-start | bytes 589832 | tf_op jit(solution)/shard_map/ppermute | solution.py:267
  33.1 7.1 %collective-permute-start.13 = (f32[64,384]{1,0:T(8,128)S(1)}, f32[64,384]{1,0:T(8,128)S(1)}, u32[]{:S(2)}, u32[]{:S(2)}) collective-permute-start(f32[64,384]{1,0:T(8,128)S(1)} %get-tuple-element.70.refs_3_), channel_id=1, source_target_pairs={{0,1},{1,8},{2,11},{3,2},{4,5},{5,12},{6,15},{7,6},{8,9},{9,0},{10... | collective-permute-start | bytes 294920 | tf_op jit(solution)/shard_map/ppermute | solution.py:308
  35.8 5.3 %collective-permute-start.14 = (f32[64,384]{1,0:T(8,128)S(1)}, f32[64,384]{1,0:T(8,128)S(1)}, u32[]{:S(2)}, u32[]{:S(2)}) collective-permute-start(f32[64,384]{1,0:T(8,128)S(1)} %get-tuple-element.69.refs_2_), channel_id=1, source_target_pairs={{0,1},{1,0},{2,3},{3,2},{4,5},{5,4},{6,7},{7,6},{8,9},{9,8},{10,11... | collective-permute-start | bytes 294920 | tf_op jit(solution)/shard_map/ppermute | solution.py:308
  36.2 5.7 %collective-permute-start.12 = (f32[64,384]{1,0:T(8,128)S(1)}, f32[64,384]{1,0:T(8,128)S(1)}, u32[]{:S(2)}, u32[]{:S(2)}) collective-permute-start(f32[64,384]{1,0:T(8,128)S(1)} %get-tuple-element.72), channel_id=1, source_target_pairs={{0,8},{4,12},{8,0},{12,4},{1,9},{5,13},{9,1},{13,5},{2,10},{6,14},... | collective-permute-start | bytes 294920 | tf_op jit(solution)/shard_map/ppermute | solution.py:267

commit v15 on v14

--- a/solution.py
+++ b/solution.py
@@ -48,7 +48,9 @@
     r, c, n_col = place[0], place[1], place[2]
     row = lax.broadcasted_iota(jnp.int32, marks.shape, 0)
     ends = ((c == 0) | (c == n_col - 1)).astype(jnp.float32)
-    marks[...] = jnp.where(row == 0, ends, (r % 2).astype(jnp.float32))
+    upper = (2 * c >= n_col).astype(jnp.float32)
+    rest = jnp.where(row == 1, (r % 2).astype(jnp.float32), jnp.where(row == 2, 1 - upper, upper))
+    marks[...] = jnp.where(row == 0, ends, rest)
     count, depth = amp_rows.shape
     occ = count // len(order)
     lane_tile = lax.broadcasted_iota(jnp.int32, (1, depth), 1) // TB
@@ -148,6 +150,14 @@
         here, there = piece[:, :depth], piece[:, depth:]
         keep[at, :] = jnp.where(second, there, here)
         give[at, :] = jnp.where(second, here, there)
+
+
+def pass_kernel(block, out):
+    out[...] = block[...]
+
+
+def choose_kernel(marks, lower, upper, out):
+    out[...] = jnp.where(marks[2:3, : out.shape[1]] > 0.5, lower[...], upper[...])
 
 
 def pick_kernel(marks, slab, block, out):
@@ -255,21 +265,23 @@
     place = jnp.stack([r, c, jnp.int32(n_col)]).astype(jnp.int32)
     order = list(range(0, n_row, 2)) + list(range(1, n_row, 2))
 
-    def swap_line(x, kind):
+    def swap_line(x, kind, among=range(n_col)):
         pairs_ = []
         for i in range(n_row):
             for j in range(n_col):
                 to = ((j + kind) ^ 1) - kind
-                pairs_.append((i * n_col + j, i * n_col + to if 0 <= to < n_col else (i ^ 1) * n_col + j))
+                there = to in among and j in among
+                pairs_.append((i * n_col + j, i * n_col + to if there else (i ^ 1) * n_col + j))
         return lax.ppermute(x, ("row", "col"), pairs_)
 
     def swap(x, d):
         return lax.ppermute(x, "row", [(i, i ^ d) for i in range(n_row)])
 
     k_tiles, tiles = depth // TB, pairs // TB
-    even = [swap_line(integrals, EVEN)]
+    corner = n_col == 4 and total <= depth and depth == width
+    among = [range(n_col // 2), range(n_col // 2, n_col)] if corner else [range(n_col)]
+    even = [swap_line(integrals, EVEN, part) for part in among]
     odd = [swap_line(integrals, ODD)]
-    corner = n_col == 4 and total <= depth and depth == width
     last = n_col - 2 if corner else n_col - 1
     kinds = [(OWN, 0)] + [(kind, step) for step in range(1, last + 1) for kind in (EVEN, ODD)]
     ends = (CORNER, n_col - 1)
@@ -286,6 +298,9 @@
     )
     masks = dict(zip(kinds + [ends], made[::2]))
     homes = dict(zip(kinds + [ends], made[1::2]))
+    even_masks = [masks[EVEN, 1]]
+    if corner:
+        even_masks = [masks[EVEN, 1] * marks[i : i + 1, :width] for i in (2, 3)]
 
     def chip_columns(d):
         start = (r // 2 ^ d) * 2 * depth
@@ -312,17 +327,18 @@
         )
 
     def multiply(name, *groups, after=()):
+        refs = [[x for slot, block in group for x in (*block, masks[slot])] for group in groups]
+        counts = [tuple(len(block) + 1 for _, block in group) for group in groups]
+        if len(groups) == 2 and len(even) == 2:
+            refs[0], counts[0] = [x for pair in zip(even, even_masks) for x in pair], (2, 2)
         keep, give = call(
-            functools.partial(
-                multiply_kernel,
-                tuple(tuple(len(block) + 1 for _, block in group) for group in groups),
-            ),
+            functools.partial(multiply_kernel, tuple(counts)),
             name,
             [f32(total // 2, len(groups) * width)] * 2,
             0,
             high,
             low,
-            *[x for group in groups for slot, block in group for x in (*block, masks[slot])],
+            *[x for group in refs for x in group],
             flops=6 * total * depth * width * len(groups),
             after=after,
         )
@@ -367,7 +383,9 @@
             going = list(odd)
             if corner:
                 shape = f32(depth, width)
-                going = [call(pick_kernel, "pick", [shape], 0, marks, slab, odd[0])[0]]
+                lower = call(pass_kernel, "pass", [shape], 0, even[0], after=())
+                going = call(pick_kernel, "pick", [shape], 0, marks, slab, odd[0], after=lower)
+                even = call(choose_kernel, "choose", [shape], 0, marks, *lower, even[1])
             odd, even = [swap_line(x, ODD) for x in even], [swap_line(x, EVEN) for x in going]
             if corner:
                 end_slab = even[0]

time: 43.1 us -> 43.7 us (1.014)
  waiting for transfers between devices: 16 us -> 20 us
  starting transfers between devices: 18.3 us -> 14.7 us
    ppermute x4 -> x5, waiting for transfers between devices: 7.07 us -> 10.3 us  [swap_line(): return lax.ppermute(x, ('row', 'col'), pairs_)]
    ppermute x4 -> x5, starting transfers between devices: 8.97 us -> 5.87 us  [swap_line(): return lax.ppermute(x, ('row', 'col'), pairs_)]
    ppermute x9, waiting for transfers between devices: 5.81 us -> 6.46 us  [swap(): return lax.ppermute(x, 'row', [(i, i ^ d) for i in range(n_row)])]
    ppermute x2, starting transfers between devices: 3 us -> 2.56 us  [next_door(): lax.ppermute(x, ('row', 'col'), [(i * n_col + j, (i ^ (d if 0 < j < n_col...]
    pallas_call x15 -> x17, Pallas kernels: 6.52 us -> 6.74 us  [call(): pl.pallas_call(body, out_shape=outs, in_specs=[SMEM] * n_smem + [VMEM] *...]
  transfers between devices with their start and end apart: 15 -> 16, of which waited for: 8 -> 9; matrix products, arithmetic and copies ran while one was open for 3% -> 3% of each run, Pallas kernels for 12% -> 12%
where the time goes in v15:
time: 43.7 us; the launch traced here: 43.5 us
  waiting for transfers between devices  20 us (46%)
  starting transfers between devices  14.7 us (34%)
  Pallas kernels  6.74 us (15%)
  local copies, waits for them, and re-layouts  1.8 us (4%)
    ppermute x5, waiting for transfers between devices, swap_line(): return lax.ppermute(x, ('row', 'col'), pairs_)  10.3 us
    pallas_call x17, Pallas kernels, call(): pl.pallas_call(body, out_shape=outs, in_specs=[SMEM] * n_smem + [VMEM] *...  6.74 us
    ppermute x9, waiting for transfers between devices, swap(): return lax.ppermute(x, 'row', [(i, i ^ d) for i in range(n_row)])  6.46 us
    ppermute x9, starting transfers between devices, swap(): return lax.ppermute(x, 'row', [(i, i ^ d) for i in range(n_row)])  6.28 us
    ppermute x5, starting transfers between devices, swap_line(): return lax.ppermute(x, ('row', 'col'), pairs_)  5.87 us
    ppermute x2, waiting for transfers between devices, next_door(): lax.ppermute(x, ('row', 'col'), [(i * n_col + j, (i ^ (d if 0 < j < n_col...  3.18 us
    ppermute x2, starting transfers between devices, next_door(): lax.ppermute(x, ('row', 'col'), [(i * n_col + j, (i ^ (d if 0 < j < n_col...  2.56 us
    dynamic_slice x1, local copies, waits for them, and re-layouts, chip_columns(): return lax.dynamic_slice_in_dim(amplitudes, start, 2 * depth, 1)  1.11 us
  transfers between devices with their start and end apart: 16, of which 9 were waited for; matrix products, arithmetic and copies ran while one was open for 3% of the time, Pallas kernels for 12%

profile of v15, /device:TPU:0, one launch (start us, length us, event | category | flops | bytes accessed | tf_op | source)
XLA Modules:
  0.0 43.5 jit_solution(6615205232624973912)
XLA Ops:
  0.0 3.0 %collective-permute-start.3 = (f32[384,384]{1,0:T(8,128)}, f32[384,384]{1,0:T(8,128)S(1)}, u32[]{:S(2)}, u32[]{:S(2)}) collective-permute-start(f32[384,384]{1,0:T(8,128)} %refs_3_.3), channel_id=1, source_target_pairs={{0,1},{1,0},{2,6},{3,7},{4,5},{5,4},{6,2},{7,3},{8,9},{9,8},{10,14... | collective-permute-start | bytes 1769480 | tf_op jit(solution)/shard_map/ppermute | solution.py:275
  3.0 0.5 %collective-permute-start.5 = (f32[384,384]{1,0:T(8,128)}, f32[384,384]{1,0:T(8,128)S(1)}, u32[]{:S(2)}, u32[]{:S(2)}) collective-permute-start(f32[384,384]{1,0:T(8,128)} %refs_3_.3), channel_id=1, source_target_pairs={{0,4},{1,5},{2,3},{3,2},{4,0},{5,1},{6,7},{7,6},{8,12},{9,13},{10,... | collective-permute-start | bytes 1769480 | tf_op jit(solution)/shard_map/ppermute | solution.py:275
  3.5 1.1 %constant_dynamic-slice_fusion = (f32[64,768]{1,0:T(8,128)S(1)}, f32[64,768]{1,0:T(8,128)S(1)}) fusion(f32[64,1536]{1,0:T(8,128)} %param.5, s32[]{:T(128)S(6)} %select_n.14, s32[]{:T(128)S(6)} %select_n.13), kind=kLoop, calls=%fused_computation.6 | loop fusion | bytes 786440 | tf_op jit(solution)/shard_map/dynamic_slice | solution.py:307
  4.7 1.6 %collective-permute-start = (f32[64,768]{1,0:T(8,128)S(1)}, f32[64,768]{1,0:T(8,128)S(1)}, u32[]{:S(2)}, u32[]{:S(2)}) collective-permute-start(f32[64,768]{1,0:T(8,128)S(1)} %get-tuple-element.79), channel_id=1, source_target_pairs={{0,8},{4,12},{8,0},{12,4},{1,9},{5,13},{9,1},{13,5},{2,10},{6,14},... | collective-permute-start | bytes 589832 | tf_op jit(solution)/shard_map/ppermute | solution.py:278
  6.4 0.5 %copy-done.1 = s32[16,16]{1,0:T(8,128)S(1)} copy-done((s32[16,16]{1,0:T(8,128)S(1)}, s32[16,16]{1,0:T(8,128)}, u32[]{:S(2)}) %copy-start.1) | copy-done | bytes 1048
  6.9 2.0 %tables.1 = (f32[8,384]{1,0:T(8,128)S(1)}, f32[8,384]{1,0:T(8,128)S(1)}, f32[4,384]{1,0:T(4,128)S(1)}, f32[16,384]{1,0:T(8,128)S(1)}, f32[4,384]{1,0:T(4,128)S(1...) custom-call(s32[3]{0:T(128)S(1)} %pad_add_fusion.refs_0_, ...), custom_call_target="tpu_custom_call" | custom-call | bytes 212044 | tf_op jit(solution)/shard_map/tables/pallas_call | solution.py:240
  9.0 2.6 %collective-permute-done.refs_2_ = f32[64,768]{1,0:T(8,128)S(1)} collective-permute-done((f32[64,768]{1,0:T(8,128)S(1)}, f32[64,768]{1,0:T(8,128)S(1)}, u32[]{:S(2)}, u32[]{:S(2)}) %collective-permute-start) | collective-permute-done | bytes 196640 | tf_op jit(solution)/shard_map/ppermute | solution.py:278
  11.7 1.4 %collective-permute-done.1.refs_2_ = f32[128,384]{1,0:T(8,128)S(1)} collective-permute-done((f32[128,384]{1,0:T(8,128)S(1)}, f32[128,384]{1,0:T(8,128)S(1)}, u32[]{:S(2)}, u32[]{:S(2)}) %collective-permute-start.1) | collective-permute-done | bytes 196640 | tf_op jit(solution)/shard_map/ppermute | solution.py:278
  13.1 0.6 %own.1 = (bf16[256,384]{1,0:T(8,128)(2,1)S(1)}, bf16[256,384]{1,0:T(8,128)(2,1)S(1)}, f32[384,384]{1,0:T(8,128)S(1)}, f32[128,384]{1,0:T(8,128)S(1)}, f32[128,384]{1,0:T(8,128)S(1)}) custom-call(f32[8,384]{1,0:T(8,128)S(1)} %get-tuple-element.43.refs_0_, f32[128,384]{1,0:T(8,128)S(1)} %get-tuple-element.45.refs_1_, ...), custom_call_target="tpu_custom_call" | custom-call | flops 226492416 | bytes 2377728 | tf_op jit(solution)/shard_map/own/pallas_call | solution.py:240
  13.7 2.9 %collective-permute-done.3.refs_0_.refs_2_ = f32[384,384]{1,0:T(8,128)S(1)} collective-permute-done((f32[384,384]{1,0:T(8,128)}, f32[384,384]{1,0:T(8,128)S(1)}, u32[]{:S(2)}, u32[]{:S(2)}) %collective-permute-start.3) | collective-permute-done | bytes 589856 | tf_op jit(solution)/shard_map/ppermute | solution.py:275
  16.6 0.1 pick.1
  16.7 2.3 %collective-permute-start.4 = (f32[384,384]{1,0:T(8,128)S(1)}, f32[384,384]{1,0:T(8,128)S(1)}, u32[]{:S(2)}, u32[]{:S(2)}) collective-permute-start(f32[384,384]{1,0:T(8,128)S(1)} %pick.1), channel_id=1, source_target_pairs={{0,1},{1,0},{2,3},{3,2},{4,5},{5,4},{6,7},{7,6},{8,9},{9,8},{10,11... | collective-permute-start | bytes 1769480 | tf_op jit(solution)/shard_map/ppermute | solution.py:275
  19.1 1.0 %pair.1 = (f32[128,768]{1,0:T(8,128)S(1)}, f32[128,768]{1,0:T(8,128)S(1)}) custom-call(bf16[256,384]{1,0:T(8,128)(2,1)S(1)} %get-tuple-element.48.refs_0_, bf16[256,384]{1,0:T(8,128)(2,1)S(1)} %get-tuple-element.49.refs_1_, f32[384,384]{1,0:T(8,128)S(1)} %collective-permute-done.3.refs_0_.refs_2_, f32[4,384]{1,0:T(4,128)S(1)} %get-tuple-element.82.refs_3_, ...), custom_call_target="tpu_custom_call" | custom-call | flops 452984832 | bytes 2967552 | tf_op jit(solution)/shard_map/pair/pallas_call | solution.py:240
  20.1 0.6 %collective-permute-start.9 = (f32[128,768]{1,0:T(8,128)S(1)}, f32[128,768]{1,0:T(8,128)S(1)}, u32[]{:S(2)}, u32[]{:S(2)}) collective-permute-start(f32[128,768]{1,0:T(8,128)S(1)} %get-tuple-element.62), channel_id=1, source_target_pairs={{0,4},{4,0},{8,12},{12,8},{1,5},{5,1},{9,13},{13,9},{2,6},{6,2},{1... | collective-permute-start | bytes 1179656 | tf_op jit(solution)/shard_map/ppermute | solution.py:278
  20.8 1.6 %collective-permute-done.7.refs_1_ = f32[128,384]{1,0:T(8,128)S(1)} collective-permute-done((f32[128,384]{1,0:T(8,128)S(1)}, f32[128,384]{1,0:T(8,128)S(1)}, u32[]{:S(2)}, u32[]{:S(2)}) %collective-permute-start.7) | collective-permute-done | bytes 196640 | tf_op jit(solution)/shard_map/ppermute | solution.py:278
  22.3 1.6 %collective-permute-start.8 = (f32[64,384]{1,0:T(8,128)S(1)}, f32[64,384]{1,0:T(8,128)S(1)}, u32[]{:S(2)}, u32[]{:S(2)}) collective-permute-start(f32[64,384]{1,0:T(8,128)S(1)} %get-tuple-element.58), channel_id=1, source_target_pairs={{0,8},{4,12},{8,0},{12,4},{1,9},{5,13},{9,1},{13,5},{2,10},{6,14},... | collective-permute-start | bytes 294920 | tf_op jit(solution)/shard_map/ppermute | solution.py:278
  24.0 0.6 %collective-permute-start.10 = (f32[64,768]{1,0:T(8,128)S(1)}, f32[64,768]{1,0:T(8,128)S(1)}, u32[]{:S(2)}, u32[]{:S(2)}) collective-permute-start(f32[64,768]{1,0:T(8,128)S(1)} %get-tuple-element.64), channel_id=1, source_target_pairs={{0,8},{4,12},{8,0},{12,4},{1,9},{5,13},{9,1},{13,5},{2,10},{6,14},... | collective-permute-start | bytes 589832 | tf_op jit(solution)/shard_map/ppermute | solution.py:278
  24.6 7.4 %collective-permute-done.4.refs_0_.refs_2_ = f32[384,384]{1,0:T(8,128)S(1)} collective-permute-done((f32[384,384]{1,0:T(8,128)S(1)}, f32[384,384]{1,0:T(8,128)S(1)}, u32[]{:S(2)}, u32[]{:S(2)}) %collective-permute-start.4) | collective-permute-done | bytes 589856 | tf_op jit(solution)/shard_map/ppermute | solution.py:275
  32.0 0.1 halves.1
  32.2 0.5 %corner.1 = (f32[128,384]{1,0:T(8,128)S(1)}, f32[128,384]{1,0:T(8,128)S(1)}) custom-call(bf16[384,384]{1,0:T(8,128)(2,1)S(1)} %get-tuple-element.53.refs_0_.refs_2_, bf16[384,384]{1,0:T(8,128)(2,1)S(1)} %get-tuple-element.54.refs_1_.refs_3_, f32[384,384]{1,0:T(8,128)S(1)} %collective-permute-done.4.refs_0_.refs_2_, ...), custom_call_target="tpu_custom_call" | custom-call | flops 226492416 | bytes 1572864 | tf_op jit(solution)/shard_map/corner/pallas_call | solution.py:240
  32.8 0.5 %last.1 = (f32[128,384]{1,0:T(8,128)S(1)}, f32[128,384]{1,0:T(8,128)S(1)}) custom-call(bf16[256,384]{1,0:T(8,128)(2,1)S(1)} %get-tuple-element.48.refs_0_, bf16[256,384]{1,0:T(8,128)(2,1)S(1)} %get-tuple-element.49.refs_1_, bf16[384,384]{1,0:T(8,128)(2,1)S(1)} %get-tuple-element.53.refs_0_.refs_2_, bf16[384,384]{1,0:T(8,128)(2,1)S(1)} %get-tuple-element.54.refs_1_.refs_3_, ...), custom_call_target="tpu_custom_call" | custom-call | flops 226492416 | bytes 1376256 | tf_op jit(solution)/shard_map/last/pallas_call | solution.py:240
  33.3 0.6 %collective-permute-start.11 = (f32[128,384]{1,0:T(8,128)S(1)}, f32[128,384]{1,0:T(8,128)S(1)}, u32[]{:S(2)}, u32[]{:S(2)}) collective-permute-start(f32[128,384]{1,0:T(8,128)S(1)} %get-tuple-element.67), channel_id=1, source_target_pairs={{0,4},{4,0},{8,12},{12,8},{1,5},{5,1},{9,13},{13,9},{2,6},{6,2},{1... | collective-permute-start | bytes 589832 | tf_op jit(solution)/shard_map/ppermute | solution.py:278
  33.9 0.3 collective-permute-done.12.refs_1_
  34.2 2.1 %collective-permute-start.14 = (f32[64,384]{1,0:T(8,128)S(1)}, f32[64,384]{1,0:T(8,128)S(1)}, u32[]{:S(2)}, u32[]{:S(2)}) collective-permute-start(f32[64,384]{1,0:T(8,128)S(1)} %get-tuple-element.70.refs_3_), channel_id=1, source_target_pairs={{0,1},{1,8},{2,11},{3,2},{4,5},{5,12},{6,15},{7,6},{8,9},{9,0},{10... | collective-permute-start | bytes 294920 | tf_op jit(solution)/shard_map/ppermute | solution.py:323
  36.4 0.4 collective-permute-start.15
  36.8 1.2 %collective-permute-start.13 = (f32[64,384]{1,0:T(8,128)S(1)}, f32[64,384]{1,0:T(8,128)S(1)}, u32[]{:S(2)}, u32[]{:S(2)}) collective-permute-start(f32[64,384]{1,0:T(8,128)S(1)} %get-tuple-element.72), channel_id=1, source_target_pairs={{0,8},{4,12},{8,0},{12,4},{1,9},{5,13},{9,1},{13,5},{2,10},{6,14},... | collective-permute-start | bytes 294920 | tf_op jit(solution)/shard_map/ppermute | solution.py:278
  38.1 0.5 %finish.3.refs_3_ = f32[64,1536]{1,0:T(8,128)S(1)} custom-call(f32[16,384]{1,0:T(8,128)S(1)} %get-tuple-element.74.refs_0_, f32[64,384]{1,0:T(8,128)S(1)} %get-tuple-element.57.refs_3_.refs_1_, f32[64,384]{1,0:T(8,128)S(1)} %collective-permute-done.8.refs_4_.refs_2_, f32[32,384]{1,0:T(8,128)S(1)} %pad_maximum_fusion.refs_3_, ...), custom_call_target="tpu_custom_call" | custom-call | flops 393216 | bytes 1056768 | tf_op jit(solution)/shard_map/finish/pallas_call | solution.py:240
  38.5 2.4 %collective-permute-done.14.refs_1_ = f32[64,384]{1,0:T(8,128)S(1)} collective-permute-done((f32[64,384]{1,0:T(8,128)S(1)}, f32[64,384]{1,0:T(8,128)S(1)}, u32[]{:S(2)}, u32[]{:S(2)}) %collective-permute-start.14) | collective-permute-done | bytes 98336 | tf_op jit(solution)/shard_map/ppermute | solution.py:323
  40.9 0.8 %collective-permute-done.15.refs_2_ = f32[64,384]{1,0:T(8,128)S(1)} collective-permute-done((f32[64,384]{1,0:T(8,128)S(1)}, f32[64,384]{1,0:T(8,128)S(1)}, u32[]{:S(2)}, u32[]{:S(2)}) %collective-permute-start.15) | collective-permute-done | bytes 98336 | tf_op jit(solution)/shard_map/ppermute | solution.py:323
  41.7 0.2 finish.4.refs_3_
  41.9 0.6 %collective-permute-done.13.refs_2_ = f32[64,384]{1,0:T(8,128)S(1)} collective-permute-done((f32[64,384]{1,0:T(8,128)S(1)}, f32[64,384]{1,0:T(8,128)S(1)}, u32[]{:S(2)}, u32[]{:S(2)}) %collective-permute-start.13) | collective-permute-done | bytes 98336 | tf_op jit(solution)/shard_map/ppermute | solution.py:278
  42.5 1.0 %finish.5 = f32[64,1536]{1,0:T(8,128)} custom-call(f32[16,384]{1,0:T(8,128)S(1)} %add.10.refs_0_, f32[64,384]{1,0:T(8,128)S(1)} %get-tuple-element.71.refs_1_, f32[64,384]{1,0:T(8,128)S(1)} %collective-permute-done.13.refs_2_, f32[64,1536]{1,0:T(8,128)S(1)} %finish.4.refs_3_), custom_call_target="tpu_custom_call" | custom-call | flops 393216 | bytes 1007616 | tf_op jit(solution)/shard_map/finish/pallas_call | solution.py:240
  (32 shorter events, 0.8 us)
Async XLA Ops:
  0.0 16.6 %collective-permute-start.3 = (f32[384,384]{1,0:T(8,128)}, f32[384,384]{1,0:T(8,128)S(1)}, u32[]{:S(2)}, u32[]{:S(2)}) collective-permute-start(f32[384,384]{1,0:T(8,128)} %refs_3_.3), channel_id=1, source_target_pairs={{0,1},{1,0},{2,6},{3,7},{4,5},{5,4},{6,2},{7,3},{8,9},{9,8},{10,14... | collective-permute-start | bytes 1769480 | tf_op jit(solution)/shard_map/ppermute | solution.py:275
  3.0 13.6 %collective-permute-start.2 = (f32[384,384]{1,0:T(8,128)}, f32[384,384]{1,0:T(8,128)S(1)}, u32[]{:S(2)}, u32[]{:S(2)}) collective-permute-start(f32[384,384]{1,0:T(8,128)} %refs_3_.3), channel_id=1, source_target_pairs={{0,4},{1,2},{2,1},{3,7},{4,0},{5,6},{6,5},{7,3},{8,12},{9,10},{10,... | collective-permute-start | bytes 1769480 | tf_op jit(solution)/shard_map/ppermute | solution.py:275
  3.0 15.9 %collective-permute-start.5 = (f32[384,384]{1,0:T(8,128)}, f32[384,384]{1,0:T(8,128)S(1)}, u32[]{:S(2)}, u32[]{:S(2)}) collective-permute-start(f32[384,384]{1,0:T(8,128)} %refs_3_.3), channel_id=1, source_target_pairs={{0,4},{1,5},{2,3},{3,2},{4,0},{5,1},{6,7},{7,6},{8,12},{9,13},{10,... | collective-permute-start | bytes 1769480 | tf_op jit(solution)/shard_map/ppermute | solution.py:275
  3.5 2.7 %copy-start.3 = (s32[32,16]{0,1:T(8,128)S(1)}, s32[32,16]{0,1:T(8,128)}, u32[]{:S(2)}) copy-start(s32[32,16]{0,1:T(8,128)} %param.7) | copy-start | bytes 6148
  3.5 9.5 %copy-start = (f32[384,384]{1,0:T(8,128)S(1)}, f32[384,384]{1,0:T(8,128)}, u32[]{:S(2)}) copy-start(f32[384,384]{1,0:T(8,128)} %refs_3_.3) | copy-start | bytes 1769476
  4.7 6.9 %collective-permute-start = (f32[64,768]{1,0:T(8,128)S(1)}, f32[64,768]{1,0:T(8,128)S(1)}, u32[]{:S(2)}, u32[]{:S(2)}) collective-permute-start(f32[64,768]{1,0:T(8,128)S(1)} %get-tuple-element.79), channel_id=1, source_target_pairs={{0,8},{4,12},{8,0},{12,4},{1,9},{5,13},{9,1},{13,5},{2,10},{6,14},... | collective-permute-start | bytes 589832 | tf_op jit(solution)/shard_map/ppermute | solution.py:278
  6.2 0.7 %copy-start.1 = (s32[16,16]{1,0:T(8,128)S(1)}, s32[16,16]{1,0:T(8,128)}, u32[]{:S(2)}) copy-start(s32[16,16]{1,0:T(8,128)} %refs_2_.1) | copy-start | bytes 3076
  6.3 0.7 %copy-start.2 = (s32[16]{0:T(128)S(1)}, s32[16]{0:T(128)}, u32[]{:S(2)}) copy-start(s32[16]{0:T(128)} %refs_3_.2) | copy-start | bytes 196
  11.6 1.5 %collective-permute-start.1 = (f32[128,384]{1,0:T(8,128)S(1)}, f32[128,384]{1,0:T(8,128)S(1)}, u32[]{:S(2)}, u32[]{:S(2)}) collective-permute-start(f32[128,384]{1,0:T(8,128)S(1)} %get-tuple-element.46), channel_id=1, source_target_pairs={{0,4},{4,0},{8,12},{12,8},{1,5},{5,1},{9,13},{13,9},{2,6},{6,2},{1... | collective-permute-start | bytes 589832 | tf_op jit(solution)/shard_map/ppermute | solution.py:278
  16.7 15.3 %collective-permute-start.4 = (f32[384,384]{1,0:T(8,128)S(1)}, f32[384,384]{1,0:T(8,128)S(1)}, u32[]{:S(2)}, u32[]{:S(2)}) collective-permute-start(f32[384,384]{1,0:T(8,128)S(1)} %pick.1), channel_id=1, source_target_pairs={{0,1},{1,0},{2,3},{3,2},{4,5},{5,4},{6,7},{7,6},{8,9},{9,8},{10,11... | collective-permute-start | bytes 1769480 | tf_op jit(solution)/shard_map/ppermute | solution.py:275
  19.0 13.0 %collective-permute-start.6 = (f32[384,384]{1,0:T(8,128)S(1)}, f32[384,384]{1,0:T(8,128)S(1)}, u32[]{:S(2)}, u32[]{:S(2)}) collective-permute-start(f32[384,384]{1,0:T(8,128)S(1)} %choose.1), channel_id=1, source_target_pairs={{0,4},{1,2},{2,1},{3,7},{4,0},{5,6},{6,5},{7,3},{8,12},{9,10},{10,... | collective-permute-start | bytes 1769480 | tf_op jit(solution)/shard_map/ppermute | solution.py:275
  20.1 3.8 %collective-permute-start.9 = (f32[128,768]{1,0:T(8,128)S(1)}, f32[128,768]{1,0:T(8,128)S(1)}, u32[]{:S(2)}, u32[]{:S(2)}) collective-permute-start(f32[128,768]{1,0:T(8,128)S(1)} %get-tuple-element.62), channel_id=1, source_target_pairs={{0,4},{4,0},{8,12},{12,8},{1,5},{5,1},{9,13},{13,9},{2,6},{6,2},{1... | collective-permute-start | bytes 1179656 | tf_op jit(solution)/shard_map/ppermute | solution.py:278
  20.7 1.6 %collective-permute-start.7 = (f32[128,384]{1,0:T(8,128)S(1)}, f32[128,384]{1,0:T(8,128)S(1)}, u32[]{:S(2)}, u32[]{:S(2)}) collective-permute-start(f32[128,384]{1,0:T(8,128)S(1)} %get-tuple-element.56), channel_id=1, source_target_pairs={{0,4},{4,0},{8,12},{12,8},{1,5},{5,1},{9,13},{13,9},{2,6},{6,2},{1... | collective-permute-start | bytes 589832 | tf_op jit(solution)/shard_map/ppermute | solution.py:278
  22.3 9.8 %collective-permute-start.8 = (f32[64,384]{1,0:T(8,128)S(1)}, f32[64,384]{1,0:T(8,128)S(1)}, u32[]{:S(2)}, u32[]{:S(2)}) collective-permute-start(f32[64,384]{1,0:T(8,128)S(1)} %get-tuple-element.58), channel_id=1, source_target_pairs={{0,8},{4,12},{8,0},{12,4},{1,9},{5,13},{9,1},{13,5},{2,10},{6,14},... | collective-permute-start | bytes 294920 | tf_op jit(solution)/shard_map/ppermute | solution.py:278
  24.0 8.2 %collective-permute-start.10 = (f32[64,768]{1,0:T(8,128)S(1)}, f32[64,768]{1,0:T(8,128)S(1)}, u32[]{:S(2)}, u32[]{:S(2)}) collective-permute-start(f32[64,768]{1,0:T(8,128)S(1)} %get-tuple-element.64), channel_id=1, source_target_pairs={{0,8},{4,12},{8,0},{12,4},{1,9},{5,13},{9,1},{13,5},{2,10},{6,14},... | collective-permute-start | bytes 589832 | tf_op jit(solution)/shard_map/ppermute | solution.py:278
  32.7 1.5 %collective-permute-start.12 = (f32[128,384]{1,0:T(8,128)S(1)}, f32[128,384]{1,0:T(8,128)S(1)}, u32[]{:S(2)}, u32[]{:S(2)}) collective-permute-start(f32[128,384]{1,0:T(8,128)S(1)} %get-tuple-element.68), channel_id=1, source_target_pairs={{0,4},{4,0},{8,12},{12,8},{1,5},{5,1},{9,13},{13,9},{2,6},{6,2},{1... | collective-permute-start | bytes 589832 | tf_op jit(solution)/shard_map/ppermute | solution.py:278
  33.3 3.5 %collective-permute-start.11 = (f32[128,384]{1,0:T(8,128)S(1)}, f32[128,384]{1,0:T(8,128)S(1)}, u32[]{:S(2)}, u32[]{:S(2)}) collective-permute-start(f32[128,384]{1,0:T(8,128)S(1)} %get-tuple-element.67), channel_id=1, source_target_pairs={{0,4},{4,0},{8,12},{12,8},{1,5},{5,1},{9,13},{13,9},{2,6},{6,2},{1... | collective-permute-start | bytes 589832 | tf_op jit(solution)/shard_map/ppermute | solution.py:278
  34.2 6.7 %collective-permute-start.14 = (f32[64,384]{1,0:T(8,128)S(1)}, f32[64,384]{1,0:T(8,128)S(1)}, u32[]{:S(2)}, u32[]{:S(2)}) collective-permute-start(f32[64,384]{1,0:T(8,128)S(1)} %get-tuple-element.70.refs_3_), channel_id=1, source_target_pairs={{0,1},{1,8},{2,11},{3,2},{4,5},{5,12},{6,15},{7,6},{8,9},{9,0},{10... | collective-permute-start | bytes 294920 | tf_op jit(solution)/shard_map/ppermute | solution.py:323
  36.4 5.3 %collective-permute-start.15 = (f32[64,384]{1,0:T(8,128)S(1)}, f32[64,384]{1,0:T(8,128)S(1)}, u32[]{:S(2)}, u32[]{:S(2)}) collective-permute-start(f32[64,384]{1,0:T(8,128)S(1)} %get-tuple-element.69.refs_2_), channel_id=1, source_target_pairs={{0,1},{1,0},{2,3},{3,2},{4,5},{5,4},{6,7},{7,6},{8,9},{9,8},{10,11... | collective-permute-start | bytes 294920 | tf_op jit(solution)/shard_map/ppermute | solution.py:323
  36.8 5.7 %collective-permute-start.13 = (f32[64,384]{1,0:T(8,128)S(1)}, f32[64,384]{1,0:T(8,128)S(1)}, u32[]{:S(2)}, u32[]{:S(2)}) collective-permute-start(f32[64,384]{1,0:T(8,128)S(1)} %get-tuple-element.72), channel_id=1, source_target_pairs={{0,8},{4,12},{8,0},{12,4},{1,9},{5,13},{9,1},{13,5},{2,10},{6,14},... | collective-permute-start | bytes 294920 | tf_op jit(solution)/shard_map/ppermute | solution.py:278

commit v16 on v14

--- a/solution.py
+++ b/solution.py
@@ -154,22 +154,16 @@
     out[...] = jnp.where(marks[0:1, : out.shape[1]] > 0.5, slab[...], block[...])
 
 
-def halves_kernel(counts, *refs):
-    refs[-2][...], refs[-1][...] = masked_halves(parted(refs[:-2], counts))
-
-
-def last_kernel(high, low, b_high, b_low, keep, give):
-    half = keep.shape[0]
-    for out, start in ((give, half), (keep, 0)):
-        at = pl.ds(start, half)
-        out[...] = product(high[at, :], low[at, :], b_high[...], b_low[...])
-
-
-def corner_kernel(b_high, b_low, slab, keep, give):
+def corner_kernel(slab, block, masks, keep, give):
+    b_high, b_low = masked_halves([(block, masks)])
     half = keep.shape[0]
     for out, start in ((give, half), (keep, 0)):
         a_high, a_low = split(slab[start : start + half, :])
-        out[...] = product(a_high, a_low, b_high[...], b_low[...])
+        out[...] = product(a_high, a_low, b_high, b_low)
+
+
+def gate_kernel(out):
+    out[...] = jnp.zeros_like(out)
 
 
 def fold_kernel(keep, got, *outs):
@@ -378,27 +372,20 @@
             slots.append(multiply("both", [((EVEN, step), even), ((ODD, step), odd)]))
             continue
         out = finish(slots)
-        b_halves = call(
-            functools.partial(halves_kernel, (len(even) + 1, len(odd) + 1)),
-            "halves",
-            [jax.ShapeDtypeStruct((depth, width), jnp.bfloat16)] * 2,
-            0,
-            *even,
-            masks[EVEN, step],
-            *odd,
-            masks[ODD, step],
-            flops=WEIGHT,
-        )
-        after = tuple(share for _, shares in slots for share in shares)
+        gate = call(gate_kernel, "gate", [f32(8, 128)], 0, flops=WEIGHT, after=(*even, *odd))
+        after = (*gate, *(share for _, shares in slots for share in shares))
         sums = [f32(total // 2, width)] * 2
         flops = 6 * total * depth * width
         slots, folded = [], ()
         if corner:
-            parts = call(corner_kernel, "corner", sums, 0, *b_halves, end_slab, flops=flops, after=after)
+            args = (end_slab, *odd, masks[ODD, step])
+            parts = call(corner_kernel, "corner", sums, 0, *args, flops=flops, after=after)
             folded = fold(*parts)
             after, pieces = (parts[0],), list(enumerate(folded))
             slots.append(([[ends]], [next_door(x, 2 * i) for i, x in reversed(pieces)]))
-        parts = call(last_kernel, "last", sums, 0, high, low, *b_halves, flops=flops, after=after)
+        args = (*even, masks[EVEN, step], *odd, masks[ODD, step])
+        kernel = functools.partial(multiply_kernel, ((len(even) + 1, len(odd) + 1),))
+        parts = call(kernel, "last", sums, 0, high, low, *args, flops=flops, after=after)
         if slots:
             out = finish(slots, out)
         slots = [([[(EVEN, step), (ODD, step)]], exchange(*parts, after=folded))]

time: 43.1 us -> 42.9 us (level)
  transfers between devices with their start and end apart: 15 -> 15, of which waited for: 8 -> 9; matrix products, arithmetic and copies ran while one was open for 3% -> 3% of each run, Pallas kernels for 12% -> 11%
where the time goes in v16:
time: 42.9 us; the launch traced here: 42.7 us
  starting transfers between devices  18.3 us (43%)
  waiting for transfers between devices  16.1 us (38%)
  Pallas kernels  6.38 us (15%)
  local copies, waits for them, and re-layouts  1.77 us (4%)
    ppermute x4, starting transfers between devices, swap_line(): return lax.ppermute(x, ('row', 'col'), pairs_)  8.97 us
    ppermute x4, waiting for transfers between devices, swap_line(): return lax.ppermute(x, ('row', 'col'), pairs_)  7.07 us
    pallas_call x15, Pallas kernels, call(): pl.pallas_call(body, out_shape=outs, in_specs=[SMEM] * n_smem + [VMEM] *...  6.38 us
    ppermute x9, starting transfers between devices, swap(): return lax.ppermute(x, 'row', [(i, i ^ d) for i in range(n_row)])  6.29 us
    ppermute x9, waiting for transfers between devices, swap(): return lax.ppermute(x, 'row', [(i, i ^ d) for i in range(n_row)])  5.8 us
    ppermute x2, waiting for transfers between devices, next_door(): lax.ppermute(x, ('row', 'col'), [(i * n_col + j, (i ^ (d if 0 < j < n_col...  3.21 us
    ppermute x2, starting transfers between devices, next_door(): lax.ppermute(x, ('row', 'col'), [(i * n_col + j, (i ^ (d if 0 < j < n_col...  3 us
    dynamic_slice x1, local copies, waits for them, and re-layouts, chip_columns(): return lax.dynamic_slice_in_dim(amplitudes, start, 2 * depth, 1)  1.11 us
  transfers between devices with their start and end apart: 15, of which 9 were waited for; matrix products, arithmetic and copies ran while one was open for 3% of the time, Pallas kernels for 11%

profile of v16, /device:TPU:0, one launch (start us, length us, event | category | flops | bytes accessed | tf_op | source)
XLA Modules:
  0.0 42.7 jit_solution(14432373913656587397)
XLA Ops:
  0.0 0.5 %collective-permute-start.2 = (f32[384,384]{1,0:T(8,128)}, f32[384,384]{1,0:T(8,128)S(1)}, u32[]{:S(2)}, u32[]{:S(2)}) collective-permute-start(f32[384,384]{1,0:T(8,128)} %refs_3_.3), channel_id=1, source_target_pairs={{0,4},{1,2},{2,1},{3,7},{4,0},{5,6},{6,5},{7,3},{8,12},{9,10},{10,... | collective-permute-start | bytes 1769480 | tf_op jit(solution)/shard_map/ppermute | solution.py:258
  0.5 4.1 %collective-permute-start.4 = (f32[384,384]{1,0:T(8,128)}, f32[384,384]{1,0:T(8,128)S(1)}, u32[]{:S(2)}, u32[]{:S(2)}) collective-permute-start(f32[384,384]{1,0:T(8,128)} %refs_3_.3), channel_id=1, source_target_pairs={{0,1},{1,0},{2,3},{3,2},{4,5},{5,4},{6,7},{7,6},{8,9},{9,8},{10,11... | collective-permute-start | bytes 1769480 | tf_op jit(solution)/shard_map/ppermute | solution.py:258
  4.6 1.1 %constant_dynamic-slice_fusion = (f32[64,768]{1,0:T(8,128)S(1)}, f32[64,768]{1,0:T(8,128)S(1)}) fusion(f32[64,1536]{1,0:T(8,128)} %param.5, s32[]{:T(128)S(6)} %select_n.14, s32[]{:T(128)S(6)} %select_n.13), kind=kLoop, calls=%fused_computation.2 | loop fusion | bytes 786440 | tf_op jit(solution)/shard_map/dynamic_slice | solution.py:286
  5.7 1.6 %collective-permute-start = (f32[64,768]{1,0:T(8,128)S(1)}, f32[64,768]{1,0:T(8,128)S(1)}, u32[]{:S(2)}, u32[]{:S(2)}) collective-permute-start(f32[64,768]{1,0:T(8,128)S(1)} %get-tuple-element.73), channel_id=1, source_target_pairs={{0,8},{4,12},{8,0},{12,4},{1,9},{5,13},{9,1},{13,5},{2,10},{6,14},... | collective-permute-start | bytes 589832 | tf_op jit(solution)/shard_map/ppermute | solution.py:261
  7.3 0.1 copy.6.refs_1_
  7.4 0.1 pad_add_fusion.refs_0_
  7.4 0.5 %copy-done.1 = s32[16,16]{1,0:T(8,128)S(1)} copy-done((s32[16,16]{1,0:T(8,128)S(1)}, s32[16,16]{1,0:T(8,128)}, u32[]{:S(2)}) %copy-start.1) | copy-done | bytes 1048
  8.0 2.0 %tables.1 = (f32[8,384]{1,0:T(8,128)S(1)}, f32[8,384]{1,0:T(8,128)S(1)}, f32[4,384]{1,0:T(4,128)S(1)}, f32[16,384]{1,0:T(8,128)S(1)}, f32[4,384]{1,0:T(4,128)S(1...) custom-call(s32[3]{0:T(128)S(1)} %pad_add_fusion.refs_0_, ...), custom_call_target="tpu_custom_call" | custom-call | bytes 212044 | tf_op jit(solution)/shard_map/tables/pallas_call | solution.py:224
  10.0 1.8 %collective-permute-done.refs_2_ = f32[64,768]{1,0:T(8,128)S(1)} collective-permute-done((f32[64,768]{1,0:T(8,128)S(1)}, f32[64,768]{1,0:T(8,128)S(1)}, u32[]{:S(2)}, u32[]{:S(2)}) %collective-permute-start) | collective-permute-done | bytes 196640 | tf_op jit(solution)/shard_map/ppermute | solution.py:261
  12.0 1.4 %collective-permute-done.1.refs_2_ = f32[128,384]{1,0:T(8,128)S(1)} collective-permute-done((f32[128,384]{1,0:T(8,128)S(1)}, f32[128,384]{1,0:T(8,128)S(1)}, u32[]{:S(2)}, u32[]{:S(2)}) %collective-permute-start.1) | collective-permute-done | bytes 196640 | tf_op jit(solution)/shard_map/ppermute | solution.py:261
  13.4 0.6 %own.1 = (bf16[256,384]{1,0:T(8,128)(2,1)S(1)}, bf16[256,384]{1,0:T(8,128)(2,1)S(1)}, f32[384,384]{1,0:T(8,128)S(1)}, f32[128,384]{1,0:T(8,128)S(1)}, f32[128,384]{1,0:T(8,128)S(1)}) custom-call(f32[8,384]{1,0:T(8,128)S(1)} %get-tuple-element.41.refs_0_, f32[128,384]{1,0:T(8,128)S(1)} %get-tuple-element.43.refs_1_, ...), custom_call_target="tpu_custom_call" | custom-call | flops 226492416 | bytes 2377728 | tf_op jit(solution)/shard_map/own/pallas_call | solution.py:224
  14.1 4.4 %collective-permute-start.3 = (f32[384,384]{1,0:T(8,128)S(1)}, f32[384,384]{1,0:T(8,128)S(1)}, u32[]{:S(2)}, u32[]{:S(2)}) collective-permute-start(f32[384,384]{1,0:T(8,128)S(1)} %pick.1), channel_id=1, source_target_pairs={{0,1},{1,0},{2,3},{3,2},{4,5},{5,4},{6,7},{7,6},{8,9},{9,8},{10,11... | collective-permute-start | bytes 1769480 | tf_op jit(solution)/shard_map/ppermute | solution.py:258
  18.4 0.9 %pair.1 = (f32[128,768]{1,0:T(8,128)S(1)}, f32[128,768]{1,0:T(8,128)S(1)}) custom-call(bf16[256,384]{1,0:T(8,128)(2,1)S(1)} %get-tuple-element.46.refs_0_, bf16[256,384]{1,0:T(8,128)(2,1)S(1)} %get-tuple-element.47.refs_1_, f32[384,384]{1,0:T(8,128)S(1)} %collective-permute-done.4.refs_2_, f32[4,384]{1,0:T(4,128)S(1)} %get-tuple-element.55.refs_3_, ...), custom_call_target="tpu_custom_call" | custom-call | flops 452984832 | bytes 2371584 | tf_op jit(solution)/shard_map/pair/pallas_call | solution.py:224
  19.4 0.6 %collective-permute-start.8 = (f32[128,768]{1,0:T(8,128)S(1)}, f32[128,768]{1,0:T(8,128)S(1)}, u32[]{:S(2)}, u32[]{:S(2)}) collective-permute-start(f32[128,768]{1,0:T(8,128)S(1)} %get-tuple-element.58), channel_id=1, source_target_pairs={{0,4},{4,0},{8,12},{12,8},{1,5},{5,1},{9,13},{13,9},{2,6},{6,2},{1... | collective-permute-start | bytes 1179656 | tf_op jit(solution)/shard_map/ppermute | solution.py:261
  20.0 0.1 collective-permute-start.6
  20.0 1.6 %collective-permute-done.6.refs_1_ = f32[128,384]{1,0:T(8,128)S(1)} collective-permute-done((f32[128,384]{1,0:T(8,128)S(1)}, f32[128,384]{1,0:T(8,128)S(1)}, u32[]{:S(2)}, u32[]{:S(2)}) %collective-permute-start.6) | collective-permute-done | bytes 196640 | tf_op jit(solution)/shard_map/ppermute | solution.py:261
  21.6 1.6 %collective-permute-start.7 = (f32[64,384]{1,0:T(8,128)S(1)}, f32[64,384]{1,0:T(8,128)S(1)}, u32[]{:S(2)}, u32[]{:S(2)}) collective-permute-start(f32[64,384]{1,0:T(8,128)S(1)} %get-tuple-element.54), channel_id=1, source_target_pairs={{0,8},{4,12},{8,0},{12,4},{1,9},{5,13},{9,1},{13,5},{2,10},{6,14},... | collective-permute-start | bytes 294920 | tf_op jit(solution)/shard_map/ppermute | solution.py:261
  23.2 0.6 %collective-permute-start.9 = (f32[64,768]{1,0:T(8,128)S(1)}, f32[64,768]{1,0:T(8,128)S(1)}, u32[]{:S(2)}, u32[]{:S(2)}) collective-permute-start(f32[64,768]{1,0:T(8,128)S(1)} %get-tuple-element.60), channel_id=1, source_target_pairs={{0,8},{4,12},{8,0},{12,4},{1,9},{5,13},{9,1},{13,5},{2,10},{6,14},... | collective-permute-start | bytes 589832 | tf_op jit(solution)/shard_map/ppermute | solution.py:261
  23.8 7.1 %collective-permute-done.3.refs_0_.refs_2_ = f32[384,384]{1,0:T(8,128)S(1)} collective-permute-done((f32[384,384]{1,0:T(8,128)S(1)}, f32[384,384]{1,0:T(8,128)S(1)}, u32[]{:S(2)}, u32[]{:S(2)}) %collective-permute-start.3) | collective-permute-done | bytes 589856 | tf_op jit(solution)/shard_map/ppermute | solution.py:258
  31.0 0.5 %corner.1 = (f32[128,384]{1,0:T(8,128)S(1)}, f32[128,384]{1,0:T(8,128)S(1)}) custom-call(f32[384,384]{1,0:T(8,128)S(1)} %collective-permute-done.3.refs_0_.refs_2_, f32[384,384]{1,0:T(8,128)S(1)} %collective-permute-done.5.refs_1_.refs_4_, f32[4,384]{1,0:T(4,128)S(1)} %get-tuple-element.50.refs_2_.refs_5_, f32[8,128]{1,0:T(8,128)S(1)} %gate.1.refs_3_, ...), custom_call_target="tpu_custom_call" | custom-call | flops 226492416 | bytes 1579008 | tf_op jit(solution)/shard_map/corner/pallas_call | solution.py:224
  31.6 0.5 %last.1 = (f32[128,384]{1,0:T(8,128)S(1)}, f32[128,384]{1,0:T(8,128)S(1)}) custom-call(bf16[256,384]{1,0:T(8,128)(2,1)S(1)} %get-tuple-element.46.refs_0_, bf16[256,384]{1,0:T(8,128)(2,1)S(1)} %get-tuple-element.47.refs_1_, f32[384,384]{1,0:T(8,128)S(1)} %collective-permute-done.3.refs_0_.refs_2_, f32[4,384]{1,0:T(4,128)S(1)} %get-tuple-element.49.refs_3_, ...), custom_call_target="tpu_custom_call" | custom-call | flops 226492416 | bytes 1978368 | tf_op jit(solution)/shard_map/last/pallas_call | solution.py:224
  32.1 0.6 %collective-permute-start.10 = (f32[128,384]{1,0:T(8,128)S(1)}, f32[128,384]{1,0:T(8,128)S(1)}, u32[]{:S(2)}, u32[]{:S(2)}) collective-permute-start(f32[128,384]{1,0:T(8,128)S(1)} %get-tuple-element.63), channel_id=1, source_target_pairs={{0,4},{4,0},{8,12},{12,8},{1,5},{5,1},{9,13},{13,9},{2,6},{6,2},{1... | collective-permute-start | bytes 589832 | tf_op jit(solution)/shard_map/ppermute | solution.py:261
  32.7 0.3 collective-permute-done.11.refs_1_
  33.0 2.6 %collective-permute-start.13 = (f32[64,384]{1,0:T(8,128)S(1)}, f32[64,384]{1,0:T(8,128)S(1)}, u32[]{:S(2)}, u32[]{:S(2)}) collective-permute-start(f32[64,384]{1,0:T(8,128)S(1)} %get-tuple-element.66.refs_3_), channel_id=1, source_target_pairs={{0,1},{1,8},{2,11},{3,2},{4,5},{5,12},{6,15},{7,6},{8,9},{9,0},{10... | collective-permute-start | bytes 294920 | tf_op jit(solution)/shard_map/ppermute | solution.py:302
  35.6 0.4 collective-permute-start.14
  36.1 1.2 %collective-permute-start.12 = (f32[64,384]{1,0:T(8,128)S(1)}, f32[64,384]{1,0:T(8,128)S(1)}, u32[]{:S(2)}, u32[]{:S(2)}) collective-permute-start(f32[64,384]{1,0:T(8,128)S(1)} %get-tuple-element.68), channel_id=1, source_target_pairs={{0,8},{4,12},{8,0},{12,4},{1,9},{5,13},{9,1},{13,5},{2,10},{6,14},... | collective-permute-start | bytes 294920 | tf_op jit(solution)/shard_map/ppermute | solution.py:261
  37.3 0.5 %finish.3.refs_3_ = f32[64,1536]{1,0:T(8,128)S(1)} custom-call(f32[16,384]{1,0:T(8,128)S(1)} %get-tuple-element.70.refs_0_, f32[64,384]{1,0:T(8,128)S(1)} %get-tuple-element.53.refs_4_.refs_1_, f32[64,384]{1,0:T(8,128)S(1)} %collective-permute-done.7.refs_5_.refs_2_, f32[32,384]{1,0:T(8,128)S(1)} %pad_maximum_fusion.refs_3_, ...), custom_call_target="tpu_custom_call" | custom-call | flops 393216 | bytes 1056768 | tf_op jit(solution)/shard_map/finish/pallas_call | solution.py:224
  37.7 2.4 %collective-permute-done.13.refs_1_ = f32[64,384]{1,0:T(8,128)S(1)} collective-permute-done((f32[64,384]{1,0:T(8,128)S(1)}, f32[64,384]{1,0:T(8,128)S(1)}, u32[]{:S(2)}, u32[]{:S(2)}) %collective-permute-start.13) | collective-permute-done | bytes 98336 | tf_op jit(solution)/shard_map/ppermute | solution.py:302
  40.1 0.8 %collective-permute-done.14.refs_2_ = f32[64,384]{1,0:T(8,128)S(1)} collective-permute-done((f32[64,384]{1,0:T(8,128)S(1)}, f32[64,384]{1,0:T(8,128)S(1)}, u32[]{:S(2)}, u32[]{:S(2)}) %collective-permute-start.14) | collective-permute-done | bytes 98336 | tf_op jit(solution)/shard_map/ppermute | solution.py:302
  41.0 0.2 finish.4.refs_3_
  41.1 0.6 %collective-permute-done.12.refs_2_ = f32[64,384]{1,0:T(8,128)S(1)} collective-permute-done((f32[64,384]{1,0:T(8,128)S(1)}, f32[64,384]{1,0:T(8,128)S(1)}, u32[]{:S(2)}, u32[]{:S(2)}) %collective-permute-start.12) | collective-permute-done | bytes 98336 | tf_op jit(solution)/shard_map/ppermute | solution.py:261
  41.7 1.0 %finish.5 = f32[64,1536]{1,0:T(8,128)} custom-call(f32[16,384]{1,0:T(8,128)S(1)} %add.10.refs_0_, f32[64,384]{1,0:T(8,128)S(1)} %get-tuple-element.67.refs_1_, f32[64,384]{1,0:T(8,128)S(1)} %collective-permute-done.12.refs_2_, f32[64,1536]{1,0:T(8,128)S(1)} %finish.4.refs_3_), custom_call_target="tpu_custom_call" | custom-call | flops 393216 | bytes 1007616 | tf_op jit(solution)/shard_map/finish/pallas_call | solution.py:224
  (26 shorter events, 0.5 us)
Async XLA Ops:
  0.0 14.0 %collective-permute-start.2 = (f32[384,384]{1,0:T(8,128)}, f32[384,384]{1,0:T(8,128)S(1)}, u32[]{:S(2)}, u32[]{:S(2)}) collective-permute-start(f32[384,384]{1,0:T(8,128)} %refs_3_.3), channel_id=1, source_target_pairs={{0,4},{1,2},{2,1},{3,7},{4,0},{5,6},{6,5},{7,3},{8,12},{9,10},{10,... | collective-permute-start | bytes 1769480 | tf_op jit(solution)/shard_map/ppermute | solution.py:258
  0.5 18.0 %collective-permute-start.4 = (f32[384,384]{1,0:T(8,128)}, f32[384,384]{1,0:T(8,128)S(1)}, u32[]{:S(2)}, u32[]{:S(2)}) collective-permute-start(f32[384,384]{1,0:T(8,128)} %refs_3_.3), channel_id=1, source_target_pairs={{0,1},{1,0},{2,3},{3,2},{4,5},{5,4},{6,7},{7,6},{8,9},{9,8},{10,11... | collective-permute-start | bytes 1769480 | tf_op jit(solution)/shard_map/ppermute | solution.py:258
  4.6 2.7 %copy-start.3 = (s32[32,16]{0,1:T(8,128)S(1)}, s32[32,16]{0,1:T(8,128)}, u32[]{:S(2)}) copy-start(s32[32,16]{0,1:T(8,128)} %param.7) | copy-start | bytes 6148
  4.6 8.8 %copy-start = (f32[384,384]{1,0:T(8,128)S(1)}, f32[384,384]{1,0:T(8,128)}, u32[]{:S(2)}) copy-start(f32[384,384]{1,0:T(8,128)} %refs_3_.3) | copy-start | bytes 1769476
  5.7 6.1 %collective-permute-start = (f32[64,768]{1,0:T(8,128)S(1)}, f32[64,768]{1,0:T(8,128)S(1)}, u32[]{:S(2)}, u32[]{:S(2)}) collective-permute-start(f32[64,768]{1,0:T(8,128)S(1)} %get-tuple-element.73), channel_id=1, source_target_pairs={{0,8},{4,12},{8,0},{12,4},{1,9},{5,13},{9,1},{13,5},{2,10},{6,14},... | collective-permute-start | bytes 589832 | tf_op jit(solution)/shard_map/ppermute | solution.py:261
  7.3 0.7 %copy-start.1 = (s32[16,16]{1,0:T(8,128)S(1)}, s32[16,16]{1,0:T(8,128)}, u32[]{:S(2)}) copy-start(s32[16,16]{1,0:T(8,128)} %refs_2_.1) | copy-start | bytes 3076
  7.4 0.7 %copy-start.2 = (s32[16]{0:T(128)S(1)}, s32[16]{0:T(128)}, u32[]{:S(2)}) copy-start(s32[16]{0:T(128)} %refs_3_.2) | copy-start | bytes 196
  11.9 1.5 %collective-permute-start.1 = (f32[128,384]{1,0:T(8,128)S(1)}, f32[128,384]{1,0:T(8,128)S(1)}, u32[]{:S(2)}, u32[]{:S(2)}) collective-permute-start(f32[128,384]{1,0:T(8,128)S(1)} %get-tuple-element.44), channel_id=1, source_target_pairs={{0,4},{4,0},{8,12},{12,8},{1,5},{5,1},{9,13},{13,9},{2,6},{6,2},{1... | collective-permute-start | bytes 589832 | tf_op jit(solution)/shard_map/ppermute | solution.py:261
  14.1 16.8 %collective-permute-start.3 = (f32[384,384]{1,0:T(8,128)S(1)}, f32[384,384]{1,0:T(8,128)S(1)}, u32[]{:S(2)}, u32[]{:S(2)}) collective-permute-start(f32[384,384]{1,0:T(8,128)S(1)} %pick.1), channel_id=1, source_target_pairs={{0,1},{1,0},{2,3},{3,2},{4,5},{5,4},{6,7},{7,6},{8,9},{9,8},{10,11... | collective-permute-start | bytes 1769480 | tf_op jit(solution)/shard_map/ppermute | solution.py:258
  18.4 12.5 %collective-permute-start.5 = (f32[384,384]{1,0:T(8,128)S(1)}, f32[384,384]{1,0:T(8,128)S(1)}, u32[]{:S(2)}, u32[]{:S(2)}) collective-permute-start(f32[384,384]{1,0:T(8,128)S(1)} %collective-permute-done.4.refs_2_), channel_id=1, source_target_pairs={{0,4},{1,2},{2,1},{3,7},{4,0},{5,6},{6,5},{7,3},{8,12},{9,10},{10,... | collective-permute-start | bytes 1769480 | tf_op jit(solution)/shard_map/ppermute | solution.py:258
  19.4 3.8 %collective-permute-start.8 = (f32[128,768]{1,0:T(8,128)S(1)}, f32[128,768]{1,0:T(8,128)S(1)}, u32[]{:S(2)}, u32[]{:S(2)}) collective-permute-start(f32[128,768]{1,0:T(8,128)S(1)} %get-tuple-element.58), channel_id=1, source_target_pairs={{0,4},{4,0},{8,12},{12,8},{1,5},{5,1},{9,13},{13,9},{2,6},{6,2},{1... | collective-permute-start | bytes 1179656 | tf_op jit(solution)/shard_map/ppermute | solution.py:261
  20.0 1.6 %collective-permute-start.6 = (f32[128,384]{1,0:T(8,128)S(1)}, f32[128,384]{1,0:T(8,128)S(1)}, u32[]{:S(2)}, u32[]{:S(2)}) collective-permute-start(f32[128,384]{1,0:T(8,128)S(1)} %get-tuple-element.52), channel_id=1, source_target_pairs={{0,4},{4,0},{8,12},{12,8},{1,5},{5,1},{9,13},{13,9},{2,6},{6,2},{1... | collective-permute-start | bytes 589832 | tf_op jit(solution)/shard_map/ppermute | solution.py:261
  21.6 9.3 %collective-permute-start.7 = (f32[64,384]{1,0:T(8,128)S(1)}, f32[64,384]{1,0:T(8,128)S(1)}, u32[]{:S(2)}, u32[]{:S(2)}) collective-permute-start(f32[64,384]{1,0:T(8,128)S(1)} %get-tuple-element.54), channel_id=1, source_target_pairs={{0,8},{4,12},{8,0},{12,4},{1,9},{5,13},{9,1},{13,5},{2,10},{6,14},... | collective-permute-start | bytes 294920 | tf_op jit(solution)/shard_map/ppermute | solution.py:261
  23.2 7.7 %collective-permute-start.9 = (f32[64,768]{1,0:T(8,128)S(1)}, f32[64,768]{1,0:T(8,128)S(1)}, u32[]{:S(2)}, u32[]{:S(2)}) collective-permute-start(f32[64,768]{1,0:T(8,128)S(1)} %get-tuple-element.60), channel_id=1, source_target_pairs={{0,8},{4,12},{8,0},{12,4},{1,9},{5,13},{9,1},{13,5},{2,10},{6,14},... | collective-permute-start | bytes 589832 | tf_op jit(solution)/shard_map/ppermute | solution.py:261
  31.5 1.5 %collective-permute-start.11 = (f32[128,384]{1,0:T(8,128)S(1)}, f32[128,384]{1,0:T(8,128)S(1)}, u32[]{:S(2)}, u32[]{:S(2)}) collective-permute-start(f32[128,384]{1,0:T(8,128)S(1)} %get-tuple-element.64), channel_id=1, source_target_pairs={{0,4},{4,0},{8,12},{12,8},{1,5},{5,1},{9,13},{13,9},{2,6},{6,2},{1... | collective-permute-start | bytes 589832 | tf_op jit(solution)/shard_map/ppermute | solution.py:261
  32.1 3.9 %collective-permute-start.10 = (f32[128,384]{1,0:T(8,128)S(1)}, f32[128,384]{1,0:T(8,128)S(1)}, u32[]{:S(2)}, u32[]{:S(2)}) collective-permute-start(f32[128,384]{1,0:T(8,128)S(1)} %get-tuple-element.63), channel_id=1, source_target_pairs={{0,4},{4,0},{8,12},{12,8},{1,5},{5,1},{9,13},{13,9},{2,6},{6,2},{1... | collective-permute-start | bytes 589832 | tf_op jit(solution)/shard_map/ppermute | solution.py:261
  33.0 7.1 %collective-permute-start.13 = (f32[64,384]{1,0:T(8,128)S(1)}, f32[64,384]{1,0:T(8,128)S(1)}, u32[]{:S(2)}, u32[]{:S(2)}) collective-permute-start(f32[64,384]{1,0:T(8,128)S(1)} %get-tuple-element.66.refs_3_), channel_id=1, source_target_pairs={{0,1},{1,8},{2,11},{3,2},{4,5},{5,12},{6,15},{7,6},{8,9},{9,0},{10... | collective-permute-start | bytes 294920 | tf_op jit(solution)/shard_map/ppermute | solution.py:302
  35.6 5.3 %collective-permute-start.14 = (f32[64,384]{1,0:T(8,128)S(1)}, f32[64,384]{1,0:T(8,128)S(1)}, u32[]{:S(2)}, u32[]{:S(2)}) collective-permute-start(f32[64,384]{1,0:T(8,128)S(1)} %get-tuple-element.65.refs_2_), channel_id=1, source_target_pairs={{0,1},{1,0},{2,3},{3,2},{4,5},{5,4},{6,7},{7,6},{8,9},{9,8},{10,11... | collective-permute-start | bytes 294920 | tf_op jit(solution)/shard_map/ppermute | solution.py:302
  36.1 5.7 %collective-permute-start.12 = (f32[64,384]{1,0:T(8,128)S(1)}, f32[64,384]{1,0:T(8,128)S(1)}, u32[]{:S(2)}, u32[]{:S(2)}) collective-permute-start(f32[64,384]{1,0:T(8,128)S(1)} %get-tuple-element.68), channel_id=1, source_target_pairs={{0,8},{4,12},{8,0},{12,4},{1,9},{5,13},{9,1},{13,5},{2,10},{6,14},... | collective-permute-start | bytes 294920 | tf_op jit(solution)/shard_map/ppermute | solution.py:261

commit v17 on v16

--- a/solution.py
+++ b/solution.py
@@ -109,7 +109,9 @@
 
 def product(a_high, a_low, b_high, b_low):
     dot = functools.partial(jnp.dot, preferred_element_type=jnp.float32)
-    return dot(a_high, b_high) + (dot(a_high, b_low) + dot(a_low, b_high))
+    rows = a_high.shape[0]
+    both = dot(jnp.concatenate([a_high, a_low], axis=0), b_high)
+    return both[:rows, :] + (dot(a_high, b_low) + both[rows:, :])
 
 
 def multiply_kernel(groups, high, low, *refs):
@@ -118,9 +120,10 @@
     for g, counts in enumerate(groups):
         b_high, b_low = masked_halves(parted(refs, counts))
         refs = refs[sum(counts) :]
-        for out, start in ((give, half), (keep, 0)):
-            at = pl.ds(start, half)
-            out[:, g * width : (g + 1) * width] = product(high[at, :], low[at, :], b_high, b_low)
+        at = pl.ds(g * width, width)
+        sums = product(high[...], low[...], b_high, b_low)
+        give[:, at] = sums[half:, :]
+        keep[:, at] = sums[:half, :]
 
 
 def own_kernel(amp_rows, *refs):
@@ -157,9 +160,10 @@
 def corner_kernel(slab, block, masks, keep, give):
     b_high, b_low = masked_halves([(block, masks)])
     half = keep.shape[0]
-    for out, start in ((give, half), (keep, 0)):
-        a_high, a_low = split(slab[start : start + half, :])
-        out[...] = product(a_high, a_low, b_high, b_low)
+    a_high, a_low = split(slab[: 2 * half, :])
+    sums = product(a_high, a_low, b_high, b_low)
+    give[...] = sums[half:, :]
+    keep[...] = sums[:half, :]
 
 
 def gate_kernel(out):
@@ -196,19 +200,23 @@
             turned = [part] + [pltpu.roll(part, t * TB, 1) for t in range(1, PER)]
             totals.append((homes, g * n_home * PER, turned))
     copies = []
-    for home in range(n_home):
-        to = pl.ds(home * GROUP, GROUP)
-        if len(refs) - 1 > n_in:
-            value = refs[n_in][:, to]
-        else:
-            value = jnp.zeros((rows, GROUP), jnp.float32)
-        for homes, base, turned in totals:
-            for t in range(PER):
-                row = base + home * PER + t
-                value = jnp.where(homes[row : row + 1, :] > 0.5, turned[t], value)
-        out[:, to] = value
+    runs = 1 if sems is None else sems.shape[0]
+    for run in range(runs):
+        at = pl.ds(run * (rows // runs), rows // runs)
+        for home in range(n_home):
+            to = pl.ds(home * GROUP, GROUP)
+            if len(refs) - 1 > n_in:
+                value = refs[n_in][at, to]
+            else:
+                value = jnp.zeros((rows // runs, GROUP), jnp.float32)
+            for homes, base, turned in totals:
+                for t in range(PER):
+                    row = base + home * PER + t
+                    part = turned[t][run * (rows // runs) : (run + 1) * (rows // runs), :]
+                    value = jnp.where(homes[row : row + 1, :] > 0.5, part, value)
+            out[at, to] = value
         if sems is not None:
-            copies.append(pltpu.make_async_copy(out.at[:, to], final.at[:, to], sems.at[home]))
+            copies.append(pltpu.make_async_copy(out.at[at, :], final.at[at, :], sems.at[run]))
             copies[-1].start()
     for copy in copies:
         copy.wait()
@@ -325,7 +333,7 @@
     def finish(slots, *so_far, final=False):
         args, counts, place_ = [], [], {}
         if final:
-            buffers = [pltpu.VMEM((rows, pairs), jnp.float32), pltpu.SemaphoreType.DMA((pairs // GROUP,))]
+            buffers = [pltpu.VMEM((rows, pairs), jnp.float32), pltpu.SemaphoreType.DMA((2,))]
             place_ = dict(scratch=buffers, out_space=pl.ANY)
         for groups, shares in slots:
             args.append(jnp.concatenate([sum(homes[name] for name in names) for names in groups]))

time: 42.9 us -> 42.9 us (level)
  transfers between devices with their start and end apart: 15 -> 15, of which waited for: 9 -> 8; matrix products, arithmetic and copies ran while one was open for 3% -> 3% of each run, Pallas kernels for 11% -> 11%
where the time goes in v17:
time: 42.9 us; the launch traced here: 42.7 us
  starting transfers between devices  18.3 us (43%)
  waiting for transfers between devices  16.1 us (38%)
  Pallas kernels  6.3 us (15%)
  local copies, waits for them, and re-layouts  1.77 us (4%)
    ppermute x4, starting transfers between devices, swap_line(): return lax.ppermute(x, ('row', 'col'), pairs_)  8.97 us
    ppermute x4, waiting for transfers between devices, swap_line(): return lax.ppermute(x, ('row', 'col'), pairs_)  7.1 us
    ppermute x9, starting transfers between devices, swap(): return lax.ppermute(x, 'row', [(i, i ^ d) for i in range(n_row)])  6.32 us
    pallas_call x15, Pallas kernels, call(): pl.pallas_call(body, out_shape=outs, in_specs=[SMEM] * n_smem + [VMEM] *...  6.3 us
    ppermute x9, waiting for transfers between devices, swap(): return lax.ppermute(x, 'row', [(i, i ^ d) for i in range(n_row)])  5.8 us
    ppermute x2, waiting for transfers between devices, next_door(): lax.ppermute(x, ('row', 'col'), [(i * n_col + j, (i ^ (d if 0 < j < n_col...  3.18 us
    ppermute x2, starting transfers between devices, next_door(): lax.ppermute(x, ('row', 'col'), [(i * n_col + j, (i ^ (d if 0 < j < n_col...  3 us
    dynamic_slice x1, local copies, waits for them, and re-layouts, chip_columns(): return lax.dynamic_slice_in_dim(amplitudes, start, 2 * depth, 1)  1.11 us
  transfers between devices with their start and end apart: 15, of which 8 were waited for; matrix products, arithmetic and copies ran while one was open for 3% of the time, Pallas kernels for 11%

profile of v17, /device:TPU:0, one launch (start us, length us, event | category | flops | bytes accessed | tf_op | source)
XLA Modules:
  0.0 42.7 jit_solution(1175158995161564328)
XLA Ops:
  0.0 0.5 %collective-permute-start.2 = (f32[384,384]{1,0:T(8,128)}, f32[384,384]{1,0:T(8,128)S(1)}, u32[]{:S(2)}, u32[]{:S(2)}) collective-permute-start(f32[384,384]{1,0:T(8,128)} %refs_3_.3), channel_id=1, source_target_pairs={{0,4},{1,2},{2,1},{3,7},{4,0},{5,6},{6,5},{7,3},{8,12},{9,10},{10,... | collective-permute-start | bytes 1769480 | tf_op jit(solution)/shard_map/ppermute | solution.py:266
  0.5 4.1 %collective-permute-start.4 = (f32[384,384]{1,0:T(8,128)}, f32[384,384]{1,0:T(8,128)S(1)}, u32[]{:S(2)}, u32[]{:S(2)}) collective-permute-start(f32[384,384]{1,0:T(8,128)} %refs_3_.3), channel_id=1, source_target_pairs={{0,1},{1,0},{2,3},{3,2},{4,5},{5,4},{6,7},{7,6},{8,9},{9,8},{10,11... | collective-permute-start | bytes 1769480 | tf_op jit(solution)/shard_map/ppermute | solution.py:266
  4.6 1.1 %constant_dynamic-slice_fusion = (f32[64,768]{1,0:T(8,128)S(1)}, f32[64,768]{1,0:T(8,128)S(1)}) fusion(f32[64,1536]{1,0:T(8,128)} %param.5, s32[]{:T(128)S(6)} %select_n.14, s32[]{:T(128)S(6)} %select_n.13), kind=kLoop, calls=%fused_computation.2 | loop fusion | bytes 786440 | tf_op jit(solution)/shard_map/dynamic_slice | solution.py:294
  5.7 1.6 %collective-permute-start = (f32[64,768]{1,0:T(8,128)S(1)}, f32[64,768]{1,0:T(8,128)S(1)}, u32[]{:S(2)}, u32[]{:S(2)}) collective-permute-start(f32[64,768]{1,0:T(8,128)S(1)} %get-tuple-element.73), channel_id=1, source_target_pairs={{0,8},{4,12},{8,0},{12,4},{1,9},{5,13},{9,1},{13,5},{2,10},{6,14},... | collective-permute-start | bytes 589832 | tf_op jit(solution)/shard_map/ppermute | solution.py:269
  7.3 0.1 copy.6.refs_1_
  7.4 0.1 pad_add_fusion.refs_0_
  7.4 0.5 %copy-done.1 = s32[16,16]{1,0:T(8,128)S(1)} copy-done((s32[16,16]{1,0:T(8,128)S(1)}, s32[16,16]{1,0:T(8,128)}, u32[]{:S(2)}) %copy-start.1) | copy-done | bytes 1048
  8.0 2.0 %tables.1 = (f32[8,384]{1,0:T(8,128)S(1)}, f32[8,384]{1,0:T(8,128)S(1)}, f32[4,384]{1,0:T(4,128)S(1)}, f32[16,384]{1,0:T(8,128)S(1)}, f32[4,384]{1,0:T(4,128)S(1...) custom-call(s32[3]{0:T(128)S(1)} %pad_add_fusion.refs_0_, ...), custom_call_target="tpu_custom_call" | custom-call | bytes 212044 | tf_op jit(solution)/shard_map/tables/pallas_call | solution.py:232
  10.0 1.8 %collective-permute-done.refs_2_ = f32[64,768]{1,0:T(8,128)S(1)} collective-permute-done((f32[64,768]{1,0:T(8,128)S(1)}, f32[64,768]{1,0:T(8,128)S(1)}, u32[]{:S(2)}, u32[]{:S(2)}) %collective-permute-start) | collective-permute-done | bytes 196640 | tf_op jit(solution)/shard_map/ppermute | solution.py:269
  12.0 1.4 %collective-permute-done.1.refs_2_ = f32[128,384]{1,0:T(8,128)S(1)} collective-permute-done((f32[128,384]{1,0:T(8,128)S(1)}, f32[128,384]{1,0:T(8,128)S(1)}, u32[]{:S(2)}, u32[]{:S(2)}) %collective-permute-start.1) | collective-permute-done | bytes 196640 | tf_op jit(solution)/shard_map/ppermute | solution.py:269
  13.4 0.6 %own.1 = (bf16[256,384]{1,0:T(8,128)(2,1)S(1)}, bf16[256,384]{1,0:T(8,128)(2,1)S(1)}, f32[384,384]{1,0:T(8,128)S(1)}, f32[128,384]{1,0:T(8,128)S(1)}, f32[128,384]{1,0:T(8,128)S(1)}) custom-call(f32[8,384]{1,0:T(8,128)S(1)} %get-tuple-element.41.refs_0_, f32[128,384]{1,0:T(8,128)S(1)} %get-tuple-element.43.refs_1_, ...), custom_call_target="tpu_custom_call" | custom-call | flops 226492416 | bytes 2377728 | tf_op jit(solution)/shard_map/own/pallas_call | solution.py:232
  14.1 4.4 %collective-permute-start.3 = (f32[384,384]{1,0:T(8,128)S(1)}, f32[384,384]{1,0:T(8,128)S(1)}, u32[]{:S(2)}, u32[]{:S(2)}) collective-permute-start(f32[384,384]{1,0:T(8,128)S(1)} %pick.1), channel_id=1, source_target_pairs={{0,1},{1,0},{2,3},{3,2},{4,5},{5,4},{6,7},{7,6},{8,9},{9,8},{10,11... | collective-permute-start | bytes 1769480 | tf_op jit(solution)/shard_map/ppermute | solution.py:266
  18.4 0.9 %pair.1 = (f32[128,768]{1,0:T(8,128)S(1)}, f32[128,768]{1,0:T(8,128)S(1)}) custom-call(bf16[256,384]{1,0:T(8,128)(2,1)S(1)} %get-tuple-element.46.refs_0_, bf16[256,384]{1,0:T(8,128)(2,1)S(1)} %get-tuple-element.47.refs_1_, f32[384,384]{1,0:T(8,128)S(1)} %collective-permute-done.4.refs_2_, f32[4,384]{1,0:T(4,128)S(1)} %get-tuple-element.55.refs_3_, ...), custom_call_target="tpu_custom_call" | custom-call | flops 452984832 | bytes 2371584 | tf_op jit(solution)/shard_map/pair/pallas_call | solution.py:232
  19.4 0.6 %collective-permute-start.8 = (f32[128,768]{1,0:T(8,128)S(1)}, f32[128,768]{1,0:T(8,128)S(1)}, u32[]{:S(2)}, u32[]{:S(2)}) collective-permute-start(f32[128,768]{1,0:T(8,128)S(1)} %get-tuple-element.58), channel_id=1, source_target_pairs={{0,4},{4,0},{8,12},{12,8},{1,5},{5,1},{9,13},{13,9},{2,6},{6,2},{1... | collective-permute-start | bytes 1179656 | tf_op jit(solution)/shard_map/ppermute | solution.py:269
  19.9 0.1 collective-permute-start.6
  20.0 1.6 %collective-permute-done.6.refs_1_ = f32[128,384]{1,0:T(8,128)S(1)} collective-permute-done((f32[128,384]{1,0:T(8,128)S(1)}, f32[128,384]{1,0:T(8,128)S(1)}, u32[]{:S(2)}, u32[]{:S(2)}) %collective-permute-start.6) | collective-permute-done | bytes 196640 | tf_op jit(solution)/shard_map/ppermute | solution.py:269
  21.6 1.6 %collective-permute-start.7 = (f32[64,384]{1,0:T(8,128)S(1)}, f32[64,384]{1,0:T(8,128)S(1)}, u32[]{:S(2)}, u32[]{:S(2)}) collective-permute-start(f32[64,384]{1,0:T(8,128)S(1)} %get-tuple-element.54), channel_id=1, source_target_pairs={{0,8},{4,12},{8,0},{12,4},{1,9},{5,13},{9,1},{13,5},{2,10},{6,14},... | collective-permute-start | bytes 294920 | tf_op jit(solution)/shard_map/ppermute | solution.py:269
  23.2 0.6 %collective-permute-start.9 = (f32[64,768]{1,0:T(8,128)S(1)}, f32[64,768]{1,0:T(8,128)S(1)}, u32[]{:S(2)}, u32[]{:S(2)}) collective-permute-start(f32[64,768]{1,0:T(8,128)S(1)} %get-tuple-element.60), channel_id=1, source_target_pairs={{0,8},{4,12},{8,0},{12,4},{1,9},{5,13},{9,1},{13,5},{2,10},{6,14},... | collective-permute-start | bytes 589832 | tf_op jit(solution)/shard_map/ppermute | solution.py:269
  23.8 7.1 %collective-permute-done.3.refs_0_.refs_2_ = f32[384,384]{1,0:T(8,128)S(1)} collective-permute-done((f32[384,384]{1,0:T(8,128)S(1)}, f32[384,384]{1,0:T(8,128)S(1)}, u32[]{:S(2)}, u32[]{:S(2)}) %collective-permute-start.3) | collective-permute-done | bytes 589856 | tf_op jit(solution)/shard_map/ppermute | solution.py:266
  30.9 0.5 %corner.1 = (f32[128,384]{1,0:T(8,128)S(1)}, f32[128,384]{1,0:T(8,128)S(1)}) custom-call(f32[384,384]{1,0:T(8,128)S(1)} %collective-permute-done.3.refs_0_.refs_2_, f32[384,384]{1,0:T(8,128)S(1)} %collective-permute-done.5.refs_1_.refs_4_, f32[4,384]{1,0:T(4,128)S(1)} %get-tuple-element.50.refs_2_.refs_5_, f32[8,128]{1,0:T(8,128)S(1)} %gate.1.refs_3_, ...), custom_call_target="tpu_custom_call" | custom-call | flops 226492416 | bytes 1579008 | tf_op jit(solution)/shard_map/corner/pallas_call | solution.py:232
  31.5 0.5 %last.1 = (f32[128,384]{1,0:T(8,128)S(1)}, f32[128,384]{1,0:T(8,128)S(1)}) custom-call(bf16[256,384]{1,0:T(8,128)(2,1)S(1)} %get-tuple-element.46.refs_0_, bf16[256,384]{1,0:T(8,128)(2,1)S(1)} %get-tuple-element.47.refs_1_, f32[384,384]{1,0:T(8,128)S(1)} %collective-permute-done.3.refs_0_.refs_2_, f32[4,384]{1,0:T(4,128)S(1)} %get-tuple-element.49.refs_3_, ...), custom_call_target="tpu_custom_call" | custom-call | flops 226492416 | bytes 1978368 | tf_op jit(solution)/shard_map/last/pallas_call | solution.py:232
  32.1 0.6 %collective-permute-start.10 = (f32[128,384]{1,0:T(8,128)S(1)}, f32[128,384]{1,0:T(8,128)S(1)}, u32[]{:S(2)}, u32[]{:S(2)}) collective-permute-start(f32[128,384]{1,0:T(8,128)S(1)} %get-tuple-element.63), channel_id=1, source_target_pairs={{0,4},{4,0},{8,12},{12,8},{1,5},{5,1},{9,13},{13,9},{2,6},{6,2},{1... | collective-permute-start | bytes 589832 | tf_op jit(solution)/shard_map/ppermute | solution.py:269
  32.6 0.3 collective-permute-done.11.refs_1_
  33.0 2.6 %collective-permute-start.13 = (f32[64,384]{1,0:T(8,128)S(1)}, f32[64,384]{1,0:T(8,128)S(1)}, u32[]{:S(2)}, u32[]{:S(2)}) collective-permute-start(f32[64,384]{1,0:T(8,128)S(1)} %get-tuple-element.66.refs_3_), channel_id=1, source_target_pairs={{0,1},{1,8},{2,11},{3,2},{4,5},{5,12},{6,15},{7,6},{8,9},{9,0},{10... | collective-permute-start | bytes 294920 | tf_op jit(solution)/shard_map/ppermute | solution.py:310
  35.6 0.4 collective-permute-start.14
  36.0 1.2 %collective-permute-start.12 = (f32[64,384]{1,0:T(8,128)S(1)}, f32[64,384]{1,0:T(8,128)S(1)}, u32[]{:S(2)}, u32[]{:S(2)}) collective-permute-start(f32[64,384]{1,0:T(8,128)S(1)} %get-tuple-element.68), channel_id=1, source_target_pairs={{0,8},{4,12},{8,0},{12,4},{1,9},{5,13},{9,1},{13,5},{2,10},{6,14},... | collective-permute-start | bytes 294920 | tf_op jit(solution)/shard_map/ppermute | solution.py:269
  37.3 0.5 %finish.3.refs_3_ = f32[64,1536]{1,0:T(8,128)S(1)} custom-call(f32[16,384]{1,0:T(8,128)S(1)} %get-tuple-element.70.refs_0_, f32[64,384]{1,0:T(8,128)S(1)} %get-tuple-element.53.refs_4_.refs_1_, f32[64,384]{1,0:T(8,128)S(1)} %collective-permute-done.7.refs_5_.refs_2_, f32[32,384]{1,0:T(8,128)S(1)} %pad_maximum_fusion.refs_3_, ...), custom_call_target="tpu_custom_call" | custom-call | flops 393216 | bytes 1056768 | tf_op jit(solution)/shard_map/finish/pallas_call | solution.py:232
  37.7 2.4 %collective-permute-done.13.refs_1_ = f32[64,384]{1,0:T(8,128)S(1)} collective-permute-done((f32[64,384]{1,0:T(8,128)S(1)}, f32[64,384]{1,0:T(8,128)S(1)}, u32[]{:S(2)}, u32[]{:S(2)}) %collective-permute-start.13) | collective-permute-done | bytes 98336 | tf_op jit(solution)/shard_map/ppermute | solution.py:310
  40.1 0.8 %collective-permute-done.14.refs_2_ = f32[64,384]{1,0:T(8,128)S(1)} collective-permute-done((f32[64,384]{1,0:T(8,128)S(1)}, f32[64,384]{1,0:T(8,128)S(1)}, u32[]{:S(2)}, u32[]{:S(2)}) %collective-permute-start.14) | collective-permute-done | bytes 98336 | tf_op jit(solution)/shard_map/ppermute | solution.py:310
  40.9 0.2 finish.4.refs_3_
  41.1 0.6 %collective-permute-done.12.refs_2_ = f32[64,384]{1,0:T(8,128)S(1)} collective-permute-done((f32[64,384]{1,0:T(8,128)S(1)}, f32[64,384]{1,0:T(8,128)S(1)}, u32[]{:S(2)}, u32[]{:S(2)}) %collective-permute-start.12) | collective-permute-done | bytes 98336 | tf_op jit(solution)/shard_map/ppermute | solution.py:269
  41.7 0.9 %finish.5 = f32[64,1536]{1,0:T(8,128)} custom-call(f32[16,384]{1,0:T(8,128)S(1)} %add.10.refs_0_, f32[64,384]{1,0:T(8,128)S(1)} %get-tuple-element.67.refs_1_, f32[64,384]{1,0:T(8,128)S(1)} %collective-permute-done.12.refs_2_, f32[64,1536]{1,0:T(8,128)S(1)} %finish.4.refs_3_), custom_call_target="tpu_custom_call" | custom-call | flops 393216 | bytes 1007616 | tf_op jit(solution)/shard_map/finish/pallas_call | solution.py:232
  (26 shorter events, 0.4 us)
Async XLA Ops:
  0.0 14.0 %collective-permute-start.2 = (f32[384,384]{1,0:T(8,128)}, f32[384,384]{1,0:T(8,128)S(1)}, u32[]{:S(2)}, u32[]{:S(2)}) collective-permute-start(f32[384,384]{1,0:T(8,128)} %refs_3_.3), channel_id=1, source_target_pairs={{0,4},{1,2},{2,1},{3,7},{4,0},{5,6},{6,5},{7,3},{8,12},{9,10},{10,... | collective-permute-start | bytes 1769480 | tf_op jit(solution)/shard_map/ppermute | solution.py:266
  0.5 18.0 %collective-permute-start.4 = (f32[384,384]{1,0:T(8,128)}, f32[384,384]{1,0:T(8,128)S(1)}, u32[]{:S(2)}, u32[]{:S(2)}) collective-permute-start(f32[384,384]{1,0:T(8,128)} %refs_3_.3), channel_id=1, source_target_pairs={{0,1},{1,0},{2,3},{3,2},{4,5},{5,4},{6,7},{7,6},{8,9},{9,8},{10,11... | collective-permute-start | bytes 1769480 | tf_op jit(solution)/shard_map/ppermute | solution.py:266
  4.6 2.7 %copy-start.3 = (s32[32,16]{0,1:T(8,128)S(1)}, s32[32,16]{0,1:T(8,128)}, u32[]{:S(2)}) copy-start(s32[32,16]{0,1:T(8,128)} %param.7) | copy-start | bytes 6148
  4.6 8.8 %copy-start = (f32[384,384]{1,0:T(8,128)S(1)}, f32[384,384]{1,0:T(8,128)}, u32[]{:S(2)}) copy-start(f32[384,384]{1,0:T(8,128)} %refs_3_.3) | copy-start | bytes 1769476
  5.7 6.1 %collective-permute-start = (f32[64,768]{1,0:T(8,128)S(1)}, f32[64,768]{1,0:T(8,128)S(1)}, u32[]{:S(2)}, u32[]{:S(2)}) collective-permute-start(f32[64,768]{1,0:T(8,128)S(1)} %get-tuple-element.73), channel_id=1, source_target_pairs={{0,8},{4,12},{8,0},{12,4},{1,9},{5,13},{9,1},{13,5},{2,10},{6,14},... | collective-permute-start | bytes 589832 | tf_op jit(solution)/shard_map/ppermute | solution.py:269
  7.3 0.7 %copy-start.1 = (s32[16,16]{1,0:T(8,128)S(1)}, s32[16,16]{1,0:T(8,128)}, u32[]{:S(2)}) copy-start(s32[16,16]{1,0:T(8,128)} %refs_2_.1) | copy-start | bytes 3076
  7.4 0.7 %copy-start.2 = (s32[16]{0:T(128)S(1)}, s32[16]{0:T(128)}, u32[]{:S(2)}) copy-start(s32[16]{0:T(128)} %refs_3_.2) | copy-start | bytes 196
  11.9 1.5 %collective-permute-start.1 = (f32[128,384]{1,0:T(8,128)S(1)}, f32[128,384]{1,0:T(8,128)S(1)}, u32[]{:S(2)}, u32[]{:S(2)}) collective-permute-start(f32[128,384]{1,0:T(8,128)S(1)} %get-tuple-element.44), channel_id=1, source_target_pairs={{0,4},{4,0},{8,12},{12,8},{1,5},{5,1},{9,13},{13,9},{2,6},{6,2},{1... | collective-permute-start | bytes 589832 | tf_op jit(solution)/shard_map/ppermute | solution.py:269
  14.1 16.8 %collective-permute-start.3 = (f32[384,384]{1,0:T(8,128)S(1)}, f32[384,384]{1,0:T(8,128)S(1)}, u32[]{:S(2)}, u32[]{:S(2)}) collective-permute-start(f32[384,384]{1,0:T(8,128)S(1)} %pick.1), channel_id=1, source_target_pairs={{0,1},{1,0},{2,3},{3,2},{4,5},{5,4},{6,7},{7,6},{8,9},{9,8},{10,11... | collective-permute-start | bytes 1769480 | tf_op jit(solution)/shard_map/ppermute | solution.py:266
  18.4 12.5 %collective-permute-start.5 = (f32[384,384]{1,0:T(8,128)S(1)}, f32[384,384]{1,0:T(8,128)S(1)}, u32[]{:S(2)}, u32[]{:S(2)}) collective-permute-start(f32[384,384]{1,0:T(8,128)S(1)} %collective-permute-done.4.refs_2_), channel_id=1, source_target_pairs={{0,4},{1,2},{2,1},{3,7},{4,0},{5,6},{6,5},{7,3},{8,12},{9,10},{10,... | collective-permute-start | bytes 1769480 | tf_op jit(solution)/shard_map/ppermute | solution.py:266
  19.4 3.8 %collective-permute-start.8 = (f32[128,768]{1,0:T(8,128)S(1)}, f32[128,768]{1,0:T(8,128)S(1)}, u32[]{:S(2)}, u32[]{:S(2)}) collective-permute-start(f32[128,768]{1,0:T(8,128)S(1)} %get-tuple-element.58), channel_id=1, source_target_pairs={{0,4},{4,0},{8,12},{12,8},{1,5},{5,1},{9,13},{13,9},{2,6},{6,2},{1... | collective-permute-start | bytes 1179656 | tf_op jit(solution)/shard_map/ppermute | solution.py:269
  19.9 1.6 %collective-permute-start.6 = (f32[128,384]{1,0:T(8,128)S(1)}, f32[128,384]{1,0:T(8,128)S(1)}, u32[]{:S(2)}, u32[]{:S(2)}) collective-permute-start(f32[128,384]{1,0:T(8,128)S(1)} %get-tuple-element.52), channel_id=1, source_target_pairs={{0,4},{4,0},{8,12},{12,8},{1,5},{5,1},{9,13},{13,9},{2,6},{6,2},{1... | collective-permute-start | bytes 589832 | tf_op jit(solution)/shard_map/ppermute | solution.py:269
  21.6 9.3 %collective-permute-start.7 = (f32[64,384]{1,0:T(8,128)S(1)}, f32[64,384]{1,0:T(8,128)S(1)}, u32[]{:S(2)}, u32[]{:S(2)}) collective-permute-start(f32[64,384]{1,0:T(8,128)S(1)} %get-tuple-element.54), channel_id=1, source_target_pairs={{0,8},{4,12},{8,0},{12,4},{1,9},{5,13},{9,1},{13,5},{2,10},{6,14},... | collective-permute-start | bytes 294920 | tf_op jit(solution)/shard_map/ppermute | solution.py:269
  23.2 7.7 %collective-permute-start.9 = (f32[64,768]{1,0:T(8,128)S(1)}, f32[64,768]{1,0:T(8,128)S(1)}, u32[]{:S(2)}, u32[]{:S(2)}) collective-permute-start(f32[64,768]{1,0:T(8,128)S(1)} %get-tuple-element.60), channel_id=1, source_target_pairs={{0,8},{4,12},{8,0},{12,4},{1,9},{5,13},{9,1},{13,5},{2,10},{6,14},... | collective-permute-start | bytes 589832 | tf_op jit(solution)/shard_map/ppermute | solution.py:269
  31.4 1.5 %collective-permute-start.11 = (f32[128,384]{1,0:T(8,128)S(1)}, f32[128,384]{1,0:T(8,128)S(1)}, u32[]{:S(2)}, u32[]{:S(2)}) collective-permute-start(f32[128,384]{1,0:T(8,128)S(1)} %get-tuple-element.64), channel_id=1, source_target_pairs={{0,4},{4,0},{8,12},{12,8},{1,5},{5,1},{9,13},{13,9},{2,6},{6,2},{1... | collective-permute-start | bytes 589832 | tf_op jit(solution)/shard_map/ppermute | solution.py:269
  32.1 3.9 %collective-permute-start.10 = (f32[128,384]{1,0:T(8,128)S(1)}, f32[128,384]{1,0:T(8,128)S(1)}, u32[]{:S(2)}, u32[]{:S(2)}) collective-permute-start(f32[128,384]{1,0:T(8,128)S(1)} %get-tuple-element.63), channel_id=1, source_target_pairs={{0,4},{4,0},{8,12},{12,8},{1,5},{5,1},{9,13},{13,9},{2,6},{6,2},{1... | collective-permute-start | bytes 589832 | tf_op jit(solution)/shard_map/ppermute | solution.py:269
  33.0 7.1 %collective-permute-start.13 = (f32[64,384]{1,0:T(8,128)S(1)}, f32[64,384]{1,0:T(8,128)S(1)}, u32[]{:S(2)}, u32[]{:S(2)}) collective-permute-start(f32[64,384]{1,0:T(8,128)S(1)} %get-tuple-element.66.refs_3_), channel_id=1, source_target_pairs={{0,1},{1,8},{2,11},{3,2},{4,5},{5,12},{6,15},{7,6},{8,9},{9,0},{10... | collective-permute-start | bytes 294920 | tf_op jit(solution)/shard_map/ppermute | solution.py:310
  35.6 5.3 %collective-permute-start.14 = (f32[64,384]{1,0:T(8,128)S(1)}, f32[64,384]{1,0:T(8,128)S(1)}, u32[]{:S(2)}, u32[]{:S(2)}) collective-permute-start(f32[64,384]{1,0:T(8,128)S(1)} %get-tuple-element.65.refs_2_), channel_id=1, source_target_pairs={{0,1},{1,0},{2,3},{3,2},{4,5},{5,4},{6,7},{7,6},{8,9},{9,8},{10,11... | collective-permute-start | bytes 294920 | tf_op jit(solution)/shard_map/ppermute | solution.py:310
  36.0 5.7 %collective-permute-start.12 = (f32[64,384]{1,0:T(8,128)S(1)}, f32[64,384]{1,0:T(8,128)S(1)}, u32[]{:S(2)}, u32[]{:S(2)}) collective-permute-start(f32[64,384]{1,0:T(8,128)S(1)} %get-tuple-element.68), channel_id=1, source_target_pairs={{0,8},{4,12},{8,0},{12,4},{1,9},{5,13},{9,1},{13,5},{2,10},{6,14},... | collective-permute-start | bytes 294920 | tf_op jit(solution)/shard_map/ppermute | solution.py:269

commit v18 on v16

--- a/solution.py
+++ b/solution.py
@@ -109,7 +109,9 @@
 
 def product(a_high, a_low, b_high, b_low):
     dot = functools.partial(jnp.dot, preferred_element_type=jnp.float32)
-    return dot(a_high, b_high) + (dot(a_high, b_low) + dot(a_low, b_high))
+    rows = a_high.shape[0]
+    both = dot(jnp.concatenate([a_high, a_low], axis=0), b_high)
+    return both[:rows, :] + (dot(a_high, b_low) + both[rows:, :])
 
 
 def multiply_kernel(groups, high, low, *refs):
@@ -118,9 +120,10 @@
     for g, counts in enumerate(groups):
         b_high, b_low = masked_halves(parted(refs, counts))
         refs = refs[sum(counts) :]
-        for out, start in ((give, half), (keep, 0)):
-            at = pl.ds(start, half)
-            out[:, g * width : (g + 1) * width] = product(high[at, :], low[at, :], b_high, b_low)
+        at = pl.ds(g * width, width)
+        sums = product(high[...], low[...], b_high, b_low)
+        give[:, at] = sums[half:, :]
+        keep[:, at] = sums[:half, :]
 
 
 def own_kernel(amp_rows, *refs):
@@ -157,9 +160,10 @@
 def corner_kernel(slab, block, masks, keep, give):
     b_high, b_low = masked_halves([(block, masks)])
     half = keep.shape[0]
-    for out, start in ((give, half), (keep, 0)):
-        a_high, a_low = split(slab[start : start + half, :])
-        out[...] = product(a_high, a_low, b_high, b_low)
+    a_high, a_low = split(slab[: 2 * half, :])
+    sums = product(a_high, a_low, b_high, b_low)
+    give[...] = sums[half:, :]
+    keep[...] = sums[:half, :]
 
 
 def gate_kernel(out):
@@ -174,10 +178,6 @@
 
 
 def finish_kernel(counts, *refs):
-    sems = None
-    if refs[-1].dtype != jnp.float32:
-        *refs, final, out, sems = refs
-        refs = (*refs, out)
     out = refs[-1]
     n_in = sum(counts) + len(counts)
     rows = out.shape[0]
@@ -195,7 +195,6 @@
             part = total[:, g * GROUP : (g + 1) * GROUP]
             turned = [part] + [pltpu.roll(part, t * TB, 1) for t in range(1, PER)]
             totals.append((homes, g * n_home * PER, turned))
-    copies = []
     for home in range(n_home):
         to = pl.ds(home * GROUP, GROUP)
         if len(refs) - 1 > n_in:
@@ -207,14 +206,9 @@
                 row = base + home * PER + t
                 value = jnp.where(homes[row : row + 1, :] > 0.5, turned[t], value)
         out[:, to] = value
-        if sems is not None:
-            copies.append(pltpu.make_async_copy(out.at[:, to], final.at[:, to], sems.at[home]))
-            copies[-1].start()
-    for copy in copies:
-        copy.wait()
-
-
-def call(kernel, name, outs, n_smem, *args, flops=0, after=(), scratch=(), out_space=pltpu.VMEM):
+
+
+def call(kernel, name, outs, n_smem, *args, flops=0, after=()):
     moved = sum(x.size * x.dtype.itemsize for x in list(args) + list(outs))
     n_args, n_after = len(args), len(after)
 
@@ -227,8 +221,7 @@
         in_specs=[SMEM] * n_smem
         + [VMEM] * (len(args) - n_smem)
         + [pl.BlockSpec(memory_space=pl.ANY)] * n_after,
-        out_specs=[pl.BlockSpec(memory_space=out_space)] * len(outs),
-        scratch_shapes=scratch,
+        out_specs=[VMEM] * len(outs),
         compiler_params=pltpu.CompilerParams(vmem_limit_bytes=40 * 2**20),
         cost_estimate=pl.CostEstimate(
             flops=int(flops), bytes_accessed=int(moved), transcendentals=0
@@ -322,11 +315,8 @@
         )
         return [[slot for slot, _ in group] for group in groups], exchange(keep, give)
 
-    def finish(slots, *so_far, final=False):
-        args, counts, place_ = [], [], {}
-        if final:
-            buffers = [pltpu.VMEM((rows, pairs), jnp.float32), pltpu.SemaphoreType.DMA((pairs // GROUP,))]
-            place_ = dict(scratch=buffers, out_space=pl.ANY)
+    def finish(slots, *so_far):
+        args, counts = [], []
         for groups, shares in slots:
             args.append(jnp.concatenate([sum(homes[name] for name in names) for names in groups]))
             args.extend(shares)
@@ -339,7 +329,6 @@
             *args,
             *so_far,
             flops=rows * pairs * n_row,
-            **place_,
         )[0]
 
     high, low, slab, keep, give = call(
@@ -389,7 +378,7 @@
         if slots:
             out = finish(slots, out)
         slots = [([[(EVEN, step), (ODD, step)]], exchange(*parts, after=folded))]
-    return finish(slots, out, final=True)
+    return finish(slots, out)
 
 
 def solution(mesh):

time: 42.9 us -> 42.9 us (level)
  transfers between devices with their start and end apart: 15 -> 15, of which waited for: 9 -> 8; matrix products, arithmetic and copies ran while one was open for 3% -> 3% of each run, Pallas kernels for 11% -> 11%
where the time goes in v18:
time: 42.9 us; the launch traced here: 42.7 us
  starting transfers between devices  18.3 us (43%)
  waiting for transfers between devices  16.1 us (38%)
  Pallas kernels  6.31 us (15%)
  local copies, waits for them, and re-layouts  1.77 us (4%)
    ppermute x4, starting transfers between devices, swap_line(): return lax.ppermute(x, ('row', 'col'), pairs_)  8.97 us
    ppermute x4, waiting for transfers between devices, swap_line(): return lax.ppermute(x, ('row', 'col'), pairs_)  7.1 us
    ppermute x9, starting transfers between devices, swap(): return lax.ppermute(x, 'row', [(i, i ^ d) for i in range(n_row)])  6.32 us
    pallas_call x15, Pallas kernels, call(): pl.pallas_call(body, out_shape=outs, in_specs=[SMEM] * n_smem + [VMEM] *...  6.31 us
    ppermute x9, waiting for transfers between devices, swap(): return lax.ppermute(x, 'row', [(i, i ^ d) for i in range(n_row)])  5.8 us
    ppermute x2, waiting for transfers between devices, next_door(): lax.ppermute(x, ('row', 'col'), [(i * n_col + j, (i ^ (d if 0 < j < n_col...  3.18 us
    ppermute x2, starting transfers between devices, next_door(): lax.ppermute(x, ('row', 'col'), [(i * n_col + j, (i ^ (d if 0 < j < n_col...  3 us
    dynamic_slice x1, local copies, waits for them, and re-layouts, chip_columns(): return lax.dynamic_slice_in_dim(amplitudes, start, 2 * depth, 1)  1.11 us
  transfers between devices with their start and end apart: 15, of which 8 were waited for; matrix products, arithmetic and copies ran while one was open for 3% of the time, Pallas kernels for 11%

profile of v18, /device:TPU:0, one launch (start us, length us, event | category | flops | bytes accessed | tf_op | source)
XLA Modules:
  0.0 42.7 jit_solution(6635189462770333985)
XLA Ops:
  0.0 0.5 %collective-permute-start.2 = (f32[384,384]{1,0:T(8,128)}, f32[384,384]{1,0:T(8,128)S(1)}, u32[]{:S(2)}, u32[]{:S(2)}) collective-permute-start(f32[384,384]{1,0:T(8,128)} %refs_3_.3), channel_id=1, source_target_pairs={{0,4},{1,2},{2,1},{3,7},{4,0},{5,6},{6,5},{7,3},{8,12},{9,10},{10,... | collective-permute-start | bytes 1769480 | tf_op jit(solution)/shard_map/ppermute | solution.py:251
  0.5 4.1 %collective-permute-start.4 = (f32[384,384]{1,0:T(8,128)}, f32[384,384]{1,0:T(8,128)S(1)}, u32[]{:S(2)}, u32[]{:S(2)}) collective-permute-start(f32[384,384]{1,0:T(8,128)} %refs_3_.3), channel_id=1, source_target_pairs={{0,1},{1,0},{2,3},{3,2},{4,5},{5,4},{6,7},{7,6},{8,9},{9,8},{10,11... | collective-permute-start | bytes 1769480 | tf_op jit(solution)/shard_map/ppermute | solution.py:251
  4.6 1.1 %constant_dynamic-slice_fusion = (f32[64,768]{1,0:T(8,128)S(1)}, f32[64,768]{1,0:T(8,128)S(1)}) fusion(f32[64,1536]{1,0:T(8,128)} %param.5, s32[]{:T(128)S(6)} %select_n.14, s32[]{:T(128)S(6)} %select_n.13), kind=kLoop, calls=%fused_computation.2 | loop fusion | bytes 786440 | tf_op jit(solution)/shard_map/dynamic_slice | solution.py:279
  5.7 1.6 %collective-permute-start = (f32[64,768]{1,0:T(8,128)S(1)}, f32[64,768]{1,0:T(8,128)S(1)}, u32[]{:S(2)}, u32[]{:S(2)}) collective-permute-start(f32[64,768]{1,0:T(8,128)S(1)} %get-tuple-element.73), channel_id=1, source_target_pairs={{0,8},{4,12},{8,0},{12,4},{1,9},{5,13},{9,1},{13,5},{2,10},{6,14},... | collective-permute-start | bytes 589832 | tf_op jit(solution)/shard_map/ppermute | solution.py:254
  7.3 0.1 copy.6.refs_1_
  7.4 0.1 pad_add_fusion.refs_0_
  7.4 0.5 %copy-done.1 = s32[16,16]{1,0:T(8,128)S(1)} copy-done((s32[16,16]{1,0:T(8,128)S(1)}, s32[16,16]{1,0:T(8,128)}, u32[]{:S(2)}) %copy-start.1) | copy-done | bytes 1048
  8.0 2.0 %tables.1 = (f32[8,384]{1,0:T(8,128)S(1)}, f32[8,384]{1,0:T(8,128)S(1)}, f32[4,384]{1,0:T(4,128)S(1)}, f32[16,384]{1,0:T(8,128)S(1)}, f32[4,384]{1,0:T(4,128)S(1...) custom-call(s32[3]{0:T(128)S(1)} %pad_add_fusion.refs_0_, ...), custom_call_target="tpu_custom_call" | custom-call | bytes 212044 | tf_op jit(solution)/shard_map/tables/pallas_call | solution.py:218
  10.0 1.8 %collective-permute-done.refs_2_ = f32[64,768]{1,0:T(8,128)S(1)} collective-permute-done((f32[64,768]{1,0:T(8,128)S(1)}, f32[64,768]{1,0:T(8,128)S(1)}, u32[]{:S(2)}, u32[]{:S(2)}) %collective-permute-start) | collective-permute-done | bytes 196640 | tf_op jit(solution)/shard_map/ppermute | solution.py:254
  12.0 1.4 %collective-permute-done.1.refs_2_ = f32[128,384]{1,0:T(8,128)S(1)} collective-permute-done((f32[128,384]{1,0:T(8,128)S(1)}, f32[128,384]{1,0:T(8,128)S(1)}, u32[]{:S(2)}, u32[]{:S(2)}) %collective-permute-start.1) | collective-permute-done | bytes 196640 | tf_op jit(solution)/shard_map/ppermute | solution.py:254
  13.4 0.6 %own.1 = (bf16[256,384]{1,0:T(8,128)(2,1)S(1)}, bf16[256,384]{1,0:T(8,128)(2,1)S(1)}, f32[384,384]{1,0:T(8,128)S(1)}, f32[128,384]{1,0:T(8,128)S(1)}, f32[128,384]{1,0:T(8,128)S(1)}) custom-call(f32[8,384]{1,0:T(8,128)S(1)} %get-tuple-element.41.refs_0_, f32[128,384]{1,0:T(8,128)S(1)} %get-tuple-element.43.refs_1_, ...), custom_call_target="tpu_custom_call" | custom-call | flops 226492416 | bytes 2377728 | tf_op jit(solution)/shard_map/own/pallas_call | solution.py:218
  14.1 4.4 %collective-permute-start.3 = (f32[384,384]{1,0:T(8,128)S(1)}, f32[384,384]{1,0:T(8,128)S(1)}, u32[]{:S(2)}, u32[]{:S(2)}) collective-permute-start(f32[384,384]{1,0:T(8,128)S(1)} %pick.1), channel_id=1, source_target_pairs={{0,1},{1,0},{2,3},{3,2},{4,5},{5,4},{6,7},{7,6},{8,9},{9,8},{10,11... | collective-permute-start | bytes 1769480 | tf_op jit(solution)/shard_map/ppermute | solution.py:251
  18.4 0.9 %pair.1 = (f32[128,768]{1,0:T(8,128)S(1)}, f32[128,768]{1,0:T(8,128)S(1)}) custom-call(bf16[256,384]{1,0:T(8,128)(2,1)S(1)} %get-tuple-element.46.refs_0_, bf16[256,384]{1,0:T(8,128)(2,1)S(1)} %get-tuple-element.47.refs_1_, f32[384,384]{1,0:T(8,128)S(1)} %collective-permute-done.4.refs_2_, f32[4,384]{1,0:T(4,128)S(1)} %get-tuple-element.55.refs_3_, ...), custom_call_target="tpu_custom_call" | custom-call | flops 452984832 | bytes 2371584 | tf_op jit(solution)/shard_map/pair/pallas_call | solution.py:218
  19.4 0.6 %collective-permute-start.8 = (f32[128,768]{1,0:T(8,128)S(1)}, f32[128,768]{1,0:T(8,128)S(1)}, u32[]{:S(2)}, u32[]{:S(2)}) collective-permute-start(f32[128,768]{1,0:T(8,128)S(1)} %get-tuple-element.58), channel_id=1, source_target_pairs={{0,4},{4,0},{8,12},{12,8},{1,5},{5,1},{9,13},{13,9},{2,6},{6,2},{1... | collective-permute-start | bytes 1179656 | tf_op jit(solution)/shard_map/ppermute | solution.py:254
  19.9 0.1 collective-permute-start.6
  20.0 1.6 %collective-permute-done.6.refs_1_ = f32[128,384]{1,0:T(8,128)S(1)} collective-permute-done((f32[128,384]{1,0:T(8,128)S(1)}, f32[128,384]{1,0:T(8,128)S(1)}, u32[]{:S(2)}, u32[]{:S(2)}) %collective-permute-start.6) | collective-permute-done | bytes 196640 | tf_op jit(solution)/shard_map/ppermute | solution.py:254
  21.6 1.6 %collective-permute-start.7 = (f32[64,384]{1,0:T(8,128)S(1)}, f32[64,384]{1,0:T(8,128)S(1)}, u32[]{:S(2)}, u32[]{:S(2)}) collective-permute-start(f32[64,384]{1,0:T(8,128)S(1)} %get-tuple-element.54), channel_id=1, source_target_pairs={{0,8},{4,12},{8,0},{12,4},{1,9},{5,13},{9,1},{13,5},{2,10},{6,14},... | collective-permute-start | bytes 294920 | tf_op jit(solution)/shard_map/ppermute | solution.py:254
  23.2 0.6 %collective-permute-start.9 = (f32[64,768]{1,0:T(8,128)S(1)}, f32[64,768]{1,0:T(8,128)S(1)}, u32[]{:S(2)}, u32[]{:S(2)}) collective-permute-start(f32[64,768]{1,0:T(8,128)S(1)} %get-tuple-element.60), channel_id=1, source_target_pairs={{0,8},{4,12},{8,0},{12,4},{1,9},{5,13},{9,1},{13,5},{2,10},{6,14},... | collective-permute-start | bytes 589832 | tf_op jit(solution)/shard_map/ppermute | solution.py:254
  23.8 7.1 %collective-permute-done.3.refs_0_.refs_2_ = f32[384,384]{1,0:T(8,128)S(1)} collective-permute-done((f32[384,384]{1,0:T(8,128)S(1)}, f32[384,384]{1,0:T(8,128)S(1)}, u32[]{:S(2)}, u32[]{:S(2)}) %collective-permute-start.3) | collective-permute-done | bytes 589856 | tf_op jit(solution)/shard_map/ppermute | solution.py:251
  30.9 0.5 %corner.1 = (f32[128,384]{1,0:T(8,128)S(1)}, f32[128,384]{1,0:T(8,128)S(1)}) custom-call(f32[384,384]{1,0:T(8,128)S(1)} %collective-permute-done.3.refs_0_.refs_2_, f32[384,384]{1,0:T(8,128)S(1)} %collective-permute-done.5.refs_1_.refs_4_, f32[4,384]{1,0:T(4,128)S(1)} %get-tuple-element.50.refs_2_.refs_5_, f32[8,128]{1,0:T(8,128)S(1)} %gate.1.refs_3_, ...), custom_call_target="tpu_custom_call" | custom-call | flops 226492416 | bytes 1579008 | tf_op jit(solution)/shard_map/corner/pallas_call | solution.py:218
  31.5 0.5 %last.1 = (f32[128,384]{1,0:T(8,128)S(1)}, f32[128,384]{1,0:T(8,128)S(1)}) custom-call(bf16[256,384]{1,0:T(8,128)(2,1)S(1)} %get-tuple-element.46.refs_0_, bf16[256,384]{1,0:T(8,128)(2,1)S(1)} %get-tuple-element.47.refs_1_, f32[384,384]{1,0:T(8,128)S(1)} %collective-permute-done.3.refs_0_.refs_2_, f32[4,384]{1,0:T(4,128)S(1)} %get-tuple-element.49.refs_3_, ...), custom_call_target="tpu_custom_call" | custom-call | flops 226492416 | bytes 1978368 | tf_op jit(solution)/shard_map/last/pallas_call | solution.py:218
  32.1 0.6 %collective-permute-start.10 = (f32[128,384]{1,0:T(8,128)S(1)}, f32[128,384]{1,0:T(8,128)S(1)}, u32[]{:S(2)}, u32[]{:S(2)}) collective-permute-start(f32[128,384]{1,0:T(8,128)S(1)} %get-tuple-element.63), channel_id=1, source_target_pairs={{0,4},{4,0},{8,12},{12,8},{1,5},{5,1},{9,13},{13,9},{2,6},{6,2},{1... | collective-permute-start | bytes 589832 | tf_op jit(solution)/shard_map/ppermute | solution.py:254
  32.6 0.3 collective-permute-done.11.refs_1_
  33.0 2.6 %collective-permute-start.13 = (f32[64,384]{1,0:T(8,128)S(1)}, f32[64,384]{1,0:T(8,128)S(1)}, u32[]{:S(2)}, u32[]{:S(2)}) collective-permute-start(f32[64,384]{1,0:T(8,128)S(1)} %get-tuple-element.66.refs_3_), channel_id=1, source_target_pairs={{0,1},{1,8},{2,11},{3,2},{4,5},{5,12},{6,15},{7,6},{8,9},{9,0},{10... | collective-permute-start | bytes 294920 | tf_op jit(solution)/shard_map/ppermute | solution.py:295
  35.6 0.4 collective-permute-start.14
  36.0 1.2 %collective-permute-start.12 = (f32[64,384]{1,0:T(8,128)S(1)}, f32[64,384]{1,0:T(8,128)S(1)}, u32[]{:S(2)}, u32[]{:S(2)}) collective-permute-start(f32[64,384]{1,0:T(8,128)S(1)} %get-tuple-element.68), channel_id=1, source_target_pairs={{0,8},{4,12},{8,0},{12,4},{1,9},{5,13},{9,1},{13,5},{2,10},{6,14},... | collective-permute-start | bytes 294920 | tf_op jit(solution)/shard_map/ppermute | solution.py:254
  37.3 0.5 %finish.3.refs_3_ = f32[64,1536]{1,0:T(8,128)S(1)} custom-call(f32[16,384]{1,0:T(8,128)S(1)} %get-tuple-element.70.refs_0_, f32[64,384]{1,0:T(8,128)S(1)} %get-tuple-element.53.refs_4_.refs_1_, f32[64,384]{1,0:T(8,128)S(1)} %collective-permute-done.7.refs_5_.refs_2_, f32[32,384]{1,0:T(8,128)S(1)} %pad_maximum_fusion.refs_3_, ...), custom_call_target="tpu_custom_call" | custom-call | flops 393216 | bytes 1056768 | tf_op jit(solution)/shard_map/finish/pallas_call | solution.py:218
  37.7 2.4 %collective-permute-done.13.refs_1_ = f32[64,384]{1,0:T(8,128)S(1)} collective-permute-done((f32[64,384]{1,0:T(8,128)S(1)}, f32[64,384]{1,0:T(8,128)S(1)}, u32[]{:S(2)}, u32[]{:S(2)}) %collective-permute-start.13) | collective-permute-done | bytes 98336 | tf_op jit(solution)/shard_map/ppermute | solution.py:295
  40.1 0.8 %collective-permute-done.14.refs_2_ = f32[64,384]{1,0:T(8,128)S(1)} collective-permute-done((f32[64,384]{1,0:T(8,128)S(1)}, f32[64,384]{1,0:T(8,128)S(1)}, u32[]{:S(2)}, u32[]{:S(2)}) %collective-permute-start.14) | collective-permute-done | bytes 98336 | tf_op jit(solution)/shard_map/ppermute | solution.py:295
  40.9 0.2 finish.4.refs_3_
  41.1 0.6 %collective-permute-done.12.refs_2_ = f32[64,384]{1,0:T(8,128)S(1)} collective-permute-done((f32[64,384]{1,0:T(8,128)S(1)}, f32[64,384]{1,0:T(8,128)S(1)}, u32[]{:S(2)}, u32[]{:S(2)}) %collective-permute-start.12) | collective-permute-done | bytes 98336 | tf_op jit(solution)/shard_map/ppermute | solution.py:254
  41.7 0.9 %finish.5 = f32[64,1536]{1,0:T(8,128)} custom-call(f32[16,384]{1,0:T(8,128)S(1)} %add.10.refs_0_, f32[64,384]{1,0:T(8,128)S(1)} %get-tuple-element.67.refs_1_, f32[64,384]{1,0:T(8,128)S(1)} %collective-permute-done.12.refs_2_, f32[64,1536]{1,0:T(8,128)S(1)} %finish.4.refs_3_), custom_call_target="tpu_custom_call" | custom-call | flops 393216 | bytes 1007616 | tf_op jit(solution)/shard_map/finish/pallas_call | solution.py:218
  (26 shorter events, 0.4 us)
Async XLA Ops:
  0.0 14.0 %collective-permute-start.2 = (f32[384,384]{1,0:T(8,128)}, f32[384,384]{1,0:T(8,128)S(1)}, u32[]{:S(2)}, u32[]{:S(2)}) collective-permute-start(f32[384,384]{1,0:T(8,128)} %refs_3_.3), channel_id=1, source_target_pairs={{0,4},{1,2},{2,1},{3,7},{4,0},{5,6},{6,5},{7,3},{8,12},{9,10},{10,... | collective-permute-start | bytes 1769480 | tf_op jit(solution)/shard_map/ppermute | solution.py:251
  0.5 18.0 %collective-permute-start.4 = (f32[384,384]{1,0:T(8,128)}, f32[384,384]{1,0:T(8,128)S(1)}, u32[]{:S(2)}, u32[]{:S(2)}) collective-permute-start(f32[384,384]{1,0:T(8,128)} %refs_3_.3), channel_id=1, source_target_pairs={{0,1},{1,0},{2,3},{3,2},{4,5},{5,4},{6,7},{7,6},{8,9},{9,8},{10,11... | collective-permute-start | bytes 1769480 | tf_op jit(solution)/shard_map/ppermute | solution.py:251
  4.6 2.7 %copy-start.3 = (s32[32,16]{0,1:T(8,128)S(1)}, s32[32,16]{0,1:T(8,128)}, u32[]{:S(2)}) copy-start(s32[32,16]{0,1:T(8,128)} %param.7) | copy-start | bytes 6148
  4.6 8.8 %copy-start = (f32[384,384]{1,0:T(8,128)S(1)}, f32[384,384]{1,0:T(8,128)}, u32[]{:S(2)}) copy-start(f32[384,384]{1,0:T(8,128)} %refs_3_.3) | copy-start | bytes 1769476
  5.7 6.1 %collective-permute-start = (f32[64,768]{1,0:T(8,128)S(1)}, f32[64,768]{1,0:T(8,128)S(1)}, u32[]{:S(2)}, u32[]{:S(2)}) collective-permute-start(f32[64,768]{1,0:T(8,128)S(1)} %get-tuple-element.73), channel_id=1, source_target_pairs={{0,8},{4,12},{8,0},{12,4},{1,9},{5,13},{9,1},{13,5},{2,10},{6,14},... | collective-permute-start | bytes 589832 | tf_op jit(solution)/shard_map/ppermute | solution.py:254
  7.3 0.7 %copy-start.1 = (s32[16,16]{1,0:T(8,128)S(1)}, s32[16,16]{1,0:T(8,128)}, u32[]{:S(2)}) copy-start(s32[16,16]{1,0:T(8,128)} %refs_2_.1) | copy-start | bytes 3076
  7.4 0.7 %copy-start.2 = (s32[16]{0:T(128)S(1)}, s32[16]{0:T(128)}, u32[]{:S(2)}) copy-start(s32[16]{0:T(128)} %refs_3_.2) | copy-start | bytes 196
  11.9 1.5 %collective-permute-start.1 = (f32[128,384]{1,0:T(8,128)S(1)}, f32[128,384]{1,0:T(8,128)S(1)}, u32[]{:S(2)}, u32[]{:S(2)}) collective-permute-start(f32[128,384]{1,0:T(8,128)S(1)} %get-tuple-element.44), channel_id=1, source_target_pairs={{0,4},{4,0},{8,12},{12,8},{1,5},{5,1},{9,13},{13,9},{2,6},{6,2},{1... | collective-permute-start | bytes 589832 | tf_op jit(solution)/shard_map/ppermute | solution.py:254
  14.1 16.8 %collective-permute-start.3 = (f32[384,384]{1,0:T(8,128)S(1)}, f32[384,384]{1,0:T(8,128)S(1)}, u32[]{:S(2)}, u32[]{:S(2)}) collective-permute-start(f32[384,384]{1,0:T(8,128)S(1)} %pick.1), channel_id=1, source_target_pairs={{0,1},{1,0},{2,3},{3,2},{4,5},{5,4},{6,7},{7,6},{8,9},{9,8},{10,11... | collective-permute-start | bytes 1769480 | tf_op jit(solution)/shard_map/ppermute | solution.py:251
  18.4 12.5 %collective-permute-start.5 = (f32[384,384]{1,0:T(8,128)S(1)}, f32[384,384]{1,0:T(8,128)S(1)}, u32[]{:S(2)}, u32[]{:S(2)}) collective-permute-start(f32[384,384]{1,0:T(8,128)S(1)} %collective-permute-done.4.refs_2_), channel_id=1, source_target_pairs={{0,4},{1,2},{2,1},{3,7},{4,0},{5,6},{6,5},{7,3},{8,12},{9,10},{10,... | collective-permute-start | bytes 1769480 | tf_op jit(solution)/shard_map/ppermute | solution.py:251
  19.4 3.8 %collective-permute-start.8 = (f32[128,768]{1,0:T(8,128)S(1)}, f32[128,768]{1,0:T(8,128)S(1)}, u32[]{:S(2)}, u32[]{:S(2)}) collective-permute-start(f32[128,768]{1,0:T(8,128)S(1)} %get-tuple-element.58), channel_id=1, source_target_pairs={{0,4},{4,0},{8,12},{12,8},{1,5},{5,1},{9,13},{13,9},{2,6},{6,2},{1... | collective-permute-start | bytes 1179656 | tf_op jit(solution)/shard_map/ppermute | solution.py:254
  19.9 1.6 %collective-permute-start.6 = (f32[128,384]{1,0:T(8,128)S(1)}, f32[128,384]{1,0:T(8,128)S(1)}, u32[]{:S(2)}, u32[]{:S(2)}) collective-permute-start(f32[128,384]{1,0:T(8,128)S(1)} %get-tuple-element.52), channel_id=1, source_target_pairs={{0,4},{4,0},{8,12},{12,8},{1,5},{5,1},{9,13},{13,9},{2,6},{6,2},{1... | collective-permute-start | bytes 589832 | tf_op jit(solution)/shard_map/ppermute | solution.py:254
  21.6 9.3 %collective-permute-start.7 = (f32[64,384]{1,0:T(8,128)S(1)}, f32[64,384]{1,0:T(8,128)S(1)}, u32[]{:S(2)}, u32[]{:S(2)}) collective-permute-start(f32[64,384]{1,0:T(8,128)S(1)} %get-tuple-element.54), channel_id=1, source_target_pairs={{0,8},{4,12},{8,0},{12,4},{1,9},{5,13},{9,1},{13,5},{2,10},{6,14},... | collective-permute-start | bytes 294920 | tf_op jit(solution)/shard_map/ppermute | solution.py:254
  23.2 7.7 %collective-permute-start.9 = (f32[64,768]{1,0:T(8,128)S(1)}, f32[64,768]{1,0:T(8,128)S(1)}, u32[]{:S(2)}, u32[]{:S(2)}) collective-permute-start(f32[64,768]{1,0:T(8,128)S(1)} %get-tuple-element.60), channel_id=1, source_target_pairs={{0,8},{4,12},{8,0},{12,4},{1,9},{5,13},{9,1},{13,5},{2,10},{6,14},... | collective-permute-start | bytes 589832 | tf_op jit(solution)/shard_map/ppermute | solution.py:254
  31.4 1.5 %collective-permute-start.11 = (f32[128,384]{1,0:T(8,128)S(1)}, f32[128,384]{1,0:T(8,128)S(1)}, u32[]{:S(2)}, u32[]{:S(2)}) collective-permute-start(f32[128,384]{1,0:T(8,128)S(1)} %get-tuple-element.64), channel_id=1, source_target_pairs={{0,4},{4,0},{8,12},{12,8},{1,5},{5,1},{9,13},{13,9},{2,6},{6,2},{1... | collective-permute-start | bytes 589832 | tf_op jit(solution)/shard_map/ppermute | solution.py:254
  32.1 3.9 %collective-permute-start.10 = (f32[128,384]{1,0:T(8,128)S(1)}, f32[128,384]{1,0:T(8,128)S(1)}, u32[]{:S(2)}, u32[]{:S(2)}) collective-permute-start(f32[128,384]{1,0:T(8,128)S(1)} %get-tuple-element.63), channel_id=1, source_target_pairs={{0,4},{4,0},{8,12},{12,8},{1,5},{5,1},{9,13},{13,9},{2,6},{6,2},{1... | collective-permute-start | bytes 589832 | tf_op jit(solution)/shard_map/ppermute | solution.py:254
  33.0 7.1 %collective-permute-start.13 = (f32[64,384]{1,0:T(8,128)S(1)}, f32[64,384]{1,0:T(8,128)S(1)}, u32[]{:S(2)}, u32[]{:S(2)}) collective-permute-start(f32[64,384]{1,0:T(8,128)S(1)} %get-tuple-element.66.refs_3_), channel_id=1, source_target_pairs={{0,1},{1,8},{2,11},{3,2},{4,5},{5,12},{6,15},{7,6},{8,9},{9,0},{10... | collective-permute-start | bytes 294920 | tf_op jit(solution)/shard_map/ppermute | solution.py:295
  35.6 5.3 %collective-permute-start.14 = (f32[64,384]{1,0:T(8,128)S(1)}, f32[64,384]{1,0:T(8,128)S(1)}, u32[]{:S(2)}, u32[]{:S(2)}) collective-permute-start(f32[64,384]{1,0:T(8,128)S(1)} %get-tuple-element.65.refs_2_), channel_id=1, source_target_pairs={{0,1},{1,0},{2,3},{3,2},{4,5},{5,4},{6,7},{7,6},{8,9},{9,8},{10,11... | collective-permute-start | bytes 294920 | tf_op jit(solution)/shard_map/ppermute | solution.py:295
  36.0 5.7 %collective-permute-start.12 = (f32[64,384]{1,0:T(8,128)S(1)}, f32[64,384]{1,0:T(8,128)S(1)}, u32[]{:S(2)}, u32[]{:S(2)}) collective-permute-start(f32[64,384]{1,0:T(8,128)S(1)} %get-tuple-element.68), channel_id=1, source_target_pairs={{0,8},{4,12},{8,0},{12,4},{1,9},{5,13},{9,1},{13,5},{2,10},{6,14},... | collective-permute-start | bytes 294920 | tf_op jit(solution)/shard_map/ppermute | solution.py:254

commit v19 on v17

--- a/solution.py
+++ b/solution.py
@@ -157,13 +157,10 @@
     out[...] = jnp.where(marks[0:1, : out.shape[1]] > 0.5, slab[...], block[...])
 
 
-def corner_kernel(slab, block, masks, keep, give):
+def corner_kernel(start, slab, block, masks, out):
     b_high, b_low = masked_halves([(block, masks)])
-    half = keep.shape[0]
-    a_high, a_low = split(slab[: 2 * half, :])
-    sums = product(a_high, a_low, b_high, b_low)
-    give[...] = sums[half:, :]
-    keep[...] = sums[:half, :]
+    a_high, a_low = split(slab[start : start + out.shape[0], :])
+    out[...] = product(a_high, a_low, b_high, b_low)
 
 
 def gate_kernel(out):
@@ -387,7 +384,12 @@
         slots, folded = [], ()
         if corner:
             args = (end_slab, *odd, masks[ODD, step])
-            parts = call(corner_kernel, "corner", sums, 0, *args, flops=flops, after=after)
+            parts = []
+            for start in (total // 2, 0):
+                kernel = functools.partial(corner_kernel, start)
+                parts += call(kernel, "corner", sums[:1], 0, *args, flops=flops // 2, after=after)
+                after = (parts[0],)
+            parts = parts[::-1]
             folded = fold(*parts)
             after, pieces = (parts[0],), list(enumerate(folded))
             slots.append(([[ends]], [next_door(x, 2 * i) for i, x in reversed(pieces)]))

time: 42.9 us -> 42.7 us (level)
    pallas_call x15 -> x16, Pallas kernels: 6.3 us -> 6.47 us  [call(): pl.pallas_call(body, out_shape=outs, in_specs=[SMEM] * n_smem + [VMEM] *...]
  transfers between devices with their start and end apart: 15 -> 15, of which waited for: 8 -> 7; matrix products, arithmetic and copies ran while one was open for 3% -> 3% of each run, Pallas kernels for 11% -> 12%
where the time goes in v19:
time: 42.7 us; the launch traced here: 42.5 us
  starting transfers between devices  18.3 us (43%)
  waiting for transfers between devices  15.7 us (37%)
  Pallas kernels  6.47 us (15%)
  local copies, waits for them, and re-layouts  1.77 us (4%)
    ppermute x4, starting transfers between devices, swap_line(): return lax.ppermute(x, ('row', 'col'), pairs_)  8.97 us
    ppermute x4, waiting for transfers between devices, swap_line(): return lax.ppermute(x, ('row', 'col'), pairs_)  7.1 us
    pallas_call x16, Pallas kernels, call(): pl.pallas_call(body, out_shape=outs, in_specs=[SMEM] * n_smem + [VMEM] *...  6.47 us
    ppermute x9, starting transfers between devices, swap(): return lax.ppermute(x, 'row', [(i, i ^ d) for i in range(n_row)])  6.32 us
    ppermute x9, waiting for transfers between devices, swap(): return lax.ppermute(x, 'row', [(i, i ^ d) for i in range(n_row)])  5.48 us
    ppermute x2, waiting for transfers between devices, next_door(): lax.ppermute(x, ('row', 'col'), [(i * n_col + j, (i ^ (d if 0 < j < n_col...  3.13 us
    ppermute x2, starting transfers between devices, next_door(): lax.ppermute(x, ('row', 'col'), [(i * n_col + j, (i ^ (d if 0 < j < n_col...  3 us
    dynamic_slice x1, local copies, waits for them, and re-layouts, chip_columns(): return lax.dynamic_slice_in_dim(amplitudes, start, 2 * depth, 1)  1.11 us
  transfers between devices with their start and end apart: 15, of which 7 were waited for; matrix products, arithmetic and copies ran while one was open for 3% of the time, Pallas kernels for 12%

profile of v19, /device:TPU:0, one launch (start us, length us, event | category | flops | bytes accessed | tf_op | source)
XLA Modules:
  0.0 42.5 jit_solution(17429273866801909987)
XLA Ops:
  0.0 0.5 %collective-permute-start.2 = (f32[384,384]{1,0:T(8,128)}, f32[384,384]{1,0:T(8,128)S(1)}, u32[]{:S(2)}, u32[]{:S(2)}) collective-permute-start(f32[384,384]{1,0:T(8,128)} %refs_3_.3), channel_id=1, source_target_pairs={{0,4},{1,2},{2,1},{3,7},{4,0},{5,6},{6,5},{7,3},{8,12},{9,10},{10,... | collective-permute-start | bytes 1769480 | tf_op jit(solution)/shard_map/ppermute | solution.py:263
  0.5 4.1 %collective-permute-start.4 = (f32[384,384]{1,0:T(8,128)}, f32[384,384]{1,0:T(8,128)S(1)}, u32[]{:S(2)}, u32[]{:S(2)}) collective-permute-start(f32[384,384]{1,0:T(8,128)} %refs_3_.3), channel_id=1, source_target_pairs={{0,1},{1,0},{2,3},{3,2},{4,5},{5,4},{6,7},{7,6},{8,9},{9,8},{10,11... | collective-permute-start | bytes 1769480 | tf_op jit(solution)/shard_map/ppermute | solution.py:263
  4.6 1.1 %constant_dynamic-slice_fusion = (f32[64,768]{1,0:T(8,128)S(1)}, f32[64,768]{1,0:T(8,128)S(1)}) fusion(f32[64,1536]{1,0:T(8,128)} %param.5, s32[]{:T(128)S(6)} %select_n.14, s32[]{:T(128)S(6)} %select_n.13), kind=kLoop, calls=%fused_computation.2 | loop fusion | bytes 786440 | tf_op jit(solution)/shard_map/dynamic_slice | solution.py:291
  5.7 1.6 %collective-permute-start = (f32[64,768]{1,0:T(8,128)S(1)}, f32[64,768]{1,0:T(8,128)S(1)}, u32[]{:S(2)}, u32[]{:S(2)}) collective-permute-start(f32[64,768]{1,0:T(8,128)S(1)} %get-tuple-element.69), channel_id=1, source_target_pairs={{0,8},{4,12},{8,0},{12,4},{1,9},{5,13},{9,1},{13,5},{2,10},{6,14},... | collective-permute-start | bytes 589832 | tf_op jit(solution)/shard_map/ppermute | solution.py:266
  7.3 0.1 copy.6.refs_1_
  7.4 0.1 pad_add_fusion.refs_0_
  7.4 0.5 %copy-done.1 = s32[16,16]{1,0:T(8,128)S(1)} copy-done((s32[16,16]{1,0:T(8,128)S(1)}, s32[16,16]{1,0:T(8,128)}, u32[]{:S(2)}) %copy-start.1) | copy-done | bytes 1048
  8.0 2.0 %tables.1 = (f32[8,384]{1,0:T(8,128)S(1)}, f32[8,384]{1,0:T(8,128)S(1)}, f32[4,384]{1,0:T(4,128)S(1)}, f32[16,384]{1,0:T(8,128)S(1)}, f32[4,384]{1,0:T(4,128)S(1...) custom-call(s32[3]{0:T(128)S(1)} %pad_add_fusion.refs_0_, ...), custom_call_target="tpu_custom_call" | custom-call | bytes 212044 | tf_op jit(solution)/shard_map/tables/pallas_call | solution.py:229
  10.0 1.8 %collective-permute-done.refs_2_ = f32[64,768]{1,0:T(8,128)S(1)} collective-permute-done((f32[64,768]{1,0:T(8,128)S(1)}, f32[64,768]{1,0:T(8,128)S(1)}, u32[]{:S(2)}, u32[]{:S(2)}) %collective-permute-start) | collective-permute-done | bytes 196640 | tf_op jit(solution)/shard_map/ppermute | solution.py:266
  12.0 1.4 %collective-permute-done.1.refs_2_ = f32[128,384]{1,0:T(8,128)S(1)} collective-permute-done((f32[128,384]{1,0:T(8,128)S(1)}, f32[128,384]{1,0:T(8,128)S(1)}, u32[]{:S(2)}, u32[]{:S(2)}) %collective-permute-start.1) | collective-permute-done | bytes 196640 | tf_op jit(solution)/shard_map/ppermute | solution.py:266
  13.4 0.6 %own.1 = (bf16[256,384]{1,0:T(8,128)(2,1)S(1)}, bf16[256,384]{1,0:T(8,128)(2,1)S(1)}, f32[384,384]{1,0:T(8,128)S(1)}, f32[128,384]{1,0:T(8,128)S(1)}, f32[128,384]{1,0:T(8,128)S(1)}) custom-call(f32[8,384]{1,0:T(8,128)S(1)} %get-tuple-element.39.refs_0_, f32[128,384]{1,0:T(8,128)S(1)} %get-tuple-element.41.refs_1_, ...), custom_call_target="tpu_custom_call" | custom-call | flops 226492416 | bytes 2377728 | tf_op jit(solution)/shard_map/own/pallas_call | solution.py:229
  14.1 4.4 %collective-permute-start.3 = (f32[384,384]{1,0:T(8,128)S(1)}, f32[384,384]{1,0:T(8,128)S(1)}, u32[]{:S(2)}, u32[]{:S(2)}) collective-permute-start(f32[384,384]{1,0:T(8,128)S(1)} %pick.1), channel_id=1, source_target_pairs={{0,1},{1,0},{2,3},{3,2},{4,5},{5,4},{6,7},{7,6},{8,9},{9,8},{10,11... | collective-permute-start | bytes 1769480 | tf_op jit(solution)/shard_map/ppermute | solution.py:263
  18.4 0.9 %pair.1 = (f32[128,768]{1,0:T(8,128)S(1)}, f32[128,768]{1,0:T(8,128)S(1)}) custom-call(bf16[256,384]{1,0:T(8,128)(2,1)S(1)} %get-tuple-element.44.refs_0_, bf16[256,384]{1,0:T(8,128)(2,1)S(1)} %get-tuple-element.45.refs_1_, f32[384,384]{1,0:T(8,128)S(1)} %collective-permute-done.4.refs_2_, f32[4,384]{1,0:T(4,128)S(1)} %get-tuple-element.53.refs_3_, ...), custom_call_target="tpu_custom_call" | custom-call | flops 452984832 | bytes 2371584 | tf_op jit(solution)/shard_map/pair/pallas_call | solution.py:229
  19.4 0.6 %collective-permute-start.8 = (f32[128,768]{1,0:T(8,128)S(1)}, f32[128,768]{1,0:T(8,128)S(1)}, u32[]{:S(2)}, u32[]{:S(2)}) collective-permute-start(f32[128,768]{1,0:T(8,128)S(1)} %get-tuple-element.56), channel_id=1, source_target_pairs={{0,4},{4,0},{8,12},{12,8},{1,5},{5,1},{9,13},{13,9},{2,6},{6,2},{1... | collective-permute-start | bytes 1179656 | tf_op jit(solution)/shard_map/ppermute | solution.py:266
  19.9 0.1 collective-permute-start.6
  20.0 1.6 %collective-permute-done.6.refs_1_ = f32[128,384]{1,0:T(8,128)S(1)} collective-permute-done((f32[128,384]{1,0:T(8,128)S(1)}, f32[128,384]{1,0:T(8,128)S(1)}, u32[]{:S(2)}, u32[]{:S(2)}) %collective-permute-start.6) | collective-permute-done | bytes 196640 | tf_op jit(solution)/shard_map/ppermute | solution.py:266
  21.6 1.6 %collective-permute-start.7 = (f32[64,384]{1,0:T(8,128)S(1)}, f32[64,384]{1,0:T(8,128)S(1)}, u32[]{:S(2)}, u32[]{:S(2)}) collective-permute-start(f32[64,384]{1,0:T(8,128)S(1)} %get-tuple-element.52), channel_id=1, source_target_pairs={{0,8},{4,12},{8,0},{12,4},{1,9},{5,13},{9,1},{13,5},{2,10},{6,14},... | collective-permute-start | bytes 294920 | tf_op jit(solution)/shard_map/ppermute | solution.py:266
  23.2 0.6 %collective-permute-start.9 = (f32[64,768]{1,0:T(8,128)S(1)}, f32[64,768]{1,0:T(8,128)S(1)}, u32[]{:S(2)}, u32[]{:S(2)}) collective-permute-start(f32[64,768]{1,0:T(8,128)S(1)} %get-tuple-element.58), channel_id=1, source_target_pairs={{0,8},{4,12},{8,0},{12,4},{1,9},{5,13},{9,1},{13,5},{2,10},{6,14},... | collective-permute-start | bytes 589832 | tf_op jit(solution)/shard_map/ppermute | solution.py:266
  23.8 7.1 %collective-permute-done.3.refs_0_.refs_2_ = f32[384,384]{1,0:T(8,128)S(1)} collective-permute-done((f32[384,384]{1,0:T(8,128)S(1)}, f32[384,384]{1,0:T(8,128)S(1)}, u32[]{:S(2)}, u32[]{:S(2)}) %collective-permute-start.3) | collective-permute-done | bytes 589856 | tf_op jit(solution)/shard_map/ppermute | solution.py:263
  30.9 0.3 corner.2.refs_3_
  31.4 0.3 corner.3.refs_6_.refs_0_
  31.7 0.5 %last.1 = (f32[128,384]{1,0:T(8,128)S(1)}, f32[128,384]{1,0:T(8,128)S(1)}) custom-call(bf16[256,384]{1,0:T(8,128)(2,1)S(1)} %get-tuple-element.44.refs_0_, bf16[256,384]{1,0:T(8,128)(2,1)S(1)} %get-tuple-element.45.refs_1_, f32[384,384]{1,0:T(8,128)S(1)} %collective-permute-done.3.refs_0_.refs_2_, f32[4,384]{1,0:T(4,128)S(1)} %get-tuple-element.47.refs_3_, ...), custom_call_target="tpu_custom_call" | custom-call | flops 226492416 | bytes 1978368 | tf_op jit(solution)/shard_map/last/pallas_call | solution.py:229
  32.3 0.6 %collective-permute-start.10 = (f32[128,384]{1,0:T(8,128)S(1)}, f32[128,384]{1,0:T(8,128)S(1)}, u32[]{:S(2)}, u32[]{:S(2)}) collective-permute-start(f32[128,384]{1,0:T(8,128)S(1)} %get-tuple-element.60), channel_id=1, source_target_pairs={{0,4},{4,0},{8,12},{12,8},{1,5},{5,1},{9,13},{13,9},{2,6},{6,2},{1... | collective-permute-start | bytes 589832 | tf_op jit(solution)/shard_map/ppermute | solution.py:266
  32.9 2.6 %collective-permute-start.13 = (f32[64,384]{1,0:T(8,128)S(1)}, f32[64,384]{1,0:T(8,128)S(1)}, u32[]{:S(2)}, u32[]{:S(2)}) collective-permute-start(f32[64,384]{1,0:T(8,128)S(1)} %get-tuple-element.62.refs_3_), channel_id=1, source_target_pairs={{0,1},{1,8},{2,11},{3,2},{4,5},{5,12},{6,15},{7,6},{8,9},{9,0},{10... | collective-permute-start | bytes 294920 | tf_op jit(solution)/shard_map/ppermute | solution.py:307
  35.5 0.4 collective-permute-start.14
  35.9 1.2 %collective-permute-start.12 = (f32[64,384]{1,0:T(8,128)S(1)}, f32[64,384]{1,0:T(8,128)S(1)}, u32[]{:S(2)}, u32[]{:S(2)}) collective-permute-start(f32[64,384]{1,0:T(8,128)S(1)} %get-tuple-element.64), channel_id=1, source_target_pairs={{0,8},{4,12},{8,0},{12,4},{1,9},{5,13},{9,1},{13,5},{2,10},{6,14},... | collective-permute-start | bytes 294920 | tf_op jit(solution)/shard_map/ppermute | solution.py:266
  37.1 0.5 %finish.3.refs_3_ = f32[64,1536]{1,0:T(8,128)S(1)} custom-call(f32[16,384]{1,0:T(8,128)S(1)} %get-tuple-element.66.refs_0_, f32[64,384]{1,0:T(8,128)S(1)} %get-tuple-element.51.refs_4_.refs_1_, f32[64,384]{1,0:T(8,128)S(1)} %collective-permute-done.7.refs_5_.refs_2_, f32[32,384]{1,0:T(8,128)S(1)} %pad_maximum_fusion.refs_3_, ...), custom_call_target="tpu_custom_call" | custom-call | flops 393216 | bytes 1056768 | tf_op jit(solution)/shard_map/finish/pallas_call | solution.py:229
  37.6 2.4 %collective-permute-done.13.refs_1_ = f32[64,384]{1,0:T(8,128)S(1)} collective-permute-done((f32[64,384]{1,0:T(8,128)S(1)}, f32[64,384]{1,0:T(8,128)S(1)}, u32[]{:S(2)}, u32[]{:S(2)}) %collective-permute-start.13) | collective-permute-done | bytes 98336 | tf_op jit(solution)/shard_map/ppermute | solution.py:307
  40.0 0.8 %collective-permute-done.14.refs_2_ = f32[64,384]{1,0:T(8,128)S(1)} collective-permute-done((f32[64,384]{1,0:T(8,128)S(1)}, f32[64,384]{1,0:T(8,128)S(1)}, u32[]{:S(2)}, u32[]{:S(2)}) %collective-permute-start.14) | collective-permute-done | bytes 98336 | tf_op jit(solution)/shard_map/ppermute | solution.py:307
  40.7 0.2 finish.4.refs_3_
  40.9 0.6 %collective-permute-done.12.refs_2_ = f32[64,384]{1,0:T(8,128)S(1)} collective-permute-done((f32[64,384]{1,0:T(8,128)S(1)}, f32[64,384]{1,0:T(8,128)S(1)}, u32[]{:S(2)}, u32[]{:S(2)}) %collective-permute-start.12) | collective-permute-done | bytes 98336 | tf_op jit(solution)/shard_map/ppermute | solution.py:266
  41.6 0.9 %finish.5 = f32[64,1536]{1,0:T(8,128)} custom-call(f32[16,384]{1,0:T(8,128)S(1)} %add.10.refs_0_, f32[64,384]{1,0:T(8,128)S(1)} %get-tuple-element.63.refs_1_, f32[64,384]{1,0:T(8,128)S(1)} %collective-permute-done.12.refs_2_, f32[64,1536]{1,0:T(8,128)S(1)} %finish.4.refs_3_), custom_call_target="tpu_custom_call" | custom-call | flops 393216 | bytes 1007616 | tf_op jit(solution)/shard_map/finish/pallas_call | solution.py:229
  (27 shorter events, 0.5 us)
Async XLA Ops:
  0.0 14.0 %collective-permute-start.2 = (f32[384,384]{1,0:T(8,128)}, f32[384,384]{1,0:T(8,128)S(1)}, u32[]{:S(2)}, u32[]{:S(2)}) collective-permute-start(f32[384,384]{1,0:T(8,128)} %refs_3_.3), channel_id=1, source_target_pairs={{0,4},{1,2},{2,1},{3,7},{4,0},{5,6},{6,5},{7,3},{8,12},{9,10},{10,... | collective-permute-start | bytes 1769480 | tf_op jit(solution)/shard_map/ppermute | solution.py:263
  0.5 18.0 %collective-permute-start.4 = (f32[384,384]{1,0:T(8,128)}, f32[384,384]{1,0:T(8,128)S(1)}, u32[]{:S(2)}, u32[]{:S(2)}) collective-permute-start(f32[384,384]{1,0:T(8,128)} %refs_3_.3), channel_id=1, source_target_pairs={{0,1},{1,0},{2,3},{3,2},{4,5},{5,4},{6,7},{7,6},{8,9},{9,8},{10,11... | collective-permute-start | bytes 1769480 | tf_op jit(solution)/shard_map/ppermute | solution.py:263
  4.6 2.7 %copy-start.3 = (s32[32,16]{0,1:T(8,128)S(1)}, s32[32,16]{0,1:T(8,128)}, u32[]{:S(2)}) copy-start(s32[32,16]{0,1:T(8,128)} %param.7) | copy-start | bytes 6148
  4.6 8.8 %copy-start = (f32[384,384]{1,0:T(8,128)S(1)}, f32[384,384]{1,0:T(8,128)}, u32[]{:S(2)}) copy-start(f32[384,384]{1,0:T(8,128)} %refs_3_.3) | copy-start | bytes 1769476
  5.7 6.1 %collective-permute-start = (f32[64,768]{1,0:T(8,128)S(1)}, f32[64,768]{1,0:T(8,128)S(1)}, u32[]{:S(2)}, u32[]{:S(2)}) collective-permute-start(f32[64,768]{1,0:T(8,128)S(1)} %get-tuple-element.69), channel_id=1, source_target_pairs={{0,8},{4,12},{8,0},{12,4},{1,9},{5,13},{9,1},{13,5},{2,10},{6,14},... | collective-permute-start | bytes 589832 | tf_op jit(solution)/shard_map/ppermute | solution.py:266
  7.3 0.7 %copy-start.1 = (s32[16,16]{1,0:T(8,128)S(1)}, s32[16,16]{1,0:T(8,128)}, u32[]{:S(2)}) copy-start(s32[16,16]{1,0:T(8,128)} %refs_2_.1) | copy-start | bytes 3076
  7.4 0.7 %copy-start.2 = (s32[16]{0:T(128)S(1)}, s32[16]{0:T(128)}, u32[]{:S(2)}) copy-start(s32[16]{0:T(128)} %refs_3_.2) | copy-start | bytes 196
  11.9 1.5 %collective-permute-start.1 = (f32[128,384]{1,0:T(8,128)S(1)}, f32[128,384]{1,0:T(8,128)S(1)}, u32[]{:S(2)}, u32[]{:S(2)}) collective-permute-start(f32[128,384]{1,0:T(8,128)S(1)} %get-tuple-element.42), channel_id=1, source_target_pairs={{0,4},{4,0},{8,12},{12,8},{1,5},{5,1},{9,13},{13,9},{2,6},{6,2},{1... | collective-permute-start | bytes 589832 | tf_op jit(solution)/shard_map/ppermute | solution.py:266
  14.1 16.8 %collective-permute-start.3 = (f32[384,384]{1,0:T(8,128)S(1)}, f32[384,384]{1,0:T(8,128)S(1)}, u32[]{:S(2)}, u32[]{:S(2)}) collective-permute-start(f32[384,384]{1,0:T(8,128)S(1)} %pick.1), channel_id=1, source_target_pairs={{0,1},{1,0},{2,3},{3,2},{4,5},{5,4},{6,7},{7,6},{8,9},{9,8},{10,11... | collective-permute-start | bytes 1769480 | tf_op jit(solution)/shard_map/ppermute | solution.py:263
  18.4 12.5 %collective-permute-start.5 = (f32[384,384]{1,0:T(8,128)S(1)}, f32[384,384]{1,0:T(8,128)S(1)}, u32[]{:S(2)}, u32[]{:S(2)}) collective-permute-start(f32[384,384]{1,0:T(8,128)S(1)} %collective-permute-done.4.refs_2_), channel_id=1, source_target_pairs={{0,4},{1,2},{2,1},{3,7},{4,0},{5,6},{6,5},{7,3},{8,12},{9,10},{10,... | collective-permute-start | bytes 1769480 | tf_op jit(solution)/shard_map/ppermute | solution.py:263
  19.4 3.8 %collective-permute-start.8 = (f32[128,768]{1,0:T(8,128)S(1)}, f32[128,768]{1,0:T(8,128)S(1)}, u32[]{:S(2)}, u32[]{:S(2)}) collective-permute-start(f32[128,768]{1,0:T(8,128)S(1)} %get-tuple-element.56), channel_id=1, source_target_pairs={{0,4},{4,0},{8,12},{12,8},{1,5},{5,1},{9,13},{13,9},{2,6},{6,2},{1... | collective-permute-start | bytes 1179656 | tf_op jit(solution)/shard_map/ppermute | solution.py:266
  19.9 1.6 %collective-permute-start.6 = (f32[128,384]{1,0:T(8,128)S(1)}, f32[128,384]{1,0:T(8,128)S(1)}, u32[]{:S(2)}, u32[]{:S(2)}) collective-permute-start(f32[128,384]{1,0:T(8,128)S(1)} %get-tuple-element.50), channel_id=1, source_target_pairs={{0,4},{4,0},{8,12},{12,8},{1,5},{5,1},{9,13},{13,9},{2,6},{6,2},{1... | collective-permute-start | bytes 589832 | tf_op jit(solution)/shard_map/ppermute | solution.py:266
  21.6 9.3 %collective-permute-start.7 = (f32[64,384]{1,0:T(8,128)S(1)}, f32[64,384]{1,0:T(8,128)S(1)}, u32[]{:S(2)}, u32[]{:S(2)}) collective-permute-start(f32[64,384]{1,0:T(8,128)S(1)} %get-tuple-element.52), channel_id=1, source_target_pairs={{0,8},{4,12},{8,0},{12,4},{1,9},{5,13},{9,1},{13,5},{2,10},{6,14},... | collective-permute-start | bytes 294920 | tf_op jit(solution)/shard_map/ppermute | solution.py:266
  23.2 7.7 %collective-permute-start.9 = (f32[64,768]{1,0:T(8,128)S(1)}, f32[64,768]{1,0:T(8,128)S(1)}, u32[]{:S(2)}, u32[]{:S(2)}) collective-permute-start(f32[64,768]{1,0:T(8,128)S(1)} %get-tuple-element.58), channel_id=1, source_target_pairs={{0,8},{4,12},{8,0},{12,4},{1,9},{5,13},{9,1},{13,5},{2,10},{6,14},... | collective-permute-start | bytes 589832 | tf_op jit(solution)/shard_map/ppermute | solution.py:266
  31.3 1.5 %collective-permute-start.11 = (f32[128,384]{1,0:T(8,128)S(1)}, f32[128,384]{1,0:T(8,128)S(1)}, u32[]{:S(2)}, u32[]{:S(2)}) collective-permute-start(f32[128,384]{1,0:T(8,128)S(1)} %corner.2.refs_3_), channel_id=1, source_target_pairs={{0,4},{4,0},{8,12},{12,8},{1,5},{5,1},{9,13},{13,9},{2,6},{6,2},{1... | collective-permute-start | bytes 589832 | tf_op jit(solution)/shard_map/ppermute | solution.py:266
  32.3 3.6 %collective-permute-start.10 = (f32[128,384]{1,0:T(8,128)S(1)}, f32[128,384]{1,0:T(8,128)S(1)}, u32[]{:S(2)}, u32[]{:S(2)}) collective-permute-start(f32[128,384]{1,0:T(8,128)S(1)} %get-tuple-element.60), channel_id=1, source_target_pairs={{0,4},{4,0},{8,12},{12,8},{1,5},{5,1},{9,13},{13,9},{2,6},{6,2},{1... | collective-permute-start | bytes 589832 | tf_op jit(solution)/shard_map/ppermute | solution.py:266
  32.9 7.1 %collective-permute-start.13 = (f32[64,384]{1,0:T(8,128)S(1)}, f32[64,384]{1,0:T(8,128)S(1)}, u32[]{:S(2)}, u32[]{:S(2)}) collective-permute-start(f32[64,384]{1,0:T(8,128)S(1)} %get-tuple-element.62.refs_3_), channel_id=1, source_target_pairs={{0,1},{1,8},{2,11},{3,2},{4,5},{5,12},{6,15},{7,6},{8,9},{9,0},{10... | collective-permute-start | bytes 294920 | tf_op jit(solution)/shard_map/ppermute | solution.py:307
  35.5 5.3 %collective-permute-start.14 = (f32[64,384]{1,0:T(8,128)S(1)}, f32[64,384]{1,0:T(8,128)S(1)}, u32[]{:S(2)}, u32[]{:S(2)}) collective-permute-start(f32[64,384]{1,0:T(8,128)S(1)} %get-tuple-element.61.refs_2_), channel_id=1, source_target_pairs={{0,1},{1,0},{2,3},{3,2},{4,5},{5,4},{6,7},{7,6},{8,9},{9,8},{10,11... | collective-permute-start | bytes 294920 | tf_op jit(solution)/shard_map/ppermute | solution.py:307
  35.9 5.7 %collective-permute-start.12 = (f32[64,384]{1,0:T(8,128)S(1)}, f32[64,384]{1,0:T(8,128)S(1)}, u32[]{:S(2)}, u32[]{:S(2)}) collective-permute-start(f32[64,384]{1,0:T(8,128)S(1)} %get-tuple-element.64), channel_id=1, source_target_pairs={{0,8},{4,12},{8,0},{12,4},{1,9},{5,13},{9,1},{13,5},{2,10},{6,14},... | collective-permute-start | bytes 294920 | tf_op jit(solution)/shard_map/ppermute | solution.py:266

commit v20 on v17

--- a/solution.py
+++ b/solution.py
@@ -157,11 +157,23 @@
     out[...] = jnp.where(marks[0:1, : out.shape[1]] > 0.5, slab[...], block[...])
 
 
-def corner_kernel(slab, block, masks, keep, give):
+def corner_first_kernel(start, slab, block, masks, out, high, low):
     b_high, b_low = masked_halves([(block, masks)])
+    high[...], low[...] = b_high, b_low
+    a_high, a_low = split(slab[start : start + out.shape[0], :])
+    out[...] = product(a_high, a_low, b_high, b_low)
+
+
+def corner_rest_kernel(slab, b_high, b_low, out):
+    a_high, a_low = split(slab[: out.shape[0], :])
+    out[...] = product(a_high, a_low, b_high[...], b_low[...])
+
+
+def last_kernel(counts, high, low, b_high, b_low, *refs):
+    keep, give = refs[-2:]
     half = keep.shape[0]
-    a_high, a_low = split(slab[: 2 * half, :])
-    sums = product(a_high, a_low, b_high, b_low)
+    other_high, other_low = masked_halves(parted(refs[:-2], counts))
+    sums = product(high[...], low[...], b_high[...] + other_high, b_low[...] + other_low)
     give[...] = sums[half:, :]
     keep[...] = sums[:half, :]
 
@@ -387,12 +399,24 @@
         slots, folded = [], ()
         if corner:
             args = (end_slab, *odd, masks[ODD, step])
-            parts = call(corner_kernel, "corner", sums, 0, *args, flops=flops, after=after)
+            half_block = [jax.ShapeDtypeStruct((depth, width), jnp.bfloat16)] * 2
+            kernel = functools.partial(corner_first_kernel, total // 2)
+            give, *halves = call(
+                kernel, "corner", sums[:1] + half_block, 0, *args, flops=flops // 2, after=after
+            )
+            parts = call(
+                corner_rest_kernel, "corner", sums[:1], 0, end_slab, *halves, flops=flops // 2, after=(give,)
+            )
+            parts = (*parts, give)
             folded = fold(*parts)
             after, pieces = (parts[0],), list(enumerate(folded))
             slots.append(([[ends]], [next_door(x, 2 * i) for i, x in reversed(pieces)]))
-        args = (*even, masks[EVEN, step], *odd, masks[ODD, step])
-        kernel = functools.partial(multiply_kernel, ((len(even) + 1, len(odd) + 1),))
+        if corner:
+            args = (*halves, *even, masks[EVEN, step])
+            kernel = functools.partial(last_kernel, (len(even) + 1,))
+        else:
+            args = (*even, masks[EVEN, step], *odd, masks[ODD, step])
+            kernel = functools.partial(multiply_kernel, ((len(even) + 1, len(odd) + 1),))
         parts = call(kernel, "last", sums, 0, high, low, *args, flops=flops, after=after)
         if slots:
             out = finish(slots, out)

time: 42.9 us -> 42.7 us (level)
    pallas_call x15 -> x16, Pallas kernels: 6.3 us -> 6.52 us  [call(): pl.pallas_call(body, out_shape=outs, in_specs=[SMEM] * n_smem + [VMEM] *...]
  transfers between devices with their start and end apart: 15 -> 15, of which waited for: 8 -> 7; matrix products, arithmetic and copies ran while one was open for 3% -> 3% of each run, Pallas kernels for 11% -> 12%
where the time goes in v20:
time: 42.7 us; the launch traced here: 42.5 us
  starting transfers between devices  18.3 us (43%)
  waiting for transfers between devices  15.7 us (37%)
  Pallas kernels  6.52 us (15%)
  local copies, waits for them, and re-layouts  1.77 us (4%)
    ppermute x4, starting transfers between devices, swap_line(): return lax.ppermute(x, ('row', 'col'), pairs_)  8.97 us
    ppermute x4, waiting for transfers between devices, swap_line(): return lax.ppermute(x, ('row', 'col'), pairs_)  7.09 us
    pallas_call x16, Pallas kernels, call(): pl.pallas_call(body, out_shape=outs, in_specs=[SMEM] * n_smem + [VMEM] *...  6.52 us
    ppermute x9, starting transfers between devices, swap(): return lax.ppermute(x, 'row', [(i, i ^ d) for i in range(n_row)])  6.31 us
    ppermute x9, waiting for transfers between devices, swap(): return lax.ppermute(x, 'row', [(i, i ^ d) for i in range(n_row)])  5.49 us
    ppermute x2, waiting for transfers between devices, next_door(): lax.ppermute(x, ('row', 'col'), [(i * n_col + j, (i ^ (d if 0 < j < n_col...  3.15 us
    ppermute x2, starting transfers between devices, next_door(): lax.ppermute(x, ('row', 'col'), [(i * n_col + j, (i ^ (d if 0 < j < n_col...  3 us
    dynamic_slice x1, local copies, waits for them, and re-layouts, chip_columns(): return lax.dynamic_slice_in_dim(amplitudes, start, 2 * depth, 1)  1.11 us
  transfers between devices with their start and end apart: 15, of which 7 were waited for; matrix products, arithmetic and copies ran while one was open for 3% of the time, Pallas kernels for 12%

profile of v20, /device:TPU:0, one launch (start us, length us, event | category | flops | bytes accessed | tf_op | source)
XLA Modules:
  0.0 42.5 jit_solution(14984770310148308289)
XLA Ops:
  0.0 0.5 %collective-permute-start.2 = (f32[384,384]{1,0:T(8,128)}, f32[384,384]{1,0:T(8,128)S(1)}, u32[]{:S(2)}, u32[]{:S(2)}) collective-permute-start(f32[384,384]{1,0:T(8,128)} %refs_3_.3), channel_id=1, source_target_pairs={{0,4},{1,2},{2,1},{3,7},{4,0},{5,6},{6,5},{7,3},{8,12},{9,10},{10,... | collective-permute-start | bytes 1769480 | tf_op jit(solution)/shard_map/ppermute | solution.py:278
  0.5 4.1 %collective-permute-start.4 = (f32[384,384]{1,0:T(8,128)}, f32[384,384]{1,0:T(8,128)S(1)}, u32[]{:S(2)}, u32[]{:S(2)}) collective-permute-start(f32[384,384]{1,0:T(8,128)} %refs_3_.3), channel_id=1, source_target_pairs={{0,1},{1,0},{2,3},{3,2},{4,5},{5,4},{6,7},{7,6},{8,9},{9,8},{10,11... | collective-permute-start | bytes 1769480 | tf_op jit(solution)/shard_map/ppermute | solution.py:278
  4.6 1.1 %constant_dynamic-slice_fusion = (f32[64,768]{1,0:T(8,128)S(1)}, f32[64,768]{1,0:T(8,128)S(1)}) fusion(f32[64,1536]{1,0:T(8,128)} %param.5, s32[]{:T(128)S(6)} %select_n.14, s32[]{:T(128)S(6)} %select_n.13), kind=kLoop, calls=%fused_computation.2 | loop fusion | bytes 786440 | tf_op jit(solution)/shard_map/dynamic_slice | solution.py:306
  5.7 1.6 %collective-permute-start = (f32[64,768]{1,0:T(8,128)S(1)}, f32[64,768]{1,0:T(8,128)S(1)}, u32[]{:S(2)}, u32[]{:S(2)}) collective-permute-start(f32[64,768]{1,0:T(8,128)S(1)} %get-tuple-element.75), channel_id=1, source_target_pairs={{0,8},{4,12},{8,0},{12,4},{1,9},{5,13},{9,1},{13,5},{2,10},{6,14},... | collective-permute-start | bytes 589832 | tf_op jit(solution)/shard_map/ppermute | solution.py:281
  7.3 0.1 copy.6.refs_1_
  7.4 0.1 pad_add_fusion.refs_0_
  7.4 0.5 %copy-done.1 = s32[16,16]{1,0:T(8,128)S(1)} copy-done((s32[16,16]{1,0:T(8,128)S(1)}, s32[16,16]{1,0:T(8,128)}, u32[]{:S(2)}) %copy-start.1) | copy-done | bytes 1048
  8.0 2.0 %tables.1 = (f32[8,384]{1,0:T(8,128)S(1)}, f32[8,384]{1,0:T(8,128)S(1)}, f32[4,384]{1,0:T(4,128)S(1)}, f32[16,384]{1,0:T(8,128)S(1)}, f32[4,384]{1,0:T(4,128)S(1...) custom-call(s32[3]{0:T(128)S(1)} %pad_add_fusion.refs_0_, ...), custom_call_target="tpu_custom_call" | custom-call | bytes 212044 | tf_op jit(solution)/shard_map/tables/pallas_call | solution.py:244
  10.0 1.8 %collective-permute-done.refs_2_ = f32[64,768]{1,0:T(8,128)S(1)} collective-permute-done((f32[64,768]{1,0:T(8,128)S(1)}, f32[64,768]{1,0:T(8,128)S(1)}, u32[]{:S(2)}, u32[]{:S(2)}) %collective-permute-start) | collective-permute-done | bytes 196640 | tf_op jit(solution)/shard_map/ppermute | solution.py:281
  12.0 1.4 %collective-permute-done.1.refs_2_ = f32[128,384]{1,0:T(8,128)S(1)} collective-permute-done((f32[128,384]{1,0:T(8,128)S(1)}, f32[128,384]{1,0:T(8,128)S(1)}, u32[]{:S(2)}, u32[]{:S(2)}) %collective-permute-start.1) | collective-permute-done | bytes 196640 | tf_op jit(solution)/shard_map/ppermute | solution.py:281
  13.4 0.6 %own.1 = (bf16[256,384]{1,0:T(8,128)(2,1)S(1)}, bf16[256,384]{1,0:T(8,128)(2,1)S(1)}, f32[384,384]{1,0:T(8,128)S(1)}, f32[128,384]{1,0:T(8,128)S(1)}, f32[128,384]{1,0:T(8,128)S(1)}) custom-call(f32[8,384]{1,0:T(8,128)S(1)} %get-tuple-element.42.refs_0_, f32[128,384]{1,0:T(8,128)S(1)} %get-tuple-element.44.refs_1_, ...), custom_call_target="tpu_custom_call" | custom-call | flops 226492416 | bytes 2377728 | tf_op jit(solution)/shard_map/own/pallas_call | solution.py:244
  14.1 4.4 %collective-permute-start.3 = (f32[384,384]{1,0:T(8,128)S(1)}, f32[384,384]{1,0:T(8,128)S(1)}, u32[]{:S(2)}, u32[]{:S(2)}) collective-permute-start(f32[384,384]{1,0:T(8,128)S(1)} %pick.1), channel_id=1, source_target_pairs={{0,1},{1,0},{2,3},{3,2},{4,5},{5,4},{6,7},{7,6},{8,9},{9,8},{10,11... | collective-permute-start | bytes 1769480 | tf_op jit(solution)/shard_map/ppermute | solution.py:278
  18.4 0.9 %pair.1 = (f32[128,768]{1,0:T(8,128)S(1)}, f32[128,768]{1,0:T(8,128)S(1)}) custom-call(bf16[256,384]{1,0:T(8,128)(2,1)S(1)} %get-tuple-element.47.refs_0_, bf16[256,384]{1,0:T(8,128)(2,1)S(1)} %get-tuple-element.48.refs_1_, f32[384,384]{1,0:T(8,128)S(1)} %collective-permute-done.4.refs_2_, f32[4,384]{1,0:T(4,128)S(1)} %get-tuple-element.55.refs_3_, ...), custom_call_target="tpu_custom_call" | custom-call | flops 452984832 | bytes 2371584 | tf_op jit(solution)/shard_map/pair/pallas_call | solution.py:244
  19.4 0.6 %collective-permute-start.8 = (f32[128,768]{1,0:T(8,128)S(1)}, f32[128,768]{1,0:T(8,128)S(1)}, u32[]{:S(2)}, u32[]{:S(2)}) collective-permute-start(f32[128,768]{1,0:T(8,128)S(1)} %get-tuple-element.58), channel_id=1, source_target_pairs={{0,4},{4,0},{8,12},{12,8},{1,5},{5,1},{9,13},{13,9},{2,6},{6,2},{1... | collective-permute-start | bytes 1179656 | tf_op jit(solution)/shard_map/ppermute | solution.py:281
  19.9 0.1 collective-permute-start.6
  20.0 1.6 %collective-permute-done.6.refs_1_ = f32[128,384]{1,0:T(8,128)S(1)} collective-permute-done((f32[128,384]{1,0:T(8,128)S(1)}, f32[128,384]{1,0:T(8,128)S(1)}, u32[]{:S(2)}, u32[]{:S(2)}) %collective-permute-start.6) | collective-permute-done | bytes 196640 | tf_op jit(solution)/shard_map/ppermute | solution.py:281
  21.6 1.6 %collective-permute-start.7 = (f32[64,384]{1,0:T(8,128)S(1)}, f32[64,384]{1,0:T(8,128)S(1)}, u32[]{:S(2)}, u32[]{:S(2)}) collective-permute-start(f32[64,384]{1,0:T(8,128)S(1)} %get-tuple-element.54), channel_id=1, source_target_pairs={{0,8},{4,12},{8,0},{12,4},{1,9},{5,13},{9,1},{13,5},{2,10},{6,14},... | collective-permute-start | bytes 294920 | tf_op jit(solution)/shard_map/ppermute | solution.py:281
  23.2 0.6 %collective-permute-start.9 = (f32[64,768]{1,0:T(8,128)S(1)}, f32[64,768]{1,0:T(8,128)S(1)}, u32[]{:S(2)}, u32[]{:S(2)}) collective-permute-start(f32[64,768]{1,0:T(8,128)S(1)} %get-tuple-element.60), channel_id=1, source_target_pairs={{0,8},{4,12},{8,0},{12,4},{1,9},{5,13},{9,1},{13,5},{2,10},{6,14},... | collective-permute-start | bytes 589832 | tf_op jit(solution)/shard_map/ppermute | solution.py:281
  23.8 7.1 %collective-permute-done.3.refs_0_.refs_4_ = f32[384,384]{1,0:T(8,128)S(1)} collective-permute-done((f32[384,384]{1,0:T(8,128)S(1)}, f32[384,384]{1,0:T(8,128)S(1)}, u32[]{:S(2)}, u32[]{:S(2)}) %collective-permute-start.3) | collective-permute-done | bytes 589856 | tf_op jit(solution)/shard_map/ppermute | solution.py:278
  30.9 0.4 corner.2
  31.4 0.3 corner.3.refs_6_.refs_0_
  31.7 0.5 %last.1 = (f32[128,384]{1,0:T(8,128)S(1)}, f32[128,384]{1,0:T(8,128)S(1)}) custom-call(bf16[256,384]{1,0:T(8,128)(2,1)S(1)} %get-tuple-element.47.refs_0_, bf16[256,384]{1,0:T(8,128)(2,1)S(1)} %get-tuple-element.48.refs_1_, bf16[384,384]{1,0:T(8,128)(2,1)S(1)} %get-tuple-element.61.refs_1_.refs_2_, bf16[384,384]{1,0:T(8,128)(2,1)S(1)} %get-tuple-element.62.refs_2_.refs_3_, ...), custom_call_target="tpu_custom_call" | custom-call | flops 226492416 | bytes 1972224 | tf_op jit(solution)/shard_map/last/pallas_call | solution.py:244
  32.3 0.6 %collective-permute-start.10 = (f32[128,384]{1,0:T(8,128)S(1)}, f32[128,384]{1,0:T(8,128)S(1)}, u32[]{:S(2)}, u32[]{:S(2)}) collective-permute-start(f32[128,384]{1,0:T(8,128)S(1)} %get-tuple-element.66), channel_id=1, source_target_pairs={{0,4},{4,0},{8,12},{12,8},{1,5},{5,1},{9,13},{13,9},{2,6},{6,2},{1... | collective-permute-start | bytes 589832 | tf_op jit(solution)/shard_map/ppermute | solution.py:281
  32.9 2.6 %collective-permute-start.13 = (f32[64,384]{1,0:T(8,128)S(1)}, f32[64,384]{1,0:T(8,128)S(1)}, u32[]{:S(2)}, u32[]{:S(2)}) collective-permute-start(f32[64,384]{1,0:T(8,128)S(1)} %get-tuple-element.68.refs_3_), channel_id=1, source_target_pairs={{0,1},{1,8},{2,11},{3,2},{4,5},{5,12},{6,15},{7,6},{8,9},{9,0},{10... | collective-permute-start | bytes 294920 | tf_op jit(solution)/shard_map/ppermute | solution.py:322
  35.5 0.4 collective-permute-start.14
  35.9 1.2 %collective-permute-start.12 = (f32[64,384]{1,0:T(8,128)S(1)}, f32[64,384]{1,0:T(8,128)S(1)}, u32[]{:S(2)}, u32[]{:S(2)}) collective-permute-start(f32[64,384]{1,0:T(8,128)S(1)} %get-tuple-element.70), channel_id=1, source_target_pairs={{0,8},{4,12},{8,0},{12,4},{1,9},{5,13},{9,1},{13,5},{2,10},{6,14},... | collective-permute-start | bytes 294920 | tf_op jit(solution)/shard_map/ppermute | solution.py:281
  37.2 0.5 %finish.3.refs_3_ = f32[64,1536]{1,0:T(8,128)S(1)} custom-call(f32[16,384]{1,0:T(8,128)S(1)} %get-tuple-element.72.refs_0_, f32[64,384]{1,0:T(8,128)S(1)} %get-tuple-element.53.refs_4_.refs_1_, f32[64,384]{1,0:T(8,128)S(1)} %collective-permute-done.7.refs_5_.refs_2_, f32[32,384]{1,0:T(8,128)S(1)} %pad_maximum_fusion.refs_3_, ...), custom_call_target="tpu_custom_call" | custom-call | flops 393216 | bytes 1056768 | tf_op jit(solution)/shard_map/finish/pallas_call | solution.py:244
  37.6 2.4 %collective-permute-done.13.refs_1_ = f32[64,384]{1,0:T(8,128)S(1)} collective-permute-done((f32[64,384]{1,0:T(8,128)S(1)}, f32[64,384]{1,0:T(8,128)S(1)}, u32[]{:S(2)}, u32[]{:S(2)}) %collective-permute-start.13) | collective-permute-done | bytes 98336 | tf_op jit(solution)/shard_map/ppermute | solution.py:322
  40.0 0.8 %collective-permute-done.14.refs_2_ = f32[64,384]{1,0:T(8,128)S(1)} collective-permute-done((f32[64,384]{1,0:T(8,128)S(1)}, f32[64,384]{1,0:T(8,128)S(1)}, u32[]{:S(2)}, u32[]{:S(2)}) %collective-permute-start.14) | collective-permute-done | bytes 98336 | tf_op jit(solution)/shard_map/ppermute | solution.py:322
  40.8 0.2 finish.4.refs_3_
  41.0 0.6 %collective-permute-done.12.refs_2_ = f32[64,384]{1,0:T(8,128)S(1)} collective-permute-done((f32[64,384]{1,0:T(8,128)S(1)}, f32[64,384]{1,0:T(8,128)S(1)}, u32[]{:S(2)}, u32[]{:S(2)}) %collective-permute-start.12) | collective-permute-done | bytes 98336 | tf_op jit(solution)/shard_map/ppermute | solution.py:281
  41.6 0.9 %finish.5 = f32[64,1536]{1,0:T(8,128)} custom-call(f32[16,384]{1,0:T(8,128)S(1)} %add.10.refs_0_, f32[64,384]{1,0:T(8,128)S(1)} %get-tuple-element.69.refs_1_, f32[64,384]{1,0:T(8,128)S(1)} %collective-permute-done.12.refs_2_, f32[64,1536]{1,0:T(8,128)S(1)} %finish.4.refs_3_), custom_call_target="tpu_custom_call" | custom-call | flops 393216 | bytes 1007616 | tf_op jit(solution)/shard_map/finish/pallas_call | solution.py:244
  (27 shorter events, 0.5 us)
Async XLA Ops:
  0.0 14.0 %collective-permute-start.2 = (f32[384,384]{1,0:T(8,128)}, f32[384,384]{1,0:T(8,128)S(1)}, u32[]{:S(2)}, u32[]{:S(2)}) collective-permute-start(f32[384,384]{1,0:T(8,128)} %refs_3_.3), channel_id=1, source_target_pairs={{0,4},{1,2},{2,1},{3,7},{4,0},{5,6},{6,5},{7,3},{8,12},{9,10},{10,... | collective-permute-start | bytes 1769480 | tf_op jit(solution)/shard_map/ppermute | solution.py:278
  0.5 18.0 %collective-permute-start.4 = (f32[384,384]{1,0:T(8,128)}, f32[384,384]{1,0:T(8,128)S(1)}, u32[]{:S(2)}, u32[]{:S(2)}) collective-permute-start(f32[384,384]{1,0:T(8,128)} %refs_3_.3), channel_id=1, source_target_pairs={{0,1},{1,0},{2,3},{3,2},{4,5},{5,4},{6,7},{7,6},{8,9},{9,8},{10,11... | collective-permute-start | bytes 1769480 | tf_op jit(solution)/shard_map/ppermute | solution.py:278
  4.6 2.7 %copy-start.3 = (s32[32,16]{0,1:T(8,128)S(1)}, s32[32,16]{0,1:T(8,128)}, u32[]{:S(2)}) copy-start(s32[32,16]{0,1:T(8,128)} %param.7) | copy-start | bytes 6148
  4.6 8.8 %copy-start = (f32[384,384]{1,0:T(8,128)S(1)}, f32[384,384]{1,0:T(8,128)}, u32[]{:S(2)}) copy-start(f32[384,384]{1,0:T(8,128)} %refs_3_.3) | copy-start | bytes 1769476
  5.7 6.1 %collective-permute-start = (f32[64,768]{1,0:T(8,128)S(1)}, f32[64,768]{1,0:T(8,128)S(1)}, u32[]{:S(2)}, u32[]{:S(2)}) collective-permute-start(f32[64,768]{1,0:T(8,128)S(1)} %get-tuple-element.75), channel_id=1, source_target_pairs={{0,8},{4,12},{8,0},{12,4},{1,9},{5,13},{9,1},{13,5},{2,10},{6,14},... | collective-permute-start | bytes 589832 | tf_op jit(solution)/shard_map/ppermute | solution.py:281
  7.3 0.7 %copy-start.1 = (s32[16,16]{1,0:T(8,128)S(1)}, s32[16,16]{1,0:T(8,128)}, u32[]{:S(2)}) copy-start(s32[16,16]{1,0:T(8,128)} %refs_2_.1) | copy-start | bytes 3076
  7.4 0.7 %copy-start.2 = (s32[16]{0:T(128)S(1)}, s32[16]{0:T(128)}, u32[]{:S(2)}) copy-start(s32[16]{0:T(128)} %refs_3_.2) | copy-start | bytes 196
  11.9 1.5 %collective-permute-start.1 = (f32[128,384]{1,0:T(8,128)S(1)}, f32[128,384]{1,0:T(8,128)S(1)}, u32[]{:S(2)}, u32[]{:S(2)}) collective-permute-start(f32[128,384]{1,0:T(8,128)S(1)} %get-tuple-element.45), channel_id=1, source_target_pairs={{0,4},{4,0},{8,12},{12,8},{1,5},{5,1},{9,13},{13,9},{2,6},{6,2},{1... | collective-permute-start | bytes 589832 | tf_op jit(solution)/shard_map/ppermute | solution.py:281
  14.1 16.8 %collective-permute-start.3 = (f32[384,384]{1,0:T(8,128)S(1)}, f32[384,384]{1,0:T(8,128)S(1)}, u32[]{:S(2)}, u32[]{:S(2)}) collective-permute-start(f32[384,384]{1,0:T(8,128)S(1)} %pick.1), channel_id=1, source_target_pairs={{0,1},{1,0},{2,3},{3,2},{4,5},{5,4},{6,7},{7,6},{8,9},{9,8},{10,11... | collective-permute-start | bytes 1769480 | tf_op jit(solution)/shard_map/ppermute | solution.py:278
  18.4 12.5 %collective-permute-start.5 = (f32[384,384]{1,0:T(8,128)S(1)}, f32[384,384]{1,0:T(8,128)S(1)}, u32[]{:S(2)}, u32[]{:S(2)}) collective-permute-start(f32[384,384]{1,0:T(8,128)S(1)} %collective-permute-done.4.refs_2_), channel_id=1, source_target_pairs={{0,4},{1,2},{2,1},{3,7},{4,0},{5,6},{6,5},{7,3},{8,12},{9,10},{10,... | collective-permute-start | bytes 1769480 | tf_op jit(solution)/shard_map/ppermute | solution.py:278
  19.4 3.8 %collective-permute-start.8 = (f32[128,768]{1,0:T(8,128)S(1)}, f32[128,768]{1,0:T(8,128)S(1)}, u32[]{:S(2)}, u32[]{:S(2)}) collective-permute-start(f32[128,768]{1,0:T(8,128)S(1)} %get-tuple-element.58), channel_id=1, source_target_pairs={{0,4},{4,0},{8,12},{12,8},{1,5},{5,1},{9,13},{13,9},{2,6},{6,2},{1... | collective-permute-start | bytes 1179656 | tf_op jit(solution)/shard_map/ppermute | solution.py:281
  19.9 1.6 %collective-permute-start.6 = (f32[128,384]{1,0:T(8,128)S(1)}, f32[128,384]{1,0:T(8,128)S(1)}, u32[]{:S(2)}, u32[]{:S(2)}) collective-permute-start(f32[128,384]{1,0:T(8,128)S(1)} %get-tuple-element.52), channel_id=1, source_target_pairs={{0,4},{4,0},{8,12},{12,8},{1,5},{5,1},{9,13},{13,9},{2,6},{6,2},{1... | collective-permute-start | bytes 589832 | tf_op jit(solution)/shard_map/ppermute | solution.py:281
  21.6 9.3 %collective-permute-start.7 = (f32[64,384]{1,0:T(8,128)S(1)}, f32[64,384]{1,0:T(8,128)S(1)}, u32[]{:S(2)}, u32[]{:S(2)}) collective-permute-start(f32[64,384]{1,0:T(8,128)S(1)} %get-tuple-element.54), channel_id=1, source_target_pairs={{0,8},{4,12},{8,0},{12,4},{1,9},{5,13},{9,1},{13,5},{2,10},{6,14},... | collective-permute-start | bytes 294920 | tf_op jit(solution)/shard_map/ppermute | solution.py:281
  23.2 7.7 %collective-permute-start.9 = (f32[64,768]{1,0:T(8,128)S(1)}, f32[64,768]{1,0:T(8,128)S(1)}, u32[]{:S(2)}, u32[]{:S(2)}) collective-permute-start(f32[64,768]{1,0:T(8,128)S(1)} %get-tuple-element.60), channel_id=1, source_target_pairs={{0,8},{4,12},{8,0},{12,4},{1,9},{5,13},{9,1},{13,5},{2,10},{6,14},... | collective-permute-start | bytes 589832 | tf_op jit(solution)/shard_map/ppermute | solution.py:281
  31.3 1.5 %collective-permute-start.11 = (f32[128,384]{1,0:T(8,128)S(1)}, f32[128,384]{1,0:T(8,128)S(1)}, u32[]{:S(2)}, u32[]{:S(2)}) collective-permute-start(f32[128,384]{1,0:T(8,128)S(1)} %get-tuple-element.64.refs_3_), channel_id=1, source_target_pairs={{0,4},{4,0},{8,12},{12,8},{1,5},{5,1},{9,13},{13,9},{2,6},{6,2},{1... | collective-permute-start | bytes 589832 | tf_op jit(solution)/shard_map/ppermute | solution.py:281
  32.3 3.6 %collective-permute-start.10 = (f32[128,384]{1,0:T(8,128)S(1)}, f32[128,384]{1,0:T(8,128)S(1)}, u32[]{:S(2)}, u32[]{:S(2)}) collective-permute-start(f32[128,384]{1,0:T(8,128)S(1)} %get-tuple-element.66), channel_id=1, source_target_pairs={{0,4},{4,0},{8,12},{12,8},{1,5},{5,1},{9,13},{13,9},{2,6},{6,2},{1... | collective-permute-start | bytes 589832 | tf_op jit(solution)/shard_map/ppermute | solution.py:281
  32.9 7.1 %collective-permute-start.13 = (f32[64,384]{1,0:T(8,128)S(1)}, f32[64,384]{1,0:T(8,128)S(1)}, u32[]{:S(2)}, u32[]{:S(2)}) collective-permute-start(f32[64,384]{1,0:T(8,128)S(1)} %get-tuple-element.68.refs_3_), channel_id=1, source_target_pairs={{0,1},{1,8},{2,11},{3,2},{4,5},{5,12},{6,15},{7,6},{8,9},{9,0},{10... | collective-permute-start | bytes 294920 | tf_op jit(solution)/shard_map/ppermute | solution.py:322
  35.5 5.3 %collective-permute-start.14 = (f32[64,384]{1,0:T(8,128)S(1)}, f32[64,384]{1,0:T(8,128)S(1)}, u32[]{:S(2)}, u32[]{:S(2)}) collective-permute-start(f32[64,384]{1,0:T(8,128)S(1)} %get-tuple-element.67.refs_2_), channel_id=1, source_target_pairs={{0,1},{1,0},{2,3},{3,2},{4,5},{5,4},{6,7},{7,6},{8,9},{9,8},{10,11... | collective-permute-start | bytes 294920 | tf_op jit(solution)/shard_map/ppermute | solution.py:322
  35.9 5.7 %collective-permute-start.12 = (f32[64,384]{1,0:T(8,128)S(1)}, f32[64,384]{1,0:T(8,128)S(1)}, u32[]{:S(2)}, u32[]{:S(2)}) collective-permute-start(f32[64,384]{1,0:T(8,128)S(1)} %get-tuple-element.70), channel_id=1, source_target_pairs={{0,8},{4,12},{8,0},{12,4},{1,9},{5,13},{9,1},{13,5},{2,10},{6,14},... | collective-permute-start | bytes 294920 | tf_op jit(solution)/shard_map/ppermute | solution.py:281

commit v21 on v19

--- a/solution.py
+++ b/solution.py
@@ -161,6 +161,13 @@
     b_high, b_low = masked_halves([(block, masks)])
     a_high, a_low = split(slab[start : start + out.shape[0], :])
     out[...] = product(a_high, a_low, b_high, b_low)
+
+
+def last_kernel(start, counts, high, low, *refs):
+    out = refs[-1]
+    b_high, b_low = masked_halves(parted(refs, counts))
+    at = pl.ds(start, out.shape[0])
+    out[...] = product(high[at, :], low[at, :], b_high, b_low)
 
 
 def gate_kernel(out):
@@ -393,9 +400,13 @@
             folded = fold(*parts)
             after, pieces = (parts[0],), list(enumerate(folded))
             slots.append(([[ends]], [next_door(x, 2 * i) for i, x in reversed(pieces)]))
-        args = (*even, masks[EVEN, step], *odd, masks[ODD, step])
-        kernel = functools.partial(multiply_kernel, ((len(even) + 1, len(odd) + 1),))
-        parts = call(kernel, "last", sums, 0, high, low, *args, flops=flops, after=after)
+        parts = []
+        args = (high, low, *even, masks[EVEN, step], *odd, masks[ODD, step])
+        for start in (total // 2, 0):
+            kernel = functools.partial(last_kernel, start, (len(even) + 1, len(odd) + 1))
+            parts += call(kernel, "last", sums[:1], 0, *args, flops=flops // 2, after=after)
+            after = (parts[0], *folded)
+        parts = parts[::-1]
         if slots:
             out = finish(slots, out)
         slots = [([[(EVEN, step), (ODD, step)]], exchange(*parts, after=folded))]

time: 42.7 us -> 42.7 us (level)
    pallas_call x16 -> x17, Pallas kernels: 6.47 us -> 6.64 us  [call(): pl.pallas_call(body, out_shape=outs, in_specs=[SMEM] * n_smem + [VMEM] *...]
  transfers between devices with their start and end apart: 15 -> 15, of which waited for: 7 -> 8; matrix products, arithmetic and copies ran while one was open for 3% -> 3% of each run, Pallas kernels for 12% -> 13%
where the time goes in v21:
time: 42.7 us; the launch traced here: 42.5 us
  starting transfers between devices  18.3 us (43%)
  waiting for transfers between devices  15.5 us (36%)
  Pallas kernels  6.64 us (16%)
  local copies, waits for them, and re-layouts  1.77 us (4%)
    ppermute x4, starting transfers between devices, swap_line(): return lax.ppermute(x, ('row', 'col'), pairs_)  8.97 us
    ppermute x4, waiting for transfers between devices, swap_line(): return lax.ppermute(x, ('row', 'col'), pairs_)  7.1 us
    pallas_call x17, Pallas kernels, call(): pl.pallas_call(body, out_shape=outs, in_specs=[SMEM] * n_smem + [VMEM] *...  6.64 us
    ppermute x9, starting transfers between devices, swap(): return lax.ppermute(x, 'row', [(i, i ^ d) for i in range(n_row)])  6.32 us
    ppermute x9, waiting for transfers between devices, swap(): return lax.ppermute(x, 'row', [(i, i ^ d) for i in range(n_row)])  5.63 us
    ppermute x2, starting transfers between devices, next_door(): lax.ppermute(x, ('row', 'col'), [(i * n_col + j, (i ^ (d if 0 < j < n_col...  3.01 us
    ppermute x2, waiting for transfers between devices, next_door(): lax.ppermute(x, ('row', 'col'), [(i * n_col + j, (i ^ (d if 0 < j < n_col...  2.8 us
    dynamic_slice x1, local copies, waits for them, and re-layouts, chip_columns(): return lax.dynamic_slice_in_dim(amplitudes, start, 2 * depth, 1)  1.11 us
  transfers between devices with their start and end apart: 15, of which 8 were waited for; matrix products, arithmetic and copies ran while one was open for 3% of the time, Pallas kernels for 13%

profile of v21, /device:TPU:0, one launch (start us, length us, event | category | flops | bytes accessed | tf_op | source)
XLA Modules:
  0.0 42.5 jit_solution(9213922643987971343)
XLA Ops:
  0.0 0.5 %collective-permute-start.2 = (f32[384,384]{1,0:T(8,128)}, f32[384,384]{1,0:T(8,128)S(1)}, u32[]{:S(2)}, u32[]{:S(2)}) collective-permute-start(f32[384,384]{1,0:T(8,128)} %refs_3_.3), channel_id=1, source_target_pairs={{0,4},{1,2},{2,1},{3,7},{4,0},{5,6},{6,5},{7,3},{8,12},{9,10},{10,... | collective-permute-start | bytes 1769480 | tf_op jit(solution)/shard_map/ppermute | solution.py:270
  0.5 4.1 %collective-permute-start.4 = (f32[384,384]{1,0:T(8,128)}, f32[384,384]{1,0:T(8,128)S(1)}, u32[]{:S(2)}, u32[]{:S(2)}) collective-permute-start(f32[384,384]{1,0:T(8,128)} %refs_3_.3), channel_id=1, source_target_pairs={{0,1},{1,0},{2,3},{3,2},{4,5},{5,4},{6,7},{7,6},{8,9},{9,8},{10,11... | collective-permute-start | bytes 1769480 | tf_op jit(solution)/shard_map/ppermute | solution.py:270
  4.6 1.1 %constant_dynamic-slice_fusion = (f32[64,768]{1,0:T(8,128)S(1)}, f32[64,768]{1,0:T(8,128)S(1)}) fusion(f32[64,1536]{1,0:T(8,128)} %param.5, s32[]{:T(128)S(6)} %select_n.14, s32[]{:T(128)S(6)} %select_n.13), kind=kLoop, calls=%fused_computation.2 | loop fusion | bytes 786440 | tf_op jit(solution)/shard_map/dynamic_slice | solution.py:298
  5.7 1.6 %collective-permute-start = (f32[64,768]{1,0:T(8,128)S(1)}, f32[64,768]{1,0:T(8,128)S(1)}, u32[]{:S(2)}, u32[]{:S(2)}) collective-permute-start(f32[64,768]{1,0:T(8,128)S(1)} %get-tuple-element.65), channel_id=1, source_target_pairs={{0,8},{4,12},{8,0},{12,4},{1,9},{5,13},{9,1},{13,5},{2,10},{6,14},... | collective-permute-start | bytes 589832 | tf_op jit(solution)/shard_map/ppermute | solution.py:273
  7.4 0.5 %copy-done.1 = s32[16,16]{1,0:T(8,128)S(1)} copy-done((s32[16,16]{1,0:T(8,128)S(1)}, s32[16,16]{1,0:T(8,128)}, u32[]{:S(2)}) %copy-start.1) | copy-done | bytes 1048
  8.0 2.0 %tables.1 = (f32[8,384]{1,0:T(8,128)S(1)}, f32[8,384]{1,0:T(8,128)S(1)}, f32[4,384]{1,0:T(4,128)S(1)}, f32[16,384]{1,0:T(8,128)S(1)}, f32[4,384]{1,0:T(4,128)S(1...) custom-call(s32[3]{0:T(128)S(1)} %pad_add_fusion.refs_0_, ...), custom_call_target="tpu_custom_call" | custom-call | bytes 212044 | tf_op jit(solution)/shard_map/tables/pallas_call | solution.py:236
  10.0 1.8 %collective-permute-done.refs_2_ = f32[64,768]{1,0:T(8,128)S(1)} collective-permute-done((f32[64,768]{1,0:T(8,128)S(1)}, f32[64,768]{1,0:T(8,128)S(1)}, u32[]{:S(2)}, u32[]{:S(2)}) %collective-permute-start) | collective-permute-done | bytes 196640 | tf_op jit(solution)/shard_map/ppermute | solution.py:273
  12.0 1.4 %collective-permute-done.1.refs_2_ = f32[128,384]{1,0:T(8,128)S(1)} collective-permute-done((f32[128,384]{1,0:T(8,128)S(1)}, f32[128,384]{1,0:T(8,128)S(1)}, u32[]{:S(2)}, u32[]{:S(2)}) %collective-permute-start.1) | collective-permute-done | bytes 196640 | tf_op jit(solution)/shard_map/ppermute | solution.py:273
  13.4 0.6 %own.1 = (bf16[256,384]{1,0:T(8,128)(2,1)S(1)}, bf16[256,384]{1,0:T(8,128)(2,1)S(1)}, f32[384,384]{1,0:T(8,128)S(1)}, f32[128,384]{1,0:T(8,128)S(1)}, f32[128,384]{1,0:T(8,128)S(1)}) custom-call(f32[8,384]{1,0:T(8,128)S(1)} %get-tuple-element.37.refs_0_, f32[128,384]{1,0:T(8,128)S(1)} %get-tuple-element.39.refs_1_, ...), custom_call_target="tpu_custom_call" | custom-call | flops 226492416 | bytes 2377728 | tf_op jit(solution)/shard_map/own/pallas_call | solution.py:236
  14.1 4.4 %collective-permute-start.3 = (f32[384,384]{1,0:T(8,128)S(1)}, f32[384,384]{1,0:T(8,128)S(1)}, u32[]{:S(2)}, u32[]{:S(2)}) collective-permute-start(f32[384,384]{1,0:T(8,128)S(1)} %pick.1), channel_id=1, source_target_pairs={{0,1},{1,0},{2,3},{3,2},{4,5},{5,4},{6,7},{7,6},{8,9},{9,8},{10,11... | collective-permute-start | bytes 1769480 | tf_op jit(solution)/shard_map/ppermute | solution.py:270
  18.4 0.9 %pair.1 = (f32[128,768]{1,0:T(8,128)S(1)}, f32[128,768]{1,0:T(8,128)S(1)}) custom-call(bf16[256,384]{1,0:T(8,128)(2,1)S(1)} %get-tuple-element.42.refs_0_, bf16[256,384]{1,0:T(8,128)(2,1)S(1)} %get-tuple-element.43.refs_1_, f32[384,384]{1,0:T(8,128)S(1)} %collective-permute-done.4.refs_2_, f32[4,384]{1,0:T(4,128)S(1)} %get-tuple-element.51.refs_3_, ...), custom_call_target="tpu_custom_call" | custom-call | flops 452984832 | bytes 2371584 | tf_op jit(solution)/shard_map/pair/pallas_call | solution.py:236
  19.4 0.6 %collective-permute-start.8 = (f32[128,768]{1,0:T(8,128)S(1)}, f32[128,768]{1,0:T(8,128)S(1)}, u32[]{:S(2)}, u32[]{:S(2)}) collective-permute-start(f32[128,768]{1,0:T(8,128)S(1)} %get-tuple-element.54), channel_id=1, source_target_pairs={{0,4},{4,0},{8,12},{12,8},{1,5},{5,1},{9,13},{13,9},{2,6},{6,2},{1... | collective-permute-start | bytes 1179656 | tf_op jit(solution)/shard_map/ppermute | solution.py:273
  19.9 0.1 collective-permute-start.6
  20.0 1.6 %collective-permute-done.6.refs_1_ = f32[128,384]{1,0:T(8,128)S(1)} collective-permute-done((f32[128,384]{1,0:T(8,128)S(1)}, f32[128,384]{1,0:T(8,128)S(1)}, u32[]{:S(2)}, u32[]{:S(2)}) %collective-permute-start.6) | collective-permute-done | bytes 196640 | tf_op jit(solution)/shard_map/ppermute | solution.py:273
  21.6 1.6 %collective-permute-start.7 = (f32[64,384]{1,0:T(8,128)S(1)}, f32[64,384]{1,0:T(8,128)S(1)}, u32[]{:S(2)}, u32[]{:S(2)}) collective-permute-start(f32[64,384]{1,0:T(8,128)S(1)} %get-tuple-element.50), channel_id=1, source_target_pairs={{0,8},{4,12},{8,0},{12,4},{1,9},{5,13},{9,1},{13,5},{2,10},{6,14},... | collective-permute-start | bytes 294920 | tf_op jit(solution)/shard_map/ppermute | solution.py:273
  23.2 0.6 %collective-permute-start.9 = (f32[64,768]{1,0:T(8,128)S(1)}, f32[64,768]{1,0:T(8,128)S(1)}, u32[]{:S(2)}, u32[]{:S(2)}) collective-permute-start(f32[64,768]{1,0:T(8,128)S(1)} %get-tuple-element.56), channel_id=1, source_target_pairs={{0,8},{4,12},{8,0},{12,4},{1,9},{5,13},{9,1},{13,5},{2,10},{6,14},... | collective-permute-start | bytes 589832 | tf_op jit(solution)/shard_map/ppermute | solution.py:273
  23.8 7.1 %collective-permute-done.3.refs_0_.refs_2_ = f32[384,384]{1,0:T(8,128)S(1)} collective-permute-done((f32[384,384]{1,0:T(8,128)S(1)}, f32[384,384]{1,0:T(8,128)S(1)}, u32[]{:S(2)}, u32[]{:S(2)}) %collective-permute-start.3) | collective-permute-done | bytes 589856 | tf_op jit(solution)/shard_map/ppermute | solution.py:270
  30.9 0.3 corner.2.refs_3_
  31.4 0.3 corner.3.refs_6_.refs_0_
  31.7 0.4 last.2.refs_6_
  32.1 0.6 %collective-permute-start.11 = (f32[128,384]{1,0:T(8,128)S(1)}, f32[128,384]{1,0:T(8,128)S(1)}, u32[]{:S(2)}, u32[]{:S(2)}) collective-permute-start(f32[128,384]{1,0:T(8,128)S(1)} %last.2.refs_6_), channel_id=1, source_target_pairs={{0,4},{4,0},{8,12},{12,8},{1,5},{5,1},{9,13},{13,9},{2,6},{6,2},{1... | collective-permute-start | bytes 589832 | tf_op jit(solution)/shard_map/ppermute | solution.py:273
  32.6 0.1 collective-permute-done.10.refs_1_
  32.8 2.6 %collective-permute-start.13 = (f32[64,384]{1,0:T(8,128)S(1)}, f32[64,384]{1,0:T(8,128)S(1)}, u32[]{:S(2)}, u32[]{:S(2)}) collective-permute-start(f32[64,384]{1,0:T(8,128)S(1)} %get-tuple-element.58.refs_8_.refs_3_), channel_id=1, source_target_pairs={{0,1},{1,8},{2,11},{3,2},{4,5},{5,12},{6,15},{7,6},{8,9},{9,0},{10... | collective-permute-start | bytes 294920 | tf_op jit(solution)/shard_map/ppermute | solution.py:314
  35.4 0.4 collective-permute-start.14
  35.8 0.4 last.3.refs_0_
  36.2 1.2 %collective-permute-start.12 = (f32[64,384]{1,0:T(8,128)S(1)}, f32[64,384]{1,0:T(8,128)S(1)}, u32[]{:S(2)}, u32[]{:S(2)}) collective-permute-start(f32[64,384]{1,0:T(8,128)S(1)} %get-tuple-element.60), channel_id=1, source_target_pairs={{0,8},{4,12},{8,0},{12,4},{1,9},{5,13},{9,1},{13,5},{2,10},{6,14},... | collective-permute-start | bytes 294920 | tf_op jit(solution)/shard_map/ppermute | solution.py:273
  37.5 0.5 %finish.3.refs_3_ = f32[64,1536]{1,0:T(8,128)S(1)} custom-call(f32[16,384]{1,0:T(8,128)S(1)} %get-tuple-element.62.refs_0_, f32[64,384]{1,0:T(8,128)S(1)} %get-tuple-element.49.refs_4_.refs_1_, f32[64,384]{1,0:T(8,128)S(1)} %collective-permute-done.7.refs_5_.refs_2_, f32[32,384]{1,0:T(8,128)S(1)} %pad_maximum_fusion.refs_3_, ...), custom_call_target="tpu_custom_call" | custom-call | flops 393216 | bytes 1056768 | tf_op jit(solution)/shard_map/finish/pallas_call | solution.py:236
  37.9 2.0 %collective-permute-done.13.refs_1_ = f32[64,384]{1,0:T(8,128)S(1)} collective-permute-done((f32[64,384]{1,0:T(8,128)S(1)}, f32[64,384]{1,0:T(8,128)S(1)}, u32[]{:S(2)}, u32[]{:S(2)}) %collective-permute-start.13) | collective-permute-done | bytes 98336 | tf_op jit(solution)/shard_map/ppermute | solution.py:314
  39.9 0.8 %collective-permute-done.14.refs_2_ = f32[64,384]{1,0:T(8,128)S(1)} collective-permute-done((f32[64,384]{1,0:T(8,128)S(1)}, f32[64,384]{1,0:T(8,128)S(1)}, u32[]{:S(2)}, u32[]{:S(2)}) %collective-permute-start.14) | collective-permute-done | bytes 98336 | tf_op jit(solution)/shard_map/ppermute | solution.py:314
  40.7 0.2 finish.4.refs_3_
  40.9 0.6 %collective-permute-done.12.refs_2_ = f32[64,384]{1,0:T(8,128)S(1)} collective-permute-done((f32[64,384]{1,0:T(8,128)S(1)}, f32[64,384]{1,0:T(8,128)S(1)}, u32[]{:S(2)}, u32[]{:S(2)}) %collective-permute-start.12) | collective-permute-done | bytes 98336 | tf_op jit(solution)/shard_map/ppermute | solution.py:273
  41.6 0.9 %finish.5 = f32[64,1536]{1,0:T(8,128)} custom-call(f32[16,384]{1,0:T(8,128)S(1)} %add.10.refs_0_, f32[64,384]{1,0:T(8,128)S(1)} %get-tuple-element.59.refs_1_, f32[64,384]{1,0:T(8,128)S(1)} %collective-permute-done.12.refs_2_, f32[64,1536]{1,0:T(8,128)S(1)} %finish.4.refs_3_), custom_call_target="tpu_custom_call" | custom-call | flops 393216 | bytes 1007616 | tf_op jit(solution)/shard_map/finish/pallas_call | solution.py:236
  (28 shorter events, 0.6 us)
Async XLA Ops:
  0.0 14.0 %collective-permute-start.2 = (f32[384,384]{1,0:T(8,128)}, f32[384,384]{1,0:T(8,128)S(1)}, u32[]{:S(2)}, u32[]{:S(2)}) collective-permute-start(f32[384,384]{1,0:T(8,128)} %refs_3_.3), channel_id=1, source_target_pairs={{0,4},{1,2},{2,1},{3,7},{4,0},{5,6},{6,5},{7,3},{8,12},{9,10},{10,... | collective-permute-start | bytes 1769480 | tf_op jit(solution)/shard_map/ppermute | solution.py:270
  0.5 18.0 %collective-permute-start.4 = (f32[384,384]{1,0:T(8,128)}, f32[384,384]{1,0:T(8,128)S(1)}, u32[]{:S(2)}, u32[]{:S(2)}) collective-permute-start(f32[384,384]{1,0:T(8,128)} %refs_3_.3), channel_id=1, source_target_pairs={{0,1},{1,0},{2,3},{3,2},{4,5},{5,4},{6,7},{7,6},{8,9},{9,8},{10,11... | collective-permute-start | bytes 1769480 | tf_op jit(solution)/shard_map/ppermute | solution.py:270
  4.6 2.7 %copy-start.3 = (s32[32,16]{0,1:T(8,128)S(1)}, s32[32,16]{0,1:T(8,128)}, u32[]{:S(2)}) copy-start(s32[32,16]{0,1:T(8,128)} %param.7) | copy-start | bytes 6148
  4.6 8.8 %copy-start = (f32[384,384]{1,0:T(8,128)S(1)}, f32[384,384]{1,0:T(8,128)}, u32[]{:S(2)}) copy-start(f32[384,384]{1,0:T(8,128)} %refs_3_.3) | copy-start | bytes 1769476
  5.7 6.1 %collective-permute-start = (f32[64,768]{1,0:T(8,128)S(1)}, f32[64,768]{1,0:T(8,128)S(1)}, u32[]{:S(2)}, u32[]{:S(2)}) collective-permute-start(f32[64,768]{1,0:T(8,128)S(1)} %get-tuple-element.65), channel_id=1, source_target_pairs={{0,8},{4,12},{8,0},{12,4},{1,9},{5,13},{9,1},{13,5},{2,10},{6,14},... | collective-permute-start | bytes 589832 | tf_op jit(solution)/shard_map/ppermute | solution.py:273
  7.3 0.7 %copy-start.1 = (s32[16,16]{1,0:T(8,128)S(1)}, s32[16,16]{1,0:T(8,128)}, u32[]{:S(2)}) copy-start(s32[16,16]{1,0:T(8,128)} %refs_2_.1) | copy-start | bytes 3076
  7.4 0.7 %copy-start.2 = (s32[16]{0:T(128)S(1)}, s32[16]{0:T(128)}, u32[]{:S(2)}) copy-start(s32[16]{0:T(128)} %refs_3_.2) | copy-start | bytes 196
  11.9 1.5 %collective-permute-start.1 = (f32[128,384]{1,0:T(8,128)S(1)}, f32[128,384]{1,0:T(8,128)S(1)}, u32[]{:S(2)}, u32[]{:S(2)}) collective-permute-start(f32[128,384]{1,0:T(8,128)S(1)} %get-tuple-element.40), channel_id=1, source_target_pairs={{0,4},{4,0},{8,12},{12,8},{1,5},{5,1},{9,13},{13,9},{2,6},{6,2},{1... | collective-permute-start | bytes 589832 | tf_op jit(solution)/shard_map/ppermute | solution.py:273
  14.1 16.8 %collective-permute-start.3 = (f32[384,384]{1,0:T(8,128)S(1)}, f32[384,384]{1,0:T(8,128)S(1)}, u32[]{:S(2)}, u32[]{:S(2)}) collective-permute-start(f32[384,384]{1,0:T(8,128)S(1)} %pick.1), channel_id=1, source_target_pairs={{0,1},{1,0},{2,3},{3,2},{4,5},{5,4},{6,7},{7,6},{8,9},{9,8},{10,11... | collective-permute-start | bytes 1769480 | tf_op jit(solution)/shard_map/ppermute | solution.py:270
  18.4 12.5 %collective-permute-start.5 = (f32[384,384]{1,0:T(8,128)S(1)}, f32[384,384]{1,0:T(8,128)S(1)}, u32[]{:S(2)}, u32[]{:S(2)}) collective-permute-start(f32[384,384]{1,0:T(8,128)S(1)} %collective-permute-done.4.refs_2_), channel_id=1, source_target_pairs={{0,4},{1,2},{2,1},{3,7},{4,0},{5,6},{6,5},{7,3},{8,12},{9,10},{10,... | collective-permute-start | bytes 1769480 | tf_op jit(solution)/shard_map/ppermute | solution.py:270
  19.4 3.8 %collective-permute-start.8 = (f32[128,768]{1,0:T(8,128)S(1)}, f32[128,768]{1,0:T(8,128)S(1)}, u32[]{:S(2)}, u32[]{:S(2)}) collective-permute-start(f32[128,768]{1,0:T(8,128)S(1)} %get-tuple-element.54), channel_id=1, source_target_pairs={{0,4},{4,0},{8,12},{12,8},{1,5},{5,1},{9,13},{13,9},{2,6},{6,2},{1... | collective-permute-start | bytes 1179656 | tf_op jit(solution)/shard_map/ppermute | solution.py:273
  19.9 1.6 %collective-permute-start.6 = (f32[128,384]{1,0:T(8,128)S(1)}, f32[128,384]{1,0:T(8,128)S(1)}, u32[]{:S(2)}, u32[]{:S(2)}) collective-permute-start(f32[128,384]{1,0:T(8,128)S(1)} %get-tuple-element.48), channel_id=1, source_target_pairs={{0,4},{4,0},{8,12},{12,8},{1,5},{5,1},{9,13},{13,9},{2,6},{6,2},{1... | collective-permute-start | bytes 589832 | tf_op jit(solution)/shard_map/ppermute | solution.py:273
  21.6 9.3 %collective-permute-start.7 = (f32[64,384]{1,0:T(8,128)S(1)}, f32[64,384]{1,0:T(8,128)S(1)}, u32[]{:S(2)}, u32[]{:S(2)}) collective-permute-start(f32[64,384]{1,0:T(8,128)S(1)} %get-tuple-element.50), channel_id=1, source_target_pairs={{0,8},{4,12},{8,0},{12,4},{1,9},{5,13},{9,1},{13,5},{2,10},{6,14},... | collective-permute-start | bytes 294920 | tf_op jit(solution)/shard_map/ppermute | solution.py:273
  23.2 7.7 %collective-permute-start.9 = (f32[64,768]{1,0:T(8,128)S(1)}, f32[64,768]{1,0:T(8,128)S(1)}, u32[]{:S(2)}, u32[]{:S(2)}) collective-permute-start(f32[64,768]{1,0:T(8,128)S(1)} %get-tuple-element.56), channel_id=1, source_target_pairs={{0,8},{4,12},{8,0},{12,4},{1,9},{5,13},{9,1},{13,5},{2,10},{6,14},... | collective-permute-start | bytes 589832 | tf_op jit(solution)/shard_map/ppermute | solution.py:273
  31.3 1.5 %collective-permute-start.10 = (f32[128,384]{1,0:T(8,128)S(1)}, f32[128,384]{1,0:T(8,128)S(1)}, u32[]{:S(2)}, u32[]{:S(2)}) collective-permute-start(f32[128,384]{1,0:T(8,128)S(1)} %corner.2.refs_3_), channel_id=1, source_target_pairs={{0,4},{4,0},{8,12},{12,8},{1,5},{5,1},{9,13},{13,9},{2,6},{6,2},{1... | collective-permute-start | bytes 589832 | tf_op jit(solution)/shard_map/ppermute | solution.py:273
  32.1 4.1 %collective-permute-start.11 = (f32[128,384]{1,0:T(8,128)S(1)}, f32[128,384]{1,0:T(8,128)S(1)}, u32[]{:S(2)}, u32[]{:S(2)}) collective-permute-start(f32[128,384]{1,0:T(8,128)S(1)} %last.2.refs_6_), channel_id=1, source_target_pairs={{0,4},{4,0},{8,12},{12,8},{1,5},{5,1},{9,13},{13,9},{2,6},{6,2},{1... | collective-permute-start | bytes 589832 | tf_op jit(solution)/shard_map/ppermute | solution.py:273
  32.8 7.1 %collective-permute-start.13 = (f32[64,384]{1,0:T(8,128)S(1)}, f32[64,384]{1,0:T(8,128)S(1)}, u32[]{:S(2)}, u32[]{:S(2)}) collective-permute-start(f32[64,384]{1,0:T(8,128)S(1)} %get-tuple-element.58.refs_8_.refs_3_), channel_id=1, source_target_pairs={{0,1},{1,8},{2,11},{3,2},{4,5},{5,12},{6,15},{7,6},{8,9},{9,0},{10... | collective-permute-start | bytes 294920 | tf_op jit(solution)/shard_map/ppermute | solution.py:314
  35.4 5.3 %collective-permute-start.14 = (f32[64,384]{1,0:T(8,128)S(1)}, f32[64,384]{1,0:T(8,128)S(1)}, u32[]{:S(2)}, u32[]{:S(2)}) collective-permute-start(f32[64,384]{1,0:T(8,128)S(1)} %get-tuple-element.57.refs_7_.refs_2_), channel_id=1, source_target_pairs={{0,1},{1,0},{2,3},{3,2},{4,5},{5,4},{6,7},{7,6},{8,9},{9,8},{10,11... | collective-permute-start | bytes 294920 | tf_op jit(solution)/shard_map/ppermute | solution.py:314
  36.2 5.3 %collective-permute-start.12 = (f32[64,384]{1,0:T(8,128)S(1)}, f32[64,384]{1,0:T(8,128)S(1)}, u32[]{:S(2)}, u32[]{:S(2)}) collective-permute-start(f32[64,384]{1,0:T(8,128)S(1)} %get-tuple-element.60), channel_id=1, source_target_pairs={{0,8},{4,12},{8,0},{12,4},{1,9},{5,13},{9,1},{13,5},{2,10},{6,14},... | collective-permute-start | bytes 294920 | tf_op jit(solution)/shard_map/ppermute | solution.py:273

commit v22 on v19

--- a/solution.py
+++ b/solution.py
@@ -330,7 +330,7 @@
     def finish(slots, *so_far, final=False):
         args, counts, place_ = [], [], {}
         if final:
-            buffers = [pltpu.VMEM((rows, pairs), jnp.float32), pltpu.SemaphoreType.DMA((2,))]
+            buffers = [pltpu.VMEM((rows, pairs), jnp.float32), pltpu.SemaphoreType.DMA((8,))]
             place_ = dict(scratch=buffers, out_space=pl.ANY)
         for groups, shares in slots:
             args.append(jnp.concatenate([sum(homes[name] for name in names) for names in groups]))

time: 42.7 us -> 42.7 us (level)
  no operation moved by 1% of the time
where the time goes in v22:
time: 42.7 us; the launch traced here: 42.5 us
  starting transfers between devices  18.3 us (43%)
  waiting for transfers between devices  15.7 us (37%)
  Pallas kernels  6.49 us (15%)
  local copies, waits for them, and re-layouts  1.77 us (4%)
    ppermute x4, starting transfers between devices, swap_line(): return lax.ppermute(x, ('row', 'col'), pairs_)  8.97 us
    ppermute x4, waiting for transfers between devices, swap_line(): return lax.ppermute(x, ('row', 'col'), pairs_)  7.1 us
    pallas_call x16, Pallas kernels, call(): pl.pallas_call(body, out_shape=outs, in_specs=[SMEM] * n_smem + [VMEM] *...  6.49 us
    ppermute x9, starting transfers between devices, swap(): return lax.ppermute(x, 'row', [(i, i ^ d) for i in range(n_row)])  6.32 us
    ppermute x9, waiting for transfers between devices, swap(): return lax.ppermute(x, 'row', [(i, i ^ d) for i in range(n_row)])  5.48 us
    ppermute x2, waiting for transfers between devices, next_door(): lax.ppermute(x, ('row', 'col'), [(i * n_col + j, (i ^ (d if 0 < j < n_col...  3.13 us
    ppermute x2, starting transfers between devices, next_door(): lax.ppermute(x, ('row', 'col'), [(i * n_col + j, (i ^ (d if 0 < j < n_col...  3 us
    dynamic_slice x1, local copies, waits for them, and re-layouts, chip_columns(): return lax.dynamic_slice_in_dim(amplitudes, start, 2 * depth, 1)  1.11 us
  transfers between devices with their start and end apart: 15, of which 7 were waited for; matrix products, arithmetic and copies ran while one was open for 3% of the time, Pallas kernels for 12%

profile of v22, /device:TPU:0, one launch (start us, length us, event | category | flops | bytes accessed | tf_op | source)
XLA Modules:
  0.0 42.5 jit_solution(13827011592534183286)
XLA Ops:
  0.0 0.5 %collective-permute-start.2 = (f32[384,384]{1,0:T(8,128)}, f32[384,384]{1,0:T(8,128)S(1)}, u32[]{:S(2)}, u32[]{:S(2)}) collective-permute-start(f32[384,384]{1,0:T(8,128)} %refs_3_.3), channel_id=1, source_target_pairs={{0,4},{1,2},{2,1},{3,7},{4,0},{5,6},{6,5},{7,3},{8,12},{9,10},{10,... | collective-permute-start | bytes 1769480 | tf_op jit(solution)/shard_map/ppermute | solution.py:263
  0.5 4.1 %collective-permute-start.4 = (f32[384,384]{1,0:T(8,128)}, f32[384,384]{1,0:T(8,128)S(1)}, u32[]{:S(2)}, u32[]{:S(2)}) collective-permute-start(f32[384,384]{1,0:T(8,128)} %refs_3_.3), channel_id=1, source_target_pairs={{0,1},{1,0},{2,3},{3,2},{4,5},{5,4},{6,7},{7,6},{8,9},{9,8},{10,11... | collective-permute-start | bytes 1769480 | tf_op jit(solution)/shard_map/ppermute | solution.py:263
  4.6 1.1 %constant_dynamic-slice_fusion = (f32[64,768]{1,0:T(8,128)S(1)}, f32[64,768]{1,0:T(8,128)S(1)}) fusion(f32[64,1536]{1,0:T(8,128)} %param.5, s32[]{:T(128)S(6)} %select_n.14, s32[]{:T(128)S(6)} %select_n.13), kind=kLoop, calls=%fused_computation.2 | loop fusion | bytes 786440 | tf_op jit(solution)/shard_map/dynamic_slice | solution.py:291
  5.7 1.6 %collective-permute-start = (f32[64,768]{1,0:T(8,128)S(1)}, f32[64,768]{1,0:T(8,128)S(1)}, u32[]{:S(2)}, u32[]{:S(2)}) collective-permute-start(f32[64,768]{1,0:T(8,128)S(1)} %get-tuple-element.69), channel_id=1, source_target_pairs={{0,8},{4,12},{8,0},{12,4},{1,9},{5,13},{9,1},{13,5},{2,10},{6,14},... | collective-permute-start | bytes 589832 | tf_op jit(solution)/shard_map/ppermute | solution.py:266
  7.3 0.1 copy.6.refs_1_
  7.4 0.1 pad_add_fusion.refs_0_
  7.4 0.5 %copy-done.1 = s32[16,16]{1,0:T(8,128)S(1)} copy-done((s32[16,16]{1,0:T(8,128)S(1)}, s32[16,16]{1,0:T(8,128)}, u32[]{:S(2)}) %copy-start.1) | copy-done | bytes 1048
  8.0 2.0 %tables.1 = (f32[8,384]{1,0:T(8,128)S(1)}, f32[8,384]{1,0:T(8,128)S(1)}, f32[4,384]{1,0:T(4,128)S(1)}, f32[16,384]{1,0:T(8,128)S(1)}, f32[4,384]{1,0:T(4,128)S(1...) custom-call(s32[3]{0:T(128)S(1)} %pad_add_fusion.refs_0_, ...), custom_call_target="tpu_custom_call" | custom-call | bytes 212044 | tf_op jit(solution)/shard_map/tables/pallas_call | solution.py:229
  10.0 1.8 %collective-permute-done.refs_2_ = f32[64,768]{1,0:T(8,128)S(1)} collective-permute-done((f32[64,768]{1,0:T(8,128)S(1)}, f32[64,768]{1,0:T(8,128)S(1)}, u32[]{:S(2)}, u32[]{:S(2)}) %collective-permute-start) | collective-permute-done | bytes 196640 | tf_op jit(solution)/shard_map/ppermute | solution.py:266
  12.0 1.4 %collective-permute-done.1.refs_2_ = f32[128,384]{1,0:T(8,128)S(1)} collective-permute-done((f32[128,384]{1,0:T(8,128)S(1)}, f32[128,384]{1,0:T(8,128)S(1)}, u32[]{:S(2)}, u32[]{:S(2)}) %collective-permute-start.1) | collective-permute-done | bytes 196640 | tf_op jit(solution)/shard_map/ppermute | solution.py:266
  13.4 0.6 %own.1 = (bf16[256,384]{1,0:T(8,128)(2,1)S(1)}, bf16[256,384]{1,0:T(8,128)(2,1)S(1)}, f32[384,384]{1,0:T(8,128)S(1)}, f32[128,384]{1,0:T(8,128)S(1)}, f32[128,384]{1,0:T(8,128)S(1)}) custom-call(f32[8,384]{1,0:T(8,128)S(1)} %get-tuple-element.39.refs_0_, f32[128,384]{1,0:T(8,128)S(1)} %get-tuple-element.41.refs_1_, ...), custom_call_target="tpu_custom_call" | custom-call | flops 226492416 | bytes 2377728 | tf_op jit(solution)/shard_map/own/pallas_call | solution.py:229
  14.1 4.4 %collective-permute-start.3 = (f32[384,384]{1,0:T(8,128)S(1)}, f32[384,384]{1,0:T(8,128)S(1)}, u32[]{:S(2)}, u32[]{:S(2)}) collective-permute-start(f32[384,384]{1,0:T(8,128)S(1)} %pick.1), channel_id=1, source_target_pairs={{0,1},{1,0},{2,3},{3,2},{4,5},{5,4},{6,7},{7,6},{8,9},{9,8},{10,11... | collective-permute-start | bytes 1769480 | tf_op jit(solution)/shard_map/ppermute | solution.py:263
  18.4 0.9 %pair.1 = (f32[128,768]{1,0:T(8,128)S(1)}, f32[128,768]{1,0:T(8,128)S(1)}) custom-call(bf16[256,384]{1,0:T(8,128)(2,1)S(1)} %get-tuple-element.44.refs_0_, bf16[256,384]{1,0:T(8,128)(2,1)S(1)} %get-tuple-element.45.refs_1_, f32[384,384]{1,0:T(8,128)S(1)} %collective-permute-done.4.refs_2_, f32[4,384]{1,0:T(4,128)S(1)} %get-tuple-element.53.refs_3_, ...), custom_call_target="tpu_custom_call" | custom-call | flops 452984832 | bytes 2371584 | tf_op jit(solution)/shard_map/pair/pallas_call | solution.py:229
  19.4 0.6 %collective-permute-start.8 = (f32[128,768]{1,0:T(8,128)S(1)}, f32[128,768]{1,0:T(8,128)S(1)}, u32[]{:S(2)}, u32[]{:S(2)}) collective-permute-start(f32[128,768]{1,0:T(8,128)S(1)} %get-tuple-element.56), channel_id=1, source_target_pairs={{0,4},{4,0},{8,12},{12,8},{1,5},{5,1},{9,13},{13,9},{2,6},{6,2},{1... | collective-permute-start | bytes 1179656 | tf_op jit(solution)/shard_map/ppermute | solution.py:266
  19.9 0.1 collective-permute-start.6
  20.0 1.6 %collective-permute-done.6.refs_1_ = f32[128,384]{1,0:T(8,128)S(1)} collective-permute-done((f32[128,384]{1,0:T(8,128)S(1)}, f32[128,384]{1,0:T(8,128)S(1)}, u32[]{:S(2)}, u32[]{:S(2)}) %collective-permute-start.6) | collective-permute-done | bytes 196640 | tf_op jit(solution)/shard_map/ppermute | solution.py:266
  21.6 1.6 %collective-permute-start.7 = (f32[64,384]{1,0:T(8,128)S(1)}, f32[64,384]{1,0:T(8,128)S(1)}, u32[]{:S(2)}, u32[]{:S(2)}) collective-permute-start(f32[64,384]{1,0:T(8,128)S(1)} %get-tuple-element.52), channel_id=1, source_target_pairs={{0,8},{4,12},{8,0},{12,4},{1,9},{5,13},{9,1},{13,5},{2,10},{6,14},... | collective-permute-start | bytes 294920 | tf_op jit(solution)/shard_map/ppermute | solution.py:266
  23.2 0.6 %collective-permute-start.9 = (f32[64,768]{1,0:T(8,128)S(1)}, f32[64,768]{1,0:T(8,128)S(1)}, u32[]{:S(2)}, u32[]{:S(2)}) collective-permute-start(f32[64,768]{1,0:T(8,128)S(1)} %get-tuple-element.58), channel_id=1, source_target_pairs={{0,8},{4,12},{8,0},{12,4},{1,9},{5,13},{9,1},{13,5},{2,10},{6,14},... | collective-permute-start | bytes 589832 | tf_op jit(solution)/shard_map/ppermute | solution.py:266
  23.8 7.1 %collective-permute-done.3.refs_0_.refs_2_ = f32[384,384]{1,0:T(8,128)S(1)} collective-permute-done((f32[384,384]{1,0:T(8,128)S(1)}, f32[384,384]{1,0:T(8,128)S(1)}, u32[]{:S(2)}, u32[]{:S(2)}) %collective-permute-start.3) | collective-permute-done | bytes 589856 | tf_op jit(solution)/shard_map/ppermute | solution.py:263
  30.9 0.3 corner.2.refs_3_
  31.4 0.3 corner.3.refs_6_.refs_0_
  31.7 0.5 %last.1 = (f32[128,384]{1,0:T(8,128)S(1)}, f32[128,384]{1,0:T(8,128)S(1)}) custom-call(bf16[256,384]{1,0:T(8,128)(2,1)S(1)} %get-tuple-element.44.refs_0_, bf16[256,384]{1,0:T(8,128)(2,1)S(1)} %get-tuple-element.45.refs_1_, f32[384,384]{1,0:T(8,128)S(1)} %collective-permute-done.3.refs_0_.refs_2_, f32[4,384]{1,0:T(4,128)S(1)} %get-tuple-element.47.refs_3_, ...), custom_call_target="tpu_custom_call" | custom-call | flops 226492416 | bytes 1978368 | tf_op jit(solution)/shard_map/last/pallas_call | solution.py:229
  32.3 0.6 %collective-permute-start.10 = (f32[128,384]{1,0:T(8,128)S(1)}, f32[128,384]{1,0:T(8,128)S(1)}, u32[]{:S(2)}, u32[]{:S(2)}) collective-permute-start(f32[128,384]{1,0:T(8,128)S(1)} %get-tuple-element.60), channel_id=1, source_target_pairs={{0,4},{4,0},{8,12},{12,8},{1,5},{5,1},{9,13},{13,9},{2,6},{6,2},{1... | collective-permute-start | bytes 589832 | tf_op jit(solution)/shard_map/ppermute | solution.py:266
  32.9 2.6 %collective-permute-start.13 = (f32[64,384]{1,0:T(8,128)S(1)}, f32[64,384]{1,0:T(8,128)S(1)}, u32[]{:S(2)}, u32[]{:S(2)}) collective-permute-start(f32[64,384]{1,0:T(8,128)S(1)} %get-tuple-element.62.refs_3_), channel_id=1, source_target_pairs={{0,1},{1,8},{2,11},{3,2},{4,5},{5,12},{6,15},{7,6},{8,9},{9,0},{10... | collective-permute-start | bytes 294920 | tf_op jit(solution)/shard_map/ppermute | solution.py:307
  35.5 0.4 collective-permute-start.14
  35.9 1.2 %collective-permute-start.12 = (f32[64,384]{1,0:T(8,128)S(1)}, f32[64,384]{1,0:T(8,128)S(1)}, u32[]{:S(2)}, u32[]{:S(2)}) collective-permute-start(f32[64,384]{1,0:T(8,128)S(1)} %get-tuple-element.64), channel_id=1, source_target_pairs={{0,8},{4,12},{8,0},{12,4},{1,9},{5,13},{9,1},{13,5},{2,10},{6,14},... | collective-permute-start | bytes 294920 | tf_op jit(solution)/shard_map/ppermute | solution.py:266
  37.1 0.5 %finish.3.refs_3_ = f32[64,1536]{1,0:T(8,128)S(1)} custom-call(f32[16,384]{1,0:T(8,128)S(1)} %get-tuple-element.66.refs_0_, f32[64,384]{1,0:T(8,128)S(1)} %get-tuple-element.51.refs_4_.refs_1_, f32[64,384]{1,0:T(8,128)S(1)} %collective-permute-done.7.refs_5_.refs_2_, f32[32,384]{1,0:T(8,128)S(1)} %pad_maximum_fusion.refs_3_, ...), custom_call_target="tpu_custom_call" | custom-call | flops 393216 | bytes 1056768 | tf_op jit(solution)/shard_map/finish/pallas_call | solution.py:229
  37.6 2.4 %collective-permute-done.13.refs_1_ = f32[64,384]{1,0:T(8,128)S(1)} collective-permute-done((f32[64,384]{1,0:T(8,128)S(1)}, f32[64,384]{1,0:T(8,128)S(1)}, u32[]{:S(2)}, u32[]{:S(2)}) %collective-permute-start.13) | collective-permute-done | bytes 98336 | tf_op jit(solution)/shard_map/ppermute | solution.py:307
  40.0 0.8 %collective-permute-done.14.refs_2_ = f32[64,384]{1,0:T(8,128)S(1)} collective-permute-done((f32[64,384]{1,0:T(8,128)S(1)}, f32[64,384]{1,0:T(8,128)S(1)}, u32[]{:S(2)}, u32[]{:S(2)}) %collective-permute-start.14) | collective-permute-done | bytes 98336 | tf_op jit(solution)/shard_map/ppermute | solution.py:307
  40.7 0.2 finish.4.refs_3_
  40.9 0.6 %collective-permute-done.12.refs_2_ = f32[64,384]{1,0:T(8,128)S(1)} collective-permute-done((f32[64,384]{1,0:T(8,128)S(1)}, f32[64,384]{1,0:T(8,128)S(1)}, u32[]{:S(2)}, u32[]{:S(2)}) %collective-permute-start.12) | collective-permute-done | bytes 98336 | tf_op jit(solution)/shard_map/ppermute | solution.py:266
  41.6 0.9 %finish.5 = f32[64,1536]{1,0:T(8,128)} custom-call(f32[16,384]{1,0:T(8,128)S(1)} %add.10.refs_0_, f32[64,384]{1,0:T(8,128)S(1)} %get-tuple-element.63.refs_1_, f32[64,384]{1,0:T(8,128)S(1)} %collective-permute-done.12.refs_2_, f32[64,1536]{1,0:T(8,128)S(1)} %finish.4.refs_3_), custom_call_target="tpu_custom_call" | custom-call | flops 393216 | bytes 1007616 | tf_op jit(solution)/shard_map/finish/pallas_call | solution.py:229
  (27 shorter events, 0.5 us)
Async XLA Ops:
  0.0 14.0 %collective-permute-start.2 = (f32[384,384]{1,0:T(8,128)}, f32[384,384]{1,0:T(8,128)S(1)}, u32[]{:S(2)}, u32[]{:S(2)}) collective-permute-start(f32[384,384]{1,0:T(8,128)} %refs_3_.3), channel_id=1, source_target_pairs={{0,4},{1,2},{2,1},{3,7},{4,0},{5,6},{6,5},{7,3},{8,12},{9,10},{10,... | collective-permute-start | bytes 1769480 | tf_op jit(solution)/shard_map/ppermute | solution.py:263
  0.5 18.0 %collective-permute-start.4 = (f32[384,384]{1,0:T(8,128)}, f32[384,384]{1,0:T(8,128)S(1)}, u32[]{:S(2)}, u32[]{:S(2)}) collective-permute-start(f32[384,384]{1,0:T(8,128)} %refs_3_.3), channel_id=1, source_target_pairs={{0,1},{1,0},{2,3},{3,2},{4,5},{5,4},{6,7},{7,6},{8,9},{9,8},{10,11... | collective-permute-start | bytes 1769480 | tf_op jit(solution)/shard_map/ppermute | solution.py:263
  4.6 2.7 %copy-start.3 = (s32[32,16]{0,1:T(8,128)S(1)}, s32[32,16]{0,1:T(8,128)}, u32[]{:S(2)}) copy-start(s32[32,16]{0,1:T(8,128)} %param.7) | copy-start | bytes 6148
  4.6 8.8 %copy-start = (f32[384,384]{1,0:T(8,128)S(1)}, f32[384,384]{1,0:T(8,128)}, u32[]{:S(2)}) copy-start(f32[384,384]{1,0:T(8,128)} %refs_3_.3) | copy-start | bytes 1769476
  5.7 6.1 %collective-permute-start = (f32[64,768]{1,0:T(8,128)S(1)}, f32[64,768]{1,0:T(8,128)S(1)}, u32[]{:S(2)}, u32[]{:S(2)}) collective-permute-start(f32[64,768]{1,0:T(8,128)S(1)} %get-tuple-element.69), channel_id=1, source_target_pairs={{0,8},{4,12},{8,0},{12,4},{1,9},{5,13},{9,1},{13,5},{2,10},{6,14},... | collective-permute-start | bytes 589832 | tf_op jit(solution)/shard_map/ppermute | solution.py:266
  7.3 0.7 %copy-start.1 = (s32[16,16]{1,0:T(8,128)S(1)}, s32[16,16]{1,0:T(8,128)}, u32[]{:S(2)}) copy-start(s32[16,16]{1,0:T(8,128)} %refs_2_.1) | copy-start | bytes 3076
  7.4 0.7 %copy-start.2 = (s32[16]{0:T(128)S(1)}, s32[16]{0:T(128)}, u32[]{:S(2)}) copy-start(s32[16]{0:T(128)} %refs_3_.2) | copy-start | bytes 196
  11.9 1.5 %collective-permute-start.1 = (f32[128,384]{1,0:T(8,128)S(1)}, f32[128,384]{1,0:T(8,128)S(1)}, u32[]{:S(2)}, u32[]{:S(2)}) collective-permute-start(f32[128,384]{1,0:T(8,128)S(1)} %get-tuple-element.42), channel_id=1, source_target_pairs={{0,4},{4,0},{8,12},{12,8},{1,5},{5,1},{9,13},{13,9},{2,6},{6,2},{1... | collective-permute-start | bytes 589832 | tf_op jit(solution)/shard_map/ppermute | solution.py:266
  14.1 16.8 %collective-permute-start.3 = (f32[384,384]{1,0:T(8,128)S(1)}, f32[384,384]{1,0:T(8,128)S(1)}, u32[]{:S(2)}, u32[]{:S(2)}) collective-permute-start(f32[384,384]{1,0:T(8,128)S(1)} %pick.1), channel_id=1, source_target_pairs={{0,1},{1,0},{2,3},{3,2},{4,5},{5,4},{6,7},{7,6},{8,9},{9,8},{10,11... | collective-permute-start | bytes 1769480 | tf_op jit(solution)/shard_map/ppermute | solution.py:263
  18.4 12.5 %collective-permute-start.5 = (f32[384,384]{1,0:T(8,128)S(1)}, f32[384,384]{1,0:T(8,128)S(1)}, u32[]{:S(2)}, u32[]{:S(2)}) collective-permute-start(f32[384,384]{1,0:T(8,128)S(1)} %collective-permute-done.4.refs_2_), channel_id=1, source_target_pairs={{0,4},{1,2},{2,1},{3,7},{4,0},{5,6},{6,5},{7,3},{8,12},{9,10},{10,... | collective-permute-start | bytes 1769480 | tf_op jit(solution)/shard_map/ppermute | solution.py:263
  19.4 3.8 %collective-permute-start.8 = (f32[128,768]{1,0:T(8,128)S(1)}, f32[128,768]{1,0:T(8,128)S(1)}, u32[]{:S(2)}, u32[]{:S(2)}) collective-permute-start(f32[128,768]{1,0:T(8,128)S(1)} %get-tuple-element.56), channel_id=1, source_target_pairs={{0,4},{4,0},{8,12},{12,8},{1,5},{5,1},{9,13},{13,9},{2,6},{6,2},{1... | collective-permute-start | bytes 1179656 | tf_op jit(solution)/shard_map/ppermute | solution.py:266
  19.9 1.6 %collective-permute-start.6 = (f32[128,384]{1,0:T(8,128)S(1)}, f32[128,384]{1,0:T(8,128)S(1)}, u32[]{:S(2)}, u32[]{:S(2)}) collective-permute-start(f32[128,384]{1,0:T(8,128)S(1)} %get-tuple-element.50), channel_id=1, source_target_pairs={{0,4},{4,0},{8,12},{12,8},{1,5},{5,1},{9,13},{13,9},{2,6},{6,2},{1... | collective-permute-start | bytes 589832 | tf_op jit(solution)/shard_map/ppermute | solution.py:266
  21.6 9.3 %collective-permute-start.7 = (f32[64,384]{1,0:T(8,128)S(1)}, f32[64,384]{1,0:T(8,128)S(1)}, u32[]{:S(2)}, u32[]{:S(2)}) collective-permute-start(f32[64,384]{1,0:T(8,128)S(1)} %get-tuple-element.52), channel_id=1, source_target_pairs={{0,8},{4,12},{8,0},{12,4},{1,9},{5,13},{9,1},{13,5},{2,10},{6,14},... | collective-permute-start | bytes 294920 | tf_op jit(solution)/shard_map/ppermute | solution.py:266
  23.2 7.7 %collective-permute-start.9 = (f32[64,768]{1,0:T(8,128)S(1)}, f32[64,768]{1,0:T(8,128)S(1)}, u32[]{:S(2)}, u32[]{:S(2)}) collective-permute-start(f32[64,768]{1,0:T(8,128)S(1)} %get-tuple-element.58), channel_id=1, source_target_pairs={{0,8},{4,12},{8,0},{12,4},{1,9},{5,13},{9,1},{13,5},{2,10},{6,14},... | collective-permute-start | bytes 589832 | tf_op jit(solution)/shard_map/ppermute | solution.py:266
  31.3 1.5 %collective-permute-start.11 = (f32[128,384]{1,0:T(8,128)S(1)}, f32[128,384]{1,0:T(8,128)S(1)}, u32[]{:S(2)}, u32[]{:S(2)}) collective-permute-start(f32[128,384]{1,0:T(8,128)S(1)} %corner.2.refs_3_), channel_id=1, source_target_pairs={{0,4},{4,0},{8,12},{12,8},{1,5},{5,1},{9,13},{13,9},{2,6},{6,2},{1... | collective-permute-start | bytes 589832 | tf_op jit(solution)/shard_map/ppermute | solution.py:266
  32.3 3.6 %collective-permute-start.10 = (f32[128,384]{1,0:T(8,128)S(1)}, f32[128,384]{1,0:T(8,128)S(1)}, u32[]{:S(2)}, u32[]{:S(2)}) collective-permute-start(f32[128,384]{1,0:T(8,128)S(1)} %get-tuple-element.60), channel_id=1, source_target_pairs={{0,4},{4,0},{8,12},{12,8},{1,5},{5,1},{9,13},{13,9},{2,6},{6,2},{1... | collective-permute-start | bytes 589832 | tf_op jit(solution)/shard_map/ppermute | solution.py:266
  32.9 7.1 %collective-permute-start.13 = (f32[64,384]{1,0:T(8,128)S(1)}, f32[64,384]{1,0:T(8,128)S(1)}, u32[]{:S(2)}, u32[]{:S(2)}) collective-permute-start(f32[64,384]{1,0:T(8,128)S(1)} %get-tuple-element.62.refs_3_), channel_id=1, source_target_pairs={{0,1},{1,8},{2,11},{3,2},{4,5},{5,12},{6,15},{7,6},{8,9},{9,0},{10... | collective-permute-start | bytes 294920 | tf_op jit(solution)/shard_map/ppermute | solution.py:307
  35.5 5.3 %collective-permute-start.14 = (f32[64,384]{1,0:T(8,128)S(1)}, f32[64,384]{1,0:T(8,128)S(1)}, u32[]{:S(2)}, u32[]{:S(2)}) collective-permute-start(f32[64,384]{1,0:T(8,128)S(1)} %get-tuple-element.61.refs_2_), channel_id=1, source_target_pairs={{0,1},{1,0},{2,3},{3,2},{4,5},{5,4},{6,7},{7,6},{8,9},{9,8},{10,11... | collective-permute-start | bytes 294920 | tf_op jit(solution)/shard_map/ppermute | solution.py:307
  35.9 5.7 %collective-permute-start.12 = (f32[64,384]{1,0:T(8,128)S(1)}, f32[64,384]{1,0:T(8,128)S(1)}, u32[]{:S(2)}, u32[]{:S(2)}) collective-permute-start(f32[64,384]{1,0:T(8,128)S(1)} %get-tuple-element.64), channel_id=1, source_target_pairs={{0,8},{4,12},{8,0},{12,4},{1,9},{5,13},{9,1},{13,5},{2,10},{6,14},... | collective-permute-start | bytes 294920 | tf_op jit(solution)/shard_map/ppermute | solution.py:266

commit v23 on v21

--- a/solution.py
+++ b/solution.py
@@ -405,7 +405,7 @@
         for start in (total // 2, 0):
             kernel = functools.partial(last_kernel, start, (len(even) + 1, len(odd) + 1))
             parts += call(kernel, "last", sums[:1], 0, *args, flops=flops // 2, after=after)
-            after = (parts[0], *folded)
+            after = (parts[0],)
         parts = parts[::-1]
         if slots:
             out = finish(slots, out)

time: 42.7 us -> 42.8 us (level)
  transfers between devices with their start and end apart: 15 -> 15, of which waited for: 8 -> 7; matrix products, arithmetic and copies ran while one was open for 3% -> 3% of each run, Pallas kernels for 13% -> 13%
where the time goes in v23:
time: 42.8 us; the launch traced here: 42.6 us
  starting transfers between devices  18.3 us (43%)
  waiting for transfers between devices  15.6 us (36%)
  Pallas kernels  6.66 us (16%)
  local copies, waits for them, and re-layouts  1.77 us (4%)
    ppermute x4, starting transfers between devices, swap_line(): return lax.ppermute(x, ('row', 'col'), pairs_)  8.97 us
    ppermute x4, waiting for transfers between devices, swap_line(): return lax.ppermute(x, ('row', 'col'), pairs_)  7.1 us
    pallas_call x17, Pallas kernels, call(): pl.pallas_call(body, out_shape=outs, in_specs=[SMEM] * n_smem + [VMEM] *...  6.66 us
    ppermute x9, starting transfers between devices, swap(): return lax.ppermute(x, 'row', [(i, i ^ d) for i in range(n_row)])  6.31 us
    ppermute x9, waiting for transfers between devices, swap(): return lax.ppermute(x, 'row', [(i, i ^ d) for i in range(n_row)])  5.48 us
    ppermute x2, waiting for transfers between devices, next_door(): lax.ppermute(x, ('row', 'col'), [(i * n_col + j, (i ^ (d if 0 < j < n_col...  3.07 us
    ppermute x2, starting transfers between devices, next_door(): lax.ppermute(x, ('row', 'col'), [(i * n_col + j, (i ^ (d if 0 < j < n_col...  3.01 us
    dynamic_slice x1, local copies, waits for them, and re-layouts, chip_columns(): return lax.dynamic_slice_in_dim(amplitudes, start, 2 * depth, 1)  1.11 us
  transfers between devices with their start and end apart: 15, of which 7 were waited for; matrix products, arithmetic and copies ran while one was open for 3% of the time, Pallas kernels for 13%

profile of v23, /device:TPU:0, one launch (start us, length us, event | category | flops | bytes accessed | tf_op | source)
XLA Modules:
  0.0 42.6 jit_solution(14244160601116763386)
XLA Ops:
  0.0 0.5 %collective-permute-start.2 = (f32[384,384]{1,0:T(8,128)}, f32[384,384]{1,0:T(8,128)S(1)}, u32[]{:S(2)}, u32[]{:S(2)}) collective-permute-start(f32[384,384]{1,0:T(8,128)} %refs_3_.3), channel_id=1, source_target_pairs={{0,4},{1,2},{2,1},{3,7},{4,0},{5,6},{6,5},{7,3},{8,12},{9,10},{10,... | collective-permute-start | bytes 1769480 | tf_op jit(solution)/shard_map/ppermute | solution.py:270
  0.5 4.1 %collective-permute-start.4 = (f32[384,384]{1,0:T(8,128)}, f32[384,384]{1,0:T(8,128)S(1)}, u32[]{:S(2)}, u32[]{:S(2)}) collective-permute-start(f32[384,384]{1,0:T(8,128)} %refs_3_.3), channel_id=1, source_target_pairs={{0,1},{1,0},{2,3},{3,2},{4,5},{5,4},{6,7},{7,6},{8,9},{9,8},{10,11... | collective-permute-start | bytes 1769480 | tf_op jit(solution)/shard_map/ppermute | solution.py:270
  4.6 1.1 %constant_dynamic-slice_fusion = (f32[64,768]{1,0:T(8,128)S(1)}, f32[64,768]{1,0:T(8,128)S(1)}) fusion(f32[64,1536]{1,0:T(8,128)} %param.5, s32[]{:T(128)S(6)} %select_n.14, s32[]{:T(128)S(6)} %select_n.13), kind=kLoop, calls=%fused_computation.2 | loop fusion | bytes 786440 | tf_op jit(solution)/shard_map/dynamic_slice | solution.py:298
  5.7 1.6 %collective-permute-start = (f32[64,768]{1,0:T(8,128)S(1)}, f32[64,768]{1,0:T(8,128)S(1)}, u32[]{:S(2)}, u32[]{:S(2)}) collective-permute-start(f32[64,768]{1,0:T(8,128)S(1)} %get-tuple-element.65), channel_id=1, source_target_pairs={{0,8},{4,12},{8,0},{12,4},{1,9},{5,13},{9,1},{13,5},{2,10},{6,14},... | collective-permute-start | bytes 589832 | tf_op jit(solution)/shard_map/ppermute | solution.py:273
  7.4 0.1 pad_add_fusion.refs_0_
  7.4 0.5 %copy-done.1 = s32[16,16]{1,0:T(8,128)S(1)} copy-done((s32[16,16]{1,0:T(8,128)S(1)}, s32[16,16]{1,0:T(8,128)}, u32[]{:S(2)}) %copy-start.1) | copy-done | bytes 1048
  8.0 2.0 %tables.1 = (f32[8,384]{1,0:T(8,128)S(1)}, f32[8,384]{1,0:T(8,128)S(1)}, f32[4,384]{1,0:T(4,128)S(1)}, f32[16,384]{1,0:T(8,128)S(1)}, f32[4,384]{1,0:T(4,128)S(1...) custom-call(s32[3]{0:T(128)S(1)} %pad_add_fusion.refs_0_, ...), custom_call_target="tpu_custom_call" | custom-call | bytes 212044 | tf_op jit(solution)/shard_map/tables/pallas_call | solution.py:236
  10.0 1.8 %collective-permute-done.refs_2_ = f32[64,768]{1,0:T(8,128)S(1)} collective-permute-done((f32[64,768]{1,0:T(8,128)S(1)}, f32[64,768]{1,0:T(8,128)S(1)}, u32[]{:S(2)}, u32[]{:S(2)}) %collective-permute-start) | collective-permute-done | bytes 196640 | tf_op jit(solution)/shard_map/ppermute | solution.py:273
  12.0 1.4 %collective-permute-done.1.refs_2_ = f32[128,384]{1,0:T(8,128)S(1)} collective-permute-done((f32[128,384]{1,0:T(8,128)S(1)}, f32[128,384]{1,0:T(8,128)S(1)}, u32[]{:S(2)}, u32[]{:S(2)}) %collective-permute-start.1) | collective-permute-done | bytes 196640 | tf_op jit(solution)/shard_map/ppermute | solution.py:273
  13.4 0.6 %own.1 = (bf16[256,384]{1,0:T(8,128)(2,1)S(1)}, bf16[256,384]{1,0:T(8,128)(2,1)S(1)}, f32[384,384]{1,0:T(8,128)S(1)}, f32[128,384]{1,0:T(8,128)S(1)}, f32[128,384]{1,0:T(8,128)S(1)}) custom-call(f32[8,384]{1,0:T(8,128)S(1)} %get-tuple-element.37.refs_0_, f32[128,384]{1,0:T(8,128)S(1)} %get-tuple-element.39.refs_1_, ...), custom_call_target="tpu_custom_call" | custom-call | flops 226492416 | bytes 2377728 | tf_op jit(solution)/shard_map/own/pallas_call | solution.py:236
  14.1 4.4 %collective-permute-start.3 = (f32[384,384]{1,0:T(8,128)S(1)}, f32[384,384]{1,0:T(8,128)S(1)}, u32[]{:S(2)}, u32[]{:S(2)}) collective-permute-start(f32[384,384]{1,0:T(8,128)S(1)} %pick.1), channel_id=1, source_target_pairs={{0,1},{1,0},{2,3},{3,2},{4,5},{5,4},{6,7},{7,6},{8,9},{9,8},{10,11... | collective-permute-start | bytes 1769480 | tf_op jit(solution)/shard_map/ppermute | solution.py:270
  18.4 0.9 %pair.1 = (f32[128,768]{1,0:T(8,128)S(1)}, f32[128,768]{1,0:T(8,128)S(1)}) custom-call(bf16[256,384]{1,0:T(8,128)(2,1)S(1)} %get-tuple-element.42.refs_0_, bf16[256,384]{1,0:T(8,128)(2,1)S(1)} %get-tuple-element.43.refs_1_, f32[384,384]{1,0:T(8,128)S(1)} %collective-permute-done.4.refs_2_, f32[4,384]{1,0:T(4,128)S(1)} %get-tuple-element.51.refs_3_, ...), custom_call_target="tpu_custom_call" | custom-call | flops 452984832 | bytes 2371584 | tf_op jit(solution)/shard_map/pair/pallas_call | solution.py:236
  19.4 0.6 %collective-permute-start.8 = (f32[128,768]{1,0:T(8,128)S(1)}, f32[128,768]{1,0:T(8,128)S(1)}, u32[]{:S(2)}, u32[]{:S(2)}) collective-permute-start(f32[128,768]{1,0:T(8,128)S(1)} %get-tuple-element.54), channel_id=1, source_target_pairs={{0,4},{4,0},{8,12},{12,8},{1,5},{5,1},{9,13},{13,9},{2,6},{6,2},{1... | collective-permute-start | bytes 1179656 | tf_op jit(solution)/shard_map/ppermute | solution.py:273
  19.9 0.1 collective-permute-start.6
  20.0 1.6 %collective-permute-done.6.refs_1_ = f32[128,384]{1,0:T(8,128)S(1)} collective-permute-done((f32[128,384]{1,0:T(8,128)S(1)}, f32[128,384]{1,0:T(8,128)S(1)}, u32[]{:S(2)}, u32[]{:S(2)}) %collective-permute-start.6) | collective-permute-done | bytes 196640 | tf_op jit(solution)/shard_map/ppermute | solution.py:273
  21.6 1.6 %collective-permute-start.7 = (f32[64,384]{1,0:T(8,128)S(1)}, f32[64,384]{1,0:T(8,128)S(1)}, u32[]{:S(2)}, u32[]{:S(2)}) collective-permute-start(f32[64,384]{1,0:T(8,128)S(1)} %get-tuple-element.50), channel_id=1, source_target_pairs={{0,8},{4,12},{8,0},{12,4},{1,9},{5,13},{9,1},{13,5},{2,10},{6,14},... | collective-permute-start | bytes 294920 | tf_op jit(solution)/shard_map/ppermute | solution.py:273
  23.2 0.6 %collective-permute-start.9 = (f32[64,768]{1,0:T(8,128)S(1)}, f32[64,768]{1,0:T(8,128)S(1)}, u32[]{:S(2)}, u32[]{:S(2)}) collective-permute-start(f32[64,768]{1,0:T(8,128)S(1)} %get-tuple-element.56), channel_id=1, source_target_pairs={{0,8},{4,12},{8,0},{12,4},{1,9},{5,13},{9,1},{13,5},{2,10},{6,14},... | collective-permute-start | bytes 589832 | tf_op jit(solution)/shard_map/ppermute | solution.py:273
  23.8 7.1 %collective-permute-done.3.refs_0_.refs_2_ = f32[384,384]{1,0:T(8,128)S(1)} collective-permute-done((f32[384,384]{1,0:T(8,128)S(1)}, f32[384,384]{1,0:T(8,128)S(1)}, u32[]{:S(2)}, u32[]{:S(2)}) %collective-permute-start.3) | collective-permute-done | bytes 589856 | tf_op jit(solution)/shard_map/ppermute | solution.py:270
  30.9 0.3 corner.2.refs_3_
  31.4 0.3 corner.3.refs_6_.refs_0_
  31.7 0.4 last.2.refs_6_
  32.1 0.6 %collective-permute-start.10 = (f32[128,384]{1,0:T(8,128)S(1)}, f32[128,384]{1,0:T(8,128)S(1)}, u32[]{:S(2)}, u32[]{:S(2)}) collective-permute-start(f32[128,384]{1,0:T(8,128)S(1)} %last.2.refs_6_), channel_id=1, source_target_pairs={{0,4},{4,0},{8,12},{12,8},{1,5},{5,1},{9,13},{13,9},{2,6},{6,2},{1... | collective-permute-start | bytes 589832 | tf_op jit(solution)/shard_map/ppermute | solution.py:273
  32.6 0.4 last.3.refs_0_
  33.1 2.6 %collective-permute-start.13 = (f32[64,384]{1,0:T(8,128)S(1)}, f32[64,384]{1,0:T(8,128)S(1)}, u32[]{:S(2)}, u32[]{:S(2)}) collective-permute-start(f32[64,384]{1,0:T(8,128)S(1)} %get-tuple-element.58.refs_3_), channel_id=1, source_target_pairs={{0,1},{1,8},{2,11},{3,2},{4,5},{5,12},{6,15},{7,6},{8,9},{9,0},{10... | collective-permute-start | bytes 294920 | tf_op jit(solution)/shard_map/ppermute | solution.py:314
  35.7 0.4 collective-permute-start.14
  36.1 1.2 %collective-permute-start.12 = (f32[64,384]{1,0:T(8,128)S(1)}, f32[64,384]{1,0:T(8,128)S(1)}, u32[]{:S(2)}, u32[]{:S(2)}) collective-permute-start(f32[64,384]{1,0:T(8,128)S(1)} %get-tuple-element.60), channel_id=1, source_target_pairs={{0,8},{4,12},{8,0},{12,4},{1,9},{5,13},{9,1},{13,5},{2,10},{6,14},... | collective-permute-start | bytes 294920 | tf_op jit(solution)/shard_map/ppermute | solution.py:273
  37.3 0.5 %finish.3.refs_3_ = f32[64,1536]{1,0:T(8,128)S(1)} custom-call(f32[16,384]{1,0:T(8,128)S(1)} %get-tuple-element.62.refs_0_, f32[64,384]{1,0:T(8,128)S(1)} %get-tuple-element.49.refs_4_.refs_1_, f32[64,384]{1,0:T(8,128)S(1)} %collective-permute-done.7.refs_5_.refs_2_, f32[32,384]{1,0:T(8,128)S(1)} %pad_maximum_fusion.refs_3_, ...), custom_call_target="tpu_custom_call" | custom-call | flops 393216 | bytes 1056768 | tf_op jit(solution)/shard_map/finish/pallas_call | solution.py:236
  37.8 2.4 %collective-permute-done.13.refs_1_ = f32[64,384]{1,0:T(8,128)S(1)} collective-permute-done((f32[64,384]{1,0:T(8,128)S(1)}, f32[64,384]{1,0:T(8,128)S(1)}, u32[]{:S(2)}, u32[]{:S(2)}) %collective-permute-start.13) | collective-permute-done | bytes 98336 | tf_op jit(solution)/shard_map/ppermute | solution.py:314
  40.2 0.7 %collective-permute-done.14.refs_2_ = f32[64,384]{1,0:T(8,128)S(1)} collective-permute-done((f32[64,384]{1,0:T(8,128)S(1)}, f32[64,384]{1,0:T(8,128)S(1)}, u32[]{:S(2)}, u32[]{:S(2)}) %collective-permute-start.14) | collective-permute-done | bytes 98336 | tf_op jit(solution)/shard_map/ppermute | solution.py:314
  40.9 0.2 finish.4.refs_3_
  41.1 0.6 %collective-permute-done.12.refs_2_ = f32[64,384]{1,0:T(8,128)S(1)} collective-permute-done((f32[64,384]{1,0:T(8,128)S(1)}, f32[64,384]{1,0:T(8,128)S(1)}, u32[]{:S(2)}, u32[]{:S(2)}) %collective-permute-start.12) | collective-permute-done | bytes 98336 | tf_op jit(solution)/shard_map/ppermute | solution.py:273
  41.7 0.9 %finish.5 = f32[64,1536]{1,0:T(8,128)} custom-call(f32[16,384]{1,0:T(8,128)S(1)} %add.10.refs_0_, f32[64,384]{1,0:T(8,128)S(1)} %get-tuple-element.59.refs_1_, f32[64,384]{1,0:T(8,128)S(1)} %collective-permute-done.12.refs_2_, f32[64,1536]{1,0:T(8,128)S(1)} %finish.4.refs_3_), custom_call_target="tpu_custom_call" | custom-call | flops 393216 | bytes 1007616 | tf_op jit(solution)/shard_map/finish/pallas_call | solution.py:236
  (28 shorter events, 0.5 us)
Async XLA Ops:
  0.0 14.0 %collective-permute-start.2 = (f32[384,384]{1,0:T(8,128)}, f32[384,384]{1,0:T(8,128)S(1)}, u32[]{:S(2)}, u32[]{:S(2)}) collective-permute-start(f32[384,384]{1,0:T(8,128)} %refs_3_.3), channel_id=1, source_target_pairs={{0,4},{1,2},{2,1},{3,7},{4,0},{5,6},{6,5},{7,3},{8,12},{9,10},{10,... | collective-permute-start | bytes 1769480 | tf_op jit(solution)/shard_map/ppermute | solution.py:270
  0.5 18.0 %collective-permute-start.4 = (f32[384,384]{1,0:T(8,128)}, f32[384,384]{1,0:T(8,128)S(1)}, u32[]{:S(2)}, u32[]{:S(2)}) collective-permute-start(f32[384,384]{1,0:T(8,128)} %refs_3_.3), channel_id=1, source_target_pairs={{0,1},{1,0},{2,3},{3,2},{4,5},{5,4},{6,7},{7,6},{8,9},{9,8},{10,11... | collective-permute-start | bytes 1769480 | tf_op jit(solution)/shard_map/ppermute | solution.py:270
  4.6 2.7 %copy-start.3 = (s32[32,16]{0,1:T(8,128)S(1)}, s32[32,16]{0,1:T(8,128)}, u32[]{:S(2)}) copy-start(s32[32,16]{0,1:T(8,128)} %param.7) | copy-start | bytes 6148
  4.6 8.8 %copy-start = (f32[384,384]{1,0:T(8,128)S(1)}, f32[384,384]{1,0:T(8,128)}, u32[]{:S(2)}) copy-start(f32[384,384]{1,0:T(8,128)} %refs_3_.3) | copy-start | bytes 1769476
  5.7 6.1 %collective-permute-start = (f32[64,768]{1,0:T(8,128)S(1)}, f32[64,768]{1,0:T(8,128)S(1)}, u32[]{:S(2)}, u32[]{:S(2)}) collective-permute-start(f32[64,768]{1,0:T(8,128)S(1)} %get-tuple-element.65), channel_id=1, source_target_pairs={{0,8},{4,12},{8,0},{12,4},{1,9},{5,13},{9,1},{13,5},{2,10},{6,14},... | collective-permute-start | bytes 589832 | tf_op jit(solution)/shard_map/ppermute | solution.py:273
  7.3 0.7 %copy-start.1 = (s32[16,16]{1,0:T(8,128)S(1)}, s32[16,16]{1,0:T(8,128)}, u32[]{:S(2)}) copy-start(s32[16,16]{1,0:T(8,128)} %refs_2_.1) | copy-start | bytes 3076
  7.4 0.7 %copy-start.2 = (s32[16]{0:T(128)S(1)}, s32[16]{0:T(128)}, u32[]{:S(2)}) copy-start(s32[16]{0:T(128)} %refs_3_.2) | copy-start | bytes 196
  11.9 1.5 %collective-permute-start.1 = (f32[128,384]{1,0:T(8,128)S(1)}, f32[128,384]{1,0:T(8,128)S(1)}, u32[]{:S(2)}, u32[]{:S(2)}) collective-permute-start(f32[128,384]{1,0:T(8,128)S(1)} %get-tuple-element.40), channel_id=1, source_target_pairs={{0,4},{4,0},{8,12},{12,8},{1,5},{5,1},{9,13},{13,9},{2,6},{6,2},{1... | collective-permute-start | bytes 589832 | tf_op jit(solution)/shard_map/ppermute | solution.py:273
  14.1 16.8 %collective-permute-start.3 = (f32[384,384]{1,0:T(8,128)S(1)}, f32[384,384]{1,0:T(8,128)S(1)}, u32[]{:S(2)}, u32[]{:S(2)}) collective-permute-start(f32[384,384]{1,0:T(8,128)S(1)} %pick.1), channel_id=1, source_target_pairs={{0,1},{1,0},{2,3},{3,2},{4,5},{5,4},{6,7},{7,6},{8,9},{9,8},{10,11... | collective-permute-start | bytes 1769480 | tf_op jit(solution)/shard_map/ppermute | solution.py:270
  18.4 12.5 %collective-permute-start.5 = (f32[384,384]{1,0:T(8,128)S(1)}, f32[384,384]{1,0:T(8,128)S(1)}, u32[]{:S(2)}, u32[]{:S(2)}) collective-permute-start(f32[384,384]{1,0:T(8,128)S(1)} %collective-permute-done.4.refs_2_), channel_id=1, source_target_pairs={{0,4},{1,2},{2,1},{3,7},{4,0},{5,6},{6,5},{7,3},{8,12},{9,10},{10,... | collective-permute-start | bytes 1769480 | tf_op jit(solution)/shard_map/ppermute | solution.py:270
  19.4 3.8 %collective-permute-start.8 = (f32[128,768]{1,0:T(8,128)S(1)}, f32[128,768]{1,0:T(8,128)S(1)}, u32[]{:S(2)}, u32[]{:S(2)}) collective-permute-start(f32[128,768]{1,0:T(8,128)S(1)} %get-tuple-element.54), channel_id=1, source_target_pairs={{0,4},{4,0},{8,12},{12,8},{1,5},{5,1},{9,13},{13,9},{2,6},{6,2},{1... | collective-permute-start | bytes 1179656 | tf_op jit(solution)/shard_map/ppermute | solution.py:273
  19.9 1.6 %collective-permute-start.6 = (f32[128,384]{1,0:T(8,128)S(1)}, f32[128,384]{1,0:T(8,128)S(1)}, u32[]{:S(2)}, u32[]{:S(2)}) collective-permute-start(f32[128,384]{1,0:T(8,128)S(1)} %get-tuple-element.48), channel_id=1, source_target_pairs={{0,4},{4,0},{8,12},{12,8},{1,5},{5,1},{9,13},{13,9},{2,6},{6,2},{1... | collective-permute-start | bytes 589832 | tf_op jit(solution)/shard_map/ppermute | solution.py:273
  21.6 9.3 %collective-permute-start.7 = (f32[64,384]{1,0:T(8,128)S(1)}, f32[64,384]{1,0:T(8,128)S(1)}, u32[]{:S(2)}, u32[]{:S(2)}) collective-permute-start(f32[64,384]{1,0:T(8,128)S(1)} %get-tuple-element.50), channel_id=1, source_target_pairs={{0,8},{4,12},{8,0},{12,4},{1,9},{5,13},{9,1},{13,5},{2,10},{6,14},... | collective-permute-start | bytes 294920 | tf_op jit(solution)/shard_map/ppermute | solution.py:273
  23.2 7.7 %collective-permute-start.9 = (f32[64,768]{1,0:T(8,128)S(1)}, f32[64,768]{1,0:T(8,128)S(1)}, u32[]{:S(2)}, u32[]{:S(2)}) collective-permute-start(f32[64,768]{1,0:T(8,128)S(1)} %get-tuple-element.56), channel_id=1, source_target_pairs={{0,8},{4,12},{8,0},{12,4},{1,9},{5,13},{9,1},{13,5},{2,10},{6,14},... | collective-permute-start | bytes 589832 | tf_op jit(solution)/shard_map/ppermute | solution.py:273
  31.3 1.7 %collective-permute-start.11 = (f32[128,384]{1,0:T(8,128)S(1)}, f32[128,384]{1,0:T(8,128)S(1)}, u32[]{:S(2)}, u32[]{:S(2)}) collective-permute-start(f32[128,384]{1,0:T(8,128)S(1)} %corner.2.refs_3_), channel_id=1, source_target_pairs={{0,4},{4,0},{8,12},{12,8},{1,5},{5,1},{9,13},{13,9},{2,6},{6,2},{1... | collective-permute-start | bytes 589832 | tf_op jit(solution)/shard_map/ppermute | solution.py:273
  32.1 4.0 %collective-permute-start.10 = (f32[128,384]{1,0:T(8,128)S(1)}, f32[128,384]{1,0:T(8,128)S(1)}, u32[]{:S(2)}, u32[]{:S(2)}) collective-permute-start(f32[128,384]{1,0:T(8,128)S(1)} %last.2.refs_6_), channel_id=1, source_target_pairs={{0,4},{4,0},{8,12},{12,8},{1,5},{5,1},{9,13},{13,9},{2,6},{6,2},{1... | collective-permute-start | bytes 589832 | tf_op jit(solution)/shard_map/ppermute | solution.py:273
  33.1 7.1 %collective-permute-start.13 = (f32[64,384]{1,0:T(8,128)S(1)}, f32[64,384]{1,0:T(8,128)S(1)}, u32[]{:S(2)}, u32[]{:S(2)}) collective-permute-start(f32[64,384]{1,0:T(8,128)S(1)} %get-tuple-element.58.refs_3_), channel_id=1, source_target_pairs={{0,1},{1,8},{2,11},{3,2},{4,5},{5,12},{6,15},{7,6},{8,9},{9,0},{10... | collective-permute-start | bytes 294920 | tf_op jit(solution)/shard_map/ppermute | solution.py:314
  35.7 5.2 %collective-permute-start.14 = (f32[64,384]{1,0:T(8,128)S(1)}, f32[64,384]{1,0:T(8,128)S(1)}, u32[]{:S(2)}, u32[]{:S(2)}) collective-permute-start(f32[64,384]{1,0:T(8,128)S(1)} %get-tuple-element.57.refs_2_), channel_id=1, source_target_pairs={{0,1},{1,0},{2,3},{3,2},{4,5},{5,4},{6,7},{7,6},{8,9},{9,8},{10,11... | collective-permute-start | bytes 294920 | tf_op jit(solution)/shard_map/ppermute | solution.py:314
  36.1 5.6 %collective-permute-start.12 = (f32[64,384]{1,0:T(8,128)S(1)}, f32[64,384]{1,0:T(8,128)S(1)}, u32[]{:S(2)}, u32[]{:S(2)}) collective-permute-start(f32[64,384]{1,0:T(8,128)S(1)} %get-tuple-element.60), channel_id=1, source_target_pairs={{0,8},{4,12},{8,0},{12,4},{1,9},{5,13},{9,1},{13,5},{2,10},{6,14},... | collective-permute-start | bytes 294920 | tf_op jit(solution)/shard_map/ppermute | solution.py:273
